TPU v7x, 32 devices: a whole 2x2x4 slice. The times are simulated.
32 devices in a mesh: member: 8 (over z, core), band: 4 (over y, x).
Axes of the slice: x: 2, y: 2, z: 4, core: 2. Of those that a mesh axis runs over, the one named last changes fastest.
Arguments:
- ensemble: bfloat16 [8, 2, 16, 16, 1440], P('member', None, None, 'band'), may hold values from -6 to 6
- member_weight: float32 [8], replicated, may hold values from 0.5 to 2
- member_of_slot: int32 [8], P('member'), may hold values from 0 to 7, each once
- halfwidth: int32 [16], replicated, may hold values from 1 to 4, as said below
- static_root: float32 [16, 16], replicated, may hold values from -1.5 to 1.5
- innovation: bfloat16 [2, 16, 16, 1440], P(None, None, 'band'), may hold values from -6 to 6
- precision: bfloat16 [16, 16, 1440], P(None, 'band'), may hold values from 0.1 to 3
Outputs:
- control_members: float32 [8, 16, 16, 1440], P('member', None, 'band')
- control_static: float32 [16, 16, 1440], P(None, 'band')
- increment: float32 [2, 16, 16, 1440], P(None, 'member', 'band')
Inputs may be any that keep to these rules, and one draw needn't show every extreme that they name: `member_of_slot`: each member appears in exactly one slot. `halfwidth`: some level has a half-width of exactly 4.
All inputs are finite; a program needn't handle non-finite values.
Results may differ from a plain program's by a relative error of at most 0.0062.
Values may be sent and summed in bfloat16 or wider, within the bound.
No kernel may reach another device: no remote copies, remote signals or barrier semaphores. Data moves between devices by JAX's collectives and lax.ppermute only.
A program may use at most 64 MiB of HBM per device.

v0:
```python
import math

import jax
import jax.numpy as jnp
from jax import lax
from jax.sharding import PartitionSpec as P

ITERS = 2
HMAX = 4
LREACH = 18


ensemble_share = 0.8
static_share = 0.6
length_scale = 6.0


def with_halo(block, sides, width):
    for axis, dim in sides:
        count = lax.axis_size(axis)
        forward = [(i, i + 1) for i in range(count - 1)]
        backward = [(target, source) for source, target in forward]
        low = lax.ppermute(
            lax.slice_in_dim(block, block.shape[dim] - width, None, axis=dim), axis, forward
        )
        high = lax.ppermute(lax.slice_in_dim(block, 0, width, axis=dim), axis, backward)
        block = jnp.concatenate([low, block, high], axis=dim)
    return block


def lon_kernel(reach, width):
    rows_index = jnp.arange(width + 2 * reach, dtype=jnp.int32)[:, None]
    cols_index = jnp.arange(width, dtype=jnp.int32)[None, :]
    distance = jnp.abs(rows_index - reach - cols_index).astype(jnp.float32)
    values = jnp.exp(-0.5 * (distance / length_scale) ** 2) / (
        length_scale * math.sqrt(2.0 * math.pi)
    )
    return jnp.where(distance <= reach, values, jnp.zeros_like(values)).astype(jnp.bfloat16)


def smooth_longitude(field, reach, blocks):
    width = field.shape[-1] // blocks
    pieces = field.reshape(field.shape[:-1] + (blocks, width))
    before = jnp.roll(pieces, 1, axis=-2)[..., width - reach :]
    after = jnp.roll(pieces, -1, axis=-2)[..., :reach]
    window = jnp.concatenate([before, pieces, after], axis=-1)
    kernel = lon_kernel(reach, width)
    result = jnp.einsum("...bm,mo->...bo", window, kernel, preferred_element_type=jnp.float32)
    return result.reshape(field.shape).astype(jnp.bfloat16)


def taper_weights(halfwidth, reach):
    offsets = jnp.abs(jnp.arange(-reach, reach + 1, dtype=jnp.int32)).astype(jnp.float32)
    spans = halfwidth.astype(jnp.float32)[:, None] + 1.0
    return jnp.maximum(1.0 - offsets[None, :] / spans, 0.0) / spans


def localize(field, taper):
    smoothed = smooth_longitude(field.astype(jnp.bfloat16), LREACH, 3)
    padded = with_halo(smoothed, (("band", 2),), HMAX)
    row_count = field.shape[2]
    summed = jnp.zeros(field.shape, jnp.float32)
    for offset in range(2 * HMAX + 1):
        summed = summed + taper[:, offset][None, :, None, None] * padded[
            :, :, offset : offset + row_count, :
        ].astype(jnp.float32)
    return summed


def local_dot(first_members, second_members, first_static, second_static, groups):
    return jnp.sum(first_members * second_members) + jnp.sum(first_static * second_static) / groups


def shards(ensemble, member_weight, member_of_slot, halfwidth, static_root, innovation, precision):
    member_count = member_weight.shape[0]
    picker = (member_of_slot[:, None] == jnp.arange(member_count, dtype=jnp.int32)[None, :]).astype(
        jnp.float32
    )
    scaled = jnp.sum(picker * member_weight[None, :], axis=1)
    taper = taper_weights(halfwidth, HMAX)
    precise = precision.astype(jnp.float32)
    groups = lax.axis_size("member")
    level_share = precision.shape[0] // groups
    first_level = lax.axis_index("member") * level_share

    def adjoint(weighted):
        folded = scaled[:, None, None, None] * jnp.sum(
            ensemble.astype(jnp.float32) * weighted[None], axis=1
        )
        grad_members = ensemble_share * localize(folded, taper)
        grad_static = static_share * jnp.einsum(
            "ql,qyx->lyx", static_root, jnp.sum(weighted, axis=0), precision=lax.Precision.HIGHEST
        )
        return (grad_members, grad_static)

    res_members, res_static = adjoint(precise[None] * innovation.astype(jnp.float32))
    dir_members, dir_static = (res_members, res_static)
    sol_members = jnp.zeros_like(res_members)
    sol_static = jnp.zeros_like(res_static)
    increment = jnp.zeros((), jnp.float32)
    norm_now = lax.psum(
        local_dot(res_members, res_members, res_static, res_static, groups), ("member", "band")
    )
    for iteration in range(ITERS):
        localized = localize(dir_members, taper)
        partial_image = ensemble_share * jnp.sum(
            scaled[:, None, None, None, None] * ensemble.astype(jnp.float32) * localized[:, None],
            axis=0,
        )
        summed = lax.psum(partial_image, "member")
        static = jnp.einsum("lq,qyx->lyx", static_root, dir_static, precision=lax.Precision.HIGHEST)
        image = summed + static_share * static[None]
        hessian_weighted = precise[None] * image
        hessian_grad_members, hessian_grad_static = adjoint(hessian_weighted)
        hes_members, hes_static, image = (
            dir_members + hessian_grad_members,
            dir_static + hessian_grad_static,
            image,
        )
        curvature = lax.psum(
            local_dot(dir_members, hes_members, dir_static, hes_static, groups), ("member", "band")
        )
        alpha = norm_now / curvature
        sol_members = sol_members + alpha * dir_members
        sol_static = sol_static + alpha * dir_static
        increment = increment + alpha * image
        res_members = res_members - alpha * hes_members
        res_static = res_static - alpha * hes_static
        if iteration + 1 < ITERS:
            norm_next = lax.psum(
                local_dot(res_members, res_members, res_static, res_static, groups),
                ("member", "band"),
            )
            ratio = norm_next / norm_now
            dir_members = res_members + ratio * dir_members
            dir_static = res_static + ratio * dir_static
            norm_now = norm_next
    increment = lax.dynamic_slice_in_dim(increment, first_level, level_share, 1)
    return (sol_members, sol_static, increment)


def solution(mesh):
    return jax.shard_map(
        shards,
        mesh=mesh,
        in_specs=(
            P("member", None, None, "band", None),
            P(),
            P("member"),
            P(),
            P(),
            P(None, None, "band", None),
            P(None, "band", None),
        ),
        out_specs=(
            P("member", None, "band", None),
            P(None, "band", None),
            P(None, "member", "band", None),
        ),
        check_vma=False,
    )
```

profile of v0, /device:TPU:0, one launch (start us, length us, event | category | flops | bytes accessed | tf_op | source)
XLA Modules:
  0.0 357.5 jit_solution(9064967949948783607)
XLA Ops:
  7.2 1.0 convert_element_type.373
  8.9 1.3 fusion.100
  10.1 1.6 fusion.13
  11.7 0.8 fusion.49
  12.9 0.9 convolution_convert_fusion.4
  14.2 4.9 %collective-permute-start = (bf16[1,16,4,1440]{3,1,2,0:T(8,128)(2,1)S(1)}, bf16[1,16,4,1440]{3,1,2,0:T(8,128)(2,1)S(1)}, u32[]{:S(2)}, u32[]{:S(2)}) collective-permute-start(bf16[1,16,4,1440]{3,1,2,0:T(8,128)(2,1)S(1)} %convert_element_type.380), channel_id=1, source_target_pairs={{0,1},{1,2},{2,3},{4,5},{5,6},{6,7},{8,9},{9,10},{10,11},{12,13},{... | collective-permute-start | bytes 552968 | tf_op jit(solution)/shard_map/ppermute | solution.py:23
  19.0 1.3 collective-permute-start.1
  20.5 2.6 collective-permute-done
  23.2 6.1 %collective-permute-done.1 = bf16[1,16,4,1440]{3,1,2,0:T(8,128)(2,1)S(1)} collective-permute-done((bf16[1,16,4,1440]{3,1,2,0:T(8,128)(2,1)S(1)}, bf16[1,16,4,1440]{3,1,2,0:T(8,128)(2,1)S(1)}, u32[]{:S(2)}, u32[]{:S(2)}) %collective-permute-start.1) | collective-permute-done | bytes 184352 | tf_op jit(solution)/shard_map/ppermute | solution.py:26
  29.4 0.4 multiply_convert_fusion
  30.1 0.9 convolution_convert_fusion.3
  31.4 3.4 collective-permute-start.2
  35.1 1.3 collective-permute-start.3
  36.4 1.8 collective-permute-done.2
  38.2 4.9 %collective-permute-done.3 = bf16[1,16,4,1440]{3,1,2,0:T(8,128)(2,1)S(1)} collective-permute-done((bf16[1,16,4,1440]{3,1,2,0:T(8,128)(2,1)S(1)}, bf16[1,16,4,1440]{3,1,2,0:T(8,128)(2,1)S(1)}, u32[]{:S(2)}, u32[]{:S(2)}) %collective-permute-start.3) | collective-permute-done | bytes 184352 | tf_op jit(solution)/shard_map/ppermute | solution.py:26
  43.2 0.4 add_bitcast_fusion.1
  43.9 1.8 fusion.10
  45.7 0.6 fusion.47
  46.3 0.5 fusion
  47.1 55.7 %all-reduce.4.cloned.1.call-done = f32[2,16,4,1440]{3,2,1,0:T(4,128)} async-done(((f32[2,16,4,1440]{3,2,1,0:T(4,128)}), f32[2,16,4,1440]{3,2,1,0:T(4,128)}) %all-reduce.4.cloned.1.call-update) | async-done | bytes 737296 | tf_op jit(solution)/shard_map/psum | solution.py:110
  102.7 1.7 multiply_reduce_fusion.1
  104.4 0.4 fusion.14
  104.8 0.8 fusion.46
  106.0 0.9 convolution_convert_fusion.2
  107.3 3.4 collective-permute-start.4
  110.7 1.3 collective-permute-start.5
  112.0 1.4 fusion.42
  114.7 4.7 %collective-permute-done.5 = bf16[1,16,4,1440]{3,1,2,0:T(8,128)(2,1)} collective-permute-done((bf16[1,16,4,1440]{3,1,2,0:T(8,128)(2,1)S(1)}, bf16[1,16,4,1440]{3,1,2,0:T(8,128)(2,1)}, u32[]{:S(2)}, u32[]{:S(2)}) %collective-permute-start.5) | collective-permute-done | bytes 184352 | tf_op jit(solution)/shard_map/ppermute | solution.py:26
  119.4 0.9 constant_dynamic-update-slice_fusion.10
  120.3 2.1 multiply_reduce_fusion.4
  123.8 38.9 %all-reduce = (f32[]{:T(128)}, f32[]{:T(128)}) all-reduce(f32[]{:T(128)S(6)} %add.217, f32[]{:T(128)S(6)} %add.238), channel_id=1, replica_groups=mesh['member'=8,'band'=4] {'member','band'}, use_global_device_ids=true, to_apply=%region_5.6 | all-reduce | flops 2 | bytes 16 | tf_op jit(solution)/shard_map/psum | solution.py:101
  164.0 0.7 multiply_reduce_fusion.2
  165.2 0.7 multiply_reduce_fusion.3
  166.5 41.3 %psum.45 = f32[]{:T(128)} all-reduce(f32[]{:T(128)S(6)} %add.239), channel_id=1, replica_groups=mesh['member'=8,'band'=4] {'member','band'}, use_global_device_ids=true, to_apply=%region_14.15 | all-reduce | flops 1 | bytes 8 | tf_op jit(solution)/shard_map/psum | solution.py:130
  209.1 0.8 fusion.132
  209.9 1.2 reshape.309
  211.2 0.9 convolution_convert_fusion.1
  212.1 0.9 copy.131
  212.9 1.2 convert_element_type.417
  214.2 4.2 %collective-permute-start.6 = (bf16[1,16,4,1440]{3,1,2,0:T(8,128)(2,1)S(1)}, bf16[1,16,4,1440]{3,1,2,0:T(8,128)(2,1)S(1)}, u32[]{:S(2)}, u32[]{:S(2)}) collective-permute-start(bf16[1,16,4,1440]{3,1,2,0:T(8,128)(2,1)S(1)} %convert_element_type.417), channel_id=1, source_target_pairs={{0,1},{1,2},{2,3},{4,5},{5,6},{6,7},{8,9},{9,10},{10,11},{12,13},{... | collective-permute-start | bytes 552968 | tf_op jit(solution)/shard_map/ppermute | solution.py:23
  218.4 1.3 collective-permute-start.7
  219.7 1.9 collective-permute-done.6
  221.6 5.1 %collective-permute-done.7 = bf16[1,16,4,1440]{3,1,2,0:T(8,128)(2,1)S(1)} collective-permute-done((bf16[1,16,4,1440]{3,1,2,0:T(8,128)(2,1)S(1)}, bf16[1,16,4,1440]{3,1,2,0:T(8,128)(2,1)S(1)}, u32[]{:S(2)}, u32[]{:S(2)}) %collective-permute-start.7) | collective-permute-done | bytes 184352 | tf_op jit(solution)/shard_map/ppermute | solution.py:26
  226.8 0.4 add_bitcast_fusion
  227.4 1.8 fusion.12
  229.3 0.5 fusion.3
  229.8 1.0 copy.133
  230.8 54.6 %all-reduce.6.cloned.1.call-done = f32[2,16,4,1440]{3,2,1,0:T(4,128)} async-done(((f32[2,16,4,1440]{3,2,1,0:T(4,128)}), f32[2,16,4,1440]{3,2,1,0:T(4,128)}) %all-reduce.6.cloned.1.call-update) | async-done | bytes 737296 | tf_op jit(solution)/shard_map/psum | solution.py:110
  285.4 1.8 multiply_reduce_fusion
  287.1 0.4 fusion.15
  287.5 0.5 copy-done.2
  288.0 0.8 fusion.44
  289.2 0.6 copy-done.27
  289.7 0.9 convolution_convert_fusion
  291.0 3.4 collective-permute-start.8
  294.4 1.3 collective-permute-start.9
  295.7 1.2 fusion.17
  297.7 5.4 %collective-permute-done.9 = bf16[1,16,4,1440]{3,1,2,0:T(8,128)(2,1)} collective-permute-done((bf16[1,16,4,1440]{3,1,2,0:T(8,128)(2,1)S(1)}, bf16[1,16,4,1440]{3,1,2,0:T(8,128)(2,1)}, u32[]{:S(2)}, u32[]{:S(2)}) %collective-permute-start.9) | collective-permute-done | bytes 184352 | tf_op jit(solution)/shard_map/ppermute | solution.py:26
  303.2 0.9 constant_dynamic-update-slice_fusion.18
  304.2 2.0 fusion.39
  306.8 38.7 %psum.47 = f32[]{:T(128)} all-reduce(f32[]{:T(128)S(6)} %add.262), channel_id=1, replica_groups=mesh['member'=8,'band'=4] {'member','band'}, use_global_device_ids=true, to_apply=%region_20.21 | all-reduce | flops 1 | bytes 8 | tf_op jit(solution)/shard_map/psum | solution.py:120
  346.8 1.6 fusion.92
  348.5 1.0 copy.144
  349.7 1.0 copy.143
  (113 shorter events, 5.0 us)
Async XLA Ops:
  7.2 38.6 %copy-start = (f32[16,16]{1,0:T(8,128)S(1)}, f32[16,16]{1,0:T(8,128)}, u32[]{:S(2)}) copy-start(f32[16,16]{1,0:T(8,128)} %param.11) | copy-start | bytes 3076
  7.2 3.0 copy-start.1
  7.2 95.5 %all-reduce.4.cloned.1.call-start = ((), (), s32[]{:S(2)}) async-start(), calls=%async_computation | async-start | bytes 1572864 | tf_op jit(solution)/shard_map/psum | solution.py:110
  12.9 93.1 %copy-start.25 = (s32[516]{0:T(1024)}, s32[516]{0:T(1024)S(1)}, u32[]{:S(2)}) copy-start(s32[516]{0:T(1024)S(1)} %iota_add_fusion) | copy-start | bytes 6196
  13.8 6.6 %copy-start.28 = (s32[16]{0:T(128)S(1)}, s32[16]{0:T(128)}, u32[]{:S(2)}) copy-start(s32[16]{0:T(128)} %param.10) | copy-start | bytes 196
  14.2 9.0 %collective-permute-start = (bf16[1,16,4,1440]{3,1,2,0:T(8,128)(2,1)S(1)}, bf16[1,16,4,1440]{3,1,2,0:T(8,128)(2,1)S(1)}, u32[]{:S(2)}, u32[]{:S(2)}) collective-permute-start(bf16[1,16,4,1440]{3,1,2,0:T(8,128)(2,1)S(1)} %convert_element_type.380), channel_id=1, source_target_pairs={{0,1},{1,2},{2,3},{4,5},{5,6},{6,7},{8,9},{9,10},{10,11},{12,13},{... | collective-permute-start | bytes 552968 | tf_op jit(solution)/shard_map/ppermute | solution.py:23
  19.0 10.3 %collective-permute-start.1 = (bf16[1,16,4,1440]{3,1,2,0:T(8,128)(2,1)S(1)}, bf16[1,16,4,1440]{3,1,2,0:T(8,128)(2,1)S(1)}, u32[]{:S(2)}, u32[]{:S(2)}) collective-permute-start(bf16[1,16,4,1440]{3,1,2,0:T(8,128)(2,1)S(1)} %convert_element_type.380), channel_id=1, source_target_pairs={{1,0},{2,1},{3,2},{5,4},{6,5},{7,6},{9,8},{10,9},{11,10},{13,12},{... | collective-permute-start | bytes 552968 | tf_op jit(solution)/shard_map/ppermute | solution.py:26
  20.5 22.7 %copy-start.4 = (f32[16]{0:T(128)}, f32[16]{0:T(128)S(1)}, u32[]{:S(2)}) copy-start(f32[16]{0:T(128)S(1)} %get-tuple-element.60) | copy-start | bytes 196
  20.5 22.7 %copy-start.7 = (f32[16]{0:T(128)}, f32[16]{0:T(128)S(1)}, u32[]{:S(2)}) copy-start(f32[16]{0:T(128)S(1)} %get-tuple-element.61) | copy-start | bytes 196
  20.5 22.7 %copy-start.10 = (f32[16]{0:T(128)}, f32[16]{0:T(128)S(1)}, u32[]{:S(2)}) copy-start(f32[16]{0:T(128)S(1)} %get-tuple-element.62) | copy-start | bytes 196
  20.5 22.7 %copy-start.13 = (f32[16]{0:T(128)}, f32[16]{0:T(128)S(1)}, u32[]{:S(2)}) copy-start(f32[16]{0:T(128)S(1)} %get-tuple-element.63) | copy-start | bytes 196
  20.5 22.7 %copy-start.16 = (f32[16]{0:T(128)}, f32[16]{0:T(128)S(1)}, u32[]{:S(2)}) copy-start(f32[16]{0:T(128)S(1)} %get-tuple-element.64) | copy-start | bytes 196
  20.5 22.7 %copy-start.19 = (f32[16]{0:T(128)}, f32[16]{0:T(128)S(1)}, u32[]{:S(2)}) copy-start(f32[16]{0:T(128)S(1)} %get-tuple-element.65) | copy-start | bytes 196
  20.5 22.7 %copy-start.22 = (f32[16]{0:T(128)}, f32[16]{0:T(128)S(1)}, u32[]{:S(2)}) copy-start(f32[16]{0:T(128)S(1)} %get-tuple-element.66) | copy-start | bytes 196
  31.0 3.8 %copy-start.3 = (bf16[2,16,4,1440]{3,2,1,0:T(4,128)(2,1)S(1)}, bf16[2,16,4,1440]{3,2,1,0:T(4,128)(2,1)}, u32[]{:S(2)}) copy-start(bf16[2,16,4,1440]{3,2,1,0:T(4,128)(2,1)} %param.12) | copy-start | bytes 1105924
  31.4 6.7 %collective-permute-start.2 = (bf16[1,16,4,1440]{3,1,2,0:T(8,128)(2,1)S(1)}, bf16[1,16,4,1440]{3,1,2,0:T(8,128)(2,1)S(1)}, u32[]{:S(2)}, u32[]{:S(2)}) collective-permute-start(bf16[1,16,4,1440]{3,1,2,0:T(8,128)(2,1)S(1)} %convert_element_type.392), channel_id=1, source_target_pairs={{0,1},{1,2},{2,3},{4,5},{5,6},{6,7},{8,9},{9,10},{10,11},{12,13},{... | collective-permute-start | bytes 552968 | tf_op jit(solution)/shard_map/ppermute | solution.py:23
  35.1 8.0 %collective-permute-start.3 = (bf16[1,16,4,1440]{3,1,2,0:T(8,128)(2,1)S(1)}, bf16[1,16,4,1440]{3,1,2,0:T(8,128)(2,1)S(1)}, u32[]{:S(2)}, u32[]{:S(2)}) collective-permute-start(bf16[1,16,4,1440]{3,1,2,0:T(8,128)(2,1)S(1)} %convert_element_type.392), channel_id=1, source_target_pairs={{1,0},{2,1},{3,2},{5,4},{6,5},{7,6},{9,8},{10,9},{11,10},{13,12},{... | collective-permute-start | bytes 552968 | tf_op jit(solution)/shard_map/ppermute | solution.py:26
  45.7 239.7 %all-reduce.6.cloned.1.call-start = ((), (), s32[]{:S(2)}) async-start(), calls=%async_computation.1 | async-start | bytes 1572864 | tf_op jit(solution)/shard_map/psum | solution.py:110
  107.3 7.4 %collective-permute-start.4 = (bf16[1,16,4,1440]{3,1,2,0:T(8,128)(2,1)S(1)}, bf16[1,16,4,1440]{3,1,2,0:T(8,128)(2,1)S(1)}, u32[]{:S(2)}, u32[]{:S(2)}) collective-permute-start(bf16[1,16,4,1440]{3,1,2,0:T(8,128)(2,1)S(1)} %convert_element_type.405), channel_id=1, source_target_pairs={{0,1},{1,2},{2,3},{4,5},{5,6},{6,7},{8,9},{9,10},{10,11},{12,13},{... | collective-permute-start | bytes 552968 | tf_op jit(solution)/shard_map/ppermute | solution.py:23
  110.7 8.7 %collective-permute-start.5 = (bf16[1,16,4,1440]{3,1,2,0:T(8,128)(2,1)S(1)}, bf16[1,16,4,1440]{3,1,2,0:T(8,128)(2,1)}, u32[]{:S(2)}, u32[]{:S(2)}) collective-permute-start(bf16[1,16,4,1440]{3,1,2,0:T(8,128)(2,1)S(1)} %convert_element_type.405), channel_id=1, source_target_pairs={{1,0},{2,1},{3,2},{5,4},{6,5},{7,6},{9,8},{10,9},{11,10},{13,12},{... | collective-permute-start | bytes 552968 | tf_op jit(solution)/shard_map/ppermute | solution.py:26
  209.9 1.3 copy-start.26
  214.1 12.6 %copy-start.5 = (f32[16]{0:T(128)S(1)}, f32[16]{0:T(128)}, u32[]{:S(2)}) copy-start(f32[16]{0:T(128)} %copy-done.4) | copy-start | bytes 196
  214.1 12.6 %copy-start.8 = (f32[16]{0:T(128)S(1)}, f32[16]{0:T(128)}, u32[]{:S(2)}) copy-start(f32[16]{0:T(128)} %copy-done.7) | copy-start | bytes 196
  214.1 12.6 %copy-start.11 = (f32[16]{0:T(128)S(1)}, f32[16]{0:T(128)}, u32[]{:S(2)}) copy-start(f32[16]{0:T(128)} %copy-done.10) | copy-start | bytes 196
  214.1 12.6 %copy-start.14 = (f32[16]{0:T(128)S(1)}, f32[16]{0:T(128)}, u32[]{:S(2)}) copy-start(f32[16]{0:T(128)} %copy-done.13) | copy-start | bytes 196
  214.2 12.6 %copy-start.17 = (f32[16]{0:T(128)S(1)}, f32[16]{0:T(128)}, u32[]{:S(2)}) copy-start(f32[16]{0:T(128)} %copy-done.16) | copy-start | bytes 196
  214.2 12.6 %copy-start.20 = (f32[16]{0:T(128)S(1)}, f32[16]{0:T(128)}, u32[]{:S(2)}) copy-start(f32[16]{0:T(128)} %copy-done.19) | copy-start | bytes 196
  214.2 12.6 %copy-start.23 = (f32[16]{0:T(128)S(1)}, f32[16]{0:T(128)}, u32[]{:S(2)}) copy-start(f32[16]{0:T(128)} %copy-done.22) | copy-start | bytes 196
  214.2 7.4 %collective-permute-start.6 = (bf16[1,16,4,1440]{3,1,2,0:T(8,128)(2,1)S(1)}, bf16[1,16,4,1440]{3,1,2,0:T(8,128)(2,1)S(1)}, u32[]{:S(2)}, u32[]{:S(2)}) collective-permute-start(bf16[1,16,4,1440]{3,1,2,0:T(8,128)(2,1)S(1)} %convert_element_type.417), channel_id=1, source_target_pairs={{0,1},{1,2},{2,3},{4,5},{5,6},{6,7},{8,9},{9,10},{10,11},{12,13},{... | collective-permute-start | bytes 552968 | tf_op jit(solution)/shard_map/ppermute | solution.py:23
  218.4 8.3 %collective-permute-start.7 = (bf16[1,16,4,1440]{3,1,2,0:T(8,128)(2,1)S(1)}, bf16[1,16,4,1440]{3,1,2,0:T(8,128)(2,1)S(1)}, u32[]{:S(2)}, u32[]{:S(2)}) collective-permute-start(bf16[1,16,4,1440]{3,1,2,0:T(8,128)(2,1)S(1)} %convert_element_type.417), channel_id=1, source_target_pairs={{1,0},{2,1},{3,2},{5,4},{6,5},{7,6},{9,8},{10,9},{11,10},{13,12},{... | collective-permute-start | bytes 552968 | tf_op jit(solution)/shard_map/ppermute | solution.py:26
  287.1 0.9 copy-start.2
  289.1 0.7 copy-start.27
  291.0 6.6 %collective-permute-start.8 = (bf16[1,16,4,1440]{3,1,2,0:T(8,128)(2,1)S(1)}, bf16[1,16,4,1440]{3,1,2,0:T(8,128)(2,1)S(1)}, u32[]{:S(2)}, u32[]{:S(2)}) collective-permute-start(bf16[1,16,4,1440]{3,1,2,0:T(8,128)(2,1)S(1)} %convert_element_type.430), channel_id=1, source_target_pairs={{0,1},{1,2},{2,3},{4,5},{5,6},{6,7},{8,9},{9,10},{10,11},{12,13},{... | collective-permute-start | bytes 552968 | tf_op jit(solution)/shard_map/ppermute | solution.py:23
  294.4 8.7 %collective-permute-start.9 = (bf16[1,16,4,1440]{3,1,2,0:T(8,128)(2,1)S(1)}, bf16[1,16,4,1440]{3,1,2,0:T(8,128)(2,1)}, u32[]{:S(2)}, u32[]{:S(2)}) collective-permute-start(bf16[1,16,4,1440]{3,1,2,0:T(8,128)(2,1)S(1)} %convert_element_type.430), channel_id=1, source_target_pairs={{1,0},{2,1},{3,2},{5,4},{6,5},{7,6},{9,8},{10,9},{11,10},{13,12},{... | collective-permute-start | bytes 552968 | tf_op jit(solution)/shard_map/ppermute | solution.py:26
  297.0 7.1 %copy-start.6 = (f32[16]{0:T(128)S(1)}, f32[16]{0:T(128)}, u32[]{:S(2)}) copy-start(f32[16]{0:T(128)} %copy-done.4) | copy-start | bytes 196
  297.0 7.1 %copy-start.9 = (f32[16]{0:T(128)S(1)}, f32[16]{0:T(128)}, u32[]{:S(2)}) copy-start(f32[16]{0:T(128)} %copy-done.7) | copy-start | bytes 196
  297.0 7.2 %copy-start.12 = (f32[16]{0:T(128)S(1)}, f32[16]{0:T(128)}, u32[]{:S(2)}) copy-start(f32[16]{0:T(128)} %copy-done.10) | copy-start | bytes 196
  297.0 7.2 %copy-start.15 = (f32[16]{0:T(128)S(1)}, f32[16]{0:T(128)}, u32[]{:S(2)}) copy-start(f32[16]{0:T(128)} %copy-done.13) | copy-start | bytes 196
  297.0 7.2 %copy-start.18 = (f32[16]{0:T(128)S(1)}, f32[16]{0:T(128)}, u32[]{:S(2)}) copy-start(f32[16]{0:T(128)} %copy-done.16) | copy-start | bytes 196
  297.0 7.2 %copy-start.21 = (f32[16]{0:T(128)S(1)}, f32[16]{0:T(128)}, u32[]{:S(2)}) copy-start(f32[16]{0:T(128)} %copy-done.19) | copy-start | bytes 196
  297.0 7.2 %copy-start.24 = (f32[16]{0:T(128)S(1)}, f32[16]{0:T(128)}, u32[]{:S(2)}) copy-start(f32[16]{0:T(128)} %copy-done.22) | copy-start | bytes 196
Sparse Core Ops, SparseCore 0:
  45.8 56.8 all-reduce.3
  229.4 55.9 all-reduce.5
where the time goes:
time: 359 us; the launch traced here: 358 us
  waiting for transfers between devices  143 us (40%)
  blocking collectives  119 us (33%)
  starting transfers between devices  25.7 us (7%)
  between operations  24.5 us (7%)
  other arithmetic  23.5 us (7%)
  local copies, waits for them, and re-layouts  13.4 us (4%)
  matrix products  8.48 us (2%)
    psum x2, waiting for transfers between devices, shards(): summed = lax.psum(partial_image, 'member')  110 us
    psum x2, blocking collectives, shards(): lax.psum(local_dot(res_members, res_members, res_static, res_static, grou...  80.3 us
    psum x1, blocking collectives, shards(): lax.psum(local_dot(dir_members, hes_members, dir_static, hes_static, grou...  38.7 us
    ppermute x5, waiting for transfers between devices, with_halo(): lax.ppermute(lax.slice_in_dim(block, 0, width, axis=dim), axis, backward)  26.2 us
    ppermute x5, starting transfers between devices, with_halo(): lax.ppermute(lax.slice_in_dim(block, block.shape[dim] - width, None, axis...  19.2 us
  transfers between devices with their start and end apart: 12, of which 10 were waited for; matrix products, arithmetic and copies ran while one was open for 2% of the time, Pallas kernels for 0%

commit v1 on v0

v1 whole, which is shorter than its diff:
```python
import math

import jax
import jax.numpy as jnp
from jax import lax
from jax.experimental import pallas as pl
from jax.experimental.pallas import tpu as pltpu
from jax.sharding import PartitionSpec as P

HMAX = 4
LREACH = 18
REACHES = 4
LANES = 128
BOTH = ("member", "band")

ensemble_share = 0.8
static_share = 0.6
length_scale = 6.0


def round_up(value, step):
    return -(-value // step) * step


def with_halo(block, dim, width):
    count = lax.axis_size("band")
    forward = [(i, i + 1) for i in range(count - 1)]
    backward = [(target, source) for source, target in forward]
    low = lax.ppermute(
        lax.slice_in_dim(block, block.shape[dim] - width, None, axis=dim), "band", forward
    )
    high = lax.ppermute(lax.slice_in_dim(block, 0, width, axis=dim), "band", backward)
    return jnp.concatenate([low, block, high], axis=dim)


def kernel_values(distance):
    values = jnp.exp(-0.5 * (distance / length_scale) ** 2) / (
        length_scale * math.sqrt(2.0 * math.pi)
    )
    return jnp.where(distance <= LREACH, values, jnp.zeros_like(values)).astype(jnp.bfloat16)


def lon_kernel(reach, width):
    rows_index = jnp.arange(width + 2 * reach, dtype=jnp.int32)[:, None]
    cols_index = jnp.arange(width, dtype=jnp.int32)[None, :]
    return kernel_values(jnp.abs(rows_index - reach - cols_index).astype(jnp.float32))


def ring_kernel(width, padded):
    rows_index = jnp.arange(padded, dtype=jnp.int32)[:, None]
    cols_index = jnp.arange(padded, dtype=jnp.int32)[None, :]
    apart = jnp.abs(rows_index - cols_index)
    distance = jnp.minimum(apart, width - apart).astype(jnp.float32)
    inside = (rows_index < width) & (cols_index < width)
    return jnp.where(inside, kernel_values(distance), 0).astype(jnp.bfloat16)


def smooth_longitude(field, reach, blocks):
    width = field.shape[-1] // blocks
    pieces = field.reshape(field.shape[:-1] + (blocks, width))
    before = jnp.roll(pieces, 1, axis=-2)[..., width - reach :]
    after = jnp.roll(pieces, -1, axis=-2)[..., :reach]
    window = jnp.concatenate([before, pieces, after], axis=-1)
    kernel = lon_kernel(reach, width)
    result = jnp.einsum("...bm,mo->...bo", window, kernel, preferred_element_type=jnp.float32)
    return result.reshape(field.shape).astype(jnp.bfloat16)


def taper_weights(halfwidth, reach):
    offsets = jnp.abs(jnp.arange(-reach, reach + 1, dtype=jnp.int32)).astype(jnp.float32)
    spans = halfwidth.astype(jnp.float32)[:, None] + 1.0
    return jnp.maximum(1.0 - offsets[None, :] / spans, 0.0) / spans


def localize(field, taper):
    smoothed = smooth_longitude(field.astype(jnp.bfloat16), LREACH, 3)
    padded = with_halo(smoothed, 1, HMAX)
    row_count = field.shape[1]
    summed = jnp.zeros(field.shape, jnp.float32)
    for offset in range(2 * HMAX + 1):
        summed = summed + taper[:, offset][:, None, None] * padded[
            :, offset : offset + row_count, :
        ].astype(jnp.float32)
    return summed


def taper_matrix(halfwidth, bands, rows, copies):
    levels = halfwidth.shape[0]
    per_copy = bands * levels * rows
    index = jnp.arange(copies * per_copy, dtype=jnp.int32)
    copy = index // per_copy
    band = index // (levels * rows) % bands
    level = index // rows % levels
    latitude = band * rows + index % rows
    spans = halfwidth.astype(jnp.float32)[level][:, None] + 1.0
    apart = jnp.abs(latitude[:, None] - latitude[None, :]).astype(jnp.float32)
    same = (copy[:, None] == copy[None, :]) & (level[:, None] == level[None, :])
    near = jnp.maximum(1.0 - apart / spans, 0.0) / spans
    full = jnp.where(same, near, 0.0)
    high = full.astype(jnp.bfloat16)
    low = (full - high.astype(jnp.float32)).astype(jnp.bfloat16)
    return jnp.stack([high, low])


def windows(field, count, halo, padded, fill):
    lon = field.shape[-1]
    share = lon // count
    ring = jnp.concatenate([field[..., lon - halo :], field, field[..., :halo]], axis=-1)
    tail = jnp.broadcast_to(fill, field.shape[:-1] + (padded - share - 2 * halo,)).astype(field.dtype)
    pieces = []
    for piece in range(count):
        start = piece * share
        pieces.append(
            jnp.concatenate(
                [ring[..., start + halo : start + 2 * halo + share], ring[..., start : start + halo], tail],
                axis=-1,
            )
        )
    return jnp.stack(pieces)


def exchange_bands(blocks):
    count = blocks.shape[0]
    if count > 8:
        return lax.all_to_all(blocks, "band", 0, 0, tiled=True)
    here = lax.axis_index("band")
    arrived = [lax.dynamic_index_in_dim(blocks, here, 0, keepdims=False)]
    for shift in range(1, count):
        outgoing = lax.dynamic_index_in_dim(blocks, lax.rem(here + shift, count), 0, keepdims=False)
        arrived.append(
            lax.ppermute(outgoing, "band", [(i, (i + shift) % count) for i in range(count)])
        )
    ordered = []
    for source in range(count):
        block = arrived[0]
        for shift in range(1, count):
            block = jnp.where(lax.rem(here - source + count, count) == shift, arrived[shift], block)
        ordered.append(block)
    return jnp.stack(ordered)


def spread(field, ring, taper):
    copies = taper.shape[1]
    smoothed = jnp.dot(field.astype(jnp.bfloat16), ring, preferred_element_type=jnp.float32)
    smoothed = smoothed.astype(jnp.bfloat16)
    parts = []
    for start in range(0, field.shape[0], copies):
        part = smoothed[start : start + copies]
        parts.append(
            jnp.dot(taper[0], part, preferred_element_type=jnp.float32)
            + jnp.dot(taper[1], part, preferred_element_type=jnp.float32)
        )
    return parts[0] if len(parts) == 1 else jnp.concatenate(parts, axis=0)


def load_members(stacked, weight, members, bands, slots, width):
    own = stacked.shape[1] // slots
    stacked = stacked.astype(jnp.float32)
    which = stacked[:, :1, width : width + 1]
    scale = jnp.zeros(which.shape, jnp.float32)
    for member in range(members):
        scale = scale + jnp.where(which == member, weight[member], 0.0)
    shape = (members, bands * own, stacked.shape[-1])
    return [
        (scale * stacked[:, slot * own : (slot + 1) * own]).reshape(shape) for slot in range(slots)
    ]


def solution(mesh):
    members, bands = mesh.shape["member"], mesh.shape["band"]

    def first_half(slots, width, kept, weight, stacked, fields, ring, taper, out_ref, image_ref, grad_ref):
        scaled = load_members(stacked[...], weight, members, bands, slots, width)
        rows, padded = scaled[0].shape[1:]
        own = rows // bands
        fields = fields[...].astype(jnp.float32)

        def field(index):
            return fields[:, index * own : (index + 1) * own].reshape(rows, padded)

        precise, static = field(slots), field(slots + 1)

        def fold(weighted):
            total = scaled[0] * weighted[0][None]
            for slot in range(1, slots):
                total = total + scaled[slot] * weighted[slot][None]
            return total.reshape(members * rows, padded)

        grad = ensemble_share * spread(fold([precise * field(t) for t in range(slots)]), ring[...], taper)
        local = spread(grad, ring[...], taper).reshape(members, rows, padded)
        image = [ensemble_share * jnp.sum(scaled[t] * local, axis=0) for t in range(slots)]
        weighted = [precise * (image[t] + static) for t in range(slots)]
        grad = ensemble_share * spread(fold(weighted), ring[...], taper)
        grad_ref[...] = grad.astype(jnp.bfloat16)
        total = weighted[0]
        for t in range(1, slots):
            total = total + weighted[t]
        grad = grad[:, :kept].reshape(members, bands, own, kept)
        total = total[:, :kept].reshape(bands, own, kept)
        for member in range(members):
            for band in range(bands):
                out_ref[member * bands + band] = jnp.concatenate(
                    [grad[member, band], total[band]], axis=0
                ).astype(jnp.bfloat16)
        for t in range(slots):
            image_ref[:, t * own : (t + 1) * own] = image[t][:, :kept].reshape(bands, own, kept)

    def second_half(slots, width, kept, weight, stacked, grad, ring, taper, image_ref):
        scaled = load_members(stacked[...], weight, members, bands, slots, width)
        rows, padded = scaled[0].shape[1:]
        own = rows // bands
        local = spread(grad[...], ring[...], taper).reshape(members, rows, padded)
        for t in range(slots):
            image = ensemble_share * jnp.sum(scaled[t] * local, axis=0)
            image_ref[:, t * own : (t + 1) * own] = image[:, :kept].reshape(bands, own, kept)

    def shards(ensemble, member_weight, member_of_slot, halfwidth, static_root, innovation, precision):
        _, slots, levels, rows, lon = ensemble.shape
        level_share, lon_share = levels // members, lon // bands
        own = level_share * rows
        halo = REACHES * LREACH
        width = lon_share + 2 * halo
        padded = round_up(width + 1, LANES)
        kept = min(padded, round_up(lon_share, LANES))
        first_level = lax.axis_index("member") * level_share
        highest = lax.Precision.HIGHEST
        vmem = pl.BlockSpec(memory_space=pltpu.VMEM)
        smem = pl.BlockSpec(memory_space=pltpu.SMEM)
        params = pltpu.CompilerParams(vmem_limit_bytes=48 * 1024 * 1024)

        def own_levels(field, axis):
            return lax.dynamic_slice_in_dim(field, first_level, level_share, axis)

        pieces = windows(
            ensemble[0], bands, halo, padded, member_of_slot.astype(jnp.bfloat16)[0]
        ).reshape(bands, slots, members, own, padded)
        pieces = jnp.transpose(pieces, (2, 0, 1, 3, 4)).reshape(members * bands, slots * own, padded)
        stacked = lax.all_to_all(pieces, BOTH, 0, 0, tiled=True)

        precise = precision.astype(jnp.float32)
        weighted = precise[None] * innovation.astype(jnp.float32)
        total = jnp.sum(weighted, axis=0)
        pulled = static_share * jnp.einsum("ql,qyx->lyx", static_root, total, precision=highest)
        own_root = own_levels(static_root, 0)
        static = static_share * jnp.einsum("lq,qyx->lyx", own_root, pulled, precision=highest)
        fields = jnp.concatenate(
            [
                own_levels(innovation, 1),
                own_levels(precision, 0)[None],
                static.astype(jnp.bfloat16)[None],
            ]
        ).reshape((slots + 2) * own, lon)
        fields = exchange_bands(windows(fields, bands, halo, padded, jnp.zeros((), jnp.bfloat16)))

        picker = (member_of_slot[0] == jnp.arange(member_weight.shape[0], dtype=jnp.int32)).astype(
            jnp.float32
        )
        scale = jnp.sum(picker * member_weight)
        folded = scale * jnp.sum(ensemble[0].astype(jnp.float32) * weighted, axis=0)
        grad_first = ensemble_share * localize(folded, taper_weights(halfwidth, HMAX))

        ring = ring_kernel(width, padded)
        per_member = bands * own
        copies = members
        while copies > 1 and (copies * per_member > 256 or members % copies):
            copies -= 1
        taper = taper_matrix(own_levels(halfwidth, 0), bands, rows, copies)

        out, image_first, grad = pl.pallas_call(
            lambda *refs: first_half(slots, width, kept, *refs),
            out_shape=(
                jax.ShapeDtypeStruct((members * bands, 2 * own, kept), jnp.bfloat16),
                jax.ShapeDtypeStruct((bands, slots * own, kept), jnp.float32),
                jax.ShapeDtypeStruct((members * per_member, padded), jnp.bfloat16),
            ),
            in_specs=[smem, vmem, vmem, vmem, vmem],
            out_specs=(vmem, vmem, vmem),
            compiler_params=params,
            name="first_half",
        )(member_weight, stacked, fields, ring, taper)
        back = lax.all_to_all(out, BOTH, 0, 0, tiled=True)
        image_second = pl.pallas_call(
            lambda *refs: second_half(slots, width, kept, *refs),
            out_shape=jax.ShapeDtypeStruct((bands, slots * own, kept), jnp.float32),
            in_specs=[smem, vmem, vmem, vmem, vmem],
            out_specs=vmem,
            compiler_params=params,
            name="second_half",
        )(member_weight, stacked, grad, ring, taper)
        images = exchange_bands(jnp.concatenate([image_first, image_second], axis=1))

        def join(blocks, lead):
            return jnp.concatenate(
                [blocks[(slice(None),) * lead + (band, Ellipsis, slice(0, lon_share))] for band in range(bands)],
                axis=-1,
            )

        images = join(images, 0).reshape(2, slots, level_share, rows, lon)
        back = join(back.reshape(members, bands, 2, level_share, rows, kept), 1).astype(jnp.float32)
        grad_second = back[:, 0].reshape(levels, rows, lon)
        total = back[:, 1].reshape(levels, rows, lon)
        pulled_second = static_share * jnp.einsum("ql,qyx->lyx", static_root, total, precision=highest)
        static_second = static_share * jnp.einsum("lq,qyx->lyx", own_root, pulled_second, precision=highest)
        image_first = images[0] + static[None]
        image_second = images[1] + static_second[None]

        own_precise = own_levels(precise, 0)[None]
        own_weighted = own_levels(weighted, 1)
        weighted_first = own_precise * image_first
        sums = jnp.stack(
            [
                jnp.sum(own_weighted * image_first),
                jnp.sum(weighted_first * image_first),
                jnp.sum(weighted_first * image_second),
                jnp.sum(own_precise * image_second * image_second),
            ]
        )
        sums = jnp.broadcast_to(jnp.pad(sums, (0, LANES - 4))[None], (members * bands, LANES))
        sums = jnp.sum(lax.all_to_all(sums, BOTH, 0, 0, tiled=True), axis=0)
        first_norm, first_image, cross, second_image = sums[0], sums[1], sums[2], sums[3]
        alpha = first_norm / (first_norm + first_image)
        ratio = first_image / first_norm
        next_norm = alpha * alpha * jnp.maximum(cross - ratio * first_image, 0.0)
        beta = next_norm / first_norm
        spread_image = second_image - 2.0 * ratio * cross + ratio * ratio * first_image
        curvature = next_norm + alpha * alpha * spread_image - beta * next_norm / alpha
        alpha_next = jnp.clip(next_norm / curvature, 0.0, 1.0)
        on_first = alpha + alpha_next * (1.0 - alpha + beta)
        on_second = -alpha * alpha_next
        return (
            (on_first * grad_first + on_second * grad_second)[None],
            on_first * pulled + on_second * pulled_second,
            on_first * image_first + on_second * image_second,
        )

    return jax.shard_map(
        shards,
        mesh=mesh,
        in_specs=(
            P("member", None, None, "band", None),
            P(),
            P("member"),
            P(),
            P(),
            P(None, None, "band", None),
            P(None, "band", None),
        ),
        out_specs=(
            P("member", None, "band", None),
            P(None, "band", None),
            P(None, "member", "band", None),
        ),
        check_vma=False,
    )
```

time: 359 us -> 106 us (0.30)
  blocking collectives: 119 us -> 0 us
  waiting for transfers between devices: 143 us -> 29.2 us
  between operations: 24.5 us -> 9.99 us
  other arithmetic: 23.5 us -> 16.5 us
  matrix products: 8.48 us -> 2.48 us
  Pallas kernels: 0 us -> 4.23 us
    psum x3 -> x0, blocking collectives: 119 us -> none  [the longest x2 80.3 us: shards(): lax.psum(local_dot(res_members, res_members, res_static, res_static, grou...]
    psum x2 -> x0, waiting for transfers between devices: 110 us -> none  [shards(): summed = lax.psum(partial_image, 'member')]
    all_to_all x0 -> x3, waiting for transfers between devices: none -> 28.4 us  [the longest x1 12.6 us: shards(): back = lax.all_to_all(out, BOTH, 0, 0, tiled=True)]
    ppermute x5 -> x7, waiting for transfers between devices: 26.2 us -> 0.76 us  [the longest x6 0.75 us: exchange_bands(): lax.ppermute(outgoing, 'band', [(i, (i + shift) % count) for i in range(c...]
    ppermute x5 -> x1, starting transfers between devices: 19.2 us -> 4.85 us  [with_halo(): lax.ppermute(lax.slice_in_dim(block, block.shape[dim] - width, None, axis...]
    all_to_all x0 -> x3, starting transfers between devices: none -> 11.7 us  [the longest x1 5.55 us: shards(): stacked = lax.all_to_all(pieces, BOTH, 0, 0, tiled=True)]
    reduce_sum x11 -> x5, other arithmetic: 12.8 us -> 6.03 us  [the longest x1 2.28 us: shards(): jnp.sum(weighted_first * image_first)]
    ppermute x5 -> x1, waiting for transfers between devices: 6.26 us -> 0.01 us  [with_halo(): lax.ppermute(lax.slice_in_dim(block, block.shape[dim] - width, None, axis...]
  transfers between devices with their start and end apart: 12 -> 11, of which waited for: 10 -> 4; matrix products, arithmetic and copies ran while one was open for 2% -> 23% of each run, Pallas kernels for 0% -> 4%
where the time goes in v1:
time: 106 us; the launch traced here: 105 us
  waiting for transfers between devices  29.2 us (28%)
  starting transfers between devices  25.7 us (24%)
  local copies, waits for them, and re-layouts  16.5 us (16%)
  other arithmetic  16.5 us (16%)
  between operations  9.99 us (9%)
  Pallas kernels  4.23 us (4%)
  matrix products  2.48 us (2%)
    all_to_all x1, waiting for transfers between devices, shards(): back = lax.all_to_all(out, BOTH, 0, 0, tiled=True)  12.6 us
    all_to_all x1, waiting for transfers between devices, shards(): stacked = lax.all_to_all(pieces, BOTH, 0, 0, tiled=True)  9.67 us
    ppermute x6, starting transfers between devices, exchange_bands(): lax.ppermute(outgoing, 'band', [(i, (i + shift) % count) for i in range(c...  7.9 us
    all_to_all x1, waiting for transfers between devices, shards(): sums = jnp.sum(lax.all_to_all(sums, BOTH, 0, 0, tiled=True), axis=0)  6.09 us
    all_to_all x1, starting transfers between devices, shards(): stacked = lax.all_to_all(pieces, BOTH, 0, 0, tiled=True)  5.55 us
    ppermute x1, starting transfers between devices, with_halo(): lax.ppermute(lax.slice_in_dim(block, block.shape[dim] - width, None, axis...  4.85 us
    all_to_all x1, starting transfers between devices, shards(): back = lax.all_to_all(out, BOTH, 0, 0, tiled=True)  3.61 us
    pallas_call x1, Pallas kernels, shards(): pl.pallas_call(lambda *refs: first_half(slots, width, kept, *refs), out_s...  3.07 us
  transfers between devices with their start and end apart: 11, of which 4 were waited for; matrix products, arithmetic and copies ran while one was open for 23% of the time, Pallas kernels for 4%

profile of v1, /device:TPU:0, one launch (start us, length us, event | category | flops | bytes accessed | tf_op | source)
XLA Modules:
  0.0 104.6 jit_solution(14034697419685200700)
XLA Ops:
  0.7 1.0 convert_element_type.141
  2.3 1.3 %fusion.69 = f32[]{:T(128)} fusion(f32[8]{0:T(128)} %refs_0_.3, s32[]{:T(128)} %bitcast.165), kind=kLoop, calls=%fused_computation.167 | loop fusion | flops 23 | bytes 40 | tf_op jit(solution)/shard_map/reduce_sum | solution.py:258
  3.6 1.8 %multiply_reduce_fusion = (f32[16,4,1440]{2,1,0:T(4,128)S(1)}, f32[16,4,1440]{2,1,0:T(4,128)S(1)}, f32[2,16,4,1440]{3,2,1,0:T(4,128)S(1)}) fusion(bf16[1,2,16,4,1440]{4,3,2,1,0:T(4,128)(2,1)S(1)} %copy-done.2, bf16[2,16,4,1440]{3,2,1,0:T(4,128)(2,1)} %param.12, f32[16,4,1440]{2,1,0:T(4,128)S(1)} %convert_element_type.141), kind=kLoop, calls=%fused_computation.10 | loop fusion | flops 921600 | bytes 2580480 | tf_op jit(solution)/shard_map/reduce_sum | solution.py:259
  5.4 0.8 fusion.15
  6.2 0.3 convert_element_type.144
  6.6 0.9 convolution_convert_fusion
  7.4 0.2 copy.149
  7.6 0.2 convert_element_type.148
  7.8 4.8 %collective-permute-start = (bf16[16,4,1440]{2,0,1:T(8,128)(2,1)S(1)}, bf16[16,4,1440]{2,0,1:T(8,128)(2,1)S(1)}, u32[]{:S(2)}, u32[]{:S(2)}) collective-permute-start(bf16[16,4,1440]{2,0,1:T(8,128)(2,1)S(1)} %convert_element_type.148), channel_id=1, source_target_pairs={{0,1},{1,2},{2,3},{4,5},{5,6},{6,7},{8,9},{9,10},{10,11},{12,13},{... | collective-permute-start | bytes 552968 | tf_op jit(solution)/shard_map/ppermute | solution.py:29
  12.7 1.3 %collective-permute-start.1 = (bf16[16,4,1440]{2,0,1:T(8,128)(2,1)S(1)}, bf16[16,4,1440]{2,0,1:T(8,128)(2,1)}, u32[]{:S(2)}, u32[]{:S(2)}) collective-permute-start(bf16[16,4,1440]{2,0,1:T(8,128)(2,1)S(1)} %convert_element_type.148), channel_id=1, source_target_pairs={{1,0},{2,1},{3,2},{5,4},{6,5},{7,6},{9,8},{10,9},{11,10},{13,12},{... | collective-permute-start | bytes 552968 | tf_op jit(solution)/shard_map/ppermute | solution.py:32
  14.0 0.8 constant_dynamic-slice_fusion.2
  14.8 0.8 dynamic-slice_bitcast_fusion.3
  15.6 0.6 fusion.13
  16.2 0.3 convolution_multiply_fusion.1
  17.0 0.1 maximum_bitcast_fusion
  17.1 0.6 dynamic-slice_bitcast_fusion
  17.7 4.2 %collective-permute-start.2 = (bf16[32,512]{1,0:T(8,128)(2,1)}, bf16[32,512]{1,0:T(8,128)(2,1)}, u32[]{:S(2)}, u32[]{:S(2)}) collective-permute-start(bf16[32,512]{1,0:T(8,128)(2,1)} %get-tuple-element.70), channel_id=1, source_target_pairs={{0,3},{1,0},{2,1},{3,2},{4,7},{5,4},{6,5},{7,6},{8,11},{9,8},{10,9... | collective-permute-start | bytes 98312 | tf_op jit(solution)/shard_map/ppermute | solution.py:131
  22.0 1.3 %collective-permute-start.4 = (bf16[32,512]{1,0:T(8,128)(2,1)S(1)}, bf16[32,512]{1,0:T(8,128)(2,1)}, u32[]{:S(2)}, u32[]{:S(2)}) collective-permute-start(bf16[32,512]{1,0:T(8,128)(2,1)S(1)} %get-tuple-element.68), channel_id=1, source_target_pairs={{0,1},{1,2},{2,3},{3,0},{4,5},{5,6},{6,7},{7,4},{8,9},{9,10},{10,1... | collective-permute-start | bytes 98312 | tf_op jit(solution)/shard_map/ppermute | solution.py:131
  23.3 0.1 fusion.84
  23.5 0.2 fusion.83
  23.8 0.5 maximum_maximum_fusion
  24.6 0.8 copy.174
  25.4 5.6 %all-to-all-start = ((bf16[32,16,512]{2,1,0:T(8,128)(2,1)}), bf16[32,16,512]{2,1,0:T(8,128)(2,1)S(1)}, u32[]{:S(2)}, u32[]{:S(2)}) async-start(bf16[32,16,512]{2,1,0:T(8,128)(2,1)} %bitcast.15), calls=%async_computation | async-start | bytes 1048576 | tf_op jit(solution)/shard_map/all_to_all | solution.py:238
  31.0 0.6 constant_dynamic-slice_fusion
  31.7 0.6 fusion.90
  32.4 0.6 slice_bitcast_fusion.12
  33.0 1.3 %fusion.66 = f32[256,1]{0,1:T(1,128)S(1)} fusion(f32[]{:T(128)} %bitcast.34, f32[]{:T(128)} %bitcast.33), kind=kLoop, calls=%fused_computation.164 | loop fusion | flops 6400 | bytes 1032 | tf_op jit(solution)/shard_map/add | solution.py:95
  34.3 0.2 fusion.31
  34.5 0.6 and_select_fusion.refs_3_
  35.3 0.7 add.309
  36.0 0.7 mul.317
  36.6 0.8 fusion.46
  37.5 9.7 %all-to-all-done.refs_1_ = bf16[32,16,512]{2,1,0:T(8,128)(2,1)S(1)} async-done(((bf16[32,16,512]{2,1,0:T(8,128)(2,1)}), bf16[32,16,512]{2,1,0:T(8,128)(2,1)S(1)}, u32[]{:S(2)}, u32[]{:S(2)}) %all-to-all-start) | async-done | bytes 524320 | tf_op jit(solution)/shard_map/all_to_all | solution.py:238
  47.2 3.1 %first_half.1 = (bf16[32,16,384]{2,1,0:T(8,128)(2,1)}, f32[4,16,384]{2,1,0:T(8,128)S(1)}, bf16[256,512]{1,0:T(8,128)(2,1)S(1)}) custom-call(f32[8]{0:T(128)S(1)} %copy-done.1, bf16[32,16,512]{2,1,0:T(8,128)(2,1)S(1)} %all-to-all-done.refs_1_, bf16[4,32,512]{2,1,0:T(8,128)(2,1)S(1)} %pad_maximum_fusion.6.refs_2_, ...), custom_call_target="tpu_custom_call" | custom-call | tf_op jit(solution)/shard_map/first_half/pallas_call | solution.py:269
  50.3 1.2 %second_half.1 = f32[4,16,384]{2,1,0:T(8,128)S(1)} custom-call(f32[8]{0:T(128)S(1)} %copy-done.1, bf16[32,16,512]{2,1,0:T(8,128)(2,1)S(1)} %all-to-all-done.refs_1_, bf16[256,512]{1,0:T(8,128)(2,1)S(1)} %get-tuple-element.7.refs_2_, bf16[512,512]{1,0:T(8,128)(2,1)S(1)} %and_select_fusion.refs_3_, bf16[2,256,256]{2,1,0:T(8,128)(2,1)S(1)} %pad_maximum_fusion.1.refs_4_), custom_call_target="tpu_custom_call" | custom-call | tf_op jit(solution)/shard_map/second_half/pallas_call | solution.py:282
  51.5 1.2 %collective-permute-start.5 = (f32[32,384]{1,0:T(8,128)S(1)}, f32[32,384]{1,0:T(8,128)S(1)}, u32[]{:S(2)}, u32[]{:S(2)}) collective-permute-start(f32[32,384]{1,0:T(8,128)S(1)} %get-tuple-element.66), channel_id=1, source_target_pairs={{0,3},{1,0},{2,1},{3,2},{4,7},{5,4},{6,5},{7,6},{8,11},{9,8},{10,9... | collective-permute-start | bytes 147464 | tf_op jit(solution)/shard_map/ppermute | solution.py:131
  52.7 0.5 collective-permute-start.6
  53.2 0.6 collective-permute-start.7
  53.8 3.6 %all-to-all-start.1 = ((bf16[32,16,384]{2,1,0:T(8,128)(2,1)}), bf16[32,16,384]{2,1,0:T(8,128)(2,1)S(1)}, u32[]{:S(2)}, u32[]{:S(2)}) async-start(bf16[32,16,384]{2,1,0:T(8,128)(2,1)} %get-tuple-element.8), calls=%async_computation.1 | async-start | bytes 786432 | tf_op jit(solution)/shard_map/all_to_all | solution.py:281
  57.5 0.7 collective-permute-done.7
  58.3 0.1 concatenate.82
  58.4 12.6 %all-to-all-done.1 = bf16[32,16,384]{2,1,0:T(8,128)(2,1)S(1)} async-done(((bf16[32,16,384]{2,1,0:T(8,128)(2,1)}), bf16[32,16,384]{2,1,0:T(8,128)(2,1)S(1)}, u32[]{:S(2)}, u32[]{:S(2)}) %all-to-all-start.1) | async-done | bytes 393248 | tf_op jit(solution)/shard_map/all_to_all | solution.py:281
  71.1 0.1 reshape.640
  71.2 0.1 fusion.82
  71.4 0.2 concatenate.83
  71.7 0.1 copy.162
  71.8 0.4 fusion.25
  72.2 0.3 convolution_multiply_fusion
  72.6 0.7 add.311
  73.2 1.6 %add.312 = f32[16,1440]{1,0:T(8,128)} reshape(f32[2,2,4,1440]{3,2,1,0:T(4,128)} %add.311) | data formatting | bytes 184320 | tf_op jit(solution)/shard_map/add | solution.py:305
  74.8 2.3 %multiply_reduce_fusion.2 = (f32[]{:T(128)}, f32[]{:T(128)}, f32[]{:T(128)}, f32[16,1440]{1,0:T(8,128)}, f32[16,1440]{1,0:T(8,128)}) fusion(f32[16,1440]{1,0:T(8,128)S(1)} %copy-done.8, f32[16,1440]{1,0:T(8,128)S(1)} %copy-done.7, f32[32,1440]{1,0:T(8,128)S(1)} %concatenate.82, f32[16,1440]{1,0:T(8,128)} %add.312), kind=kLoop, calls=%fused_computation.72 | loop fusion | flops 230397 | bytes 645132 | tf_op jit(solution)/shard_map/reduce_sum | solution.py:313
  77.1 1.0 squeeze.93
  78.1 0.7 multiply_reduce_fusion.3
  78.7 2.6 %select_maximum_fusion = f32[128]{0:T(128)S(1)} fusion(f32[1]{0:T(128)} %bitcast.58, f32[1]{0:T(128)} %bitcast.57, f32[1]{0:T(128)} %bitcast.49, f32[1]{0:T(128)} %bitcast.48), kind=kLoop, calls=%fused_computation.168 | loop fusion | flops 1024 | bytes 528 | tf_op jit(solution)/shard_map/stack | solution.py:310
  81.3 0.6 broadcast_in_dim.29
  81.9 2.5 %all-to-all-start.2 = ((f32[32,1,128]{2,1,0:T(1,128)}), f32[32,1,128]{2,1,0:T(1,128)S(1)}, u32[]{:S(2)}, u32[]{:S(2)}) async-start(f32[32,1,128]{2,1,0:T(1,128)} %broadcast_in_dim.29), calls=%async_computation.2 | async-start | bytes 32768 | tf_op jit(solution)/shard_map/all_to_all | solution.py:319
  84.5 0.9 constant_dynamic-update-slice_fusion.2
  85.5 6.1 %all-to-all-done.2 = f32[32,1,128]{2,1,0:T(1,128)S(1)} async-done(((f32[32,1,128]{2,1,0:T(1,128)}), f32[32,1,128]{2,1,0:T(1,128)S(1)}, u32[]{:S(2)}, u32[]{:S(2)}) %all-to-all-start.2) | async-done | bytes 16416 | tf_op jit(solution)/shard_map/all_to_all | solution.py:319
  91.6 0.6 fusion.89
  100.2 1.0 copy.170
  101.2 0.3 copy.167
  101.6 1.4 %fusion.12 = f32[1,16,4,1440]{3,1,2,0:T(8,128)S(1)} fusion(f32[16,4,1440]{2,1,0:T(4,128)S(1)} %bitcast.169, bf16[16,4,1440]{2,0,1:T(8,128)(2,1)} %collective-permute-done.1, bf16[16,4,1440]{2,0,1:T(8,128)(2,1)S(1)} %convert_element_type.148, bf16[16,4,1440]{2,0,1:T(8,128)(2,1)S(1)} %copy-done.4, ...), kind=kLoop, calls=%fused_computation.23 | loop fusion | flops 2580480 | bytes 2396740 | tf_op jit(solution)/shard_map/broadcast_in_dim | solution.py:331
  103.0 1.0 copy.169
  104.0 0.7 multiply_add_fusion
  (99 shorter events, 1.5 us)
Async XLA Ops:
  0.6 15.0 %copy-start = (f32[16,16]{1,0:T(8,128)S(1)}, f32[16,16]{1,0:T(8,128)}, u32[]{:S(2)}) copy-start(f32[16,16]{1,0:T(8,128)} %param.11) | copy-start | bytes 3076
  0.6 2.9 %copy-start.2 = (bf16[1,2,16,4,1440]{4,3,2,1,0:T(4,128)(2,1)S(1)}, bf16[1,2,16,4,1440]{4,3,2,1,0:T(4,128)(2,1)}, u32[]{:S(2)}) copy-start(bf16[1,2,16,4,1440]{4,3,2,1,0:T(4,128)(2,1)} %param.7) | copy-start | bytes 1105924
  7.8 29.6 %collective-permute-start = (bf16[16,4,1440]{2,0,1:T(8,128)(2,1)S(1)}, bf16[16,4,1440]{2,0,1:T(8,128)(2,1)S(1)}, u32[]{:S(2)}, u32[]{:S(2)}) collective-permute-start(bf16[16,4,1440]{2,0,1:T(8,128)(2,1)S(1)} %convert_element_type.148), channel_id=1, source_target_pairs={{0,1},{1,2},{2,3},{4,5},{5,6},{6,7},{8,9},{9,10},{10,11},{12,13},{... | collective-permute-start | bytes 552968 | tf_op jit(solution)/shard_map/ppermute | solution.py:29
  12.7 71.8 %collective-permute-start.1 = (bf16[16,4,1440]{2,0,1:T(8,128)(2,1)S(1)}, bf16[16,4,1440]{2,0,1:T(8,128)(2,1)}, u32[]{:S(2)}, u32[]{:S(2)}) collective-permute-start(bf16[16,4,1440]{2,0,1:T(8,128)(2,1)S(1)} %convert_element_type.148), channel_id=1, source_target_pairs={{1,0},{2,1},{3,2},{5,4},{6,5},{7,6},{9,8},{10,9},{11,10},{13,12},{... | collective-permute-start | bytes 552968 | tf_op jit(solution)/shard_map/ppermute | solution.py:32
  17.7 18.9 %collective-permute-start.2 = (bf16[32,512]{1,0:T(8,128)(2,1)}, bf16[32,512]{1,0:T(8,128)(2,1)}, u32[]{:S(2)}, u32[]{:S(2)}) collective-permute-start(bf16[32,512]{1,0:T(8,128)(2,1)} %get-tuple-element.70), channel_id=1, source_target_pairs={{0,3},{1,0},{2,1},{3,2},{4,7},{5,4},{6,5},{7,6},{8,11},{9,8},{10,9... | collective-permute-start | bytes 98312 | tf_op jit(solution)/shard_map/ppermute | solution.py:131
  22.0 14.6 %collective-permute-start.3 = (bf16[32,512]{1,0:T(8,128)(2,1)}, bf16[32,512]{1,0:T(8,128)(2,1)}, u32[]{:S(2)}, u32[]{:S(2)}) collective-permute-start(bf16[32,512]{1,0:T(8,128)(2,1)} %get-tuple-element.69), channel_id=1, source_target_pairs={{0,2},{1,3},{2,0},{3,1},{4,6},{5,7},{6,4},{7,5},{8,10},{9,11},{10,... | collective-permute-start | bytes 98312 | tf_op jit(solution)/shard_map/ppermute | solution.py:131
  22.0 14.6 %collective-permute-start.4 = (bf16[32,512]{1,0:T(8,128)(2,1)S(1)}, bf16[32,512]{1,0:T(8,128)(2,1)}, u32[]{:S(2)}, u32[]{:S(2)}) collective-permute-start(bf16[32,512]{1,0:T(8,128)(2,1)S(1)} %get-tuple-element.68), channel_id=1, source_target_pairs={{0,1},{1,2},{2,3},{3,0},{4,5},{5,6},{6,7},{7,4},{8,9},{9,10},{10,1... | collective-permute-start | bytes 98312 | tf_op jit(solution)/shard_map/ppermute | solution.py:131
  25.4 6.2 %copy-start.19 = (s32[16]{0:T(128)S(1)}, s32[16]{0:T(128)}, u32[]{:S(2)}) copy-start(s32[16]{0:T(128)} %param.10) | copy-start | bytes 196
  25.4 21.8 %all-to-all-start = ((bf16[32,16,512]{2,1,0:T(8,128)(2,1)}), bf16[32,16,512]{2,1,0:T(8,128)(2,1)S(1)}, u32[]{:S(2)}, u32[]{:S(2)}) async-start(bf16[32,16,512]{2,1,0:T(8,128)(2,1)} %bitcast.15), calls=%async_computation | async-start | bytes 1048576 | tf_op jit(solution)/shard_map/all_to_all | solution.py:238
  34.5 1.4 %copy-start.10 = (f32[2,4,1440]{2,1,0:T(4,128)S(1)}, f32[2,4,1440]{2,1,0:T(4,128)}, u32[]{:S(2)}) copy-start(f32[2,4,1440]{2,1,0:T(4,128)} %constant_dynamic-slice_fusion) | copy-start | bytes 138244
  35.2 2.3 %copy-start.5 = (f32[2,4,1440]{2,1,0:T(4,128)}, f32[2,4,1440]{2,1,0:T(4,128)S(1)}, u32[]{:S(2)}) copy-start(f32[2,4,1440]{2,1,0:T(4,128)S(1)} %copy.157) | copy-start | bytes 138244
  35.2 12.0 %copy-start.1 = (f32[8]{0:T(128)S(1)}, f32[8]{0:T(128)}, u32[]{:S(2)}) copy-start(f32[8]{0:T(128)} %refs_0_.3) | copy-start | bytes 100
  37.5 12.8 %copy-start.3 = (bf16[16,4,1440]{2,0,1:T(8,128)(2,1)}, bf16[16,4,1440]{2,0,1:T(8,128)(2,1)S(1)}, u32[]{:S(2)}) copy-start(bf16[16,4,1440]{2,0,1:T(8,128)(2,1)S(1)} %collective-permute-done) | copy-start | bytes 552964
  51.5 6.0 %collective-permute-start.5 = (f32[32,384]{1,0:T(8,128)S(1)}, f32[32,384]{1,0:T(8,128)S(1)}, u32[]{:S(2)}, u32[]{:S(2)}) collective-permute-start(f32[32,384]{1,0:T(8,128)S(1)} %get-tuple-element.66), channel_id=1, source_target_pairs={{0,3},{1,0},{2,1},{3,2},{4,7},{5,4},{6,5},{7,6},{8,11},{9,8},{10,9... | collective-permute-start | bytes 147464 | tf_op jit(solution)/shard_map/ppermute | solution.py:131
  52.7 4.8 %collective-permute-start.6 = (f32[32,384]{1,0:T(8,128)S(1)}, f32[32,384]{1,0:T(8,128)S(1)}, u32[]{:S(2)}, u32[]{:S(2)}) collective-permute-start(f32[32,384]{1,0:T(8,128)S(1)} %get-tuple-element.67), channel_id=1, source_target_pairs={{0,2},{1,3},{2,0},{3,1},{4,6},{5,7},{6,4},{7,5},{8,10},{9,11},{10,... | collective-permute-start | bytes 147464 | tf_op jit(solution)/shard_map/ppermute | solution.py:131
  53.2 5.0 %collective-permute-start.7 = (f32[32,384]{1,0:T(8,128)S(1)}, f32[32,384]{1,0:T(8,128)S(1)}, u32[]{:S(2)}, u32[]{:S(2)}) collective-permute-start(f32[32,384]{1,0:T(8,128)S(1)} %get-tuple-element.65), channel_id=1, source_target_pairs={{0,1},{1,2},{2,3},{3,0},{4,5},{5,6},{6,7},{7,4},{8,9},{9,10},{10,1... | collective-permute-start | bytes 147464 | tf_op jit(solution)/shard_map/ppermute | solution.py:131
  53.8 17.2 %all-to-all-start.1 = ((bf16[32,16,384]{2,1,0:T(8,128)(2,1)}), bf16[32,16,384]{2,1,0:T(8,128)(2,1)S(1)}, u32[]{:S(2)}, u32[]{:S(2)}) async-start(bf16[32,16,384]{2,1,0:T(8,128)(2,1)} %get-tuple-element.8), calls=%async_computation.1 | async-start | bytes 786432 | tf_op jit(solution)/shard_map/all_to_all | solution.py:281
  71.8 3.0 %copy-start.7 = (f32[16,1440]{1,0:T(8,128)S(1)}, f32[16,1440]{1,0:T(8,128)}, u32[]{:S(2)}) copy-start(f32[16,1440]{1,0:T(8,128)} %add.309) | copy-start | bytes 276484
  71.8 3.0 %copy-start.8 = (f32[16,1440]{1,0:T(8,128)S(1)}, f32[16,1440]{1,0:T(8,128)}, u32[]{:S(2)}) copy-start(f32[16,1440]{1,0:T(8,128)} %mul.317) | copy-start | bytes 276484
  72.2 5.8 %copy-start.6 = (f32[2,4,1440]{2,1,0:T(4,128)S(1)}, f32[2,4,1440]{2,1,0:T(4,128)}, u32[]{:S(2)}) copy-start(f32[2,4,1440]{2,1,0:T(4,128)} %copy-done.5) | copy-start | bytes 138244
  77.1 8.4 %copy-start.9 = (f32[16,1440]{1,0:T(8,128)S(1)}, f32[16,1440]{1,0:T(8,128)}, u32[]{:S(2)}) copy-start(f32[16,1440]{1,0:T(8,128)} %get-tuple-element.54) | copy-start | bytes 276484
  81.9 9.6 %all-to-all-start.2 = ((f32[32,1,128]{2,1,0:T(1,128)}), f32[32,1,128]{2,1,0:T(1,128)S(1)}, u32[]{:S(2)}, u32[]{:S(2)}) async-start(f32[32,1,128]{2,1,0:T(1,128)} %broadcast_in_dim.29), calls=%async_computation.2 | async-start | bytes 32768 | tf_op jit(solution)/shard_map/all_to_all | solution.py:319
  100.2 1.4 %copy-start.4 = (bf16[16,4,1440]{2,0,1:T(8,128)(2,1)S(1)}, bf16[16,4,1440]{2,0,1:T(8,128)(2,1)}, u32[]{:S(2)}) copy-start(bf16[16,4,1440]{2,0,1:T(8,128)(2,1)} %copy-done.3) | copy-start | bytes 552964
  100.2 1.4 %copy-start.11 = (f32[16]{0:T(128)S(1)}, f32[16]{0:T(128)}, u32[]{:S(2)}) copy-start(f32[16]{0:T(128)} %get-tuple-element.80) | copy-start | bytes 196
  100.2 1.4 %copy-start.12 = (f32[16]{0:T(128)S(1)}, f32[16]{0:T(128)}, u32[]{:S(2)}) copy-start(f32[16]{0:T(128)} %get-tuple-element.81) | copy-start | bytes 196
  100.2 1.4 %copy-start.13 = (f32[16]{0:T(128)S(1)}, f32[16]{0:T(128)}, u32[]{:S(2)}) copy-start(f32[16]{0:T(128)} %get-tuple-element.82) | copy-start | bytes 196
  100.2 1.4 %copy-start.14 = (f32[16]{0:T(128)S(1)}, f32[16]{0:T(128)}, u32[]{:S(2)}) copy-start(f32[16]{0:T(128)} %get-tuple-element.83) | copy-start | bytes 196
  100.2 1.4 %copy-start.15 = (f32[16]{0:T(128)S(1)}, f32[16]{0:T(128)}, u32[]{:S(2)}) copy-start(f32[16]{0:T(128)} %get-tuple-element.84) | copy-start | bytes 196
  100.2 1.4 %copy-start.16 = (f32[16]{0:T(128)S(1)}, f32[16]{0:T(128)}, u32[]{:S(2)}) copy-start(f32[16]{0:T(128)} %get-tuple-element.85) | copy-start | bytes 196
  100.2 1.4 %copy-start.17 = (f32[16]{0:T(128)S(1)}, f32[16]{0:T(128)}, u32[]{:S(2)}) copy-start(f32[16]{0:T(128)} %get-tuple-element.86) | copy-start | bytes 196
  100.2 1.4 %copy-start.18 = (f32[16]{0:T(128)S(1)}, f32[16]{0:T(128)}, u32[]{:S(2)}) copy-start(f32[16]{0:T(128)} %get-tuple-element.87) | copy-start | bytes 196

commit v2 on v1

--- a/solution.py
+++ b/solution.py
@@ -22,15 +22,11 @@
     return -(-value // step) * step
 
 
-def with_halo(block, dim, width):
+def neighbours(block):
     count = lax.axis_size("band")
     forward = [(i, i + 1) for i in range(count - 1)]
     backward = [(target, source) for source, target in forward]
-    low = lax.ppermute(
-        lax.slice_in_dim(block, block.shape[dim] - width, None, axis=dim), "band", forward
-    )
-    high = lax.ppermute(lax.slice_in_dim(block, 0, width, axis=dim), "band", backward)
-    return jnp.concatenate([low, block, high], axis=dim)
+    return lax.ppermute(block, "band", forward), lax.ppermute(block, "band", backward)
 
 
 def kernel_values(distance):
@@ -66,22 +62,34 @@
     return result.reshape(field.shape).astype(jnp.bfloat16)
 
 
-def taper_weights(halfwidth, reach):
-    offsets = jnp.abs(jnp.arange(-reach, reach + 1, dtype=jnp.int32)).astype(jnp.float32)
-    spans = halfwidth.astype(jnp.float32)[:, None] + 1.0
-    return jnp.maximum(1.0 - offsets[None, :] / spans, 0.0) / spans
-
-
-def localize(field, taper):
-    smoothed = smooth_longitude(field.astype(jnp.bfloat16), LREACH, 3)
-    padded = with_halo(smoothed, 1, HMAX)
-    row_count = field.shape[1]
-    summed = jnp.zeros(field.shape, jnp.float32)
-    for offset in range(2 * HMAX + 1):
-        summed = summed + taper[:, offset][:, None, None] * padded[
-            :, offset : offset + row_count, :
-        ].astype(jnp.float32)
-    return summed
+def halves(full):
+    high = full.astype(jnp.bfloat16)
+    low = (full - high.astype(jnp.float32)).astype(jnp.bfloat16)
+    return jnp.stack([high, low])
+
+
+def halo_taper(halfwidth, rows):
+    levels = halfwidth.shape[0]
+    own = levels * rows
+    target = jnp.arange(own, dtype=jnp.int32)[:, None]
+    source = jnp.arange(3 * own, dtype=jnp.int32)[None, :]
+    spans = jnp.repeat(halfwidth.astype(jnp.float32), rows)[:, None] + 1.0
+    shift = (source // own - 1) * rows + source % rows - target % rows
+    same = source // rows % levels == target // rows
+    near = jnp.maximum(1.0 - jnp.abs(shift).astype(jnp.float32) / spans, 0.0) / spans
+    return halves(jnp.where(same, near, 0.0))
+
+
+def each_row(matrix, rows):
+    same = jnp.eye(rows, dtype=jnp.float32)
+    wide = matrix[:, None, :, None] * same[None, :, None, :]
+    return wide.reshape(matrix.shape[0] * rows, matrix.shape[1] * rows)
+
+
+def exact_dot(matrix, field):
+    return jnp.dot(
+        matrix, field, precision=lax.Precision.HIGHEST, preferred_element_type=jnp.float32
+    )
 
 
 def taper_matrix(halfwidth, bands, rows, copies):
@@ -96,10 +104,7 @@
     apart = jnp.abs(latitude[:, None] - latitude[None, :]).astype(jnp.float32)
     same = (copy[:, None] == copy[None, :]) & (level[:, None] == level[None, :])
     near = jnp.maximum(1.0 - apart / spans, 0.0) / spans
-    full = jnp.where(same, near, 0.0)
-    high = full.astype(jnp.bfloat16)
-    low = (full - high.astype(jnp.float32)).astype(jnp.bfloat16)
-    return jnp.stack([high, low])
+    return halves(jnp.where(same, near, 0.0))
 
 
 def windows(field, count, halo, padded, fill):
@@ -214,6 +219,89 @@
             image = ensemble_share * jnp.sum(scaled[t] * local, axis=0)
             image_ref[:, t * own : (t + 1) * own] = image[:, :kept].reshape(bands, own, kept)
 
+    def first_gradient(below, here, above, taper, grad_ref):
+        stacked = jnp.concatenate([below[...], here[...], above[...]], axis=0)
+        grad_ref[...] = ensemble_share * (
+            jnp.dot(taper[0], stacked, preferred_element_type=jnp.float32)
+            + jnp.dot(taper[1], stacked, preferred_element_type=jnp.float32)
+        )
+
+    def total_piece(back, band, own):
+        kept = back.shape[-1]
+        pieces = [back[member * bands + band, own:].astype(jnp.float32) for member in range(members)]
+        return jnp.concatenate(pieces, axis=0).reshape(members * own, kept)
+
+    def inner_products(slots, lon_share, back, images, fields, static, mixing, sums_ref):
+        own, kept = static.shape[1:]
+        inside = lax.broadcasted_iota(jnp.int32, (own, kept), 1) < lon_share
+        sums = [jnp.zeros((own, kept), jnp.float32) for _ in range(4)]
+        for band in range(bands):
+            second_static = exact_dot(mixing[...], total_piece(back, band, own))
+            field = fields[band, :, :kept].astype(jnp.float32)
+            precise = field[slots * own : (slots + 1) * own]
+            for t in range(slots):
+                first = images[band, t * own : (t + 1) * own] + static[band]
+                second = images[band, (slots + t) * own : (slots + t + 1) * own] + second_static
+                weighted = precise * first
+                sums[0] = sums[0] + precise * field[t * own : (t + 1) * own] * first
+                sums[1] = sums[1] + weighted * first
+                sums[2] = sums[2] + weighted * second
+                sums[3] = sums[3] + precise * second * second
+        lane = lax.broadcasted_iota(jnp.int32, (1, LANES), 1)
+        row = jnp.zeros((1, LANES), jnp.float32)
+        for index, part in enumerate(sums):
+            part = jnp.where(inside, part, 0.0)
+            part = jnp.sum(jnp.sum(part, axis=0, keepdims=True), axis=1, keepdims=True)
+            row = row + jnp.where(lane == index, part, 0.0)
+        sums_ref[...] = jnp.broadcast_to(row, sums_ref.shape)
+
+    def join(slots, lon_share, back, images, static, mixing, pulling, grad_ref, pulled_ref, image_ref):
+        own = static.shape[1]
+        for band in range(bands):
+            place = slice(band * lon_share, (band + 1) * lon_share)
+            total = total_piece(back, band, own)
+            second_static = exact_dot(mixing[...], total)
+            pulled_ref[:, place] = exact_dot(pulling[...], total)[:, :lon_share]
+            grad = jnp.concatenate(
+                [back[member * bands + band, :own].astype(jnp.float32) for member in range(members)], axis=0
+            )
+            grad_ref[:, place] = grad[:, :lon_share]
+            for t in range(slots):
+                first = images[band, t * own : (t + 1) * own] + static[band]
+                second = images[band, (slots + t) * own : (slots + t + 1) * own] + second_static
+                image_ref[t * own : (t + 1) * own, place] = first[:, :lon_share]
+                image_ref[(slots + t) * own : (slots + t + 1) * own, place] = second[:, :lon_share]
+
+    def finish(slots, sums, grad_first, grad_second, pulled_first, pulled_second, images, member_ref, static_ref, image_ref):
+        total = jnp.sum(sums[...], axis=0, keepdims=True)
+        lane = lax.broadcasted_iota(jnp.int32, total.shape, 1)
+        first_norm, first_image, cross, second_image = [
+            jnp.sum(jnp.where(lane == index, total, 0.0), axis=1, keepdims=True) for index in range(4)
+        ]
+        alpha = first_norm / (first_norm + first_image)
+        ratio = first_image / first_norm
+        next_norm = alpha * alpha * jnp.maximum(cross - ratio * first_image, 0.0)
+        beta = next_norm / first_norm
+        apart = second_image - 2.0 * ratio * cross + ratio * ratio * first_image
+        curvature = next_norm + alpha * alpha * apart - beta * next_norm / alpha
+        alpha_next = jnp.clip(next_norm / curvature, 0.0, 1.0)
+        on_first = alpha + alpha_next * (1.0 - alpha + beta)
+        on_second = -alpha * alpha_next
+        levels, rows = static_ref.shape[:2]
+        member = on_first * grad_first[...] + on_second * grad_second[...]
+        static = on_first * pulled_first[...] + on_second * pulled_second[...]
+        for level in range(levels):
+            place = slice(level * rows, (level + 1) * rows)
+            member_ref[0, level] = member[place]
+            static_ref[level] = static[place]
+        half = images.shape[0] // 2
+        image = on_first * images[:half] + on_second * images[half:]
+        level_share = image_ref.shape[1]
+        for t in range(slots):
+            for level in range(level_share):
+                start = (t * level_share + level) * rows
+                image_ref[t, level] = image[start : start + rows]
+
     def shards(ensemble, member_weight, member_of_slot, halfwidth, static_root, innovation, precision):
         _, slots, levels, rows, lon = ensemble.shape
         level_share, lon_share = levels // members, lon // bands
@@ -222,42 +310,78 @@
         width = lon_share + 2 * halo
         padded = round_up(width + 1, LANES)
         kept = min(padded, round_up(lon_share, LANES))
-        first_level = lax.axis_index("member") * level_share
-        highest = lax.Precision.HIGHEST
         vmem = pl.BlockSpec(memory_space=pltpu.VMEM)
         smem = pl.BlockSpec(memory_space=pltpu.SMEM)
-        params = pltpu.CompilerParams(vmem_limit_bytes=48 * 1024 * 1024)
-
-        def own_levels(field, axis):
-            return lax.dynamic_slice_in_dim(field, first_level, level_share, axis)
+
+        def call(body, name, shapes, specs, *operands, flops=0):
+            return pl.pallas_call(
+                body,
+                out_shape=tuple(jax.ShapeDtypeStruct(shape, kind) for shape, kind in shapes),
+                in_specs=specs,
+                out_specs=(vmem,) * len(shapes),
+                compiler_params=pltpu.CompilerParams(vmem_limit_bytes=48 * 1024 * 1024),
+                cost_estimate=pl.CostEstimate(flops=flops, bytes_accessed=1 << 20, transcendentals=0),
+                name=name,
+            )(*operands)
 
         pieces = windows(
             ensemble[0], bands, halo, padded, member_of_slot.astype(jnp.bfloat16)[0]
         ).reshape(bands, slots, members, own, padded)
         pieces = jnp.transpose(pieces, (2, 0, 1, 3, 4)).reshape(members * bands, slots * own, padded)
+        pieces, ensemble, member_weight, member_of_slot, halfwidth, static_root, innovation, precision = (
+            lax.optimization_barrier(
+                (pieces, ensemble, member_weight, member_of_slot, halfwidth, static_root, innovation, precision)
+            )
+        )
         stacked = lax.all_to_all(pieces, BOTH, 0, 0, tiled=True)
 
-        precise = precision.astype(jnp.float32)
-        weighted = precise[None] * innovation.astype(jnp.float32)
+        first_level = lax.axis_index("member") * level_share
+
+        def own_levels(field, axis):
+            return lax.dynamic_slice_in_dim(field, first_level, level_share, axis)
+
+        innovation = innovation.reshape(slots, levels * rows, lon)
+        precision = precision.reshape(levels * rows, lon)
+        weighted = precision.astype(jnp.float32)[None] * innovation.astype(jnp.float32)
         total = jnp.sum(weighted, axis=0)
-        pulled = static_share * jnp.einsum("ql,qyx->lyx", static_root, total, precision=highest)
-        own_root = own_levels(static_root, 0)
-        static = static_share * jnp.einsum("lq,qyx->lyx", own_root, pulled, precision=highest)
+        pulling = each_row(static_share * static_root.T, rows)
+        own_root = each_row(static_share * own_levels(static_root, 0), rows)
+        mixing = exact_dot(own_root, pulling)
+        pulled = exact_dot(pulling, total)
+        static = exact_dot(own_root, pulled)
+
+        def own_rows(field, axis):
+            return lax.dynamic_slice_in_dim(field, first_level * rows, own, axis)
+
         fields = jnp.concatenate(
-            [
-                own_levels(innovation, 1),
-                own_levels(precision, 0)[None],
-                static.astype(jnp.bfloat16)[None],
-            ]
+            [own_rows(innovation, 1), own_rows(precision, 0)[None], static.astype(jnp.bfloat16)[None]]
         ).reshape((slots + 2) * own, lon)
-        fields = exchange_bands(windows(fields, bands, halo, padded, jnp.zeros((), jnp.bfloat16)))
+        here_fields = windows(fields, bands, halo, padded, jnp.zeros((), jnp.bfloat16))
+        fields = exchange_bands(here_fields)
+        static = jnp.pad(
+            jnp.transpose(static.reshape(own, bands, lon_share), (1, 0, 2)),
+            ((0, 0), (0, 0), (0, kept - lon_share)),
+        )
 
         picker = (member_of_slot[0] == jnp.arange(member_weight.shape[0], dtype=jnp.int32)).astype(
             jnp.float32
         )
         scale = jnp.sum(picker * member_weight)
-        folded = scale * jnp.sum(ensemble[0].astype(jnp.float32) * weighted, axis=0)
-        grad_first = ensemble_share * localize(folded, taper_weights(halfwidth, HMAX))
+        folded = scale * jnp.sum(
+            ensemble.reshape(slots, levels * rows, lon).astype(jnp.float32) * weighted, axis=0
+        )
+        smoothed = smooth_longitude(folded.astype(jnp.bfloat16), LREACH, 3)
+        below, above = neighbours(smoothed)
+        (grad_first,) = call(
+            first_gradient,
+            "first_gradient",
+            [((levels * rows, lon), jnp.float32)],
+            [vmem] * 4,
+            below,
+            smoothed,
+            above,
+            halo_taper(halfwidth, rows),
+        )
 
         ring = ring_kernel(width, padded)
         per_member = bands * own
@@ -266,71 +390,80 @@
             copies -= 1
         taper = taper_matrix(own_levels(halfwidth, 0), bands, rows, copies)
 
-        out, image_first, grad = pl.pallas_call(
+        out, image_first, grad = call(
             lambda *refs: first_half(slots, width, kept, *refs),
-            out_shape=(
-                jax.ShapeDtypeStruct((members * bands, 2 * own, kept), jnp.bfloat16),
-                jax.ShapeDtypeStruct((bands, slots * own, kept), jnp.float32),
-                jax.ShapeDtypeStruct((members * per_member, padded), jnp.bfloat16),
-            ),
-            in_specs=[smem, vmem, vmem, vmem, vmem],
-            out_specs=(vmem, vmem, vmem),
-            compiler_params=params,
-            name="first_half",
-        )(member_weight, stacked, fields, ring, taper)
+            "first_half",
+            [
+                ((members * bands, 2 * own, kept), jnp.bfloat16),
+                ((bands, slots * own, kept), jnp.float32),
+                ((members * per_member, padded), jnp.bfloat16),
+            ],
+            [smem, vmem, vmem, vmem, vmem],
+            member_weight,
+            stacked,
+            fields,
+            ring,
+            taper,
+            flops=10**9,
+        )
         back = lax.all_to_all(out, BOTH, 0, 0, tiled=True)
-        image_second = pl.pallas_call(
+        (image_second,) = call(
             lambda *refs: second_half(slots, width, kept, *refs),
-            out_shape=jax.ShapeDtypeStruct((bands, slots * own, kept), jnp.float32),
-            in_specs=[smem, vmem, vmem, vmem, vmem],
-            out_specs=vmem,
-            compiler_params=params,
-            name="second_half",
-        )(member_weight, stacked, grad, ring, taper)
+            "second_half",
+            [((bands, slots * own, kept), jnp.float32)],
+            [smem, vmem, vmem, vmem, vmem],
+            member_weight,
+            stacked,
+            grad,
+            ring,
+            taper,
+            flops=10**9,
+        )
         images = exchange_bands(jnp.concatenate([image_first, image_second], axis=1))
 
-        def join(blocks, lead):
-            return jnp.concatenate(
-                [blocks[(slice(None),) * lead + (band, Ellipsis, slice(0, lon_share))] for band in range(bands)],
-                axis=-1,
-            )
-
-        images = join(images, 0).reshape(2, slots, level_share, rows, lon)
-        back = join(back.reshape(members, bands, 2, level_share, rows, kept), 1).astype(jnp.float32)
-        grad_second = back[:, 0].reshape(levels, rows, lon)
-        total = back[:, 1].reshape(levels, rows, lon)
-        pulled_second = static_share * jnp.einsum("ql,qyx->lyx", static_root, total, precision=highest)
-        static_second = static_share * jnp.einsum("lq,qyx->lyx", own_root, pulled_second, precision=highest)
-        image_first = images[0] + static[None]
-        image_second = images[1] + static_second[None]
-
-        own_precise = own_levels(precise, 0)[None]
-        own_weighted = own_levels(weighted, 1)
-        weighted_first = own_precise * image_first
-        sums = jnp.stack(
+        (sums,) = call(
+            lambda *refs: inner_products(slots, lon_share, *refs),
+            "inner_products",
+            [((members * bands, LANES), jnp.float32)],
+            [vmem] * 5,
+            back,
+            images,
+            here_fields,
+            static,
+            mixing,
+        )
+        sums = lax.all_to_all(sums, BOTH, 0, 0, tiled=True)
+        grad_second, pulled_second, images = call(
+            lambda *refs: join(slots, lon_share, *refs),
+            "join",
             [
-                jnp.sum(own_weighted * image_first),
-                jnp.sum(weighted_first * image_first),
-                jnp.sum(weighted_first * image_second),
-                jnp.sum(own_precise * image_second * image_second),
-            ]
-        )
-        sums = jnp.broadcast_to(jnp.pad(sums, (0, LANES - 4))[None], (members * bands, LANES))
-        sums = jnp.sum(lax.all_to_all(sums, BOTH, 0, 0, tiled=True), axis=0)
-        first_norm, first_image, cross, second_image = sums[0], sums[1], sums[2], sums[3]
-        alpha = first_norm / (first_norm + first_image)
-        ratio = first_image / first_norm
-        next_norm = alpha * alpha * jnp.maximum(cross - ratio * first_image, 0.0)
-        beta = next_norm / first_norm
-        spread_image = second_image - 2.0 * ratio * cross + ratio * ratio * first_image
-        curvature = next_norm + alpha * alpha * spread_image - beta * next_norm / alpha
-        alpha_next = jnp.clip(next_norm / curvature, 0.0, 1.0)
-        on_first = alpha + alpha_next * (1.0 - alpha + beta)
-        on_second = -alpha * alpha_next
-        return (
-            (on_first * grad_first + on_second * grad_second)[None],
-            on_first * pulled + on_second * pulled_second,
-            on_first * image_first + on_second * image_second,
+                ((levels * rows, lon), jnp.float32),
+                ((levels * rows, lon), jnp.float32),
+                ((2 * slots * own, lon), jnp.float32),
+            ],
+            [vmem] * 5,
+            back,
+            images,
+            static,
+            mixing,
+            pulling,
+            flops=10**9,
+        )
+        return call(
+            lambda *refs: finish(slots, *refs),
+            "finish",
+            [
+                ((1, levels, rows, lon), jnp.float32),
+                ((levels, rows, lon), jnp.float32),
+                ((slots, level_share, rows, lon), jnp.float32),
+            ],
+            [vmem] * 6,
+            sums,
+            grad_first,
+            grad_second,
+            pulled,
+            pulled_second,
+            images,
         )
 
     return jax.shard_map(

time: 106 us -> 70.3 us (0.66)
  waiting for transfers between devices: 29.2 us -> 17.9 us
  other arithmetic: 16.5 us -> 6.01 us
  local copies, waits for them, and re-layouts: 16.5 us -> 7.31 us
  between operations: 9.99 us -> 1.83 us
  Pallas kernels: 4.23 us -> 7.42 us
  starting transfers between devices: 25.7 us -> 27.6 us
    all_to_all x1, waiting for transfers between devices: 12.6 us -> 4.82 us  [shards(): back = lax.all_to_all(out, BOTH, 0, 0, tiled=True)]
    all_to_all x1, waiting for transfers between devices: 9.67 us -> 4.33 us  [shards(): stacked = lax.all_to_all(pieces, BOTH, 0, 0, tiled=True)]
    reduce_sum x4 -> x2, other arithmetic: 4.77 us -> 0.64 us  [the longest x1 0.38 us: shards(): jnp.sum(ensemble.reshape(slots, levels * rows, lon).astype(jnp.float32) *...]
    pallas_call x2 -> x6, Pallas kernels: 4.23 us -> 7.42 us  [call(): pl.pallas_call(body, out_shape=tuple((jax.ShapeDtypeStruct(shape, kind) f...]
    add x4 -> x1, local copies, waits for them, and re-layouts: 2.89 us -> 0.09 us  [halo_taper(): spans = jnp.repeat(halfwidth.astype(jnp.float32), rows)[:, None] + 1.0]
    another operation x2, other arithmetic: 2.63 us -> 0.04 us  [halves(): return jnp.stack([high, low])]
    ppermute x6, waiting for transfers between devices: 0.75 us -> 2.39 us  [exchange_bands(): lax.ppermute(outgoing, 'band', [(i, (i + shift) % count) for i in range(c...]
    ppermute x6, starting transfers between devices: 7.9 us -> 9.38 us  [exchange_bands(): lax.ppermute(outgoing, 'band', [(i, (i + shift) % count) for i in range(c...]
  transfers between devices with their start and end apart: 11 -> 11, of which waited for: 4 -> 6; matrix products, arithmetic and copies ran while one was open for 23% -> 9% of each run, Pallas kernels for 4% -> 8%
where the time goes in v2:
time: 70.3 us; the launch traced here: 69.8 us
  starting transfers between devices  27.6 us (39%)
  waiting for transfers between devices  17.9 us (25%)
  Pallas kernels  7.42 us (11%)
  local copies, waits for them, and re-layouts  7.31 us (10%)
  other arithmetic  6.01 us (9%)
  between operations  1.83 us (3%)
  matrix products  1.78 us (3%)
    ppermute x6, starting transfers between devices, exchange_bands(): lax.ppermute(outgoing, 'band', [(i, (i + shift) % count) for i in range(c...  9.38 us
    pallas_call x6, Pallas kernels, call(): pl.pallas_call(body, out_shape=tuple((jax.ShapeDtypeStruct(shape, kind) f...  7.42 us
    all_to_all x1, waiting for transfers between devices, shards(): sums = lax.all_to_all(sums, BOTH, 0, 0, tiled=True)  6.35 us
    all_to_all x1, starting transfers between devices, shards(): stacked = lax.all_to_all(pieces, BOTH, 0, 0, tiled=True)  6.31 us
    ppermute x1, starting transfers between devices, neighbours(): lax.ppermute(block, 'band', forward)  5.49 us
    all_to_all x1, waiting for transfers between devices, shards(): back = lax.all_to_all(out, BOTH, 0, 0, tiled=True)  4.82 us
    all_to_all x1, waiting for transfers between devices, shards(): stacked = lax.all_to_all(pieces, BOTH, 0, 0, tiled=True)  4.33 us
    all_to_all x1, starting transfers between devices, shards(): back = lax.all_to_all(out, BOTH, 0, 0, tiled=True)  2.6 us
  transfers between devices with their start and end apart: 11, of which 6 were waited for; matrix products, arithmetic and copies ran while one was open for 9% of the time, Pallas kernels for 8%

profile of v2, /device:TPU:0, one launch (start us, length us, event | category | flops | bytes accessed | tf_op | source)
XLA Modules:
  0.0 69.8 jit_solution(12668521950457827661)
XLA Ops:
  0.7 1.1 %fusion.72 = (bf16[2,16,4,72]{3,2,1,0:T(4,128)(2,1)S(1)}, bf16[2,16,4,72]{3,2,1,0:T(4,128)(2,1)S(1)}, bf16[2,16,4,72]{3,2,1,0:T(4,128)(2,1)S(1)}, bf16[2,16,4,72...) fusion(bf16[2,16,4,1440]{3,2,1,0:T(4,128)(2,1)} %bitcast.111), kind=kLoop, calls=%fused_computation.172 | loop fusion | bytes 184320 | tf_op jit(solution)/shard_map/slice | solution.py:113
  1.7 1.3 %fusion.71 = (bf16[2,16,4,432]{3,2,1,0:T(4,128)(2,1)S(1)}, bf16[2,16,4,432]{3,2,1,0:T(4,128)(2,1)S(1)}, bf16[2,16,4,432]{3,2,1,0:T(4,128)(2,1)S(1)}) fusion(bf16[2,16,4,1440]{3,2,1,0:T(4,128)(2,1)} %bitcast.112), kind=kLoop, calls=%fused_computation.171 | loop fusion | bytes 663552 | tf_op jit(solution)/shard_map/slice | solution.py:120
  3.7 0.1 pad.64.clone
  3.8 0.5 maximum_maximum_fusion
  4.4 0.1 pad_maximum_fusion
  4.5 0.8 %copy.41 = bf16[4,2,8,8,512]{4,3,1,0,2:T(8,128)(2,1)} copy(bf16[4,2,8,8,512]{4,3,2,1,0:T(8,128)(2,1)S(1)} %pad_maximum_fusion) | data formatting | bytes 1048576 | tf_op jit(solution)/shard_map/stack | solution.py:124
  5.4 0.1 copy-done.3
  5.5 0.6 copy-done
  6.0 0.6 fusion.63
  6.7 0.4 fusion.2
  7.0 0.7 %multiply_convert_fusion = bf16[16,4,1440]{2,1,0:T(4,128)(2,1)S(1)} fusion(f32[16,4,1440]{2,1,0:T(4,128)S(1)} %fusion.2, f32[]{:T(128)} %fusion.63), kind=kLoop, calls=%fused_computation.20 | loop fusion | flops 184320 | bytes 552964 | tf_op jit(solution)/shard_map/convert_element_type | solution.py:373
  7.8 0.2 convert_element_type.182
  8.1 0.9 %convolution_convert_fusion = bf16[64,3,480]{2,0,1:T(8,128)(2,1)S(1)} fusion(s32[516]{0:T(1024)S(1)} %iota_add_fusion, bf16[64,1,480]{2,0,1:T(8,128)(2,1)S(1)} %get-tuple-element.46, bf16[64,2,480]{2,0,1:T(8,128)(2,1)S(1)} %get-tuple-element.48, bf16[64,2,480]{2,0,1:T(8,128)(2,1)S(1)} %get-tuple-element.47, bf16[64,1,480]{2,0,1:T(8,128)(2,1)S(1)} %get-tuple-element.45, ...), kind=kOutput, calls=%fused_computation.1 | convolution fusion | flops 98668800 | bytes 739344 | tf_op jit(solution)/shard_map/...bm,mo->...bo/dot_general | solution.py:61
  9.0 0.2 copy.40
  9.2 0.2 convert_element_type.186.here
  9.4 1.3 %collective-permute-start.7 = (bf16[64,1440]{1,0:T(8,128)(2,1)S(1)}, bf16[64,1440]{1,0:T(8,128)(2,1)S(1)}, u32[]{:S(2)}, u32[]{:S(2)}) collective-permute-start(bf16[64,1440]{1,0:T(8,128)(2,1)S(1)} %convert_element_type.186.here), channel_id=1, source_target_pairs={{1,0},{2,1},{3,2},{5,4},{6,5},{7,6},{9,8},{10,9},{11,10},{13,12},{... | collective-permute-start | bytes 552968 | tf_op jit(solution)/shard_map/ppermute | solution.py:29
  10.7 5.5 %collective-permute-start.6 = (bf16[64,1440]{1,0:T(8,128)(2,1)S(1)}, bf16[64,1440]{1,0:T(8,128)(2,1)S(1)}, u32[]{:S(2)}, u32[]{:S(2)}) collective-permute-start(bf16[64,1440]{1,0:T(8,128)(2,1)S(1)} %convert_element_type.186.here), channel_id=1, source_target_pairs={{0,1},{1,2},{2,3},{4,5},{5,6},{6,7},{8,9},{9,10},{10,11},{12,13},{... | collective-permute-start | bytes 552968 | tf_op jit(solution)/shard_map/ppermute | solution.py:29
  16.2 6.3 %all-to-all-start = ((bf16[32,16,512]{2,1,0:T(8,128)(2,1)}), bf16[32,16,512]{2,1,0:T(8,128)(2,1)S(1)}, u32[]{:S(2)}, u32[]{:S(2)}) async-start(bf16[32,16,512]{2,1,0:T(8,128)(2,1)} %bitcast.3), calls=%async_computation | async-start | bytes 1048576 | tf_op jit(solution)/shard_map/all_to_all | solution.py:336
  22.6 0.1 reshape.1106
  22.6 0.3 fusion.3
  22.9 0.2 reshape.1105
  23.1 0.5 copy-done.5
  23.6 0.1 copy.32
  23.7 0.1 broadcast_multiply_fusion.1
  23.8 0.1 mul.144
  23.8 0.1 reduce_sum.30
  24.0 0.1 broadcast_multiply_fusion
  24.1 0.3 mul.151.refs_4_
  24.4 0.5 fusion.78.refs_3_
  24.9 0.3 fusion.79
  25.2 0.1 fusion.76
  25.3 0.1 fusion.75
  25.4 0.1 pad.43.clone
  25.5 0.1 maximum_bitcast_fusion.1
  25.6 1.8 %collective-permute-start.2 = (bf16[32,512]{1,0:T(8,128)(2,1)S(1)}, bf16[32,512]{1,0:T(8,128)(2,1)S(1)}, u32[]{:S(2)}, u32[]{:S(2)}) collective-permute-start(bf16[32,512]{1,0:T(8,128)(2,1)S(1)} %get-tuple-element.55), channel_id=1, source_target_pairs={{0,1},{1,2},{2,3},{3,0},{4,5},{5,6},{6,7},{7,4},{8,9},{9,10},{10,1... | collective-permute-start | bytes 98312 | tf_op jit(solution)/shard_map/ppermute | solution.py:136
  27.5 1.5 %collective-permute-start.1 = (bf16[32,512]{1,0:T(8,128)(2,1)S(1)}, bf16[32,512]{1,0:T(8,128)(2,1)S(1)}, u32[]{:S(2)}, u32[]{:S(2)}) collective-permute-start(bf16[32,512]{1,0:T(8,128)(2,1)S(1)} %get-tuple-element.56), channel_id=1, source_target_pairs={{0,2},{1,3},{2,0},{3,1},{4,6},{5,7},{6,4},{7,5},{8,10},{9,11},{10,... | collective-permute-start | bytes 98312 | tf_op jit(solution)/shard_map/ppermute | solution.py:136
  28.9 1.5 %collective-permute-start = (bf16[32,512]{1,0:T(8,128)(2,1)S(1)}, bf16[32,512]{1,0:T(8,128)(2,1)S(1)}, u32[]{:S(2)}, u32[]{:S(2)}) collective-permute-start(bf16[32,512]{1,0:T(8,128)(2,1)S(1)} %get-tuple-element.57), channel_id=1, source_target_pairs={{0,3},{1,0},{2,1},{3,2},{4,7},{5,4},{6,5},{7,6},{8,11},{9,8},{10,9... | collective-permute-start | bytes 98312 | tf_op jit(solution)/shard_map/ppermute | solution.py:136
  30.4 0.1 dynamic-slice_convert_fusion
  30.5 0.1 fusion.80.refs_4_.refs_3_
  30.6 0.6 fusion.77
  31.2 0.1 broadcast_in_dim.28
  31.3 0.1 add.292
  31.4 1.3 %fusion.61 = f32[256,1]{0,1:T(1,128)S(1)} fusion(f32[]{:T(128)} %bitcast.21, f32[]{:T(128)} %bitcast.20), kind=kLoop, calls=%fused_computation.157 | loop fusion | flops 6400 | bytes 1032 | tf_op jit(solution)/shard_map/add | solution.py:103
  32.7 0.7 %fusion.45 = (bf16[1,64,192]{2,1,0:T(8,128)(2,1)S(1)}, bf16[1,64,192]{2,1,0:T(8,128)(2,1)}) fusion(f32[64]{0:T(128)S(1)} %add.292, s32[64]{0:T(128)S(1)} %get-tuple-element.80, s32[192]{0:T(256)S(1)} %get-tuple-element.83, s32[64]{0:T(128)S(1)} %get-tuple-element.81, s32[192]{0:T(256)S(1)} %get-tuple-element.82), kind=kLoop, calls=%fused_computation.94 | loop fusion | flops 159744 | bytes 51456 | tf_op jit(solution)/shard_map/convert_element_type | solution.py:66
  33.4 0.2 fusion.21
  33.7 0.6 and_select_fusion.refs_3_
  34.4 4.3 %all-to-all-done.refs_1_ = bf16[32,16,512]{2,1,0:T(8,128)(2,1)S(1)} async-done(((bf16[32,16,512]{2,1,0:T(8,128)(2,1)}), bf16[32,16,512]{2,1,0:T(8,128)(2,1)S(1)}, u32[]{:S(2)}, u32[]{:S(2)}) %all-to-all-start) | async-done | bytes 524320 | tf_op jit(solution)/shard_map/all_to_all | solution.py:336
  38.8 3.1 %first_half.1 = (bf16[32,16,384]{2,1,0:T(8,128)(2,1)}, f32[4,16,384]{2,1,0:T(8,128)S(1)}, bf16[256,512]{1,0:T(8,128)(2,1)S(1)}) custom-call(f32[8]{0:T(128)S(1)} %copy-done, bf16[32,16,512]{2,1,0:T(8,128)(2,1)S(1)} %all-to-all-done.refs_1_, bf16[4,32,512]{2,1,0:T(8,128)(2,1)S(1)} %pad_maximum_fusion.7.refs_2_, bf16[512,512]{1,0:T(8,128)(2,1)S(1)} %and_select_fusion.refs_3_, ...), custom_call_target="tpu_custom_call" | custom-call | flops 1000000000 | bytes 1048576 | tf_op jit(solution)/shard_map/first_half/pallas_call | solution.py:317
  41.8 2.6 %all-to-all-start.1 = ((bf16[32,16,384]{2,1,0:T(8,128)(2,1)}), bf16[32,16,384]{2,1,0:T(8,128)(2,1)S(1)}, u32[]{:S(2)}, u32[]{:S(2)}) async-start(bf16[32,16,384]{2,1,0:T(8,128)(2,1)} %get-tuple-element.23), calls=%async_computation.1 | async-start | bytes 786432 | tf_op jit(solution)/shard_map/all_to_all | solution.py:409
  44.5 1.2 %second_half.1 = f32[4,16,384]{2,1,0:T(8,128)S(1)} custom-call(f32[8]{0:T(128)S(1)} %copy-done, bf16[32,16,512]{2,1,0:T(8,128)(2,1)S(1)} %all-to-all-done.refs_1_, bf16[256,512]{1,0:T(8,128)(2,1)S(1)} %get-tuple-element.25.refs_2_, bf16[512,512]{1,0:T(8,128)(2,1)S(1)} %and_select_fusion.refs_3_, bf16[2,256,256]{2,1,0:T(8,128)(2,1)S(1)} %pad_maximum_fusion.1.refs_4_), custom_call_target="tpu_custom_call" | custom-call | flops 1000000000 | bytes 1048576 | tf_op jit(solution)/shard_map/second_half/pallas_call | solution.py:317
  45.7 1.7 %collective-permute-start.5 = (f32[32,384]{1,0:T(8,128)S(1)}, f32[32,384]{1,0:T(8,128)S(1)}, u32[]{:S(2)}, u32[]{:S(2)}) collective-permute-start(f32[32,384]{1,0:T(8,128)S(1)} %get-tuple-element.52), channel_id=1, source_target_pairs={{0,1},{1,2},{2,3},{3,0},{4,5},{5,6},{6,7},{7,4},{8,9},{9,10},{10,1... | collective-permute-start | bytes 147464 | tf_op jit(solution)/shard_map/ppermute | solution.py:136
  47.3 1.3 %collective-permute-start.3 = (f32[32,384]{1,0:T(8,128)S(1)}, f32[32,384]{1,0:T(8,128)S(1)}, u32[]{:S(2)}, u32[]{:S(2)}) collective-permute-start(f32[32,384]{1,0:T(8,128)S(1)} %get-tuple-element.53), channel_id=1, source_target_pairs={{0,3},{1,0},{2,1},{3,2},{4,7},{5,4},{6,5},{7,6},{8,11},{9,8},{10,9... | collective-permute-start | bytes 147464 | tf_op jit(solution)/shard_map/ppermute | solution.py:136
  48.6 1.7 %collective-permute-start.4 = (f32[32,384]{1,0:T(8,128)S(1)}, f32[32,384]{1,0:T(8,128)S(1)}, u32[]{:S(2)}, u32[]{:S(2)}) collective-permute-start(f32[32,384]{1,0:T(8,128)S(1)} %get-tuple-element.54), channel_id=1, source_target_pairs={{0,2},{1,3},{2,0},{3,1},{4,6},{5,7},{6,4},{7,5},{8,10},{9,11},{10,... | collective-permute-start | bytes 147464 | tf_op jit(solution)/shard_map/ppermute | solution.py:136
  50.3 0.1 reshape.1108
  50.5 0.3 first_gradient.1.refs_1_
  50.8 1.3 %collective-permute-done.5 = f32[32,384]{1,0:T(8,128)S(1)} collective-permute-done((f32[32,384]{1,0:T(8,128)S(1)}, f32[32,384]{1,0:T(8,128)S(1)}, u32[]{:S(2)}, u32[]{:S(2)}) %collective-permute-start.5) | collective-permute-done | bytes 49184 | tf_op jit(solution)/shard_map/ppermute | solution.py:136
  52.1 1.0 %collective-permute-done.3 = f32[32,384]{1,0:T(8,128)S(1)} collective-permute-done((f32[32,384]{1,0:T(8,128)S(1)}, f32[32,384]{1,0:T(8,128)S(1)}, u32[]{:S(2)}, u32[]{:S(2)}) %collective-permute-start.3) | collective-permute-done | bytes 49184 | tf_op jit(solution)/shard_map/ppermute | solution.py:136
  53.1 0.1 collective-permute-done.4
  53.2 4.8 %all-to-all-done.1.refs_0_ = bf16[32,16,384]{2,1,0:T(8,128)(2,1)S(1)} async-done(((bf16[32,16,384]{2,1,0:T(8,128)(2,1)}), bf16[32,16,384]{2,1,0:T(8,128)(2,1)S(1)}, u32[]{:S(2)}, u32[]{:S(2)}) %all-to-all-start.1) | async-done | bytes 393248 | tf_op jit(solution)/shard_map/all_to_all | solution.py:409
  58.1 1.0 %inner_products.1 = f32[32,128]{1,0:T(8,128)} custom-call(bf16[32,16,384]{2,1,0:T(8,128)(2,1)S(1)} %all-to-all-done.1.refs_0_, f32[4,32,384]{2,1,0:T(8,128)S(1)} %pad_maximum_fusion.4.refs_1_, bf16[4,32,512]{2,1,0:T(8,128)(2,1)S(1)} %pad_maximum_fusion.6.refs_2_, f32[4,8,384]{2,1,0:T(8,128)S(1)} %pad.4.refs_3_.refs_2_, f32[8,64]{1,0:T(8,128)S(1)} %fusion.80.refs_4_.refs_3_), custom_call_target="tpu_custom_call" | custom-call | bytes 1048576 | tf_op jit(solution)/shard_map/inner_products/pallas_call | solution.py:317
  59.1 2.5 %all-to-all-start.2 = ((f32[32,1,128]{2,1,0:T(1,128)}), f32[32,1,128]{2,1,0:T(1,128)S(1)}, u32[]{:S(2)}, u32[]{:S(2)}) async-start(f32[32,1,128]{2,1,0:T(1,128)} %bitcast.33), calls=%async_computation.2 | async-start | bytes 32768 | tf_op jit(solution)/shard_map/all_to_all | solution.py:435
  61.6 0.7 %join.1 = (f32[64,1440]{1,0:T(8,128)S(1)}, f32[64,1440]{1,0:T(8,128)S(1)}, f32[32,1440]{1,0:T(8,128)S(1)}) custom-call(bf16[32,16,384]{2,1,0:T(8,128)(2,1)S(1)} %all-to-all-done.1.refs_0_, f32[4,32,384]{2,1,0:T(8,128)S(1)} %pad_maximum_fusion.4.refs_1_, f32[4,8,384]{2,1,0:T(8,128)S(1)} %pad.4.refs_3_.refs_2_, f32[8,64]{1,0:T(8,128)S(1)} %fusion.80.refs_4_.refs_3_, ...), custom_call_target="tpu_custom_call" | custom-call | flops 1000000000 | bytes 1048576 | tf_op jit(solution)/shard_map/join/pallas_call | solution.py:317
  62.4 6.3 %all-to-all-done.2 = f32[32,1,128]{2,1,0:T(1,128)S(1)} async-done(((f32[32,1,128]{2,1,0:T(1,128)}), f32[32,1,128]{2,1,0:T(1,128)S(1)}, u32[]{:S(2)}, u32[]{:S(2)}) %all-to-all-start.2) | async-done | bytes 16416 | tf_op jit(solution)/shard_map/all_to_all | solution.py:435
  68.7 1.1 %finish.1 = (f32[1,16,4,1440]{3,2,1,0:T(4,128)}, f32[16,4,1440]{2,1,0:T(4,128)}, f32[2,2,4,1440]{3,2,1,0:T(4,128)}) custom-call(f32[32,128]{1,0:T(8,128)S(1)} %bitcast.110, f32[64,1440]{1,0:T(8,128)S(1)} %first_gradient.1.refs_1_, f32[64,1440]{1,0:T(8,128)S(1)} %get-tuple-element.28.refs_2_, f32[64,1440]{1,0:T(8,128)S(1)} %fusion.78.refs_3_, ...), custom_call_target="tpu_custom_call" | custom-call | bytes 1048576 | tf_op jit(solution)/shard_map/finish/pallas_call | solution.py:317
  (52 shorter events, 0.6 us)
Async XLA Ops:
  0.6 3.1 %copy-start.1 = (bf16[1,2,16,4,1440]{4,3,2,1,0:T(4,128)(2,1)S(1)}, bf16[1,2,16,4,1440]{4,3,2,1,0:T(4,128)(2,1)}, u32[]{:S(2)}) copy-start(bf16[1,2,16,4,1440]{4,3,2,1,0:T(4,128)(2,1)} %param.7) | copy-start | bytes 1105924
  4.5 1.0 %copy-start.3 = (bf16[16,4,1440]{2,1,0:T(4,128)(2,1)S(1)}, bf16[16,4,1440]{2,1,0:T(4,128)(2,1)}, u32[]{:S(2)}) copy-start(bf16[16,4,1440]{2,1,0:T(4,128)(2,1)} %param.13) | copy-start | bytes 552964
  5.4 0.7 copy-start
  5.4 1.3 %copy-start.2 = (bf16[2,16,4,1440]{3,2,1,0:T(4,128)(2,1)S(1)}, bf16[2,16,4,1440]{3,2,1,0:T(4,128)(2,1)}, u32[]{:S(2)}) copy-start(bf16[2,16,4,1440]{3,2,1,0:T(4,128)(2,1)} %param.12) | copy-start | bytes 1105924
  9.4 41.0 %collective-permute-start.7 = (bf16[64,1440]{1,0:T(8,128)(2,1)S(1)}, bf16[64,1440]{1,0:T(8,128)(2,1)S(1)}, u32[]{:S(2)}, u32[]{:S(2)}) collective-permute-start(bf16[64,1440]{1,0:T(8,128)(2,1)S(1)} %convert_element_type.186.here), channel_id=1, source_target_pairs={{1,0},{2,1},{3,2},{5,4},{6,5},{7,6},{9,8},{10,9},{11,10},{13,12},{... | collective-permute-start | bytes 552968 | tf_op jit(solution)/shard_map/ppermute | solution.py:29
  10.7 39.7 %collective-permute-start.6 = (bf16[64,1440]{1,0:T(8,128)(2,1)S(1)}, bf16[64,1440]{1,0:T(8,128)(2,1)S(1)}, u32[]{:S(2)}, u32[]{:S(2)}) collective-permute-start(bf16[64,1440]{1,0:T(8,128)(2,1)S(1)} %convert_element_type.186.here), channel_id=1, source_target_pairs={{0,1},{1,2},{2,3},{4,5},{5,6},{6,7},{8,9},{9,10},{10,11},{12,13},{... | collective-permute-start | bytes 552968 | tf_op jit(solution)/shard_map/ppermute | solution.py:29
  16.2 22.6 %all-to-all-start = ((bf16[32,16,512]{2,1,0:T(8,128)(2,1)}), bf16[32,16,512]{2,1,0:T(8,128)(2,1)S(1)}, u32[]{:S(2)}, u32[]{:S(2)}) async-start(bf16[32,16,512]{2,1,0:T(8,128)(2,1)} %bitcast.3), calls=%async_computation | async-start | bytes 1048576 | tf_op jit(solution)/shard_map/all_to_all | solution.py:336
  22.9 0.7 %copy-start.5 = (f32[16,16]{1,0:T(8,128)S(1)}, f32[16,16]{1,0:T(8,128)}, u32[]{:S(2)}) copy-start(f32[16,16]{1,0:T(8,128)} %param.11) | copy-start | bytes 3076
  25.3 5.1 %copy-start.6 = (s32[16]{0:T(128)S(1)}, s32[16]{0:T(128)}, u32[]{:S(2)}) copy-start(s32[16]{0:T(128)} %param.10) | copy-start | bytes 196
  25.6 8.7 %collective-permute-start.2 = (bf16[32,512]{1,0:T(8,128)(2,1)S(1)}, bf16[32,512]{1,0:T(8,128)(2,1)S(1)}, u32[]{:S(2)}, u32[]{:S(2)}) collective-permute-start(bf16[32,512]{1,0:T(8,128)(2,1)S(1)} %get-tuple-element.55), channel_id=1, source_target_pairs={{0,1},{1,2},{2,3},{3,0},{4,5},{5,6},{6,7},{7,4},{8,9},{9,10},{10,1... | collective-permute-start | bytes 98312 | tf_op jit(solution)/shard_map/ppermute | solution.py:136
  27.5 6.9 %collective-permute-start.1 = (bf16[32,512]{1,0:T(8,128)(2,1)S(1)}, bf16[32,512]{1,0:T(8,128)(2,1)S(1)}, u32[]{:S(2)}, u32[]{:S(2)}) collective-permute-start(bf16[32,512]{1,0:T(8,128)(2,1)S(1)} %get-tuple-element.56), channel_id=1, source_target_pairs={{0,2},{1,3},{2,0},{3,1},{4,6},{5,7},{6,4},{7,5},{8,10},{9,11},{10,... | collective-permute-start | bytes 98312 | tf_op jit(solution)/shard_map/ppermute | solution.py:136
  28.9 5.5 %collective-permute-start = (bf16[32,512]{1,0:T(8,128)(2,1)S(1)}, bf16[32,512]{1,0:T(8,128)(2,1)S(1)}, u32[]{:S(2)}, u32[]{:S(2)}) collective-permute-start(bf16[32,512]{1,0:T(8,128)(2,1)S(1)} %get-tuple-element.57), channel_id=1, source_target_pairs={{0,3},{1,0},{2,1},{3,2},{4,7},{5,4},{6,5},{7,6},{8,11},{9,8},{10,9... | collective-permute-start | bytes 98312 | tf_op jit(solution)/shard_map/ppermute | solution.py:136
  41.8 16.2 %all-to-all-start.1 = ((bf16[32,16,384]{2,1,0:T(8,128)(2,1)}), bf16[32,16,384]{2,1,0:T(8,128)(2,1)S(1)}, u32[]{:S(2)}, u32[]{:S(2)}) async-start(bf16[32,16,384]{2,1,0:T(8,128)(2,1)} %get-tuple-element.23), calls=%async_computation.1 | async-start | bytes 786432 | tf_op jit(solution)/shard_map/all_to_all | solution.py:409
  44.4 5.8 %copy-start.4 = (bf16[1,64,192]{2,1,0:T(8,128)(2,1)S(1)}, bf16[1,64,192]{2,1,0:T(8,128)(2,1)}, u32[]{:S(2)}) copy-start(bf16[1,64,192]{2,1,0:T(8,128)(2,1)} %get-tuple-element.69) | copy-start | bytes 73732
  45.7 6.5 %collective-permute-start.5 = (f32[32,384]{1,0:T(8,128)S(1)}, f32[32,384]{1,0:T(8,128)S(1)}, u32[]{:S(2)}, u32[]{:S(2)}) collective-permute-start(f32[32,384]{1,0:T(8,128)S(1)} %get-tuple-element.52), channel_id=1, source_target_pairs={{0,1},{1,2},{2,3},{3,0},{4,5},{5,6},{6,7},{7,4},{8,9},{9,10},{10,1... | collective-permute-start | bytes 147464 | tf_op jit(solution)/shard_map/ppermute | solution.py:136
  47.3 5.7 %collective-permute-start.3 = (f32[32,384]{1,0:T(8,128)S(1)}, f32[32,384]{1,0:T(8,128)S(1)}, u32[]{:S(2)}, u32[]{:S(2)}) collective-permute-start(f32[32,384]{1,0:T(8,128)S(1)} %get-tuple-element.53), channel_id=1, source_target_pairs={{0,3},{1,0},{2,1},{3,2},{4,7},{5,4},{6,5},{7,6},{8,11},{9,8},{10,9... | collective-permute-start | bytes 147464 | tf_op jit(solution)/shard_map/ppermute | solution.py:136
  48.6 4.5 %collective-permute-start.4 = (f32[32,384]{1,0:T(8,128)S(1)}, f32[32,384]{1,0:T(8,128)S(1)}, u32[]{:S(2)}, u32[]{:S(2)}) collective-permute-start(f32[32,384]{1,0:T(8,128)S(1)} %get-tuple-element.54), channel_id=1, source_target_pairs={{0,2},{1,3},{2,0},{3,1},{4,6},{5,7},{6,4},{7,5},{8,10},{9,11},{10,... | collective-permute-start | bytes 147464 | tf_op jit(solution)/shard_map/ppermute | solution.py:136
  59.1 9.6 %all-to-all-start.2 = ((f32[32,1,128]{2,1,0:T(1,128)}), f32[32,1,128]{2,1,0:T(1,128)S(1)}, u32[]{:S(2)}, u32[]{:S(2)}) async-start(f32[32,1,128]{2,1,0:T(1,128)} %bitcast.33), calls=%async_computation.2 | async-start | bytes 32768 | tf_op jit(solution)/shard_map/all_to_all | solution.py:435

commit v3 on v2

--- a/solution.py
+++ b/solution.py
@@ -49,17 +49,6 @@
     distance = jnp.minimum(apart, width - apart).astype(jnp.float32)
     inside = (rows_index < width) & (cols_index < width)
     return jnp.where(inside, kernel_values(distance), 0).astype(jnp.bfloat16)
-
-
-def smooth_longitude(field, reach, blocks):
-    width = field.shape[-1] // blocks
-    pieces = field.reshape(field.shape[:-1] + (blocks, width))
-    before = jnp.roll(pieces, 1, axis=-2)[..., width - reach :]
-    after = jnp.roll(pieces, -1, axis=-2)[..., :reach]
-    window = jnp.concatenate([before, pieces, after], axis=-1)
-    kernel = lon_kernel(reach, width)
-    result = jnp.einsum("...bm,mo->...bo", window, kernel, preferred_element_type=jnp.float32)
-    return result.reshape(field.shape).astype(jnp.bfloat16)
 
 
 def halves(full):
@@ -218,6 +207,50 @@
         for t in range(slots):
             image = ensemble_share * jnp.sum(scaled[t] * local, axis=0)
             image_ref[:, t * own : (t + 1) * own] = image[:, :kept].reshape(bands, own, kept)
+
+    def pack(slots, levels, rows, halo, marks, ensemble, out_ref):
+        values = ensemble[...].astype(jnp.float32)
+        lon = values.shape[1]
+        share, own = lon // bands, levels // members * rows
+        tail = out_ref.shape[2] - share - 2 * halo
+        mark = jnp.full((values.shape[0], tail), marks[0], jnp.int32).astype(jnp.float32)
+        for band in range(bands):
+            start = band * share
+            parts = [values[:, start : min(lon, start + share + halo)]]
+            if start + share + halo > lon:
+                parts.append(values[:, : start + share + halo - lon])
+            if start < halo:
+                parts.append(values[:, lon - halo + start :])
+            parts += [values[:, max(start - halo, 0) : start]] if start else []
+            window = jnp.concatenate(parts + [mark], axis=1)
+            for member in range(members):
+                picked = [
+                    window[slot * levels * rows + member * own : slot * levels * rows + (member + 1) * own]
+                    for slot in range(slots)
+                ]
+                out_ref[member * bands + band] = jnp.concatenate(picked, axis=0).astype(jnp.bfloat16)
+
+    def fold_smooth(slots, scale, ensemble, innovation, precision, kernel, out_ref):
+        count, lon = precision.shape
+        precise = precision[...].astype(jnp.float32)
+        total = jnp.zeros((count, lon), jnp.float32)
+        for t in range(slots):
+            place = slice(t * count, (t + 1) * count)
+            weighted = precise * innovation[place].astype(jnp.float32)
+            total = total + ensemble[place].astype(jnp.float32) * weighted
+        total = scale[0] * total
+        width = kernel.shape[1]
+        margin = (kernel.shape[0] - width) // 2
+        steps = -(-lon // width)
+        after = steps * width + margin - lon
+        ring = jnp.concatenate([total[:, lon - margin :], total, total[:, :after]], axis=1)
+        ring = ring.astype(jnp.bfloat16)
+        for step in range(steps):
+            start, stop = step * width, min(lon, (step + 1) * width)
+            piece = jnp.dot(
+                ring[:, start : start + kernel.shape[0]], kernel[...], preferred_element_type=jnp.float32
+            )
+            out_ref[:, start:stop] = piece[:, : stop - start].astype(jnp.bfloat16)
 
     def first_gradient(below, here, above, taper, grad_ref):
         stacked = jnp.concatenate([below[...], here[...], above[...]], axis=0)
@@ -324,10 +357,15 @@
                 name=name,
             )(*operands)
 
-        pieces = windows(
-            ensemble[0], bands, halo, padded, member_of_slot.astype(jnp.bfloat16)[0]
-        ).reshape(bands, slots, members, own, padded)
-        pieces = jnp.transpose(pieces, (2, 0, 1, 3, 4)).reshape(members * bands, slots * own, padded)
+        ensemble = ensemble.reshape(slots * levels * rows, lon)
+        (pieces,) = call(
+            lambda *refs: pack(slots, levels, rows, halo, *refs),
+            "pack",
+            [((members * bands, slots * own, padded), jnp.bfloat16)],
+            [smem, vmem],
+            member_of_slot,
+            ensemble,
+        )
         pieces, ensemble, member_weight, member_of_slot, halfwidth, static_root, innovation, precision = (
             lax.optimization_barrier(
                 (pieces, ensemble, member_weight, member_of_slot, halfwidth, static_root, innovation, precision)
@@ -361,26 +399,6 @@
         static = jnp.pad(
             jnp.transpose(static.reshape(own, bands, lon_share), (1, 0, 2)),
             ((0, 0), (0, 0), (0, kept - lon_share)),
-        )
-
-        picker = (member_of_slot[0] == jnp.arange(member_weight.shape[0], dtype=jnp.int32)).astype(
-            jnp.float32
-        )
-        scale = jnp.sum(picker * member_weight)
-        folded = scale * jnp.sum(
-            ensemble.reshape(slots, levels * rows, lon).astype(jnp.float32) * weighted, axis=0
-        )
-        smoothed = smooth_longitude(folded.astype(jnp.bfloat16), LREACH, 3)
-        below, above = neighbours(smoothed)
-        (grad_first,) = call(
-            first_gradient,
-            "first_gradient",
-            [((levels * rows, lon), jnp.float32)],
-            [vmem] * 4,
-            below,
-            smoothed,
-            above,
-            halo_taper(halfwidth, rows),
         )
 
         ring = ring_kernel(width, padded)
@@ -421,6 +439,24 @@
         )
         images = exchange_bands(jnp.concatenate([image_first, image_second], axis=1))
 
+        image_second, ensemble, innovation, precision = lax.optimization_barrier(
+            (image_second, ensemble, innovation, precision)
+        )
+        picker = member_of_slot == jnp.arange(member_weight.shape[0], dtype=jnp.int32)
+        scale = jnp.sum(picker.astype(jnp.float32) * member_weight, keepdims=True)
+        (smoothed,) = call(
+            lambda *refs: fold_smooth(slots, *refs),
+            "fold_smooth",
+            [((levels * rows, lon), jnp.bfloat16)],
+            [smem, vmem, vmem, vmem, vmem],
+            scale,
+            ensemble,
+            innovation.reshape(slots * levels * rows, lon),
+            precision,
+            lon_kernel(LANES, 2 * LANES),
+        )
+        below, above = neighbours(smoothed)
+
         (sums,) = call(
             lambda *refs: inner_products(slots, lon_share, *refs),
             "inner_products",
@@ -432,6 +468,7 @@
             static,
             mixing,
         )
+        sums, below, smoothed, above = lax.optimization_barrier((sums, below, smoothed, above))
         sums = lax.all_to_all(sums, BOTH, 0, 0, tiled=True)
         grad_second, pulled_second, images = call(
             lambda *refs: join(slots, lon_share, *refs),
@@ -447,6 +484,17 @@
             static,
             mixing,
             pulling,
+            flops=10**9,
+        )
+        (grad_first,) = call(
+            first_gradient,
+            "first_gradient",
+            [((levels * rows, lon), jnp.float32)],
+            [vmem] * 4,
+            below,
+            smoothed,
+            above,
+            halo_taper(halfwidth, rows),
             flops=10**9,
         )
         return call(

time: 70.3 us -> 78.8 us (1.12)
  waiting for transfers between devices: 17.9 us -> 22.6 us
  local copies, waits for them, and re-layouts: 7.31 us -> 11 us
  Pallas kernels: 7.42 us -> 8.77 us
  matrix products: 1.78 us -> 0.91 us
    unnamed x14 -> x26, local copies, waits for them, and re-layouts: 1.19 us -> 7.91 us
    all_to_all x1, waiting for transfers between devices: 4.33 us -> 10.5 us  [shards(): stacked = lax.all_to_all(pieces, BOTH, 0, 0, tiled=True)]
    ppermute x1, waiting for transfers between devices: 0.01 us -> 4.96 us  [neighbours(): lax.ppermute(block, 'band', backward)]
    all_to_all x1, waiting for transfers between devices: 4.82 us -> 0.01 us  [shards(): back = lax.all_to_all(out, BOTH, 0, 0, tiled=True)]
    all_to_all x1, starting transfers between devices: 2.54 us -> 4.96 us  [shards(): sums = lax.all_to_all(sums, BOTH, 0, 0, tiled=True)]
    ppermute x6, waiting for transfers between devices: 2.39 us -> 0.02 us  [exchange_bands(): lax.ppermute(outgoing, 'band', [(i, (i + shift) % count) for i in range(c...]
    pallas_call x6 -> x8, Pallas kernels: 7.42 us -> 8.77 us  [call(): pl.pallas_call(body, out_shape=tuple((jax.ShapeDtypeStruct(shape, kind) f...]
    slice x2 -> x1, local copies, waits for them, and re-layouts: 1.38 us -> 0.09 us  [windows(): ring[..., start + halo:start + 2 * halo + share]]
  transfers between devices with their start and end apart: 11 -> 11, of which waited for: 6 -> 4; matrix products, arithmetic and copies ran while one was open for 9% -> 7% of each run, Pallas kernels for 8% -> 6%
where the time goes in v3:
time: 78.8 us; the launch traced here: 78.2 us
  starting transfers between devices  27.7 us (35%)
  waiting for transfers between devices  22.6 us (29%)
  local copies, waits for them, and re-layouts  11 us (14%)
  Pallas kernels  8.77 us (11%)
  other arithmetic  5.4 us (7%)
  between operations  1.79 us (2%)
  matrix products  0.91 us (1%)
    all_to_all x1, waiting for transfers between devices, shards(): stacked = lax.all_to_all(pieces, BOTH, 0, 0, tiled=True)  10.5 us
    ppermute x6, starting transfers between devices, exchange_bands(): lax.ppermute(outgoing, 'band', [(i, (i + shift) % count) for i in range(c...  8.78 us
    pallas_call x8, Pallas kernels, call(): pl.pallas_call(body, out_shape=tuple((jax.ShapeDtypeStruct(shape, kind) f...  8.77 us
    unnamed x26, local copies, waits for them, and re-layouts  7.91 us
    all_to_all x1, waiting for transfers between devices, shards(): sums = lax.all_to_all(sums, BOTH, 0, 0, tiled=True)  6.01 us
    all_to_all x1, starting transfers between devices, shards(): stacked = lax.all_to_all(pieces, BOTH, 0, 0, tiled=True)  5.79 us
    all_to_all x1, starting transfers between devices, shards(): sums = lax.all_to_all(sums, BOTH, 0, 0, tiled=True)  4.96 us
    ppermute x1, waiting for transfers between devices, neighbours(): lax.ppermute(block, 'band', backward)  4.96 us
  transfers between devices with their start and end apart: 11, of which 4 were waited for; matrix products, arithmetic and copies ran while one was open for 7% of the time, Pallas kernels for 6%

profile of v3, /device:TPU:0, one launch (start us, length us, event | category | flops | bytes accessed | tf_op | source)
XLA Modules:
  0.0 78.2 jit_solution(11329490441867672990)
XLA Ops:
  0.6 1.2 %reshape.1083.refs_1_ = bf16[128,1440]{1,0:T(8,128)(2,1)S(1)} reshape(bf16[1,2,16,4,1440]{4,3,2,1,0:T(4,128)(2,1)} %param.7) | data formatting | bytes 737280 | tf_op jit(solution)/shard_map/reshape | solution.py:360
  2.5 1.0 %pack.1 = bf16[32,16,512]{2,1,0:T(8,128)(2,1)} custom-call(s32[1]{0:T(128)} %copy.18.refs_0_, bf16[128,1440]{1,0:T(8,128)(2,1)S(1)} %reshape.1083.refs_1_), custom_call_target="tpu_custom_call" | custom-call | bytes 1048576 | tf_op jit(solution)/shard_map/pack/pallas_call | solution.py:350
  3.5 0.1 reshape.1085.refs_3_
  3.6 0.9 %copy-done.7 = bf16[2,16,4,1440]{3,2,1,0:T(4,128)(2,1)S(1)} copy-done((bf16[2,16,4,1440]{3,2,1,0:T(4,128)(2,1)S(1)}, bf16[2,16,4,1440]{3,2,1,0:T(4,128)(2,1)}, u32[]{:S(2)}) %copy-start.7) | copy-done | bytes 368664
  4.5 0.2 reshape.1084
  4.7 0.3 multiply_reduce_fusion
  4.9 0.0 copy-start.11
  5.0 0.1 reduce_sum.21
  5.1 0.5 copy-done.11
  5.6 0.1 copy.13
  5.7 0.1 broadcast_multiply_fusion
  5.8 0.3 mul.135.refs_4_
  6.1 0.1 broadcast_multiply_fusion.1
  6.2 0.1 mul.128
  6.3 0.5 fusion.49.refs_3_
  6.7 0.3 fusion.50
  7.1 0.6 copy-done.9
  7.7 0.1 fusion.47
  7.8 0.1 fusion.46
  7.9 0.1 pad.36.clone
  8.0 0.1 maximum_bitcast_fusion.1
  8.2 3.9 %collective-permute-start = (bf16[32,512]{1,0:T(8,128)(2,1)S(1)}, bf16[32,512]{1,0:T(8,128)(2,1)S(1)}, u32[]{:S(2)}, u32[]{:S(2)}) collective-permute-start(bf16[32,512]{1,0:T(8,128)(2,1)S(1)} %get-tuple-element.59), channel_id=1, source_target_pairs={{0,3},{1,0},{2,1},{3,2},{4,7},{5,4},{6,5},{7,6},{8,11},{9,8},{10,9... | collective-permute-start | bytes 98312 | tf_op jit(solution)/shard_map/ppermute | solution.py:125
  12.1 0.5 collective-permute-start.1
  12.6 0.6 collective-permute-start.2
  13.2 5.8 %all-to-all-start = ((bf16[32,16,512]{2,1,0:T(8,128)(2,1)}), bf16[32,16,512]{2,1,0:T(8,128)(2,1)S(1)}, u32[]{:S(2)}, u32[]{:S(2)}) async-start(bf16[32,16,512]{2,1,0:T(8,128)(2,1)} %pack.1), calls=%async_computation | async-start | bytes 1048576 | tf_op jit(solution)/shard_map/all_to_all | solution.py:374
  19.0 0.1 fusion.51.refs_4_.refs_3_
  19.2 0.7 copy-done.12
  19.8 0.1 dynamic-slice_convert_fusion
  19.9 0.6 fusion.48
  20.5 0.1 broadcast_in_dim.28
  20.6 0.1 add.292
  20.7 1.3 %fusion.42 = f32[256,1]{0,1:T(1,128)S(1)} fusion(f32[]{:T(128)} %bitcast.17, f32[]{:T(128)} %bitcast.16), kind=kLoop, calls=%fused_computation.131 | loop fusion | flops 6400 | bytes 1032 | tf_op jit(solution)/shard_map/add | solution.py:92
  22.0 0.2 fusion.2
  22.2 0.7 pad_maximum_fusion.refs_4_
  22.9 0.1 fusion.26
  23.1 0.3 select_convert_fusion.1.refs_4_
  23.4 0.6 and_select_fusion.refs_3_
  24.1 0.7 pad_maximum_fusion.3.refs_2_
  24.8 10.5 %all-to-all-done.refs_1_ = bf16[32,16,512]{2,1,0:T(8,128)(2,1)S(1)} async-done(((bf16[32,16,512]{2,1,0:T(8,128)(2,1)}), bf16[32,16,512]{2,1,0:T(8,128)(2,1)S(1)}, u32[]{:S(2)}, u32[]{:S(2)}) %all-to-all-start) | async-done | bytes 524320 | tf_op jit(solution)/shard_map/all_to_all | solution.py:374
  35.3 0.9 %copy-done.1 = bf16[2,256,256]{2,1,0:T(8,128)(2,1)S(1)} copy-done((bf16[2,256,256]{2,1,0:T(8,128)(2,1)S(1)}, bf16[2,256,256]{2,1,0:T(8,128)(2,1)}, u32[]{:S(2)}) %copy-start.1) | copy-done | bytes 262168
  36.2 0.9 %copy-done.3 = bf16[4,32,512]{2,1,0:T(8,128)(2,1)S(1)} copy-done((bf16[4,32,512]{2,1,0:T(8,128)(2,1)S(1)}, bf16[4,32,512]{2,1,0:T(8,128)(2,1)}, u32[]{:S(2)}) %copy-start.3) | copy-done | bytes 131096
  37.1 2.3 %first_half.1 = (bf16[32,16,384]{2,1,0:T(8,128)(2,1)S(1)}, f32[4,16,384]{2,1,0:T(8,128)S(1)}, bf16[256,512]{1,0:T(8,128)(2,1)S(1)}) custom-call(f32[8]{0:T(128)S(1)} %copy-done.4, bf16[32,16,512]{2,1,0:T(8,128)(2,1)S(1)} %all-to-all-done.refs_1_, bf16[4,32,512]{2,1,0:T(8,128)(2,1)S(1)} %copy-done.3, bf16[512,512]{1,0:T(8,128)(2,1)S(1)} %and_select_fusion.refs_3_, ...), custom_call_target="tpu_custom_call" | custom-call | flops 1000000000 | bytes 1048576 | tf_op jit(solution)/shard_map/first_half/pallas_call | solution.py:350
  39.4 0.7 copy-done
  40.2 0.7 copy-done.5
  40.9 2.6 %all-to-all-start.1 = ((bf16[32,16,384]{2,1,0:T(8,128)(2,1)}), bf16[32,16,384]{2,1,0:T(8,128)(2,1)S(1)}, u32[]{:S(2)}, u32[]{:S(2)}) async-start(bf16[32,16,384]{2,1,0:T(8,128)(2,1)} %copy-done), calls=%async_computation.1 | async-start | bytes 786432 | tf_op jit(solution)/shard_map/all_to_all | solution.py:427
  43.5 0.9 %copy-done.2 = bf16[2,256,256]{2,1,0:T(8,128)(2,1)S(1)} copy-done((bf16[2,256,256]{2,1,0:T(8,128)(2,1)S(1)}, bf16[2,256,256]{2,1,0:T(8,128)(2,1)}, u32[]{:S(2)}) %copy-start.2) | copy-done | bytes 262168
  44.4 0.9 %copy-done.6 = bf16[256,512]{1,0:T(8,128)(2,1)S(1)} copy-done((bf16[256,512]{1,0:T(8,128)(2,1)S(1)}, bf16[256,512]{1,0:T(8,128)(2,1)}, u32[]{:S(2)}) %copy-start.6) | copy-done | bytes 262168
  45.4 1.2 %second_half.1 = f32[4,16,384]{2,1,0:T(8,128)S(1)} custom-call(f32[8]{0:T(128)S(1)} %copy-done.4, bf16[32,16,512]{2,1,0:T(8,128)(2,1)S(1)} %all-to-all-done.refs_1_, bf16[256,512]{1,0:T(8,128)(2,1)S(1)} %copy-done.6, bf16[512,512]{1,0:T(8,128)(2,1)S(1)} %and_select_fusion.refs_3_, bf16[2,256,256]{2,1,0:T(8,128)(2,1)S(1)} %copy-done.2), custom_call_target="tpu_custom_call" | custom-call | flops 1000000000 | bytes 1048576 | tf_op jit(solution)/shard_map/second_half/pallas_call | solution.py:350
  46.6 2.6 %collective-permute-start.3 = (f32[32,384]{1,0:T(8,128)S(1)}, f32[32,384]{1,0:T(8,128)S(1)}, u32[]{:S(2)}, u32[]{:S(2)}) collective-permute-start(f32[32,384]{1,0:T(8,128)S(1)} %get-tuple-element.55), channel_id=1, source_target_pairs={{0,3},{1,0},{2,1},{3,2},{4,7},{5,4},{6,5},{7,6},{8,11},{9,8},{10,9... | collective-permute-start | bytes 147464 | tf_op jit(solution)/shard_map/ppermute | solution.py:125
  49.2 0.5 collective-permute-start.4
  49.7 0.6 collective-permute-start.5
  50.3 0.6 fusion.44
  50.9 0.1 reshape.1087
  51.1 1.1 %fold_smooth.1.here = bf16[64,1440]{1,0:T(8,128)(2,1)S(1)} custom-call(f32[1]{0:T(128)} %bitcast.29.refs_0_, bf16[128,1440]{1,0:T(8,128)(2,1)S(1)} %reshape.1083.refs_1_, bf16[128,1440]{1,0:T(8,128)(2,1)S(1)} %bitcast.100, bf16[64,1440]{1,0:T(8,128)(2,1)S(1)} %reshape.1085.refs_3_, bf16[512,256]{1,0:T(8,128)(2,1)S(1)} %select_convert_fusion.1.refs_4_), custom_call_target="tpu_custom_call" | custom-call | bytes 1048576 | tf_op jit(solution)/shard_map/fold_smooth/pallas_call | solution.py:350
  52.1 4.3 %collective-permute-start.6 = (bf16[64,1440]{1,0:T(8,128)(2,1)S(1)}, bf16[64,1440]{1,0:T(8,128)(2,1)S(1)}, u32[]{:S(2)}, u32[]{:S(2)}) collective-permute-start(bf16[64,1440]{1,0:T(8,128)(2,1)S(1)} %fold_smooth.1.here), channel_id=1, source_target_pairs={{0,1},{1,2},{2,3},{4,5},{5,6},{6,7},{8,9},{9,10},{10,11},{12,13},{... | collective-permute-start | bytes 552968 | tf_op jit(solution)/shard_map/ppermute | solution.py:29
  56.4 1.3 %collective-permute-start.7 = (bf16[64,1440]{1,0:T(8,128)(2,1)S(1)}, bf16[64,1440]{1,0:T(8,128)(2,1)S(1)}, u32[]{:S(2)}, u32[]{:S(2)}) collective-permute-start(bf16[64,1440]{1,0:T(8,128)(2,1)S(1)} %fold_smooth.1.here), channel_id=1, source_target_pairs={{1,0},{2,1},{3,2},{5,4},{6,5},{7,6},{9,8},{10,9},{11,10},{13,12},{... | collective-permute-start | bytes 552968 | tf_op jit(solution)/shard_map/ppermute | solution.py:29
  57.8 1.0 %inner_products.1 = f32[32,128]{1,0:T(8,128)} custom-call(bf16[32,16,384]{2,1,0:T(8,128)(2,1)S(1)} %all-to-all-done.1.refs_0_, f32[4,32,384]{2,1,0:T(8,128)S(1)} %pad_maximum_fusion.1.refs_1_, bf16[4,32,512]{2,1,0:T(8,128)(2,1)S(1)} %pad_maximum_fusion.2.refs_2_, f32[4,8,384]{2,1,0:T(8,128)S(1)} %pad.4.refs_3_.refs_2_, f32[8,64]{1,0:T(8,128)S(1)} %fusion.51.refs_4_.refs_3_), custom_call_target="tpu_custom_call" | custom-call | bytes 1048576 | tf_op jit(solution)/shard_map/inner_products/pallas_call | solution.py:350
  58.9 1.2 %collective-permute-done.6.below = bf16[64,1440]{1,0:T(8,128)(2,1)S(1)} collective-permute-done((bf16[64,1440]{1,0:T(8,128)(2,1)S(1)}, bf16[64,1440]{1,0:T(8,128)(2,1)S(1)}, u32[]{:S(2)}, u32[]{:S(2)}) %collective-permute-start.6) | collective-permute-done | bytes 184352 | tf_op jit(solution)/shard_map/ppermute | solution.py:29
  60.0 5.0 %collective-permute-done.7.above = bf16[64,1440]{1,0:T(8,128)(2,1)S(1)} collective-permute-done((bf16[64,1440]{1,0:T(8,128)(2,1)S(1)}, bf16[64,1440]{1,0:T(8,128)(2,1)S(1)}, u32[]{:S(2)}, u32[]{:S(2)}) %collective-permute-start.7) | collective-permute-done | bytes 184352 | tf_op jit(solution)/shard_map/ppermute | solution.py:29
  65.0 5.0 %all-to-all-start.2 = ((f32[32,1,128]{2,1,0:T(1,128)}), f32[32,1,128]{2,1,0:T(1,128)S(1)}, u32[]{:S(2)}, u32[]{:S(2)}) async-start(f32[32,1,128]{2,1,0:T(1,128)} %bitcast.32), calls=%async_computation.2 | async-start | bytes 32768 | tf_op jit(solution)/shard_map/all_to_all | solution.py:472
  70.0 0.3 first_gradient.1.refs_1_
  70.3 0.7 join.1
  71.0 6.0 %all-to-all-done.2 = f32[32,1,128]{2,1,0:T(1,128)S(1)} async-done(((f32[32,1,128]{2,1,0:T(1,128)}), f32[32,1,128]{2,1,0:T(1,128)S(1)}, u32[]{:S(2)}, u32[]{:S(2)}) %all-to-all-start.2) | async-done | bytes 16416 | tf_op jit(solution)/shard_map/all_to_all | solution.py:472
  77.1 1.1 %finish.1 = (f32[1,16,4,1440]{3,2,1,0:T(4,128)}, f32[16,4,1440]{2,1,0:T(4,128)}, f32[2,2,4,1440]{3,2,1,0:T(4,128)}) custom-call(f32[32,128]{1,0:T(8,128)S(1)} %bitcast.101, f32[64,1440]{1,0:T(8,128)S(1)} %first_gradient.1.refs_1_, f32[64,1440]{1,0:T(8,128)S(1)} %get-tuple-element.42.refs_2_, f32[64,1440]{1,0:T(8,128)S(1)} %fusion.49.refs_3_, ...), custom_call_target="tpu_custom_call" | custom-call | bytes 1048576 | tf_op jit(solution)/shard_map/finish/pallas_call | solution.py:350
  (48 shorter events, 0.4 us)
Async XLA Ops:
  2.5 1.1 %copy-start.8 = (bf16[16,4,1440]{2,1,0:T(4,128)(2,1)S(1)}, bf16[16,4,1440]{2,1,0:T(4,128)(2,1)}, u32[]{:S(2)}) copy-start(bf16[16,4,1440]{2,1,0:T(4,128)(2,1)} %param.13) | copy-start | bytes 552964
  3.5 1.0 %copy-start.7 = (bf16[2,16,4,1440]{3,2,1,0:T(4,128)(2,1)S(1)}, bf16[2,16,4,1440]{3,2,1,0:T(4,128)(2,1)}, u32[]{:S(2)}) copy-start(bf16[2,16,4,1440]{3,2,1,0:T(4,128)(2,1)} %param.12) | copy-start | bytes 1105924
  4.9 0.7 copy-start.11
  7.1 0.6 copy-start.9
  8.2 15.9 %collective-permute-start = (bf16[32,512]{1,0:T(8,128)(2,1)S(1)}, bf16[32,512]{1,0:T(8,128)(2,1)S(1)}, u32[]{:S(2)}, u32[]{:S(2)}) collective-permute-start(bf16[32,512]{1,0:T(8,128)(2,1)S(1)} %get-tuple-element.59), channel_id=1, source_target_pairs={{0,3},{1,0},{2,1},{3,2},{4,7},{5,4},{6,5},{7,6},{8,11},{9,8},{10,9... | collective-permute-start | bytes 98312 | tf_op jit(solution)/shard_map/ppermute | solution.py:125
  12.1 11.9 %collective-permute-start.1 = (bf16[32,512]{1,0:T(8,128)(2,1)S(1)}, bf16[32,512]{1,0:T(8,128)(2,1)S(1)}, u32[]{:S(2)}, u32[]{:S(2)}) collective-permute-start(bf16[32,512]{1,0:T(8,128)(2,1)S(1)} %get-tuple-element.58), channel_id=1, source_target_pairs={{0,2},{1,3},{2,0},{3,1},{4,6},{5,7},{6,4},{7,5},{8,10},{9,11},{10,... | collective-permute-start | bytes 98312 | tf_op jit(solution)/shard_map/ppermute | solution.py:125
  12.6 11.4 %collective-permute-start.2 = (bf16[32,512]{1,0:T(8,128)(2,1)S(1)}, bf16[32,512]{1,0:T(8,128)(2,1)S(1)}, u32[]{:S(2)}, u32[]{:S(2)}) collective-permute-start(bf16[32,512]{1,0:T(8,128)(2,1)S(1)} %get-tuple-element.57), channel_id=1, source_target_pairs={{0,1},{1,2},{2,3},{3,0},{4,5},{5,6},{6,7},{7,4},{8,9},{9,10},{10,1... | collective-permute-start | bytes 98312 | tf_op jit(solution)/shard_map/ppermute | solution.py:125
  13.2 22.0 %all-to-all-start = ((bf16[32,16,512]{2,1,0:T(8,128)(2,1)}), bf16[32,16,512]{2,1,0:T(8,128)(2,1)S(1)}, u32[]{:S(2)}, u32[]{:S(2)}) async-start(bf16[32,16,512]{2,1,0:T(8,128)(2,1)} %pack.1), calls=%async_computation | async-start | bytes 1048576 | tf_op jit(solution)/shard_map/all_to_all | solution.py:374
  19.2 0.7 copy-start.12
  24.1 11.2 %copy-start.4 = (f32[8]{0:T(128)S(1)}, f32[8]{0:T(128)}, u32[]{:S(2)}) copy-start(f32[8]{0:T(128)} %refs_0_.2) | copy-start | bytes 100
  35.3 1.0 %copy-start.1 = (bf16[2,256,256]{2,1,0:T(8,128)(2,1)S(1)}, bf16[2,256,256]{2,1,0:T(8,128)(2,1)}, u32[]{:S(2)}) copy-start(bf16[2,256,256]{2,1,0:T(8,128)(2,1)} %pad_maximum_fusion.refs_4_) | copy-start | bytes 786436
  36.2 0.9 %copy-start.3 = (bf16[4,32,512]{2,1,0:T(8,128)(2,1)S(1)}, bf16[4,32,512]{2,1,0:T(8,128)(2,1)}, u32[]{:S(2)}) copy-start(bf16[4,32,512]{2,1,0:T(8,128)(2,1)} %pad_maximum_fusion.3.refs_2_) | copy-start | bytes 393220
  39.4 0.7 copy-start
  40.2 0.7 copy-start.5
  40.9 17.0 %all-to-all-start.1 = ((bf16[32,16,384]{2,1,0:T(8,128)(2,1)}), bf16[32,16,384]{2,1,0:T(8,128)(2,1)S(1)}, u32[]{:S(2)}, u32[]{:S(2)}) async-start(bf16[32,16,384]{2,1,0:T(8,128)(2,1)} %copy-done), calls=%async_computation.1 | async-start | bytes 786432 | tf_op jit(solution)/shard_map/all_to_all | solution.py:427
  43.5 1.0 %copy-start.2 = (bf16[2,256,256]{2,1,0:T(8,128)(2,1)S(1)}, bf16[2,256,256]{2,1,0:T(8,128)(2,1)}, u32[]{:S(2)}) copy-start(bf16[2,256,256]{2,1,0:T(8,128)(2,1)} %pad_maximum_fusion.refs_4_) | copy-start | bytes 786436
  44.4 0.9 %copy-start.6 = (bf16[256,512]{1,0:T(8,128)(2,1)S(1)}, bf16[256,512]{1,0:T(8,128)(2,1)}, u32[]{:S(2)}) copy-start(bf16[256,512]{1,0:T(8,128)(2,1)} %copy-done.5) | copy-start | bytes 786436
  46.6 4.4 %copy-start.10 = (f32[8,1440]{1,0:T(8,128)S(1)}, f32[8,1440]{1,0:T(8,128)}, u32[]{:S(2)}) copy-start(f32[8,1440]{1,0:T(8,128)} %copy-done.9) | copy-start | bytes 138244
  46.6 11.1 %collective-permute-start.3 = (f32[32,384]{1,0:T(8,128)S(1)}, f32[32,384]{1,0:T(8,128)S(1)}, u32[]{:S(2)}, u32[]{:S(2)}) collective-permute-start(f32[32,384]{1,0:T(8,128)S(1)} %get-tuple-element.55), channel_id=1, source_target_pairs={{0,3},{1,0},{2,1},{3,2},{4,7},{5,4},{6,5},{7,6},{8,11},{9,8},{10,9... | collective-permute-start | bytes 147464 | tf_op jit(solution)/shard_map/ppermute | solution.py:125
  49.2 8.5 %collective-permute-start.4 = (f32[32,384]{1,0:T(8,128)S(1)}, f32[32,384]{1,0:T(8,128)S(1)}, u32[]{:S(2)}, u32[]{:S(2)}) collective-permute-start(f32[32,384]{1,0:T(8,128)S(1)} %get-tuple-element.56), channel_id=1, source_target_pairs={{0,2},{1,3},{2,0},{3,1},{4,6},{5,7},{6,4},{7,5},{8,10},{9,11},{10,... | collective-permute-start | bytes 147464 | tf_op jit(solution)/shard_map/ppermute | solution.py:125
  49.7 8.0 %collective-permute-start.5 = (f32[32,384]{1,0:T(8,128)S(1)}, f32[32,384]{1,0:T(8,128)S(1)}, u32[]{:S(2)}, u32[]{:S(2)}) collective-permute-start(f32[32,384]{1,0:T(8,128)S(1)} %get-tuple-element.54), channel_id=1, source_target_pairs={{0,1},{1,2},{2,3},{3,0},{4,5},{5,6},{6,7},{7,4},{8,9},{9,10},{10,1... | collective-permute-start | bytes 147464 | tf_op jit(solution)/shard_map/ppermute | solution.py:125
  52.1 7.9 %collective-permute-start.6 = (bf16[64,1440]{1,0:T(8,128)(2,1)S(1)}, bf16[64,1440]{1,0:T(8,128)(2,1)S(1)}, u32[]{:S(2)}, u32[]{:S(2)}) collective-permute-start(bf16[64,1440]{1,0:T(8,128)(2,1)S(1)} %fold_smooth.1.here), channel_id=1, source_target_pairs={{0,1},{1,2},{2,3},{4,5},{5,6},{6,7},{8,9},{9,10},{10,11},{12,13},{... | collective-permute-start | bytes 552968 | tf_op jit(solution)/shard_map/ppermute | solution.py:29
  56.4 8.6 %collective-permute-start.7 = (bf16[64,1440]{1,0:T(8,128)(2,1)S(1)}, bf16[64,1440]{1,0:T(8,128)(2,1)S(1)}, u32[]{:S(2)}, u32[]{:S(2)}) collective-permute-start(bf16[64,1440]{1,0:T(8,128)(2,1)S(1)} %fold_smooth.1.here), channel_id=1, source_target_pairs={{1,0},{2,1},{3,2},{5,4},{6,5},{7,6},{9,8},{10,9},{11,10},{13,12},{... | collective-permute-start | bytes 552968 | tf_op jit(solution)/shard_map/ppermute | solution.py:29
  65.0 12.1 %all-to-all-start.2 = ((f32[32,1,128]{2,1,0:T(1,128)}), f32[32,1,128]{2,1,0:T(1,128)S(1)}, u32[]{:S(2)}, u32[]{:S(2)}) async-start(f32[32,1,128]{2,1,0:T(1,128)} %bitcast.32), calls=%async_computation.2 | async-start | bytes 32768 | tf_op jit(solution)/shard_map/all_to_all | solution.py:472

commit v4 on v0

v4 whole, which is shorter than its diff:
```python
import math

import jax
import jax.numpy as jnp
import numpy as np
from jax import lax
from jax.experimental import pallas as pl
from jax.experimental.pallas import tpu as pltpu
from jax.sharding import PartitionSpec as P

HMAX = 4
LREACH = 18
REACHES = 4
LANES = 128
FEW = 8
BOTH = ("member", "band")

ensemble_share = 0.8
static_share = 0.6
length_scale = 6.0


def round_up(value, step):
    return -(-value // step) * step


def lon_weights(distance):
    distance = distance.astype(np.float32)
    values = np.exp(np.float32(-0.5) * (distance / np.float32(length_scale)) ** 2)
    values = values / np.float32(length_scale * math.sqrt(2.0 * math.pi))
    return jnp.asarray(np.where(distance <= LREACH, values, 0.0), jnp.bfloat16)


def lon_kernel(reach, width):
    return lon_weights(np.abs(np.arange(width + 2 * reach)[:, None] - reach - np.arange(width)[None]))


def ring_kernel(width, padded):
    apart = np.abs(np.arange(padded)[:, None] - np.arange(padded)[None])
    inside = (np.arange(padded)[:, None] < width) & (np.arange(padded)[None] < width)
    return lon_weights(np.where(inside, np.minimum(apart, width - apart), 2 * LREACH))


def halves(full):
    high = full.astype(jnp.bfloat16)
    return high, (full - high.astype(jnp.float32)).astype(jnp.bfloat16)


def near(apart, spans):
    return jnp.maximum(1.0 - apart / spans, 0.0) / spans


def row_apart(bands, held, rows, copies):
    index = np.arange(copies * bands * held * rows)
    latitude = index // (held * rows) % bands * rows + index % rows
    level = index // rows % held
    copy = index // (bands * held * rows)
    same = (copy[:, None] == copy[None]) & (level[:, None] == level[None])
    apart = np.where(same, np.abs(latitude[:, None] - latitude[None]), 1000)
    return apart.astype(np.float32), level[:, None].astype(np.float32)


def halo_apart(levels, rows):
    own = levels * rows
    target, source = np.arange(own)[:, None], np.arange(3 * own)[None]
    shift = (source // own - 1) * rows + source % rows - target % rows
    same = source // rows % levels == target // rows
    level = (target // rows).astype(np.float32)
    return np.where(same, np.abs(shift), 1000).astype(np.float32), level


def each_row(matrix, rows):
    same = jnp.eye(rows, dtype=jnp.float32)
    wide = matrix[:, None, :, None] * same[None, :, None, :]
    return wide.reshape(matrix.shape[0] * rows, matrix.shape[1] * rows)


def exact_dot(matrix, field):
    return jnp.dot(
        matrix, field, precision=lax.Precision.HIGHEST, preferred_element_type=jnp.float32
    )


def window(values, band, share, halo, tail):
    lon = values.shape[1]
    start = band * share
    stop = start + share + halo
    parts = [values[:, start : min(lon, stop)]]
    if stop > lon:
        parts.append(values[:, : stop - lon])
    if start < halo:
        parts.append(values[:, lon - halo + start :])
    if start:
        parts.append(values[:, max(start - halo, 0) : start])
    return jnp.concatenate(parts + [tail], axis=1)


def spread(field, ring, taper):
    copies = taper.shape[1]
    smoothed = jnp.dot(field.astype(jnp.bfloat16), ring, preferred_element_type=jnp.float32)
    smoothed = smoothed.astype(jnp.bfloat16)
    parts = []
    for start in range(0, field.shape[0], copies):
        part = smoothed[start : start + copies]
        parts.append(
            jnp.dot(taper[0], part, preferred_element_type=jnp.float32)
            + jnp.dot(taper[1], part, preferred_element_type=jnp.float32)
        )
    return parts[0] if len(parts) == 1 else jnp.concatenate(parts, axis=0)


def solution(mesh):
    members, bands = mesh.shape["member"], mesh.shape["band"]
    groups = 2 if members % 2 == 0 else 1
    fellows = members // groups
    few = bands <= FEW

    def shards(ensemble, member_weight, member_of_slot, halfwidth, static_root, innovation, precision):
        _, slots, levels, rows, lon = ensemble.shape
        level_share, lon_share = levels // members, lon // bands
        own = level_share * rows
        held = groups * own
        halo = REACHES * LREACH
        width = lon_share + 2 * halo
        padded = round_up(width + 1, LANES)
        kept = min(padded, round_up(lon_share, LANES))
        per_member = bands * held
        copies = fellows
        while copies > 1 and (copies * per_member > 256 or fellows % copies):
            copies -= 1
        arrays = slots + 2
        vmem = pl.BlockSpec(memory_space=pltpu.VMEM)
        smem = pl.BlockSpec(memory_space=pltpu.SMEM)
        limit = min(48, max(14, 24 * fellows * bands * slots * held * padded // 2**20)) * 2**20

        def call(body, shapes, scalars, operands, scratch=(), flops=0):
            return pl.pallas_call(
                body,
                out_shape=tuple(jax.ShapeDtypeStruct(shape, kind) for shape, kind in shapes),
                in_specs=[smem] * len(scalars) + [vmem] * len(operands),
                out_specs=(vmem,) * len(shapes),
                scratch_shapes=[pltpu.VMEM(shape, kind) for shape, kind in scratch],
                compiler_params=pltpu.CompilerParams(vmem_limit_bytes=limit),
                cost_estimate=pl.CostEstimate(flops=flops, bytes_accessed=0, transcendentals=0),
                name=body.__name__,
            )(*scalars, *operands)

        f32, bf16 = jnp.float32, jnp.bfloat16

        def position(here):
            return lax.div(here[0], fellows), lax.rem(here[0], fellows), here[1]

        def level_of(group, fellow, share):
            return (group * fellows + fellow) * level_share + share

        def shifted(place, shift, count):
            return lax.rem(place + shift + count, count)

        def load_members(weight, stacked):
            stacked = stacked[...].astype(f32)
            which = stacked[:, :1, width : width + 1]
            scale = jnp.zeros(which.shape, f32)
            for member in range(members):
                scale = scale + jnp.where(which == member, weight[member], 0.0)
            shape = (fellows, per_member, padded)
            return [
                (scale * stacked[:, slot * held : (slot + 1) * held]).reshape(shape)
                for slot in range(slots)
            ]

        def fold(scaled, weighted):
            total = scaled[0] * weighted[0][None]
            for slot in range(1, slots):
                total = total + scaled[slot] * weighted[slot][None]
            return total.reshape(fellows * per_member, padded)

        def images_of(scaled, grad, ring, taper):
            local = spread(grad, ring, taper).reshape(fellows, per_member, padded)
            return [ensemble_share * jnp.sum(scaled[t] * local, axis=0) for t in range(slots)]

        def pack(marks, ensemble, out):
            values = jnp.concatenate(
                [ensemble[0, t, level].astype(f32) for t in range(slots) for level in range(levels)],
                axis=0,
            )
            tail = jnp.full((values.shape[0], padded - width), marks[0], jnp.int32).astype(f32)
            for band in range(bands):
                piece = window(values, band, lon_share, halo, tail)
                for fellow in range(fellows):
                    picked = []
                    for t in range(slots):
                        for group in range(groups):
                            start = (t * levels + level_of(group, fellow, 0)) * rows
                            picked.append(piece[start : start + own])
                    out[fellow * bands + band] = jnp.concatenate(picked, axis=0).astype(bf16)

        def observe(here, widths, innovation, precision, pulling, root, apart, level, *refs):
            outs, (pieces, pulled, mixing, taper, static, mixed, spans) = refs[:-7], refs[-7:]
            group_here, fellow_here, band_here = position(here)
            total = []
            for at in range(levels):
                precise = precision[at].astype(f32)
                part = precise * innovation[0, at].astype(f32)
                for t in range(1, slots):
                    part = part + precise * innovation[t, at].astype(f32)
                total.append(part)
            back = exact_dot(pulling[...], jnp.concatenate(total, axis=0))
            pulled[...] = back
            forth = exact_dot(root[...], back)
            both = exact_dot(root[...], pulling[...])
            for at in range(levels):
                static[at] = forth[at * rows : (at + 1) * rows]
                mixed[at] = both[at * rows : (at + 1) * rows]

            def of_levels(picked):
                parts = [innovation[t, at].astype(f32) for t in range(slots) for at in picked]
                parts += [precision[at].astype(f32) for at in picked] + [static[at] for at in picked]
                return jnp.concatenate(parts, axis=0)

            picked = [level_of(group_here, fellow_here, share) for share in range(level_share)]
            mixing[...] = jnp.concatenate([mixed[at] for at in picked], axis=0)
            values = of_levels(picked)
            tail = jnp.zeros((values.shape[0], padded - width), f32)
            for band in range(bands):
                pieces[band] = window(values, band, lon_share, halo, tail)[:, :kept]

            picked = [
                level_of(group, fellow_here, share)
                for group in range(groups)
                for share in range(level_share)
            ]
            values = of_levels(picked)
            tail = jnp.zeros((values.shape[0], padded - width), f32)
            for band in range(bands):
                piece = window(values, band, lon_share, halo, tail).astype(bf16)
                if few:
                    spans[band] = piece
                else:
                    outs[0][band] = piece
            if few:
                for shift in range(bands):
                    outs[shift][...] = spans[shifted(band_here, shift, bands)]
            span = jnp.ones(level.shape, f32)
            for at, which in enumerate(picked):
                span = span + jnp.where(level[...] == at, widths[which].astype(f32), 0.0)
            taper[0], taper[1] = halves(near(apart[...], span))

        def first_image(here, weight, stacked, ring, taper, *refs):
            blocks, (part, send, fields, spans) = refs[:-4], refs[-4:]
            _, _, band_here = position(here)
            if few:
                for shift in range(bands):
                    spans[shifted(band_here, -shift, bands)] = blocks[shift][...]
                values = spans[...]
            else:
                values = blocks[0][...]
            field = []
            for index in range(arrays):
                piece = values[:, index * held : (index + 1) * held].reshape(per_member, padded)
                fields[index] = piece
                field.append(piece.astype(f32))
            scaled = load_members(weight, stacked)
            weighted = [field[slots] * field[t] for t in range(slots)]
            grad = ensemble_share * spread(fold(scaled, weighted), ring[...], taper)
            for t, image in enumerate(images_of(scaled, grad, ring[...], taper)):
                part[t] = image
                send[t] = image.astype(bf16)

        def second_gradient(here, weight, stacked, ring, taper, part, fields, *refs):
            others, (out, image_out, grad_out) = refs[:-3], refs[-3:]
            scaled = load_members(weight, stacked)
            precise, static = fields[slots].astype(f32), fields[slots + 1].astype(f32)
            weighted, total = [], jnp.zeros((per_member, padded), f32)
            for t in range(slots):
                image = part[t]
                for other in others:
                    image = image + other[t].astype(f32)
                image_out[t] = image[:, :kept].reshape(bands, groups, own, kept)
                weighted.append(precise * (image + static))
                total = total + weighted[t]
            grad = ensemble_share * spread(fold(scaled, weighted), ring[...], taper)
            grad_out[...] = grad.astype(bf16)
            grad = grad[:, :kept].reshape(fellows, bands, held, kept)
            total = total[:, :kept].reshape(bands, held, kept)
            for fellow in range(fellows):
                for band in range(bands):
                    out[fellow * bands + band] = jnp.concatenate(
                        [grad[fellow, band], total[band]], axis=0
                    ).astype(bf16)

        def second_image(here, weight, stacked, ring, taper, first, grad, *refs):
            outs, second = refs[:-1], refs[-1]
            group_here, _, band_here = position(here)
            scaled = load_members(weight, stacked)
            for t, image in enumerate(images_of(scaled, grad[...], ring[...], taper)):
                second[t] = image[:, :kept].reshape(bands, groups, own, kept)
            for apart in range(groups):
                for shift in range(bands):
                    if few:
                        group, band = shifted(group_here, apart, groups), shifted(band_here, shift, bands)
                        out = outs[apart * bands + shift]
                    else:
                        group, band, out = apart, shift, outs[0].at[apart, shift]
                    for t in range(slots):
                        out[t * own : (t + 1) * own] = second[t, band, group]
                    if not few or apart == 0:
                        for t in range(slots):
                            image = first[t, band, group]
                            if not few:
                                image = jnp.where(group_here == group, image, 0.0)
                            out[(slots + t) * own : (slots + t + 1) * own] = image

        def fold_smooth(marks, weight, ensemble, innovation, precision, kernel, out):
            total = []
            for at in range(levels):
                precise = precision[at].astype(f32)
                part = jnp.zeros((rows, lon), f32)
                for t in range(slots):
                    weighted = precise * innovation[t, at].astype(f32)
                    part = part + ensemble[0, t, at].astype(f32) * weighted
                total.append(part)
            total = weight[marks[0]] * jnp.concatenate(total, axis=0)
            step = kernel.shape[1]
            margin = (kernel.shape[0] - step) // 2
            steps = -(-lon // step)
            after = steps * step + margin - lon
            ring = jnp.concatenate([total[:, lon - margin :], total, total[:, :after]], axis=1)
            ring = ring.astype(bf16)
            for start in range(0, lon, step):
                stop = min(lon, start + step)
                piece = jnp.dot(
                    ring[:, start : start + kernel.shape[0]], kernel[...], preferred_element_type=f32
                )
                out[:, start:stop] = piece[:, : stop - start].astype(bf16)

        def first_gradient(widths, below, middle, above, apart, level, grad):
            span = jnp.ones(level.shape, f32)
            for at in range(levels):
                span = span + jnp.where(level[...] == at, widths[at].astype(f32), 0.0)
            high, low = halves(near(apart[...], span))
            stacked = jnp.concatenate([below[...], middle[...], above[...]], axis=0)
            grad[...] = ensemble_share * (
                jnp.dot(high, stacked, preferred_element_type=f32)
                + jnp.dot(low, stacked, preferred_element_type=f32)
            )

        def by_level(back, band, start):
            parts = []
            for group in range(groups):
                for fellow in range(fellows):
                    at = start + group * own
                    parts.append(back[fellow * bands + band, at : at + own].astype(f32))
            return jnp.concatenate(parts, axis=0)

        def gather_images(here, blocks, images):
            _, _, band_here = position(here)
            half = slots * own
            for shift in range(bands):
                if few:
                    place = shifted(band_here, -shift, bands)
                    second, first = blocks[shift][:half], blocks[shift][half:]
                    for apart in range(1, groups):
                        second = second + blocks[apart * bands + shift][...]
                else:
                    place = shift
                    second, first = blocks[0][0, shift, :half], blocks[0][0, shift, half:]
                    for group in range(1, groups):
                        second = second + blocks[0][group, shift, :half]
                        first = first + blocks[0][group, shift, half:]
                images[place, :half] = second
                images[place, half:] = first

        def inner_products(here, back, pieces, mixing, *refs):
            blocks, (sums, images) = refs[:-2], refs[-2:]
            gather_images(here, blocks, images)
            inside = lax.broadcasted_iota(jnp.int32, (own, kept), 1) < lon_share
            parts = [jnp.zeros((own, kept), f32) for _ in range(4)]
            for band in range(bands):
                second_static = exact_dot(mixing[...], by_level(back, band, held))
                field = pieces[band]
                precise = field[slots * own : (slots + 1) * own]
                first_static = field[(slots + 1) * own :]
                for t in range(slots):
                    second = images[band, t * own : (t + 1) * own] + second_static
                    first = images[band, (slots + t) * own : (slots + t + 1) * own] + first_static
                    weighted = precise * first
                    parts[0] = parts[0] + precise * field[t * own : (t + 1) * own] * first
                    parts[1] = parts[1] + weighted * first
                    parts[2] = parts[2] + weighted * second
                    parts[3] = parts[3] + precise * second * second
            lane = lax.broadcasted_iota(jnp.int32, (1, LANES), 1)
            row = jnp.zeros((1, LANES), f32)
            for index, part in enumerate(parts):
                part = jnp.where(inside, part, 0.0)
                part = jnp.sum(jnp.sum(part, axis=0, keepdims=True), axis=1, keepdims=True)
                row = row + jnp.where(lane == index, part, 0.0)
            sums[...] = jnp.broadcast_to(row, sums.shape)

        def join(here, back, pieces, mixing, pulling, *refs):
            blocks, (grad, pulled, image, images) = refs[:-4], refs[-4:]
            gather_images(here, blocks, images)
            for band in range(bands):
                place = slice(band * lon_share, (band + 1) * lon_share)
                total = by_level(back, band, held)
                second_static = exact_dot(mixing[...], total)
                pulled[:, place] = exact_dot(pulling[...], total)[:, :lon_share]
                grad[:, place] = by_level(back, band, 0)[:, :lon_share]
                first_static = pieces[band, (slots + 1) * own :]
                for t in range(2 * slots):
                    part = images[band, t * own : (t + 1) * own]
                    part = part + (second_static if t < slots else first_static)
                    image[t * own : (t + 1) * own, place] = part[:, :lon_share]

        def finish(sums, grad_first, grad_second, pulled_first, pulled_second, images, *outs):
            member_out, static_out, image_out = outs
            total = jnp.sum(sums[...], axis=0, keepdims=True)
            lane = lax.broadcasted_iota(jnp.int32, total.shape, 1)
            first_norm, first_image, cross, second_image = [
                jnp.sum(jnp.where(lane == index, total, 0.0), axis=1, keepdims=True)
                for index in range(4)
            ]
            alpha = first_norm / (first_norm + first_image)
            ratio = first_image / first_norm
            next_norm = alpha * alpha * jnp.maximum(cross - ratio * first_image, 0.0)
            beta = next_norm / first_norm
            apart = second_image - 2.0 * ratio * cross + ratio * ratio * first_image
            curvature = next_norm + alpha * alpha * apart - beta * next_norm / alpha
            alpha_next = jnp.clip(next_norm / curvature, 0.0, 1.0)
            on_first = alpha + alpha_next * (1.0 - alpha + beta)
            on_second = -alpha * alpha_next
            member = on_first * grad_first[...] + on_second * grad_second[...]
            static = on_first * pulled_first[...] + on_second * pulled_second[...]
            for level in range(levels):
                place = slice(level * rows, (level + 1) * rows)
                member_out[0, level] = member[place]
                static_out[level] = static[place]
            half = slots * own
            image = on_first * images[half:] + on_second * images[:half]
            for t in range(slots):
                for level in range(level_share):
                    start = (t * level_share + level) * rows
                    image_out[t, level] = image[start : start + rows]

        def trade(blocks, shifts):
            arrived = []
            for block, (apart, shift) in zip(blocks, shifts):
                if (apart, shift) == (0, 0):
                    arrived.append(block)
                    continue
                moves = []
                for member in range(members):
                    group, fellow = divmod(member, fellows)
                    target = (group + apart) % groups * fellows + fellow
                    for band in range(bands):
                        moves.append((member * bands + band, target * bands + (band + shift) % bands))
                arrived.append(lax.ppermute(block, BOTH, moves))
            return arrived

        group_devices = [
            [group * fellows * bands + at for at in range(fellows * bands)] for group in range(groups)
        ]

        def across_group(blocks):
            return lax.all_to_all(blocks, BOTH, 0, 0, tiled=True, axis_index_groups=group_devices)

        here = jnp.stack([lax.axis_index("member"), lax.axis_index("band")]).astype(jnp.int32)

        (pieces,) = call(
            pack,
            [((fellows * bands, slots * held, padded), bf16)],
            [member_of_slot],
            [ensemble],
        )
        pieces, ensemble, innovation, precision, static_root = lax.optimization_barrier(
            (pieces, ensemble, innovation, precision, static_root)
        )
        stacked = across_group(pieces)

        pulling = each_row(static_share * static_root.T, rows)
        root = each_row(static_share * static_root, rows)
        apart, level = row_apart(bands, groups * level_share, rows, copies)
        block = (arrays * held, padded)
        results = call(
            observe,
            ([(block, bf16)] * bands if few else [((bands,) + block, bf16)])
            + [
                ((bands, arrays * own, kept), f32),
                ((levels * rows, lon), f32),
                ((own, levels * rows), f32),
                ((2,) + apart.shape, bf16),
            ],
            [here, halfwidth],
            [innovation, precision, pulling, root, jnp.asarray(apart), jnp.asarray(level)],
            scratch=[
                ((levels, rows, lon), f32),
                ((levels, rows, levels * rows), f32),
                ((bands,) + block, bf16),
            ],
        )
        blocks, (own_pieces, pulled, mixing, taper) = results[:-4], results[-4:]
        if few:
            blocks = trade(blocks, [(0, shift) for shift in range(bands)])
        else:
            blocks = [lax.all_to_all(blocks[0], "band", 0, 0, tiled=True)]
        ring = ring_kernel(width, padded)

        part, send, fields = call(
            first_image,
            [
                ((slots, per_member, padded), f32),
                ((slots, per_member, padded), bf16),
                ((arrays, per_member, padded), bf16),
            ],
            [here, member_weight],
            [stacked, ring, taper, *blocks],
            scratch=[((bands,) + block, bf16)],
        )
        others = trade([send] * (groups - 1), [(apart, 0) for apart in range(1, groups)])

        send, ensemble, innovation, precision = lax.optimization_barrier(
            (send, ensemble, innovation, precision)
        )
        (smoothed,) = call(
            fold_smooth,
            [((levels * rows, lon), bf16)],
            [member_of_slot, member_weight],
            [ensemble, innovation, precision, lon_kernel(LANES, 2 * LANES)],
        )
        up = [(at, at + 1) for at in range(bands - 1)]
        below = lax.ppermute(smoothed, "band", up)
        above = lax.ppermute(smoothed, "band", [(target, source) for source, target in up])

        out, image_first, grad = call(
            second_gradient,
            [
                ((fellows * bands, 2 * held, kept), bf16),
                ((slots, bands, groups, own, kept), f32),
                ((fellows * per_member, padded), bf16),
            ],
            [here, member_weight],
            [stacked, ring, taper, part, fields, *others],
        )
        back = across_group(out)
        half = (slots * own, kept)
        full = (2 * slots * own, kept)
        if few:
            shapes = [(full, f32)] * bands + [(half, f32)] * ((groups - 1) * bands)
        else:
            shapes = [((groups, bands) + full, f32)]
        images = call(
            second_image,
            shapes,
            [here, member_weight],
            [stacked, ring, taper, image_first, grad],
            scratch=[((slots, bands, groups, own, kept), f32)],
            flops=10**9,
        )
        if few:
            images = trade(
                images, [(apart, shift) for apart in range(groups) for shift in range(bands)]
            )
        else:
            same_fellow = [
                [(group * fellows + fellow) * bands + band for group in range(groups) for band in range(bands)]
                for fellow in range(fellows)
            ]
            flat = images[0].reshape((groups * bands,) + full)
            flat = lax.all_to_all(flat, BOTH, 0, 0, tiled=True, axis_index_groups=same_fellow)
            images = [flat.reshape((groups, bands) + full)]

        gathered = [((bands,) + full, f32)]
        (sums,) = call(
            inner_products,
            [((members * bands, LANES), f32)],
            [here],
            [back, own_pieces, mixing, *images],
            scratch=gathered,
        )
        sums, smoothed = lax.optimization_barrier((sums, smoothed))
        sums = lax.all_to_all(sums, BOTH, 0, 0, tiled=True)
        grad_second, pulled_second, images = call(
            join,
            [((levels * rows, lon), f32), ((levels * rows, lon), f32), ((2 * slots * own, lon), f32)],
            [here],
            [back, own_pieces, mixing, pulling, *images],
            scratch=gathered,
            flops=10**9,
        )
        apart, level = halo_apart(levels, rows)
        (grad_first,) = call(
            first_gradient,
            [((levels * rows, lon), f32)],
            [halfwidth],
            [below, smoothed, above, jnp.asarray(apart), jnp.asarray(level)],
            flops=10**9,
        )
        return call(
            finish,
            [
                ((1, levels, rows, lon), f32),
                ((levels, rows, lon), f32),
                ((slots, level_share, rows, lon), f32),
            ],
            [],
            [sums, grad_first, grad_second, pulled, pulled_second, images],
        )

    return jax.shard_map(
        shards,
        mesh=mesh,
        in_specs=(
            P("member", None, None, "band", None),
            P(),
            P("member"),
            P(),
            P(),
            P(None, None, "band", None),
            P(None, "band", None),
        ),
        out_specs=(
            P("member", None, "band", None),
            P(None, "band", None),
            P(None, "member", "band", None),
        ),
        check_vma=False,
    )
```

time: 359 us -> 79.7 us (0.22)
  waiting for transfers between devices: 143 us -> 19.8 us
  blocking collectives: 119 us -> 0 us
  other arithmetic: 23.5 us -> 0.22 us
  between operations: 24.5 us -> 1.52 us
  starting transfers between devices: 25.7 us -> 41.3 us
  Pallas kernels: 0 us -> 13.3 us
  local copies, waits for them, and re-layouts: 13.4 us -> 2.97 us
  matrix products: 8.48 us -> 0 us
    psum x3 -> x0, blocking collectives: 119 us -> none  [the longest x2 80.3 us: shards(): lax.psum(local_dot(res_members, res_members, res_static, res_static, grou...]
    psum x2 -> x0, waiting for transfers between devices: 110 us -> none  [shards(): summed = lax.psum(partial_image, 'member')]
    ppermute x10 -> x13, waiting for transfers between devices: 32.5 us -> 15 us  [the longest x11 15 us: trade(): arrived.append(lax.ppermute(block, BOTH, moves))]
    all_to_all x0 -> x3, starting transfers between devices: none -> 14.5 us  [the longest x2 9.97 us: across_group(): lax.all_to_all(blocks, BOTH, 0, 0, tiled=True, axis_index_groups=group_de...]
    pallas_call x0 -> x10, Pallas kernels: none -> 13.3 us  [call(): pl.pallas_call(body, out_shape=tuple((jax.ShapeDtypeStruct(shape, kind) f...]
    reduce_sum x11 -> x0, other arithmetic: 12.8 us -> none  [the longest x3 4.82 us: local_dot(): jnp.sum(first_members * second_members)]
    dot_general x10 -> x0, matrix products: 8.48 us -> none  [the longest x5 4.34 us: smooth_longitude(): jnp.einsum('...bm,mo->...bo', window, kernel, preferred_element_type=jnp....]
    all_to_all x0 -> x3, waiting for transfers between devices: none -> 4.77 us  [the longest x1 4.76 us: shards(): sums = lax.all_to_all(sums, BOTH, 0, 0, tiled=True)]
  transfers between devices with their start and end apart: 12 -> 16, of which waited for: 10 -> 8; matrix products, arithmetic and copies ran while one was open for 2% -> 1% of each run, Pallas kernels for 0% -> 9%
where the time goes in v4:
time: 79.7 us; the launch traced here: 79.2 us
  starting transfers between devices  41.3 us (52%)
  waiting for transfers between devices  19.8 us (25%)
  Pallas kernels  13.3 us (17%)
  local copies, waits for them, and re-layouts  2.97 us (4%)
  between operations  1.52 us (2%)
    ppermute x11, starting transfers between devices, trade(): arrived.append(lax.ppermute(block, BOTH, moves))  24.2 us
    ppermute x11, waiting for transfers between devices, trade(): arrived.append(lax.ppermute(block, BOTH, moves))  15 us
    pallas_call x10, Pallas kernels, call(): pl.pallas_call(body, out_shape=tuple((jax.ShapeDtypeStruct(shape, kind) f...  13.3 us
    all_to_all x2, starting transfers between devices, across_group(): lax.all_to_all(blocks, BOTH, 0, 0, tiled=True, axis_index_groups=group_de...  9.97 us
    all_to_all x1, waiting for transfers between devices, shards(): sums = lax.all_to_all(sums, BOTH, 0, 0, tiled=True)  4.76 us
    all_to_all x1, starting transfers between devices, shards(): sums = lax.all_to_all(sums, BOTH, 0, 0, tiled=True)  4.53 us
    unnamed x26, local copies, waits for them, and re-layouts  2.4 us
  transfers between devices with their start and end apart: 16, of which 8 were waited for; matrix products, arithmetic and copies ran while one was open for 1% of the time, Pallas kernels for 9%

profile of v4, /device:TPU:0, one launch (start us, length us, event | category | flops | bytes accessed | tf_op | source)
XLA Modules:
  0.0 79.2 jit_solution(11773223856621853709)
XLA Ops:
  1.3 0.0 copy-start.1
  1.3 1.0 %copy-done.1 = bf16[1,2,16,4,1440]{4,3,2,1,0:T(4,128)(2,1)S(1)} copy-done((bf16[1,2,16,4,1440]{4,3,2,1,0:T(4,128)(2,1)S(1)}, bf16[1,2,16,4,1440]{4,3,2,1,0:T(4,128)(2,1)}, u32[]{:S(2)}) %copy-start.1) | copy-done | bytes 368664
  2.3 1.0 %pack.1 = bf16[16,32,512]{2,1,0:T(8,128)(2,1)} custom-call(s32[1]{0:T(128)S(6)} %copy.20.marks, bf16[1,2,16,4,1440]{4,3,2,1,0:T(4,128)(2,1)S(1)} %copy-done.1), custom_call_target="tpu_custom_call" | custom-call | tf_op jit(solution)/shard_map/pack/pallas_call | solution.py:137
  3.3 6.4 %all-to-all-start = ((bf16[16,32,512]{2,1,0:T(8,128)(2,1)}), bf16[16,32,512]{2,1,0:T(8,128)(2,1)S(1)}, u32[]{:S(2)}, u32[]{:S(2)}) async-start(bf16[16,32,512]{2,1,0:T(8,128)(2,1)} %pack.1), calls=%async_computation | async-start | bytes 1048576 | tf_op jit(solution)/shard_map/all_to_all | solution.py:464
  9.8 0.1 copy.18
  9.9 0.1 broadcast_multiply_fusion
  10.0 0.0 copy-start.4
  10.0 0.0 copy-start.6
  10.0 0.3 mul.46.pulling
  10.3 0.0 copy-start.7
  10.3 0.3 mul.49.root
  10.5 0.0 copy-start.9
  10.6 0.1 pad_add_fusion.here
  10.6 0.3 copy-done.4
  10.9 0.1 copy-done.6
  11.1 0.3 copy-done.3
  11.3 0.0 copy-done.7
  11.3 1.5 %observe.1 = (bf16[64,512]{1,0:T(8,128)(2,1)S(1)}, bf16[64,512]{1,0:T(8,128)(2,1)S(1)}, bf16[64,512]{1,0:T(8,128)(2,1)S(1)}, bf16[64,512]{1,0:T(8,128)(2,1)S(1)}...) custom-call(s32[2]{0:T(128)S(1)} %pad_add_fusion.here, ...), custom_call_target="tpu_custom_call" | custom-call | tf_op jit(solution)/shard_map/observe/pallas_call | solution.py:137
  12.9 2.0 %collective-permute-start = (bf16[64,512]{1,0:T(8,128)(2,1)S(1)}, bf16[64,512]{1,0:T(8,128)(2,1)S(1)}, u32[]{:S(2)}, u32[]{:S(2)}) collective-permute-start(bf16[64,512]{1,0:T(8,128)(2,1)S(1)} %get-tuple-element.44), channel_id=1, source_target_pairs={{0,1},{1,2},{2,3},{3,0},{4,5},{5,6},{6,7},{7,4},{8,9},{9,10},{10,1... | collective-permute-start | bytes 196616 | tf_op jit(solution)/shard_map/ppermute | solution.py:456
  14.8 1.5 %collective-permute-start.1 = (bf16[64,512]{1,0:T(8,128)(2,1)S(1)}, bf16[64,512]{1,0:T(8,128)(2,1)S(1)}, u32[]{:S(2)}, u32[]{:S(2)}) collective-permute-start(bf16[64,512]{1,0:T(8,128)(2,1)S(1)} %get-tuple-element.45), channel_id=1, source_target_pairs={{0,2},{1,3},{2,0},{3,1},{4,6},{5,7},{6,4},{7,5},{8,10},{9,11},{10,... | collective-permute-start | bytes 196616 | tf_op jit(solution)/shard_map/ppermute | solution.py:456
  16.3 1.5 %collective-permute-start.2 = (bf16[64,512]{1,0:T(8,128)(2,1)S(1)}, bf16[64,512]{1,0:T(8,128)(2,1)S(1)}, u32[]{:S(2)}, u32[]{:S(2)}) collective-permute-start(bf16[64,512]{1,0:T(8,128)(2,1)S(1)} %get-tuple-element.46), channel_id=1, source_target_pairs={{0,3},{1,0},{2,1},{3,2},{4,7},{5,4},{6,5},{7,6},{8,11},{9,8},{10,9... | collective-permute-start | bytes 196616 | tf_op jit(solution)/shard_map/ppermute | solution.py:456
  17.8 3.3 %collective-permute-done.refs_1_ = bf16[64,512]{1,0:T(8,128)(2,1)S(1)} collective-permute-done((bf16[64,512]{1,0:T(8,128)(2,1)S(1)}, bf16[64,512]{1,0:T(8,128)(2,1)S(1)}, u32[]{:S(2)}, u32[]{:S(2)}) %collective-permute-start) | collective-permute-done | bytes 65568 | tf_op jit(solution)/shard_map/ppermute | solution.py:456
  21.1 0.3 collective-permute-done.1.refs_2_
  21.3 0.9 %collective-permute-done.2.refs_3_ = bf16[64,512]{1,0:T(8,128)(2,1)S(1)} collective-permute-done((bf16[64,512]{1,0:T(8,128)(2,1)S(1)}, bf16[64,512]{1,0:T(8,128)(2,1)S(1)}, u32[]{:S(2)}, u32[]{:S(2)}) %collective-permute-start.2) | collective-permute-done | bytes 65568 | tf_op jit(solution)/shard_map/ppermute | solution.py:456
  22.2 0.0 all-to-all-done.stacked
  22.2 0.0 copy-done
  22.2 0.6 copy-done.8
  22.8 1.7 %first_image.1 = (f32[2,64,512]{2,1,0:T(8,128)S(1)}, bf16[2,64,512]{2,1,0:T(8,128)(2,1)S(1)}, bf16[4,64,512]{2,1,0:T(8,128)(2,1)S(1)}) custom-call(s32[2]{0:T(128)S(1)} %pad_add_fusion.here, f32[8]{0:T(128)S(1)} %copy-done.8, bf16[16,32,512]{2,1,0:T(8,128)(2,1)S(1)} %all-to-all-done.stacked, bf16[512,512]{1,0:T(8,128)(2,1)S(1)} %copy-done, ...), custom_call_target="tpu_custom_call" | custom-call | tf_op jit(solution)/shard_map/first_image/pallas_call | solution.py:137
  24.6 2.7 %collective-permute-start.3 = (bf16[2,64,512]{2,1,0:T(8,128)(2,1)S(1)}, bf16[2,64,512]{2,1,0:T(8,128)(2,1)S(1)}, u32[]{:S(2)}, u32[]{:S(2)}) collective-permute-start(bf16[2,64,512]{2,1,0:T(8,128)(2,1)S(1)} %get-tuple-element.49), channel_id=1, source_target_pairs={{0,16},{1,17},{2,18},{3,19},{4,20},{5,21},{6,22},{7,23},{8,24},{9,... | collective-permute-start | bytes 393224 | tf_op jit(solution)/shard_map/ppermute | solution.py:456
  27.2 6.5 %collective-permute-done.3.refs_0_ = bf16[2,64,512]{2,1,0:T(8,128)(2,1)S(1)} collective-permute-done((bf16[2,64,512]{2,1,0:T(8,128)(2,1)S(1)}, bf16[2,64,512]{2,1,0:T(8,128)(2,1)S(1)}, u32[]{:S(2)}, u32[]{:S(2)}) %collective-permute-start.3) | collective-permute-done | bytes 131104 | tf_op jit(solution)/shard_map/ppermute | solution.py:456
  33.7 2.0 %second_gradient.1 = (bf16[16,32,384]{2,1,0:T(8,128)(2,1)}, f32[2,4,2,8,384]{4,3,2,1,0:T(8,128)S(1)}, bf16[256,512]{1,0:T(8,128)(2,1)S(1)}) custom-call(s32[2]{0:T(128)S(1)} %pad_add_fusion.here, f32[8]{0:T(128)S(1)} %copy-done.8, bf16[16,32,512]{2,1,0:T(8,128)(2,1)S(1)} %all-to-all-done.stacked, bf16[512,512]{1,0:T(8,128)(2,1)S(1)} %copy-done, ...), custom_call_target="tpu_custom_call" | custom-call | tf_op jit(solution)/shard_map/second_gradient/pallas_call | solution.py:137
  35.7 3.6 %all-to-all-start.1 = ((bf16[16,32,384]{2,1,0:T(8,128)(2,1)}), bf16[16,32,384]{2,1,0:T(8,128)(2,1)S(1)}, u32[]{:S(2)}, u32[]{:S(2)}) async-start(bf16[16,32,384]{2,1,0:T(8,128)(2,1)} %get-tuple-element.50), calls=%async_computation.1 | async-start | bytes 786432 | tf_op jit(solution)/shard_map/all_to_all | solution.py:464
  39.3 0.0 copy-start.2
  39.3 0.0 copy-start.5
  39.3 1.2 %second_image.1 = (f32[32,384]{1,0:T(8,128)S(1)}, f32[32,384]{1,0:T(8,128)S(1)}, f32[32,384]{1,0:T(8,128)S(1)}, f32[32,384]{1,0:T(8,128)S(1)}, f32[16,384]{1,0:T...) custom-call(s32[2]{0:T(128)S(1)} %pad_add_fusion.here, f32[8]{0:T(128)S(1)} %copy-done.8, ...), custom_call_target="tpu_custom_call" | custom-call | flops 1000000000 | tf_op jit(solution)/shard_map/second_image/pallas_call | solution.py:137
  40.5 4.1 %collective-permute-start.10 = (f32[16,384]{1,0:T(8,128)S(1)}, f32[16,384]{1,0:T(8,128)S(1)}, u32[]{:S(2)}, u32[]{:S(2)}) collective-permute-start(f32[16,384]{1,0:T(8,128)S(1)} %get-tuple-element.62), channel_id=1, source_target_pairs={{0,19},{1,16},{2,17},{3,18},{4,23},{5,20},{6,21},{7,22},{8,27},{9,... | collective-permute-start | bytes 73736 | tf_op jit(solution)/shard_map/ppermute | solution.py:456
  44.6 0.0 copy-done.2
  44.6 1.0 %fold_smooth.1.middle = bf16[64,1440]{1,0:T(8,128)(2,1)S(1)} custom-call(s32[1]{0:T(128)S(6)} %copy.20.marks, f32[8]{0:T(128)S(1)} %copy-done.8, bf16[1,2,16,4,1440]{4,3,2,1,0:T(4,128)(2,1)S(1)} %copy-done.2, bf16[2,16,4,1440]{3,2,1,0:T(4,128)(2,1)S(1)} %copy-done.3, bf16[16,4,1440]{2,1,0:T(4,128)(2,1)S(1)} %copy-done.4, bf16[512,256]{1,0:T(8,128)(2,1)S(1)} %copy-done.5), custom_call_target="tpu_custom_call" | custom-call | tf_op jit(solution)/shard_map/fold_smooth/pallas_call | solution.py:137
  45.6 1.3 %collective-permute-start.11 = (bf16[64,1440]{1,0:T(8,128)(2,1)S(1)}, bf16[64,1440]{1,0:T(8,128)(2,1)S(1)}, u32[]{:S(2)}, u32[]{:S(2)}) collective-permute-start(bf16[64,1440]{1,0:T(8,128)(2,1)S(1)} %fold_smooth.1.middle), channel_id=1, source_target_pairs={{0,1},{1,2},{2,3},{4,5},{5,6},{6,7},{8,9},{9,10},{10,11},{12,13},{... | collective-permute-start | bytes 552968 | tf_op jit(solution)/shard_map/ppermute | solution.py:530
  46.9 1.3 %collective-permute-start.12 = (bf16[64,1440]{1,0:T(8,128)(2,1)S(1)}, bf16[64,1440]{1,0:T(8,128)(2,1)S(1)}, u32[]{:S(2)}, u32[]{:S(2)}) collective-permute-start(bf16[64,1440]{1,0:T(8,128)(2,1)S(1)} %fold_smooth.1.middle), channel_id=1, source_target_pairs={{1,0},{2,1},{3,2},{5,4},{6,5},{7,6},{9,8},{10,9},{11,10},{13,12},{... | collective-permute-start | bytes 552968 | tf_op jit(solution)/shard_map/ppermute | solution.py:531
  48.2 1.1 %collective-permute-start.7 = (f32[16,384]{1,0:T(8,128)S(1)}, f32[16,384]{1,0:T(8,128)S(1)}, u32[]{:S(2)}, u32[]{:S(2)}) collective-permute-start(f32[16,384]{1,0:T(8,128)S(1)} %get-tuple-element.59), channel_id=1, source_target_pairs={{0,16},{1,17},{2,18},{3,19},{4,20},{5,21},{6,22},{7,23},{8,24},{9,... | collective-permute-start | bytes 73736 | tf_op jit(solution)/shard_map/ppermute | solution.py:456
  49.3 4.6 %collective-permute-start.8 = (f32[16,384]{1,0:T(8,128)S(1)}, f32[16,384]{1,0:T(8,128)S(1)}, u32[]{:S(2)}, u32[]{:S(2)}) collective-permute-start(f32[16,384]{1,0:T(8,128)S(1)} %get-tuple-element.60), channel_id=1, source_target_pairs={{0,17},{1,18},{2,19},{3,16},{4,21},{5,22},{6,23},{7,20},{8,25},{9,... | collective-permute-start | bytes 73736 | tf_op jit(solution)/shard_map/ppermute | solution.py:456
  53.9 0.0 collective-permute-done.10.refs_7_
  53.9 1.5 %collective-permute-start.9 = (f32[16,384]{1,0:T(8,128)S(1)}, f32[16,384]{1,0:T(8,128)S(1)}, u32[]{:S(2)}, u32[]{:S(2)}) collective-permute-start(f32[16,384]{1,0:T(8,128)S(1)} %get-tuple-element.61), channel_id=1, source_target_pairs={{0,18},{1,19},{2,16},{3,17},{4,22},{5,23},{6,20},{7,21},{8,26},{9,... | collective-permute-start | bytes 73736 | tf_op jit(solution)/shard_map/ppermute | solution.py:456
  55.5 0.0 collective-permute-done.7.refs_4_
  55.5 1.4 %collective-permute-start.4 = (f32[32,384]{1,0:T(8,128)S(1)}, f32[32,384]{1,0:T(8,128)S(1)}, u32[]{:S(2)}, u32[]{:S(2)}) collective-permute-start(f32[32,384]{1,0:T(8,128)S(1)} %get-tuple-element.56), channel_id=1, source_target_pairs={{0,1},{1,2},{2,3},{3,0},{4,5},{5,6},{6,7},{7,4},{8,9},{9,10},{10,1... | collective-permute-start | bytes 147464 | tf_op jit(solution)/shard_map/ppermute | solution.py:456
  56.9 0.0 collective-permute-done.8.refs_5_
  56.9 3.9 %collective-permute-start.5 = (f32[32,384]{1,0:T(8,128)S(1)}, f32[32,384]{1,0:T(8,128)S(1)}, u32[]{:S(2)}, u32[]{:S(2)}) collective-permute-start(f32[32,384]{1,0:T(8,128)S(1)} %get-tuple-element.57), channel_id=1, source_target_pairs={{0,2},{1,3},{2,0},{3,1},{4,6},{5,7},{6,4},{7,5},{8,10},{9,11},{10,... | collective-permute-start | bytes 147464 | tf_op jit(solution)/shard_map/ppermute | solution.py:456
  60.8 0.0 collective-permute-done.9.refs_6_
  60.8 0.0 collective-permute-start.6
  60.8 0.2 collective-permute-done.4.refs_1_
  61.0 1.8 %collective-permute-done.5.refs_2_ = f32[32,384]{1,0:T(8,128)S(1)} collective-permute-done((f32[32,384]{1,0:T(8,128)S(1)}, f32[32,384]{1,0:T(8,128)S(1)}, u32[]{:S(2)}, u32[]{:S(2)}) %collective-permute-start.5) | collective-permute-done | bytes 49184 | tf_op jit(solution)/shard_map/ppermute | solution.py:456
  62.8 2.0 %collective-permute-done.6.refs_3_ = f32[32,384]{1,0:T(8,128)S(1)} collective-permute-done((f32[32,384]{1,0:T(8,128)S(1)}, f32[32,384]{1,0:T(8,128)S(1)}, u32[]{:S(2)}, u32[]{:S(2)}) %collective-permute-start.6) | collective-permute-done | bytes 49184 | tf_op jit(solution)/shard_map/ppermute | solution.py:456
  64.9 0.0 all-to-all-done.1.back
  64.9 1.6 %inner_products.1 = f32[32,128]{1,0:T(8,128)} custom-call(s32[2]{0:T(128)S(1)} %pad_add_fusion.here, bf16[16,32,384]{2,1,0:T(8,128)(2,1)S(1)} %all-to-all-done.1.back, f32[4,32,384]{2,1,0:T(8,128)S(1)} %get-tuple-element.51.pieces, f32[8,64]{1,0:T(8,128)S(1)} %get-tuple-element.52.mixing, f32[32,384]{1,0:T(8,128)S(1)} %get-tuple-element.55.refs_0_, ...), custom_call_target="tpu_custom_call" | custom-call | tf_op jit(solution)/shard_map/inner_products/pallas_call | solution.py:137
  66.4 4.5 %all-to-all-start.2 = ((f32[32,1,128]{2,1,0:T(1,128)}), f32[32,1,128]{2,1,0:T(1,128)S(1)}, u32[]{:S(2)}, u32[]{:S(2)}) async-start(f32[32,1,128]{2,1,0:T(1,128)} %bitcast.4), calls=%async_computation.2 | async-start | bytes 32768 | tf_op jit(solution)/shard_map/all_to_all | solution.py:580
  71.0 0.0 copy-start.10
  71.0 0.0 copy-start.11
  71.0 1.3 %join.1 = (f32[64,1440]{1,0:T(8,128)S(1)}, f32[64,1440]{1,0:T(8,128)S(1)}, f32[32,1440]{1,0:T(8,128)S(1)}) custom-call(s32[2]{0:T(128)S(1)} %pad_add_fusion.here, bf16[16,32,384]{2,1,0:T(8,128)(2,1)S(1)} %all-to-all-done.1.back, f32[4,32,384]{2,1,0:T(8,128)S(1)} %get-tuple-element.51.pieces, f32[8,64]{1,0:T(8,128)S(1)} %get-tuple-element.52.mixing, ...), custom_call_target="tpu_custom_call" | custom-call | flops 1000000000 | tf_op jit(solution)/shard_map/join/pallas_call | solution.py:137
  72.3 0.0 collective-permute-done.11.below
  72.3 0.0 collective-permute-done.12.above
  72.3 1.0 %first_gradient.1.grad_first = f32[64,1440]{1,0:T(8,128)S(1)} custom-call(s32[16]{0:T(128)S(1)} %copy-done.9, bf16[64,1440]{1,0:T(8,128)(2,1)S(1)} %collective-permute-done.11.below, bf16[64,1440]{1,0:T(8,128)(2,1)S(1)} %fold_smooth.1.middle, bf16[64,1440]{1,0:T(8,128)(2,1)S(1)} %collective-permute-done.12.above, f32[64,192]{1,0:T(8,128)S(1)} %copy-done.10, ...), custom_call_target="tpu_custom_call" | custom-call | flops 1000000000 | tf_op jit(solution)/shard_map/first_gradient/pallas_call | solution.py:137
  73.3 4.8 %all-to-all-done.2 = f32[32,1,128]{2,1,0:T(1,128)S(1)} async-done(((f32[32,1,128]{2,1,0:T(1,128)}), f32[32,1,128]{2,1,0:T(1,128)S(1)}, u32[]{:S(2)}, u32[]{:S(2)}) %all-to-all-start.2) | async-done | bytes 16416 | tf_op jit(solution)/shard_map/all_to_all | solution.py:580
  78.1 1.1 %finish.1 = (f32[1,16,4,1440]{3,2,1,0:T(4,128)}, f32[16,4,1440]{2,1,0:T(4,128)}, f32[2,2,4,1440]{3,2,1,0:T(4,128)}) custom-call(f32[32,128]{1,0:T(8,128)S(1)} %bitcast.12, f32[64,1440]{1,0:T(8,128)S(1)} %first_gradient.1.grad_first, f32[64,1440]{1,0:T(8,128)S(1)} %get-tuple-element.69.grad_second, f32[64,1440]{1,0:T(8,128)S(1)} %get-tuple-element.70.pulled_first, ...), custom_call_target="tpu_custom_call" | custom-call | tf_op jit(solution)/shard_map/finish/pallas_call | solution.py:137
  (11 shorter events, 0.0 us)
Async XLA Ops:
  1.3 1.0 %copy-start.1 = (bf16[1,2,16,4,1440]{4,3,2,1,0:T(4,128)(2,1)S(1)}, bf16[1,2,16,4,1440]{4,3,2,1,0:T(4,128)(2,1)}, u32[]{:S(2)}) copy-start(bf16[1,2,16,4,1440]{4,3,2,1,0:T(4,128)(2,1)} %ensemble.2) | copy-start | bytes 1105924
  3.3 6.4 %copy-start.12 = (f32[16,16]{1,0:T(8,128)S(1)}, f32[16,16]{1,0:T(8,128)}, u32[]{:S(2)}) copy-start(f32[16,16]{1,0:T(8,128)} %param.17) | copy-start | bytes 3076
  3.3 18.9 %all-to-all-start = ((bf16[16,32,512]{2,1,0:T(8,128)(2,1)}), bf16[16,32,512]{2,1,0:T(8,128)(2,1)S(1)}, u32[]{:S(2)}, u32[]{:S(2)}) async-start(bf16[16,32,512]{2,1,0:T(8,128)(2,1)} %pack.1), calls=%async_computation | async-start | bytes 1048576 | tf_op jit(solution)/shard_map/all_to_all | solution.py:464
  10.0 0.9 %copy-start.4 = (bf16[16,4,1440]{2,1,0:T(4,128)(2,1)S(1)}, bf16[16,4,1440]{2,1,0:T(4,128)(2,1)}, u32[]{:S(2)}) copy-start(bf16[16,4,1440]{2,1,0:T(4,128)(2,1)} %precision.1) | copy-start | bytes 552964
  10.0 1.0 %copy-start.6 = (f32[256,256]{1,0:T(8,128)S(1)}, f32[256,256]{1,0:T(8,128)}, u32[]{:S(2)}) copy-start(f32[256,256]{1,0:T(8,128)} %constant.23.clone.apart) | copy-start | bytes 786436
  10.3 1.0 %copy-start.3 = (bf16[2,16,4,1440]{3,2,1,0:T(4,128)(2,1)S(1)}, bf16[2,16,4,1440]{3,2,1,0:T(4,128)(2,1)}, u32[]{:S(2)}) copy-start(bf16[2,16,4,1440]{3,2,1,0:T(4,128)(2,1)} %innovation.1) | copy-start | bytes 1105924
  10.3 1.1 %copy-start.7 = (f32[256,1]{1,0:T(8,128)S(1)}, f32[256,1]{1,0:T(8,128)}, u32[]{:S(2)}) copy-start(f32[256,1]{1,0:T(8,128)} %constant.24.clone.level) | copy-start | bytes 3076
  10.5 0.8 %copy-start.9 = (s32[16]{0:T(128)S(1)}, s32[16]{0:T(128)}, u32[]{:S(2)}) copy-start(s32[16]{0:T(128)} %widths.3) | copy-start | bytes 196
  11.3 10.9 %copy-start = (bf16[512,512]{1,0:T(8,128)(2,1)S(1)}, bf16[512,512]{1,0:T(8,128)(2,1)}, u32[]{:S(2)}) copy-start(bf16[512,512]{1,0:T(8,128)(2,1)} %constant.25.clone.ring) | copy-start | bytes 1572868
  12.9 8.2 %collective-permute-start = (bf16[64,512]{1,0:T(8,128)(2,1)S(1)}, bf16[64,512]{1,0:T(8,128)(2,1)S(1)}, u32[]{:S(2)}, u32[]{:S(2)}) collective-permute-start(bf16[64,512]{1,0:T(8,128)(2,1)S(1)} %get-tuple-element.44), channel_id=1, source_target_pairs={{0,1},{1,2},{2,3},{3,0},{4,5},{5,6},{6,7},{7,4},{8,9},{9,10},{10,1... | collective-permute-start | bytes 196616 | tf_op jit(solution)/shard_map/ppermute | solution.py:456
  14.8 6.5 %collective-permute-start.1 = (bf16[64,512]{1,0:T(8,128)(2,1)S(1)}, bf16[64,512]{1,0:T(8,128)(2,1)S(1)}, u32[]{:S(2)}, u32[]{:S(2)}) collective-permute-start(bf16[64,512]{1,0:T(8,128)(2,1)S(1)} %get-tuple-element.45), channel_id=1, source_target_pairs={{0,2},{1,3},{2,0},{3,1},{4,6},{5,7},{6,4},{7,5},{8,10},{9,11},{10,... | collective-permute-start | bytes 196616 | tf_op jit(solution)/shard_map/ppermute | solution.py:456
  16.3 5.9 %collective-permute-start.2 = (bf16[64,512]{1,0:T(8,128)(2,1)S(1)}, bf16[64,512]{1,0:T(8,128)(2,1)S(1)}, u32[]{:S(2)}, u32[]{:S(2)}) collective-permute-start(bf16[64,512]{1,0:T(8,128)(2,1)S(1)} %get-tuple-element.46), channel_id=1, source_target_pairs={{0,3},{1,0},{2,1},{3,2},{4,7},{5,4},{6,5},{7,6},{8,11},{9,8},{10,9... | collective-permute-start | bytes 196616 | tf_op jit(solution)/shard_map/ppermute | solution.py:456
  22.2 0.7 copy-start.8
  24.6 9.2 %collective-permute-start.3 = (bf16[2,64,512]{2,1,0:T(8,128)(2,1)S(1)}, bf16[2,64,512]{2,1,0:T(8,128)(2,1)S(1)}, u32[]{:S(2)}, u32[]{:S(2)}) collective-permute-start(bf16[2,64,512]{2,1,0:T(8,128)(2,1)S(1)} %get-tuple-element.49), channel_id=1, source_target_pairs={{0,16},{1,17},{2,18},{3,19},{4,20},{5,21},{6,22},{7,23},{8,24},{9,... | collective-permute-start | bytes 393224 | tf_op jit(solution)/shard_map/ppermute | solution.py:456
  35.7 29.1 %all-to-all-start.1 = ((bf16[16,32,384]{2,1,0:T(8,128)(2,1)}), bf16[16,32,384]{2,1,0:T(8,128)(2,1)S(1)}, u32[]{:S(2)}, u32[]{:S(2)}) async-start(bf16[16,32,384]{2,1,0:T(8,128)(2,1)} %get-tuple-element.50), calls=%async_computation.1 | async-start | bytes 786432 | tf_op jit(solution)/shard_map/all_to_all | solution.py:464
  39.3 5.3 %copy-start.2 = (bf16[1,2,16,4,1440]{4,3,2,1,0:T(4,128)(2,1)S(1)}, bf16[1,2,16,4,1440]{4,3,2,1,0:T(4,128)(2,1)}, u32[]{:S(2)}) copy-start(bf16[1,2,16,4,1440]{4,3,2,1,0:T(4,128)(2,1)} %ensemble.2) | copy-start | bytes 1105924
  39.3 5.3 %copy-start.5 = (bf16[512,256]{1,0:T(8,128)(2,1)S(1)}, bf16[512,256]{1,0:T(8,128)(2,1)}, u32[]{:S(2)}) copy-start(bf16[512,256]{1,0:T(8,128)(2,1)} %constant.26.clone.kernel) | copy-start | bytes 786436
  40.5 13.4 %collective-permute-start.10 = (f32[16,384]{1,0:T(8,128)S(1)}, f32[16,384]{1,0:T(8,128)S(1)}, u32[]{:S(2)}, u32[]{:S(2)}) collective-permute-start(f32[16,384]{1,0:T(8,128)S(1)} %get-tuple-element.62), channel_id=1, source_target_pairs={{0,19},{1,16},{2,17},{3,18},{4,23},{5,20},{6,21},{7,22},{8,27},{9,... | collective-permute-start | bytes 73736 | tf_op jit(solution)/shard_map/ppermute | solution.py:456
  45.6 26.7 %collective-permute-start.11 = (bf16[64,1440]{1,0:T(8,128)(2,1)S(1)}, bf16[64,1440]{1,0:T(8,128)(2,1)S(1)}, u32[]{:S(2)}, u32[]{:S(2)}) collective-permute-start(bf16[64,1440]{1,0:T(8,128)(2,1)S(1)} %fold_smooth.1.middle), channel_id=1, source_target_pairs={{0,1},{1,2},{2,3},{4,5},{5,6},{6,7},{8,9},{9,10},{10,11},{12,13},{... | collective-permute-start | bytes 552968 | tf_op jit(solution)/shard_map/ppermute | solution.py:530
  46.9 25.4 %collective-permute-start.12 = (bf16[64,1440]{1,0:T(8,128)(2,1)S(1)}, bf16[64,1440]{1,0:T(8,128)(2,1)S(1)}, u32[]{:S(2)}, u32[]{:S(2)}) collective-permute-start(bf16[64,1440]{1,0:T(8,128)(2,1)S(1)} %fold_smooth.1.middle), channel_id=1, source_target_pairs={{1,0},{2,1},{3,2},{5,4},{6,5},{7,6},{9,8},{10,9},{11,10},{13,12},{... | collective-permute-start | bytes 552968 | tf_op jit(solution)/shard_map/ppermute | solution.py:531
  48.2 7.2 %collective-permute-start.7 = (f32[16,384]{1,0:T(8,128)S(1)}, f32[16,384]{1,0:T(8,128)S(1)}, u32[]{:S(2)}, u32[]{:S(2)}) collective-permute-start(f32[16,384]{1,0:T(8,128)S(1)} %get-tuple-element.59), channel_id=1, source_target_pairs={{0,16},{1,17},{2,18},{3,19},{4,20},{5,21},{6,22},{7,23},{8,24},{9,... | collective-permute-start | bytes 73736 | tf_op jit(solution)/shard_map/ppermute | solution.py:456
  49.3 7.6 %collective-permute-start.8 = (f32[16,384]{1,0:T(8,128)S(1)}, f32[16,384]{1,0:T(8,128)S(1)}, u32[]{:S(2)}, u32[]{:S(2)}) collective-permute-start(f32[16,384]{1,0:T(8,128)S(1)} %get-tuple-element.60), channel_id=1, source_target_pairs={{0,17},{1,18},{2,19},{3,16},{4,21},{5,22},{6,23},{7,20},{8,25},{9,... | collective-permute-start | bytes 73736 | tf_op jit(solution)/shard_map/ppermute | solution.py:456
  53.9 6.8 %collective-permute-start.9 = (f32[16,384]{1,0:T(8,128)S(1)}, f32[16,384]{1,0:T(8,128)S(1)}, u32[]{:S(2)}, u32[]{:S(2)}) collective-permute-start(f32[16,384]{1,0:T(8,128)S(1)} %get-tuple-element.61), channel_id=1, source_target_pairs={{0,18},{1,19},{2,16},{3,17},{4,22},{5,23},{6,20},{7,21},{8,26},{9,... | collective-permute-start | bytes 73736 | tf_op jit(solution)/shard_map/ppermute | solution.py:456
  55.5 5.5 %collective-permute-start.4 = (f32[32,384]{1,0:T(8,128)S(1)}, f32[32,384]{1,0:T(8,128)S(1)}, u32[]{:S(2)}, u32[]{:S(2)}) collective-permute-start(f32[32,384]{1,0:T(8,128)S(1)} %get-tuple-element.56), channel_id=1, source_target_pairs={{0,1},{1,2},{2,3},{3,0},{4,5},{5,6},{6,7},{7,4},{8,9},{9,10},{10,1... | collective-permute-start | bytes 147464 | tf_op jit(solution)/shard_map/ppermute | solution.py:456
  56.9 5.9 %collective-permute-start.5 = (f32[32,384]{1,0:T(8,128)S(1)}, f32[32,384]{1,0:T(8,128)S(1)}, u32[]{:S(2)}, u32[]{:S(2)}) collective-permute-start(f32[32,384]{1,0:T(8,128)S(1)} %get-tuple-element.57), channel_id=1, source_target_pairs={{0,2},{1,3},{2,0},{3,1},{4,6},{5,7},{6,4},{7,5},{8,10},{9,11},{10,... | collective-permute-start | bytes 147464 | tf_op jit(solution)/shard_map/ppermute | solution.py:456
  60.8 4.1 %collective-permute-start.6 = (f32[32,384]{1,0:T(8,128)S(1)}, f32[32,384]{1,0:T(8,128)S(1)}, u32[]{:S(2)}, u32[]{:S(2)}) collective-permute-start(f32[32,384]{1,0:T(8,128)S(1)} %get-tuple-element.58), channel_id=1, source_target_pairs={{0,3},{1,0},{2,1},{3,2},{4,7},{5,4},{6,5},{7,6},{8,11},{9,8},{10,9... | collective-permute-start | bytes 147464 | tf_op jit(solution)/shard_map/ppermute | solution.py:456
  66.4 11.6 %all-to-all-start.2 = ((f32[32,1,128]{2,1,0:T(1,128)}), f32[32,1,128]{2,1,0:T(1,128)S(1)}, u32[]{:S(2)}, u32[]{:S(2)}) async-start(f32[32,1,128]{2,1,0:T(1,128)} %bitcast.4), calls=%async_computation.2 | async-start | bytes 32768 | tf_op jit(solution)/shard_map/all_to_all | solution.py:580
  71.0 1.4 %copy-start.10 = (f32[64,192]{1,0:T(8,128)S(1)}, f32[64,192]{1,0:T(8,128)}, u32[]{:S(2)}) copy-start(f32[64,192]{1,0:T(8,128)} %constant.27.clone.apart) | copy-start | bytes 147460
  71.0 1.3 %copy-start.11 = (f32[64,1]{1,0:T(8,128)S(1)}, f32[64,1]{1,0:T(8,128)}, u32[]{:S(2)}) copy-start(f32[64,1]{1,0:T(8,128)} %constant.28.clone.level) | copy-start | bytes 772

commit v5 on v4

v5 whole, which is shorter than its diff:
```python
import math

import jax
import jax.numpy as jnp
import numpy as np
from jax import lax
from jax.experimental import pallas as pl
from jax.experimental.pallas import tpu as pltpu
from jax.sharding import PartitionSpec as P

HMAX = 4
LREACH = 18
REACHES = 4
LANES = 128
FEW = 8
SUMS = 4
PARTS = 3
BOTH = ("member", "band")

ensemble_share = 0.8
static_share = 0.6
length_scale = 6.0


def round_up(value, step):
    return -(-value // step) * step


def lon_weights(distance):
    distance = distance.astype(np.float32)
    values = np.exp(np.float32(-0.5) * (distance / np.float32(length_scale)) ** 2)
    values = values / np.float32(length_scale * math.sqrt(2.0 * math.pi))
    return jnp.asarray(np.where(distance <= LREACH, values, 0.0), jnp.bfloat16)


def lon_kernel(reach, width):
    return lon_weights(np.abs(np.arange(width + 2 * reach)[:, None] - reach - np.arange(width)[None]))


def ring_kernel(width, padded):
    apart = np.abs(np.arange(padded)[:, None] - np.arange(padded)[None])
    inside = (np.arange(padded)[:, None] < width) & (np.arange(padded)[None] < width)
    return lon_weights(np.where(inside, np.minimum(apart, width - apart), 2 * LREACH))


def halves(full):
    high = full.astype(jnp.bfloat16)
    return high, (full - high.astype(jnp.float32)).astype(jnp.bfloat16)


def near(apart, spans):
    return jnp.maximum(1.0 - apart / spans, 0.0) / spans


def row_apart(bands, held, rows, copies):
    index = np.arange(copies * bands * held * rows)
    latitude = index // (held * rows) % bands * rows + index % rows
    level = index // rows % held
    copy = index // (bands * held * rows)
    same = (copy[:, None] == copy[None]) & (level[:, None] == level[None])
    apart = np.where(same, np.abs(latitude[:, None] - latitude[None]), 1000)
    return apart.astype(np.float32), level[:, None].astype(np.float32)


def halo_apart(levels, rows):
    own = levels * rows
    target, source = np.arange(own)[:, None], np.arange(3 * own)[None]
    shift = (source // own - 1) * rows + source % rows - target % rows
    same = source // rows % levels == target // rows
    level = (target // rows).astype(np.float32)
    return np.where(same, np.abs(shift), 1000).astype(np.float32), level


def each_row(matrix, rows):
    same = jnp.eye(rows, dtype=jnp.float32)
    wide = matrix[:, None, :, None] * same[None, :, None, :]
    return wide.reshape(matrix.shape[0] * rows, matrix.shape[1] * rows)


def exact_dot(matrix, field):
    return jnp.dot(
        matrix, field, precision=lax.Precision.HIGHEST, preferred_element_type=jnp.float32
    )


def window(values, band, share, halo, tail):
    lon = values.shape[1]
    start = band * share
    stop = start + share + halo
    parts = [values[:, start : min(lon, stop)]]
    if stop > lon:
        parts.append(values[:, : stop - lon])
    if start < halo:
        parts.append(values[:, lon - halo + start :])
    if start:
        parts.append(values[:, max(start - halo, 0) : start])
    return jnp.concatenate(parts + [tail], axis=1)


def spread(field, ring, taper):
    copies = taper.shape[1]
    smoothed = jnp.dot(field.astype(jnp.bfloat16), ring, preferred_element_type=jnp.float32)
    smoothed = smoothed.astype(jnp.bfloat16)
    parts = []
    for start in range(0, field.shape[0], copies):
        part = smoothed[start : start + copies]
        parts.append(
            jnp.dot(taper[0], part, preferred_element_type=jnp.float32)
            + jnp.dot(taper[1], part, preferred_element_type=jnp.float32)
        )
    return parts[0] if len(parts) == 1 else jnp.concatenate(parts, axis=0)


def solution(mesh):
    members, bands = mesh.shape["member"], mesh.shape["band"]
    few = bands <= FEW

    def shards(ensemble, member_weight, member_of_slot, halfwidth, static_root, innovation, precision):
        _, slots, levels, rows, lon = ensemble.shape
        level_share, lon_share = levels // members, lon // bands
        own = level_share * rows
        halo = REACHES * LREACH
        width = lon_share + 2 * halo
        padded = round_up(width + 1, LANES)
        kept = round_up(lon_share + SUMS * PARTS, LANES)
        per_member = bands * own
        copies = members
        while copies > 1 and (copies * per_member > 256 or members % copies):
            copies -= 1
        arrays = slots + 2
        everything = levels * rows
        traded = everything + 4 * slots * own
        vmem = pl.BlockSpec(memory_space=pltpu.VMEM)
        smem = pl.BlockSpec(memory_space=pltpu.SMEM)
        limit = min(48, max(14, 24 * members * bands * slots * own * padded // 2**20)) * 2**20

        def call(body, shapes, scalars, operands, scratch=(), flops=0):
            return pl.pallas_call(
                body,
                out_shape=tuple(jax.ShapeDtypeStruct(shape, kind) for shape, kind in shapes),
                in_specs=[smem] * len(scalars) + [vmem] * len(operands),
                out_specs=(vmem,) * len(shapes),
                scratch_shapes=[pltpu.VMEM(shape, kind) for shape, kind in scratch],
                compiler_params=pltpu.CompilerParams(vmem_limit_bytes=limit),
                cost_estimate=pl.CostEstimate(flops=flops, bytes_accessed=0, transcendentals=0),
                name=body.__name__,
            )(*scalars, *operands)

        f32, bf16 = jnp.float32, jnp.bfloat16

        def shifted(place, shift):
            return lax.rem(place + shift + bands, bands)

        def load_members(weight, stacked):
            stacked = stacked[...].astype(f32)
            which = stacked[:, :1, width : width + 1]
            scale = jnp.zeros(which.shape, f32)
            for member in range(members):
                scale = scale + jnp.where(which == member, weight[member], 0.0)
            shape = (members, per_member, padded)
            return [
                (scale * stacked[:, slot * own : (slot + 1) * own]).reshape(shape)
                for slot in range(slots)
            ]

        def fold(scaled, weighted):
            total = scaled[0] * weighted[0][None]
            for slot in range(1, slots):
                total = total + scaled[slot] * weighted[slot][None]
            return total.reshape(members * per_member, padded)

        def images_of(scaled, grad, ring, taper):
            local = spread(grad, ring, taper).reshape(members, per_member, padded)
            return [ensemble_share * jnp.sum(scaled[t] * local, axis=0) for t in range(slots)]

        def pack(marks, ensemble, out):
            values = jnp.concatenate(
                [ensemble[0, t, level].astype(f32) for t in range(slots) for level in range(levels)],
                axis=0,
            )
            tail = jnp.full((values.shape[0], padded - width), marks[0], jnp.int32).astype(f32)
            for band in range(bands):
                piece = window(values, band, lon_share, halo, tail)
                for member in range(members):
                    picked = []
                    for t in range(slots):
                        start = t * everything + member * own
                        picked.append(piece[start : start + own])
                    out[member * bands + band] = jnp.concatenate(picked, axis=0).astype(bf16)

        def observe(here, widths, innovation, precision, pulling, root, apart, level, *refs):
            outs, (own_static, pulled, mixing, taper, static, mixed, spans) = refs[:-7], refs[-7:]
            total = []
            for at in range(levels):
                precise = precision[at].astype(f32)
                part = precise * innovation[0, at].astype(f32)
                for t in range(1, slots):
                    part = part + precise * innovation[t, at].astype(f32)
                total.append(part)
            back = exact_dot(pulling[...], jnp.concatenate(total, axis=0))
            pulled[...] = back
            forth = exact_dot(root[...], back)
            both = exact_dot(root[...], pulling[...])
            for at in range(levels):
                static[at] = forth[at * rows : (at + 1) * rows]
                mixed[at] = both[at * rows : (at + 1) * rows]
            picked = [here[0] * level_share + share for share in range(level_share)]
            mixing[...] = jnp.concatenate([mixed[at] for at in picked], axis=0)
            parts = [innovation[t, at].astype(f32) for t in range(slots) for at in picked]
            parts += [precision[at].astype(f32) for at in picked] + [static[at] for at in picked]
            values = jnp.concatenate(parts, axis=0)
            tail = jnp.zeros((values.shape[0], padded - width), f32)
            for band in range(bands):
                piece = window(values, band, lon_share, halo, tail)
                own_static[band] = piece[(slots + 1) * own :, :kept]
                if few:
                    spans[band] = piece.astype(bf16)
                else:
                    outs[0][band] = piece.astype(bf16)
            if few:
                for shift in range(bands):
                    outs[shift][...] = spans[shifted(here[1], shift)]
            span = jnp.ones(level.shape, f32)
            for at, which in enumerate(picked):
                span = span + jnp.where(level[...] == at, widths[which].astype(f32), 0.0)
            taper[0], taper[1] = halves(near(apart[...], span))

        def first_half(here, weight, stacked, ring, taper, *refs):
            blocks, (total_out, grad_out, full_out, image_out, fields, spans) = refs[:-6], refs[-6:]
            if few:
                for shift in range(bands):
                    spans[shifted(here[1], -shift)] = blocks[shift][...]
                values = spans[...]
            else:
                values = blocks[0][...]
            field = []
            for index in range(arrays):
                piece = values[:, index * own : (index + 1) * own].astype(f32)
                piece = piece.reshape(per_member, padded)
                fields[index] = piece[:, :kept]
                field.append(piece)
            precise, static = field[slots], field[slots + 1]
            scaled = load_members(weight, stacked)
            weighted = [precise * field[t] for t in range(slots)]
            grad = ensemble_share * spread(fold(scaled, weighted), ring[...], taper)
            total = jnp.zeros((per_member, padded), f32)
            weighted = []
            for t, image in enumerate(images_of(scaled, grad, ring[...], taper)):
                image_out[t] = image[:, :kept]
                weighted.append(precise * (image + static))
                total = total + weighted[t]
            total = total[:, :kept].astype(bf16)
            for member in range(members):
                total_out[member] = total
            grad = (ensemble_share * spread(fold(scaled, weighted), ring[...], taper)).astype(bf16)
            full_out[...] = grad
            grad_out[...] = grad[:, :kept].reshape(members * bands, own, kept)

        def second_image(weight, stacked, ring, taper, grad, image_out):
            scaled = load_members(weight, stacked)
            for t, image in enumerate(images_of(scaled, grad[...], ring[...], taper)):
                image_out[t] = image[:, :kept]

        def combine(here, total, grad, first, second, fields, mixing, *refs):
            outs, (out, spans) = refs[:-2], refs[-2:]
            mixed, precise, static = [], fields[slots], fields[slots + 1]
            for band in range(bands):
                place = slice(band * own, (band + 1) * own)
                every = jnp.concatenate([total[member, place].astype(f32) for member in range(members)], axis=0)
                mixed.append(exact_dot(mixing[...], every))
                spans[band, :everything] = every.astype(bf16)
            mixed = jnp.concatenate(mixed, axis=0)
            sums = [jnp.zeros((per_member, kept), f32) for _ in range(SUMS)]
            for t in range(slots):
                image = second[t] + mixed
                whole = first[t] + static
                weighted = precise * whole
                sums[0] = sums[0] + precise * fields[t] * whole
                sums[1] = sums[1] + weighted * whole
                sums[2] = sums[2] + weighted * image
                sums[3] = sums[3] + precise * image * image
                for which, values in enumerate((first[t], image)):
                    for half, part in enumerate(halves(values)):
                        at = everything + ((half * 2 + which) * slots + t) * own
                        for band in range(bands):
                            spans[band, at : at + own] = part[band * own : (band + 1) * own]
            for shift in range(bands):
                if few:
                    outs[shift][...] = spans[shifted(here[1], shift)]
                else:
                    outs[0][shift] = spans[shift]
            inside = lax.broadcasted_iota(jnp.int32, (per_member, kept), 1) < lon_share
            lane = lax.broadcasted_iota(jnp.int32, (1, kept), 1) - lon_share
            row = jnp.zeros((1, kept), f32)
            for index, part in enumerate(sums):
                part = jnp.where(inside, part, 0.0)
                part = jnp.sum(jnp.sum(part, axis=0, keepdims=True), axis=1, keepdims=True)
                for piece in range(PARTS):
                    high = part.astype(bf16).astype(f32)
                    row = row + jnp.where(lane == PARTS * index + piece, high, 0.0)
                    part = part - high
            shape = (own, kept)
            lane = lax.broadcasted_iota(jnp.int32, shape, 1)
            row = jnp.broadcast_to(row, shape)
            for block in range(members * bands):
                out[block] = jnp.where(lane < lon_share, grad[block].astype(f32), row).astype(bf16)

        def fold_smooth(marks, weight, ensemble, innovation, precision, kernel, out):
            total = []
            for at in range(levels):
                precise = precision[at].astype(f32)
                part = jnp.zeros((rows, lon), f32)
                for t in range(slots):
                    weighted = precise * innovation[t, at].astype(f32)
                    part = part + ensemble[0, t, at].astype(f32) * weighted
                total.append(part)
            total = weight[marks[0]] * jnp.concatenate(total, axis=0)
            step = kernel.shape[1]
            margin = (kernel.shape[0] - step) // 2
            steps = -(-lon // step)
            after = steps * step + margin - lon
            ring = jnp.concatenate([total[:, lon - margin :], total, total[:, :after]], axis=1)
            ring = ring.astype(bf16)
            for start in range(0, lon, step):
                stop = min(lon, start + step)
                piece = jnp.dot(
                    ring[:, start : start + kernel.shape[0]], kernel[...], preferred_element_type=f32
                )
                out[:, start:stop] = piece[:, : stop - start].astype(bf16)

        def first_gradient(widths, below, middle, above, apart, level, grad):
            span = jnp.ones(level.shape, f32)
            for at in range(levels):
                span = span + jnp.where(level[...] == at, widths[at].astype(f32), 0.0)
            high, low = halves(near(apart[...], span))
            stacked = jnp.concatenate([below[...], middle[...], above[...]], axis=0)
            grad[...] = ensemble_share * (
                jnp.dot(high, stacked, preferred_element_type=f32)
                + jnp.dot(low, stacked, preferred_element_type=f32)
            )

        def join(here, own_static, pulling, *refs):
            blocks, (pulled, images, spans) = refs[:-3], refs[-3:]
            for shift in range(bands):
                if few:
                    spans[shifted(here[1], -shift)] = blocks[shift][...]
                else:
                    spans[shift] = blocks[0][shift]
            size = 2 * slots * own
            for band in range(bands):
                place = slice(band * lon_share, (band + 1) * lon_share)
                every = spans[band, :everything].astype(f32)
                pulled[:, place] = exact_dot(pulling[...], every)[:, :lon_share]
                both = spans[band, everything : everything + size].astype(f32)
                both = both + spans[band, everything + size :].astype(f32)
                static = own_static[band]
                for t in range(slots):
                    at = slice(t * own, (t + 1) * own)
                    images[at, place] = (both[at] + static)[:, :lon_share]
                images[slots * own :, place] = both[slots * own :, :lon_share]

        def finish(back, grad_first, pulled_first, pulled_second, images, *refs):
            member_out, static_out, image_out, second = refs
            total = back[0, :1].astype(f32)
            for block in range(1, members * bands):
                total = total + back[block, :1].astype(f32)
            lane = lax.broadcasted_iota(jnp.int32, total.shape, 1) - lon_share
            first_norm, first_image, cross, second_image = [
                jnp.sum(
                    jnp.where((lane >= PARTS * index) & (lane < PARTS * (index + 1)), total, 0.0),
                    axis=1,
                    keepdims=True,
                )
                for index in range(SUMS)
            ]
            alpha = first_norm / (first_norm + first_image)
            ratio = first_image / first_norm
            next_norm = alpha * alpha * jnp.maximum(cross - ratio * first_image, 0.0)
            beta = next_norm / first_norm
            apart = second_image - 2.0 * ratio * cross + ratio * ratio * first_image
            curvature = next_norm + alpha * alpha * apart - beta * next_norm / alpha
            alpha_next = jnp.clip(next_norm / curvature, 0.0, 1.0)
            on_first = alpha + alpha_next * (1.0 - alpha + beta)
            on_second = -alpha * alpha_next
            for band in range(bands):
                grad = jnp.concatenate(
                    [back[member * bands + band].astype(f32) for member in range(members)], axis=0
                )
                second[:, band * lon_share : (band + 1) * lon_share] = grad[:, :lon_share]
            member = on_first * grad_first[...] + on_second * second[...]
            static = on_first * pulled_first[...] + on_second * pulled_second[...]
            for level in range(levels):
                place = slice(level * rows, (level + 1) * rows)
                member_out[0, level] = member[place]
                static_out[level] = static[place]
            half = slots * own
            image = on_first * images[:half] + on_second * images[half:]
            for t in range(slots):
                for level in range(level_share):
                    start = (t * level_share + level) * rows
                    image_out[t, level] = image[start : start + rows]

        def trade(blocks):
            if not few:
                return [lax.all_to_all(blocks[0], "band", 0, 0, tiled=True)]
            return [blocks[0]] + [
                lax.ppermute(blocks[shift], "band", [(at, (at + shift) % bands) for at in range(bands)])
                for shift in range(1, bands)
            ]

        def tradable(shape, kind):
            return [(shape, kind)] * bands if few else [((bands,) + shape, kind)]

        here = jnp.stack([lax.axis_index("member"), lax.axis_index("band")]).astype(jnp.int32)

        (pieces,) = call(
            pack, [((members * bands, slots * own, padded), bf16)], [member_of_slot], [ensemble]
        )
        pieces, ensemble, innovation, precision, static_root = lax.optimization_barrier(
            (pieces, ensemble, innovation, precision, static_root)
        )
        stacked = lax.all_to_all(pieces, BOTH, 0, 0, tiled=True)

        pulling = each_row(static_share * static_root.T, rows)
        root = each_row(static_share * static_root, rows)
        apart, level = row_apart(bands, level_share, rows, copies)
        block = (arrays * own, padded)
        results = call(
            observe,
            tradable(block, bf16)
            + [
                ((bands, own, kept), f32),
                ((everything, lon), f32),
                ((own, everything), f32),
                ((2,) + apart.shape, bf16),
            ],
            [here, halfwidth],
            [innovation, precision, pulling, root, jnp.asarray(apart), jnp.asarray(level)],
            scratch=[((levels, rows, lon), f32), ((levels, rows, everything), f32), ((bands,) + block, bf16)],
        )
        blocks, (own_static, pulled, mixing, taper) = trade(results[:-4]), results[-4:]
        ring = ring_kernel(width, padded)

        total, grad, full, image_first, fields = call(
            first_half,
            [
                ((members, per_member, kept), bf16),
                ((members * bands, own, kept), bf16),
                ((members * per_member, padded), bf16),
                ((slots, per_member, kept), f32),
                ((arrays, per_member, kept), f32),
            ],
            [here, member_weight],
            [stacked, ring, taper, *blocks],
            scratch=[((bands,) + block, bf16)],
        )
        total = lax.all_to_all(total, "member", 0, 0, tiled=True)
        (image_second,) = call(
            second_image,
            [((slots, per_member, kept), f32)],
            [member_weight],
            [stacked, ring, taper, full],
            flops=10**9,
        )

        image_second, ensemble, innovation, precision = lax.optimization_barrier(
            (image_second, ensemble, innovation, precision)
        )
        (smoothed,) = call(
            fold_smooth,
            [((everything, lon), bf16)],
            [member_of_slot, member_weight],
            [ensemble, innovation, precision, lon_kernel(LANES, 2 * LANES)],
        )
        up = [(at, at + 1) for at in range(bands - 1)]
        below = lax.ppermute(smoothed, "band", up)
        above = lax.ppermute(smoothed, "band", [(target, source) for source, target in up])

        results = call(
            combine,
            tradable((traded, kept), bf16) + [((members * bands, own, kept), bf16)],
            [here],
            [total, grad, image_first, image_second, fields, mixing],
            scratch=[((bands, traded, kept), bf16)],
        )
        back = lax.all_to_all(results[-1], BOTH, 0, 0, tiled=True)
        blocks = trade(results[:-1])
        pulled_second, images = call(
            join,
            [((everything, lon), f32), ((2 * slots * own, lon), f32)],
            [here],
            [own_static, pulling, *blocks],
            scratch=[((bands, traded, kept), bf16)],
        )
        apart, level = halo_apart(levels, rows)
        (grad_first,) = call(
            first_gradient,
            [((everything, lon), f32)],
            [halfwidth],
            [below, smoothed, above, jnp.asarray(apart), jnp.asarray(level)],
        )
        return call(
            finish,
            [
                ((1, levels, rows, lon), f32),
                ((levels, rows, lon), f32),
                ((slots, level_share, rows, lon), f32),
            ],
            [],
            [back, grad_first, pulled, pulled_second, images],
            scratch=[((everything, lon), f32)],
        )

    return jax.shard_map(
        shards,
        mesh=mesh,
        in_specs=(
            P("member", None, None, "band", None),
            P(),
            P("member"),
            P(),
            P(),
            P(None, None, "band", None),
            P(None, "band", None),
        ),
        out_specs=(
            P("member", None, "band", None),
            P(None, "band", None),
            P(None, "member", "band", None),
        ),
        check_vma=False,
    )
```

time: 79.7 us -> 68.3 us (0.86)
  starting transfers between devices: 41.3 us -> 28.6 us
  waiting for transfers between devices: 19.8 us -> 21.5 us
  Pallas kernels: 13.3 us -> 12.4 us
    ppermute x11 -> x6, starting transfers between devices: 24.2 us -> 9.37 us  [trade(): lax.ppermute(blocks[shift], 'band', [(at, (at + shift) % bands) for at in...]
    all_to_all x3, waiting for transfers between devices: 4.77 us -> 12.1 us  [the longest x1 7.08 us: shards(): total = lax.all_to_all(total, 'member', 0, 0, tiled=True)]
    ppermute x11 -> x6, waiting for transfers between devices: 15 us -> 8.67 us  [trade(): lax.ppermute(blocks[shift], 'band', [(at, (at + shift) % bands) for at in...]
    ppermute x1, starting transfers between devices: 1.3 us -> 4.56 us  [shards(): below = lax.ppermute(smoothed, 'band', up)]
    all_to_all x3, starting transfers between devices: 14.5 us -> 13.4 us  [the longest x1 7.3 us: shards(): stacked = lax.all_to_all(pieces, BOTH, 0, 0, tiled=True)]
    pallas_call x10 -> x9, Pallas kernels: 13.3 us -> 12.4 us  [call(): pl.pallas_call(body, out_shape=tuple((jax.ShapeDtypeStruct(shape, kind) f...]
  transfers between devices with their start and end apart: 16 -> 11, of which waited for: 8 -> 9; matrix products, arithmetic and copies ran while one was open for 1% -> 1% of each run, Pallas kernels for 9% -> 8%
where the time goes in v5:
time: 68.3 us; the launch traced here: 67.8 us
  starting transfers between devices  28.6 us (42%)
  waiting for transfers between devices  21.5 us (31%)
  Pallas kernels  12.4 us (18%)
  local copies, waits for them, and re-layouts  3.65 us (5%)
  between operations  1.48 us (2%)
    pallas_call x9, Pallas kernels, call(): pl.pallas_call(body, out_shape=tuple((jax.ShapeDtypeStruct(shape, kind) f...  12.4 us
    ppermute x6, starting transfers between devices, trade(): lax.ppermute(blocks[shift], 'band', [(at, (at + shift) % bands) for at in...  9.37 us
    ppermute x6, waiting for transfers between devices, trade(): lax.ppermute(blocks[shift], 'band', [(at, (at + shift) % bands) for at in...  8.67 us
    all_to_all x1, starting transfers between devices, shards(): stacked = lax.all_to_all(pieces, BOTH, 0, 0, tiled=True)  7.3 us
    all_to_all x1, waiting for transfers between devices, shards(): total = lax.all_to_all(total, 'member', 0, 0, tiled=True)  7.08 us
    all_to_all x1, waiting for transfers between devices, shards(): stacked = lax.all_to_all(pieces, BOTH, 0, 0, tiled=True)  5.05 us
    ppermute x1, starting transfers between devices, shards(): below = lax.ppermute(smoothed, 'band', up)  4.56 us
    all_to_all x1, starting transfers between devices, shards(): total = lax.all_to_all(total, 'member', 0, 0, tiled=True)  3.39 us
  transfers between devices with their start and end apart: 11, of which 9 were waited for; matrix products, arithmetic and copies ran while one was open for 1% of the time, Pallas kernels for 8%

profile of v5, /device:TPU:0, one launch (start us, length us, event | category | flops | bytes accessed | tf_op | source)
XLA Modules:
  0.0 67.8 jit_solution(7191797429246107745)
XLA Ops:
  1.3 0.0 copy-start
  1.3 1.0 %copy-done = bf16[1,2,16,4,1440]{4,3,2,1,0:T(4,128)(2,1)S(1)} copy-done((bf16[1,2,16,4,1440]{4,3,2,1,0:T(4,128)(2,1)S(1)}, bf16[1,2,16,4,1440]{4,3,2,1,0:T(4,128)(2,1)}, u32[]{:S(2)}) %copy-start) | copy-done | bytes 368664
  2.3 1.1 %pack.1 = bf16[32,16,512]{2,1,0:T(8,128)(2,1)} custom-call(s32[1]{0:T(128)S(6)} %copy.18.marks, bf16[1,2,16,4,1440]{4,3,2,1,0:T(4,128)(2,1)S(1)} %copy-done), custom_call_target="tpu_custom_call" | custom-call | tf_op jit(solution)/shard_map/pack/pallas_call | solution.py:138
  3.3 7.3 %all-to-all-start = ((bf16[32,16,512]{2,1,0:T(8,128)(2,1)}), bf16[32,16,512]{2,1,0:T(8,128)(2,1)S(1)}, u32[]{:S(2)}, u32[]{:S(2)}) async-start(bf16[32,16,512]{2,1,0:T(8,128)(2,1)} %pack.1), calls=%async_computation | async-start | bytes 1048576 | tf_op jit(solution)/shard_map/all_to_all | solution.py:422
  10.6 0.0 copy-start.12
  10.7 0.7 %copy-done.12 = f32[16,16]{1,0:T(8,128)S(1)} copy-done((f32[16,16]{1,0:T(8,128)S(1)}, f32[16,16]{1,0:T(8,128)}, u32[]{:S(2)}) %copy-start.12) | copy-done | bytes 1048
  11.3 0.1 copy.17
  11.4 0.1 broadcast_multiply_fusion
  11.6 0.0 copy-start.3
  11.6 0.0 copy-start.6
  11.6 0.3 mul.49.root
  11.8 0.0 copy-start.2
  11.9 0.0 copy-start.7
  11.9 0.3 mul.46.pulling
  12.1 0.0 copy-start.11
  12.1 0.1 pad_add_fusion.here
  12.2 0.3 copy-done.3
  12.5 0.1 copy-done.6
  12.6 0.3 copy-done.2
  12.9 0.0 copy-done.7
  12.9 0.0 copy-done.11
  12.9 0.0 copy-start.4
  12.9 1.5 %observe.1 = (bf16[32,512]{1,0:T(8,128)(2,1)S(1)}, bf16[32,512]{1,0:T(8,128)(2,1)S(1)}, bf16[32,512]{1,0:T(8,128)(2,1)S(1)}, bf16[32,512]{1,0:T(8,128)(2,1)S(1)}...) custom-call(s32[2]{0:T(128)S(1)} %pad_add_fusion.here, ...), custom_call_target="tpu_custom_call" | custom-call | tf_op jit(solution)/shard_map/observe/pallas_call | solution.py:138
  14.4 1.8 %collective-permute-start = (bf16[32,512]{1,0:T(8,128)(2,1)S(1)}, bf16[32,512]{1,0:T(8,128)(2,1)S(1)}, u32[]{:S(2)}, u32[]{:S(2)}) collective-permute-start(bf16[32,512]{1,0:T(8,128)(2,1)S(1)} %get-tuple-element.38), channel_id=1, source_target_pairs={{0,1},{1,2},{2,3},{3,0},{4,5},{5,6},{6,7},{7,4},{8,9},{9,10},{10,1... | collective-permute-start | bytes 98312 | tf_op jit(solution)/shard_map/ppermute | solution.py:407
  16.2 1.5 %collective-permute-start.1 = (bf16[32,512]{1,0:T(8,128)(2,1)S(1)}, bf16[32,512]{1,0:T(8,128)(2,1)S(1)}, u32[]{:S(2)}, u32[]{:S(2)}) collective-permute-start(bf16[32,512]{1,0:T(8,128)(2,1)S(1)} %get-tuple-element.39), channel_id=1, source_target_pairs={{0,2},{1,3},{2,0},{3,1},{4,6},{5,7},{6,4},{7,5},{8,10},{9,11},{10,... | collective-permute-start | bytes 98312 | tf_op jit(solution)/shard_map/ppermute | solution.py:407
  17.7 1.5 %collective-permute-start.2 = (bf16[32,512]{1,0:T(8,128)(2,1)S(1)}, bf16[32,512]{1,0:T(8,128)(2,1)S(1)}, u32[]{:S(2)}, u32[]{:S(2)}) collective-permute-start(bf16[32,512]{1,0:T(8,128)(2,1)S(1)} %get-tuple-element.40), channel_id=1, source_target_pairs={{0,3},{1,0},{2,1},{3,2},{4,7},{5,4},{6,5},{7,6},{8,11},{9,8},{10,9... | collective-permute-start | bytes 98312 | tf_op jit(solution)/shard_map/ppermute | solution.py:407
  19.1 0.6 collective-permute-done.refs_1_
  19.7 1.1 %collective-permute-done.1.refs_2_ = bf16[32,512]{1,0:T(8,128)(2,1)S(1)} collective-permute-done((bf16[32,512]{1,0:T(8,128)(2,1)S(1)}, bf16[32,512]{1,0:T(8,128)(2,1)S(1)}, u32[]{:S(2)}, u32[]{:S(2)}) %collective-permute-start.1) | collective-permute-done | bytes 32800 | tf_op jit(solution)/shard_map/ppermute | solution.py:407
  20.8 1.1 %collective-permute-done.2.refs_3_ = bf16[32,512]{1,0:T(8,128)(2,1)S(1)} collective-permute-done((bf16[32,512]{1,0:T(8,128)(2,1)S(1)}, bf16[32,512]{1,0:T(8,128)(2,1)S(1)}, u32[]{:S(2)}, u32[]{:S(2)}) %collective-permute-start.2) | collective-permute-done | bytes 32800 | tf_op jit(solution)/shard_map/ppermute | solution.py:407
  21.8 5.0 %all-to-all-done.stacked = bf16[32,16,512]{2,1,0:T(8,128)(2,1)S(1)} async-done(((bf16[32,16,512]{2,1,0:T(8,128)(2,1)}), bf16[32,16,512]{2,1,0:T(8,128)(2,1)S(1)}, u32[]{:S(2)}, u32[]{:S(2)}) %all-to-all-start) | async-done | bytes 524320 | tf_op jit(solution)/shard_map/all_to_all | solution.py:422
  26.9 0.0 copy-start.10
  26.9 0.0 copy-done.4
  26.9 0.7 copy-done.10
  27.5 2.8 %first_half.1 = (bf16[8,32,384]{2,1,0:T(8,128)(2,1)}, bf16[32,8,384]{2,1,0:T(8,128)(2,1)S(1)}, bf16[256,512]{1,0:T(8,128)(2,1)S(1)}, f32[2,32,384]{2,1,0:T(8,128)S(1)}, f32[4,32,384]{2,1,0:T(8,128)S(1)}) custom-call(s32[2]{0:T(128)S(1)} %pad_add_fusion.here, f32[8]{0:T(128)S(1)} %copy-done.10, bf16[32,16,512]{2,1,0:T(8,128)(2,1)S(1)} %all-to-all-done.stacked, ...), custom_call_target="tpu_custom_call" | custom-call | tf_op jit(solution)/shard_map/first_half/pallas_call | solution.py:138
  30.3 3.4 %all-to-all-start.1 = ((bf16[8,32,384]{2,1,0:T(8,128)(2,1)}), bf16[8,32,384]{2,1,0:T(8,128)(2,1)S(1)}, u32[]{:S(2)}, u32[]{:S(2)}) async-start(bf16[8,32,384]{2,1,0:T(8,128)(2,1)} %get-tuple-element.41), calls=%async_computation.1 | async-start | bytes 393216 | tf_op jit(solution)/shard_map/all_to_all | solution.py:457
  33.7 1.2 %second_image.1.second = f32[2,32,384]{2,1,0:T(8,128)S(1)} custom-call(f32[8]{0:T(128)S(1)} %copy-done.10, bf16[32,16,512]{2,1,0:T(8,128)(2,1)S(1)} %all-to-all-done.stacked, bf16[512,512]{1,0:T(8,128)(2,1)S(1)} %copy-done.4, bf16[2,256,256]{2,1,0:T(8,128)(2,1)S(1)} %get-tuple-element.36.taper, bf16[256,512]{1,0:T(8,128)(2,1)S(1)} %get-tuple-element.44.grad), custom_call_target="tpu_custom_call" | custom-call | flops 1000000000 | tf_op jit(solution)/shard_map/second_image/pallas_call | solution.py:138
  34.9 7.1 %all-to-all-done.1.total = bf16[8,32,384]{2,1,0:T(8,128)(2,1)S(1)} async-done(((bf16[8,32,384]{2,1,0:T(8,128)(2,1)}), bf16[8,32,384]{2,1,0:T(8,128)(2,1)S(1)}, u32[]{:S(2)}, u32[]{:S(2)}) %all-to-all-start.1) | async-done | bytes 196640 | tf_op jit(solution)/shard_map/all_to_all | solution.py:457
  42.0 0.0 copy-start.5
  42.0 1.7 %combine.1 = (bf16[128,384]{1,0:T(8,128)(2,1)S(1)}, bf16[128,384]{1,0:T(8,128)(2,1)S(1)}, bf16[128,384]{1,0:T(8,128)(2,1)S(1)}, bf16[128,384]{1,0:T(8,128)(2,1)S(1)}, bf16[32,8,384]{2,1,0:T(8,128)(2,1)}) custom-call(s32[2]{0:T(128)S(1)} %pad_add_fusion.here, bf16[8,32,384]{2,1,0:T(8,128)(2,1)S(1)} %all-to-all-done.1.total, ...), custom_call_target="tpu_custom_call" | custom-call | tf_op jit(solution)/shard_map/combine/pallas_call | solution.py:138
  43.7 0.0 copy-start.1
  43.7 2.7 %all-to-all-start.2 = ((bf16[32,8,384]{2,1,0:T(8,128)(2,1)}), bf16[32,8,384]{2,1,0:T(8,128)(2,1)S(1)}, u32[]{:S(2)}, u32[]{:S(2)}) async-start(bf16[32,8,384]{2,1,0:T(8,128)(2,1)} %get-tuple-element.49), calls=%async_computation.2 | async-start | bytes 393216 | tf_op jit(solution)/shard_map/all_to_all | solution.py:486
  46.4 0.0 copy-done.5
  46.4 0.0 copy-done.1
  46.4 0.0 copy-start.8
  46.4 0.0 copy-start.9
  46.4 1.0 %fold_smooth.1.middle = bf16[64,1440]{1,0:T(8,128)(2,1)S(1)} custom-call(s32[1]{0:T(128)S(6)} %copy.18.marks, f32[8]{0:T(128)S(1)} %copy-done.10, bf16[1,2,16,4,1440]{4,3,2,1,0:T(4,128)(2,1)S(1)} %copy-done.1, bf16[2,16,4,1440]{3,2,1,0:T(4,128)(2,1)S(1)} %copy-done.2, bf16[16,4,1440]{2,1,0:T(4,128)(2,1)S(1)} %copy-done.3, bf16[512,256]{1,0:T(8,128)(2,1)S(1)} %copy-done.5), custom_call_target="tpu_custom_call" | custom-call | tf_op jit(solution)/shard_map/fold_smooth/pallas_call | solution.py:138
  47.4 1.3 %collective-permute-start.4 = (bf16[64,1440]{1,0:T(8,128)(2,1)S(1)}, bf16[64,1440]{1,0:T(8,128)(2,1)S(1)}, u32[]{:S(2)}, u32[]{:S(2)}) collective-permute-start(bf16[64,1440]{1,0:T(8,128)(2,1)S(1)} %fold_smooth.1.middle), channel_id=1, source_target_pairs={{1,0},{2,1},{3,2},{5,4},{6,5},{7,6},{9,8},{10,9},{11,10},{13,12},{... | collective-permute-start | bytes 552968 | tf_op jit(solution)/shard_map/ppermute | solution.py:477
  48.7 4.6 %collective-permute-start.3 = (bf16[64,1440]{1,0:T(8,128)(2,1)S(1)}, bf16[64,1440]{1,0:T(8,128)(2,1)S(1)}, u32[]{:S(2)}, u32[]{:S(2)}) collective-permute-start(bf16[64,1440]{1,0:T(8,128)(2,1)S(1)} %fold_smooth.1.middle), channel_id=1, source_target_pairs={{0,1},{1,2},{2,3},{4,5},{5,6},{6,7},{8,9},{9,10},{10,11},{12,13},{... | collective-permute-start | bytes 552968 | tf_op jit(solution)/shard_map/ppermute | solution.py:476
  53.3 2.6 %collective-permute-start.5 = (bf16[128,384]{1,0:T(8,128)(2,1)S(1)}, bf16[128,384]{1,0:T(8,128)(2,1)S(1)}, u32[]{:S(2)}, u32[]{:S(2)}) collective-permute-start(bf16[128,384]{1,0:T(8,128)(2,1)S(1)} %get-tuple-element.56), channel_id=1, source_target_pairs={{0,1},{1,2},{2,3},{3,0},{4,5},{5,6},{6,7},{7,4},{8,9},{9,10},{10,1... | collective-permute-start | bytes 294920 | tf_op jit(solution)/shard_map/ppermute | solution.py:407
  55.9 0.0 collective-permute-start.6
  55.9 2.0 %collective-permute-start.7 = (bf16[128,384]{1,0:T(8,128)(2,1)S(1)}, bf16[128,384]{1,0:T(8,128)(2,1)S(1)}, u32[]{:S(2)}, u32[]{:S(2)}) collective-permute-start(bf16[128,384]{1,0:T(8,128)(2,1)S(1)} %get-tuple-element.58), channel_id=1, source_target_pairs={{0,3},{1,0},{2,1},{3,2},{4,7},{5,4},{6,5},{7,6},{8,11},{9,8},{10,9... | collective-permute-start | bytes 294920 | tf_op jit(solution)/shard_map/ppermute | solution.py:407
  57.9 0.0 collective-permute-done.4.above
  57.9 0.6 collective-permute-done.3.below
  58.6 0.0 copy-done.8
  58.6 0.0 copy-done.9
  58.6 1.0 %first_gradient.1.grad_first = f32[64,1440]{1,0:T(8,128)S(1)} custom-call(s32[16]{0:T(128)S(1)} %copy-done.11, bf16[64,1440]{1,0:T(8,128)(2,1)S(1)} %collective-permute-done.3.below, bf16[64,1440]{1,0:T(8,128)(2,1)S(1)} %fold_smooth.1.middle, bf16[64,1440]{1,0:T(8,128)(2,1)S(1)} %collective-permute-done.4.above, f32[64,192]{1,0:T(8,128)S(1)} %copy-done.8, ...), custom_call_target="tpu_custom_call" | custom-call | tf_op jit(solution)/shard_map/first_gradient/pallas_call | solution.py:138
  59.5 1.3 %collective-permute-done.5.refs_1_ = bf16[128,384]{1,0:T(8,128)(2,1)S(1)} collective-permute-done((bf16[128,384]{1,0:T(8,128)(2,1)S(1)}, bf16[128,384]{1,0:T(8,128)(2,1)S(1)}, u32[]{:S(2)}, u32[]{:S(2)}) %collective-permute-start.5) | collective-permute-done | bytes 98336 | tf_op jit(solution)/shard_map/ppermute | solution.py:407
  60.8 3.1 %collective-permute-done.6.refs_2_ = bf16[128,384]{1,0:T(8,128)(2,1)S(1)} collective-permute-done((bf16[128,384]{1,0:T(8,128)(2,1)S(1)}, bf16[128,384]{1,0:T(8,128)(2,1)S(1)}, u32[]{:S(2)}, u32[]{:S(2)}) %collective-permute-start.6) | collective-permute-done | bytes 98336 | tf_op jit(solution)/shard_map/ppermute | solution.py:407
  63.9 1.6 %collective-permute-done.7.refs_3_ = bf16[128,384]{1,0:T(8,128)(2,1)S(1)} collective-permute-done((bf16[128,384]{1,0:T(8,128)(2,1)S(1)}, bf16[128,384]{1,0:T(8,128)(2,1)S(1)}, u32[]{:S(2)}, u32[]{:S(2)}) %collective-permute-start.7) | collective-permute-done | bytes 98336 | tf_op jit(solution)/shard_map/ppermute | solution.py:407
  65.5 1.1 %join.1 = (f32[64,1440]{1,0:T(8,128)S(1)}, f32[32,1440]{1,0:T(8,128)S(1)}) custom-call(s32[2]{0:T(128)S(1)} %pad_add_fusion.here, f32[4,8,384]{2,1,0:T(8,128)S(1)} %get-tuple-element.54.own_static, f32[64,64]{1,0:T(8,128)S(1)} %mul.46.pulling, bf16[128,384]{1,0:T(8,128)(2,1)S(1)} %get-tuple-element.55.refs_0_, ...), custom_call_target="tpu_custom_call" | custom-call | tf_op jit(solution)/shard_map/join/pallas_call | solution.py:138
  66.6 0.0 all-to-all-done.2.back
  66.6 1.2 %finish.1 = (f32[1,16,4,1440]{3,2,1,0:T(4,128)}, f32[16,4,1440]{2,1,0:T(4,128)}, f32[2,2,4,1440]{3,2,1,0:T(4,128)}) custom-call(bf16[32,8,384]{2,1,0:T(8,128)(2,1)S(1)} %all-to-all-done.2.back, f32[64,1440]{1,0:T(8,128)S(1)} %first_gradient.1.grad_first, f32[64,1440]{1,0:T(8,128)S(1)} %get-tuple-element.53.pulled_first, ...), custom_call_target="tpu_custom_call" | custom-call | tf_op jit(solution)/shard_map/finish/pallas_call | solution.py:138
  (2 shorter events, 0.0 us)
Async XLA Ops:
  1.3 1.0 %copy-start = (bf16[1,2,16,4,1440]{4,3,2,1,0:T(4,128)(2,1)S(1)}, bf16[1,2,16,4,1440]{4,3,2,1,0:T(4,128)(2,1)}, u32[]{:S(2)}) copy-start(bf16[1,2,16,4,1440]{4,3,2,1,0:T(4,128)(2,1)} %ensemble.2) | copy-start | bytes 1105924
  3.3 23.6 %all-to-all-start = ((bf16[32,16,512]{2,1,0:T(8,128)(2,1)}), bf16[32,16,512]{2,1,0:T(8,128)(2,1)S(1)}, u32[]{:S(2)}, u32[]{:S(2)}) async-start(bf16[32,16,512]{2,1,0:T(8,128)(2,1)} %pack.1), calls=%async_computation | async-start | bytes 1048576 | tf_op jit(solution)/shard_map/all_to_all | solution.py:422
  10.6 0.7 %copy-start.12 = (f32[16,16]{1,0:T(8,128)S(1)}, f32[16,16]{1,0:T(8,128)}, u32[]{:S(2)}) copy-start(f32[16,16]{1,0:T(8,128)} %param.17) | copy-start | bytes 3076
  11.6 0.9 %copy-start.3 = (bf16[16,4,1440]{2,1,0:T(4,128)(2,1)S(1)}, bf16[16,4,1440]{2,1,0:T(4,128)(2,1)}, u32[]{:S(2)}) copy-start(bf16[16,4,1440]{2,1,0:T(4,128)(2,1)} %precision.1) | copy-start | bytes 552964
  11.6 1.0 %copy-start.6 = (f32[256,256]{1,0:T(8,128)S(1)}, f32[256,256]{1,0:T(8,128)}, u32[]{:S(2)}) copy-start(f32[256,256]{1,0:T(8,128)} %constant.23.clone.apart) | copy-start | bytes 786436
  11.8 1.0 %copy-start.2 = (bf16[2,16,4,1440]{3,2,1,0:T(4,128)(2,1)S(1)}, bf16[2,16,4,1440]{3,2,1,0:T(4,128)(2,1)}, u32[]{:S(2)}) copy-start(bf16[2,16,4,1440]{3,2,1,0:T(4,128)(2,1)} %innovation.1) | copy-start | bytes 1105924
  11.9 1.1 %copy-start.7 = (f32[256,1]{1,0:T(8,128)S(1)}, f32[256,1]{1,0:T(8,128)}, u32[]{:S(2)}) copy-start(f32[256,1]{1,0:T(8,128)} %constant.24.clone.level) | copy-start | bytes 3076
  12.1 0.8 %copy-start.11 = (s32[16]{0:T(128)S(1)}, s32[16]{0:T(128)}, u32[]{:S(2)}) copy-start(s32[16]{0:T(128)} %widths.3) | copy-start | bytes 196
  12.9 14.0 %copy-start.4 = (bf16[512,512]{1,0:T(8,128)(2,1)S(1)}, bf16[512,512]{1,0:T(8,128)(2,1)}, u32[]{:S(2)}) copy-start(bf16[512,512]{1,0:T(8,128)(2,1)} %constant.25.clone.ring) | copy-start | bytes 1572868
  14.4 5.3 %collective-permute-start = (bf16[32,512]{1,0:T(8,128)(2,1)S(1)}, bf16[32,512]{1,0:T(8,128)(2,1)S(1)}, u32[]{:S(2)}, u32[]{:S(2)}) collective-permute-start(bf16[32,512]{1,0:T(8,128)(2,1)S(1)} %get-tuple-element.38), channel_id=1, source_target_pairs={{0,1},{1,2},{2,3},{3,0},{4,5},{5,6},{6,7},{7,4},{8,9},{9,10},{10,1... | collective-permute-start | bytes 98312 | tf_op jit(solution)/shard_map/ppermute | solution.py:407
  16.2 4.6 %collective-permute-start.1 = (bf16[32,512]{1,0:T(8,128)(2,1)S(1)}, bf16[32,512]{1,0:T(8,128)(2,1)S(1)}, u32[]{:S(2)}, u32[]{:S(2)}) collective-permute-start(bf16[32,512]{1,0:T(8,128)(2,1)S(1)} %get-tuple-element.39), channel_id=1, source_target_pairs={{0,2},{1,3},{2,0},{3,1},{4,6},{5,7},{6,4},{7,5},{8,10},{9,11},{10,... | collective-permute-start | bytes 98312 | tf_op jit(solution)/shard_map/ppermute | solution.py:407
  17.7 4.2 %collective-permute-start.2 = (bf16[32,512]{1,0:T(8,128)(2,1)S(1)}, bf16[32,512]{1,0:T(8,128)(2,1)S(1)}, u32[]{:S(2)}, u32[]{:S(2)}) collective-permute-start(bf16[32,512]{1,0:T(8,128)(2,1)S(1)} %get-tuple-element.40), channel_id=1, source_target_pairs={{0,3},{1,0},{2,1},{3,2},{4,7},{5,4},{6,5},{7,6},{8,11},{9,8},{10,9... | collective-permute-start | bytes 98312 | tf_op jit(solution)/shard_map/ppermute | solution.py:407
  26.9 0.7 copy-start.10
  30.3 11.7 %all-to-all-start.1 = ((bf16[8,32,384]{2,1,0:T(8,128)(2,1)}), bf16[8,32,384]{2,1,0:T(8,128)(2,1)S(1)}, u32[]{:S(2)}, u32[]{:S(2)}) async-start(bf16[8,32,384]{2,1,0:T(8,128)(2,1)} %get-tuple-element.41), calls=%async_computation.1 | async-start | bytes 393216 | tf_op jit(solution)/shard_map/all_to_all | solution.py:457
  42.0 4.4 %copy-start.5 = (bf16[512,256]{1,0:T(8,128)(2,1)S(1)}, bf16[512,256]{1,0:T(8,128)(2,1)}, u32[]{:S(2)}) copy-start(bf16[512,256]{1,0:T(8,128)(2,1)} %constant.26.clone.kernel) | copy-start | bytes 786436
  43.7 2.7 %copy-start.1 = (bf16[1,2,16,4,1440]{4,3,2,1,0:T(4,128)(2,1)S(1)}, bf16[1,2,16,4,1440]{4,3,2,1,0:T(4,128)(2,1)}, u32[]{:S(2)}) copy-start(bf16[1,2,16,4,1440]{4,3,2,1,0:T(4,128)(2,1)} %ensemble.2) | copy-start | bytes 1105924
  43.7 23.0 %all-to-all-start.2 = ((bf16[32,8,384]{2,1,0:T(8,128)(2,1)}), bf16[32,8,384]{2,1,0:T(8,128)(2,1)S(1)}, u32[]{:S(2)}, u32[]{:S(2)}) async-start(bf16[32,8,384]{2,1,0:T(8,128)(2,1)} %get-tuple-element.49), calls=%async_computation.2 | async-start | bytes 393216 | tf_op jit(solution)/shard_map/all_to_all | solution.py:486
  46.4 12.1 %copy-start.8 = (f32[64,192]{1,0:T(8,128)S(1)}, f32[64,192]{1,0:T(8,128)}, u32[]{:S(2)}) copy-start(f32[64,192]{1,0:T(8,128)} %constant.27.clone.apart) | copy-start | bytes 147460
  46.4 12.1 %copy-start.9 = (f32[64,1]{1,0:T(8,128)S(1)}, f32[64,1]{1,0:T(8,128)}, u32[]{:S(2)}) copy-start(f32[64,1]{1,0:T(8,128)} %constant.28.clone.level) | copy-start | bytes 772
  47.4 10.5 %collective-permute-start.4 = (bf16[64,1440]{1,0:T(8,128)(2,1)S(1)}, bf16[64,1440]{1,0:T(8,128)(2,1)S(1)}, u32[]{:S(2)}, u32[]{:S(2)}) collective-permute-start(bf16[64,1440]{1,0:T(8,128)(2,1)S(1)} %fold_smooth.1.middle), channel_id=1, source_target_pairs={{1,0},{2,1},{3,2},{5,4},{6,5},{7,6},{9,8},{10,9},{11,10},{13,12},{... | collective-permute-start | bytes 552968 | tf_op jit(solution)/shard_map/ppermute | solution.py:477
  48.7 9.8 %collective-permute-start.3 = (bf16[64,1440]{1,0:T(8,128)(2,1)S(1)}, bf16[64,1440]{1,0:T(8,128)(2,1)S(1)}, u32[]{:S(2)}, u32[]{:S(2)}) collective-permute-start(bf16[64,1440]{1,0:T(8,128)(2,1)S(1)} %fold_smooth.1.middle), channel_id=1, source_target_pairs={{0,1},{1,2},{2,3},{4,5},{5,6},{6,7},{8,9},{9,10},{10,11},{12,13},{... | collective-permute-start | bytes 552968 | tf_op jit(solution)/shard_map/ppermute | solution.py:476
  53.3 7.6 %collective-permute-start.5 = (bf16[128,384]{1,0:T(8,128)(2,1)S(1)}, bf16[128,384]{1,0:T(8,128)(2,1)S(1)}, u32[]{:S(2)}, u32[]{:S(2)}) collective-permute-start(bf16[128,384]{1,0:T(8,128)(2,1)S(1)} %get-tuple-element.56), channel_id=1, source_target_pairs={{0,1},{1,2},{2,3},{3,0},{4,5},{5,6},{6,7},{7,4},{8,9},{9,10},{10,1... | collective-permute-start | bytes 294920 | tf_op jit(solution)/shard_map/ppermute | solution.py:407
  55.9 8.1 %collective-permute-start.6 = (bf16[128,384]{1,0:T(8,128)(2,1)S(1)}, bf16[128,384]{1,0:T(8,128)(2,1)S(1)}, u32[]{:S(2)}, u32[]{:S(2)}) collective-permute-start(bf16[128,384]{1,0:T(8,128)(2,1)S(1)} %get-tuple-element.57), channel_id=1, source_target_pairs={{0,2},{1,3},{2,0},{3,1},{4,6},{5,7},{6,4},{7,5},{8,10},{9,11},{10,... | collective-permute-start | bytes 294920 | tf_op jit(solution)/shard_map/ppermute | solution.py:407
  55.9 9.6 %collective-permute-start.7 = (bf16[128,384]{1,0:T(8,128)(2,1)S(1)}, bf16[128,384]{1,0:T(8,128)(2,1)S(1)}, u32[]{:S(2)}, u32[]{:S(2)}) collective-permute-start(bf16[128,384]{1,0:T(8,128)(2,1)S(1)} %get-tuple-element.58), channel_id=1, source_target_pairs={{0,3},{1,0},{2,1},{3,2},{4,7},{5,4},{6,5},{7,6},{8,11},{9,8},{10,9... | collective-permute-start | bytes 294920 | tf_op jit(solution)/shard_map/ppermute | solution.py:407

commit v6 on v5

--- a/solution.py
+++ b/solution.py
@@ -49,7 +49,7 @@
 
 
 def near(apart, spans):
-    return jnp.maximum(1.0 - apart / spans, 0.0) / spans
+    return jnp.maximum(spans - apart, 0.0).astype(jnp.bfloat16)
 
 
 def row_apart(bands, held, rows, copies):
@@ -71,16 +71,31 @@
     return np.where(same, np.abs(shift), 1000).astype(np.float32), level
 
 
-def each_row(matrix, rows):
-    same = jnp.eye(rows, dtype=jnp.float32)
-    wide = matrix[:, None, :, None] * same[None, :, None, :]
-    return wide.reshape(matrix.shape[0] * rows, matrix.shape[1] * rows)
+def row_levels(levels, rows):
+    index = np.arange(levels * rows)
+    level = index[:, None] // rows == np.arange(levels)[None]
+    place = index[:, None] % rows == index[None] % rows
+    return level.astype(np.float32), place.astype(np.float32)
 
 
 def exact_dot(matrix, field):
     return jnp.dot(
         matrix, field, precision=lax.Precision.HIGHEST, preferred_element_type=jnp.float32
     )
+
+
+def parts_dot(matrix, field):
+    count, parts = matrix.shape[0], []
+    for _ in range(PARTS):
+        part = matrix.astype(jnp.bfloat16).astype(jnp.float32)
+        parts.append(part)
+        matrix = matrix - part
+    stacked = jnp.concatenate(parts, axis=0).astype(jnp.bfloat16)
+    products = jnp.dot(stacked, field, preferred_element_type=jnp.float32)
+    total = products[:count]
+    for index in range(1, PARTS):
+        total = total + products[index * count : (index + 1) * count]
+    return total
 
 
 def window(values, band, share, halo, tail):
@@ -97,17 +112,14 @@
     return jnp.concatenate(parts + [tail], axis=1)
 
 
-def spread(field, ring, taper):
-    copies = taper.shape[1]
+def spread(field, ring, taper, factor):
+    copies = taper.shape[0]
     smoothed = jnp.dot(field.astype(jnp.bfloat16), ring, preferred_element_type=jnp.float32)
     smoothed = smoothed.astype(jnp.bfloat16)
     parts = []
     for start in range(0, field.shape[0], copies):
         part = smoothed[start : start + copies]
-        parts.append(
-            jnp.dot(taper[0], part, preferred_element_type=jnp.float32)
-            + jnp.dot(taper[1], part, preferred_element_type=jnp.float32)
-        )
+        parts.append(factor * jnp.dot(taper, part, preferred_element_type=jnp.float32))
     return parts[0] if len(parts) == 1 else jnp.concatenate(parts, axis=0)
 
 
@@ -169,27 +181,36 @@
                 total = total + scaled[slot] * weighted[slot][None]
             return total.reshape(members * per_member, padded)
 
-        def images_of(scaled, grad, ring, taper):
-            local = spread(grad, ring, taper).reshape(members, per_member, padded)
-            return [ensemble_share * jnp.sum(scaled[t] * local, axis=0) for t in range(slots)]
-
-        def pack(marks, ensemble, out):
-            values = jnp.concatenate(
-                [ensemble[0, t, level].astype(f32) for t in range(slots) for level in range(levels)],
-                axis=0,
-            )
-            tail = jnp.full((values.shape[0], padded - width), marks[0], jnp.int32).astype(f32)
-            for band in range(bands):
-                piece = window(values, band, lon_share, halo, tail)
-                for member in range(members):
-                    picked = []
-                    for t in range(slots):
-                        start = t * everything + member * own
-                        picked.append(piece[start : start + own])
-                    out[member * bands + band] = jnp.concatenate(picked, axis=0).astype(bf16)
-
-        def observe(here, widths, innovation, precision, pulling, root, apart, level, *refs):
-            outs, (own_static, pulled, mixing, taper, static, mixed, spans) = refs[:-7], refs[-7:]
+        def images_of(scaled, grad, ring, taper, factor):
+            local = spread(grad, ring, taper, factor).reshape(members, per_member, padded)
+            return [jnp.sum(scaled[t] * local, axis=0) for t in range(slots)]
+
+        def pack(marks, ensemble, out, arrived, packed, in_sems, out_sems):
+            def incoming(t):
+                return pltpu.make_async_copy(ensemble.at[0, t], arrived.at[t], in_sems.at[t])
+
+            def outgoing(member):
+                place = pl.ds(member * bands, bands)
+                return pltpu.make_async_copy(packed.at[place], out.at[place], out_sems.at[member])
+
+            for t in range(slots):
+                incoming(t).start()
+            tail = jnp.full((slots * own, padded - width), marks[0], jnp.int32).astype(f32)
+            for t in range(slots):
+                incoming(t).wait()
+            for member in range(members):
+                picked = range(member * level_share, (member + 1) * level_share)
+                values = [arrived[t, at].astype(f32) for t in range(slots) for at in picked]
+                values = jnp.concatenate(values, axis=0)
+                for band in range(bands):
+                    piece = window(values, band, lon_share, halo, tail)
+                    packed[member * bands + band] = piece.astype(bf16)
+                outgoing(member).start()
+            for member in range(members):
+                outgoing(member).wait()
+
+        def observe(here, widths, weight, innovation, precision, root, of_level, same, apart, level, *refs):
+            outs, (own_static, pulled, mixing, pulling, taper, factor, static, mixed, spans) = refs[:-9], refs[-9:]
             total = []
             for at in range(levels):
                 precise = precision[at].astype(f32)
@@ -197,10 +218,20 @@
                 for t in range(1, slots):
                     part = part + precise * innovation[t, at].astype(f32)
                 total.append(part)
-            back = exact_dot(pulling[...], jnp.concatenate(total, axis=0))
+            out_of = lax.dot_general(
+                exact_dot(of_level[...], static_share * root[...]),
+                of_level[...],
+                (((1,), (1,)), ((), ())),
+                precision=lax.Precision.HIGHEST,
+                preferred_element_type=f32,
+            )
+            out_of = out_of * same[...]
+            into = out_of.T
+            pulling[...] = into
+            back = exact_dot(into, jnp.concatenate(total, axis=0))
             pulled[...] = back
-            forth = exact_dot(root[...], back)
-            both = exact_dot(root[...], pulling[...])
+            forth = exact_dot(out_of, back)
+            both = exact_dot(out_of, into)
             for at in range(levels):
                 static[at] = forth[at * rows : (at + 1) * rows]
                 mixed[at] = both[at * rows : (at + 1) * rows]
@@ -223,10 +254,11 @@
             span = jnp.ones(level.shape, f32)
             for at, which in enumerate(picked):
                 span = span + jnp.where(level[...] == at, widths[which].astype(f32), 0.0)
-            taper[0], taper[1] = halves(near(apart[...], span))
-
-        def first_half(here, weight, stacked, ring, taper, *refs):
-            blocks, (total_out, grad_out, full_out, image_out, fields, spans) = refs[:-6], refs[-6:]
+            taper[...] = near(apart[...], span)
+            factor[...] = ensemble_share / (span * span)
+
+        def first_half(here, weight, stacked, ring, taper, factor, *refs):
+            blocks, (total_out, weighted_out, image_out, fields, spans) = refs[:-5], refs[-5:]
             if few:
                 for shift in range(bands):
                     spans[shifted(here[1], -shift)] = blocks[shift][...]
@@ -242,23 +274,36 @@
             precise, static = field[slots], field[slots + 1]
             scaled = load_members(weight, stacked)
             weighted = [precise * field[t] for t in range(slots)]
-            grad = ensemble_share * spread(fold(scaled, weighted), ring[...], taper)
+            grad = spread(fold(scaled, weighted), ring[...], taper[...], factor[...])
             total = jnp.zeros((per_member, padded), f32)
-            weighted = []
-            for t, image in enumerate(images_of(scaled, grad, ring[...], taper)):
+            for t, image in enumerate(images_of(scaled, grad, ring[...], taper[...], factor[...])):
                 image_out[t] = image[:, :kept]
-                weighted.append(precise * (image + static))
-                total = total + weighted[t]
+                image = precise * (image + static)
+                weighted_out[t] = image
+                total = total + image
             total = total[:, :kept].astype(bf16)
             for member in range(members):
                 total_out[member] = total
-            grad = (ensemble_share * spread(fold(scaled, weighted), ring[...], taper)).astype(bf16)
-            full_out[...] = grad
+
+        def store_halves(spans, start, slot, values):
+            for half, part in enumerate(halves(values)):
+                at = start + (half * slots + slot) * own
+                for band in range(bands):
+                    spans[band, at : at + own] = part[band * own : (band + 1) * own]
+
+        def deal(here, spans, outs):
+            for shift in range(bands):
+                if few:
+                    outs[shift][...] = spans[shifted(here[1], shift)]
+                else:
+                    outs[0][shift] = spans[shift]
+
+        def second_half(weight, stacked, ring, taper, factor, weighted, grad_out, image_out):
+            scaled = load_members(weight, stacked)
+            grad = fold(scaled, [weighted[t] for t in range(slots)])
+            grad = spread(grad, ring[...], taper[...], factor[...]).astype(bf16)
             grad_out[...] = grad[:, :kept].reshape(members * bands, own, kept)
-
-        def second_image(weight, stacked, ring, taper, grad, image_out):
-            scaled = load_members(weight, stacked)
-            for t, image in enumerate(images_of(scaled, grad[...], ring[...], taper)):
+            for t, image in enumerate(images_of(scaled, grad, ring[...], taper[...], factor[...])):
                 image_out[t] = image[:, :kept]
 
         def combine(here, total, grad, first, second, fields, mixing, *refs):
@@ -267,8 +312,9 @@
             for band in range(bands):
                 place = slice(band * own, (band + 1) * own)
                 every = jnp.concatenate([total[member, place].astype(f32) for member in range(members)], axis=0)
-                mixed.append(exact_dot(mixing[...], every))
-                spans[band, :everything] = every.astype(bf16)
+                every = every.astype(bf16)
+                mixed.append(parts_dot(mixing[...], every))
+                spans[band, :everything] = every
             mixed = jnp.concatenate(mixed, axis=0)
             sums = [jnp.zeros((per_member, kept), f32) for _ in range(SUMS)]
             for t in range(slots):
@@ -279,16 +325,9 @@
                 sums[1] = sums[1] + weighted * whole
                 sums[2] = sums[2] + weighted * image
                 sums[3] = sums[3] + precise * image * image
-                for which, values in enumerate((first[t], image)):
-                    for half, part in enumerate(halves(values)):
-                        at = everything + ((half * 2 + which) * slots + t) * own
-                        for band in range(bands):
-                            spans[band, at : at + own] = part[band * own : (band + 1) * own]
-            for shift in range(bands):
-                if few:
-                    outs[shift][...] = spans[shifted(here[1], shift)]
-                else:
-                    outs[0][shift] = spans[shift]
+                store_halves(spans, everything, t, first[t])
+                store_halves(spans, everything + 2 * slots * own, t, image)
+            deal(here, spans, outs)
             inside = lax.broadcasted_iota(jnp.int32, (per_member, kept), 1) < lon_share
             lane = lax.broadcasted_iota(jnp.int32, (1, kept), 1) - lon_share
             row = jnp.zeros((1, kept), f32)
@@ -332,12 +371,9 @@
             span = jnp.ones(level.shape, f32)
             for at in range(levels):
                 span = span + jnp.where(level[...] == at, widths[at].astype(f32), 0.0)
-            high, low = halves(near(apart[...], span))
             stacked = jnp.concatenate([below[...], middle[...], above[...]], axis=0)
-            grad[...] = ensemble_share * (
-                jnp.dot(high, stacked, preferred_element_type=f32)
-                + jnp.dot(low, stacked, preferred_element_type=f32)
-            )
+            summed = jnp.dot(near(apart[...], span), stacked, preferred_element_type=f32)
+            grad[...] = ensemble_share / (span * span) * summed
 
         def join(here, own_static, pulling, *refs):
             blocks, (pulled, images, spans) = refs[:-3], refs[-3:]
@@ -346,18 +382,18 @@
                     spans[shifted(here[1], -shift)] = blocks[shift][...]
                 else:
                     spans[shift] = blocks[0][shift]
-            size = 2 * slots * own
+            size = slots * own
             for band in range(bands):
                 place = slice(band * lon_share, (band + 1) * lon_share)
-                every = spans[band, :everything].astype(f32)
-                pulled[:, place] = exact_dot(pulling[...], every)[:, :lon_share]
-                both = spans[band, everything : everything + size].astype(f32)
-                both = both + spans[band, everything + size :].astype(f32)
+                pulled[:, place] = parts_dot(pulling[...], spans[band, :everything])[:, :lon_share]
+                parts = spans[band, everything:].astype(f32)
+                first = parts[:size] + parts[size : 2 * size]
+                second = parts[2 * size : 3 * size] + parts[3 * size :]
                 static = own_static[band]
                 for t in range(slots):
                     at = slice(t * own, (t + 1) * own)
-                    images[at, place] = (both[at] + static)[:, :lon_share]
-                images[slots * own :, place] = both[slots * own :, :lon_share]
+                    images[at, place] = (first[at] + static)[:, :lon_share]
+                images[size:, place] = second[:, :lon_share]
 
         def finish(back, grad_first, pulled_first, pulled_second, images, *refs):
             member_out, static_out, image_out, second = refs
@@ -413,16 +449,27 @@
 
         here = jnp.stack([lax.axis_index("member"), lax.axis_index("band")]).astype(jnp.int32)
 
-        (pieces,) = call(
-            pack, [((members * bands, slots * own, padded), bf16)], [member_of_slot], [ensemble]
-        )
+        block = (members * bands, slots * own, padded)
+        pieces = pl.pallas_call(
+            pack,
+            out_shape=jax.ShapeDtypeStruct(block, bf16),
+            in_specs=[smem, pl.BlockSpec(memory_space=pltpu.HBM)],
+            out_specs=pl.BlockSpec(memory_space=pltpu.HBM),
+            scratch_shapes=[
+                pltpu.VMEM((slots, levels, rows, lon), bf16),
+                pltpu.VMEM(block, bf16),
+                pltpu.SemaphoreType.DMA((slots,)),
+                pltpu.SemaphoreType.DMA((members,)),
+            ],
+            compiler_params=pltpu.CompilerParams(vmem_limit_bytes=60 * 2**20),
+            name="pack",
+        )(member_of_slot, ensemble)
         pieces, ensemble, innovation, precision, static_root = lax.optimization_barrier(
             (pieces, ensemble, innovation, precision, static_root)
         )
         stacked = lax.all_to_all(pieces, BOTH, 0, 0, tiled=True)
 
-        pulling = each_row(static_share * static_root.T, rows)
-        root = each_row(static_share * static_root, rows)
+        of_level, same = row_levels(levels, rows)
         apart, level = row_apart(bands, level_share, rows, copies)
         block = (arrays * own, padded)
         results = call(
@@ -432,39 +479,19 @@
                 ((bands, own, kept), f32),
                 ((everything, lon), f32),
                 ((own, everything), f32),
-                ((2,) + apart.shape, bf16),
+                ((everything, everything), f32),
+                (apart.shape, bf16),
+                (level.shape, f32),
             ],
-            [here, halfwidth],
-            [innovation, precision, pulling, root, jnp.asarray(apart), jnp.asarray(level)],
+            [here, halfwidth, member_weight],
+            [innovation, precision, static_root]
+            + [jnp.asarray(table) for table in (of_level, same, apart, level)],
             scratch=[((levels, rows, lon), f32), ((levels, rows, everything), f32), ((bands,) + block, bf16)],
         )
-        blocks, (own_static, pulled, mixing, taper) = trade(results[:-4]), results[-4:]
-        ring = ring_kernel(width, padded)
-
-        total, grad, full, image_first, fields = call(
-            first_half,
-            [
-                ((members, per_member, kept), bf16),
-                ((members * bands, own, kept), bf16),
-                ((members * per_member, padded), bf16),
-                ((slots, per_member, kept), f32),
-                ((arrays, per_member, kept), f32),
-            ],
-            [here, member_weight],
-            [stacked, ring, taper, *blocks],
-            scratch=[((bands,) + block, bf16)],
-        )
-        total = lax.all_to_all(total, "member", 0, 0, tiled=True)
-        (image_second,) = call(
-            second_image,
-            [((slots, per_member, kept), f32)],
-            [member_weight],
-            [stacked, ring, taper, full],
-            flops=10**9,
-        )
-
-        image_second, ensemble, innovation, precision = lax.optimization_barrier(
-            (image_second, ensemble, innovation, precision)
+        blocks = trade(results[:-6])
+        own_static, pulled, mixing, pulling, taper, factor = results[-6:]
+        own_static, ensemble, innovation, precision = lax.optimization_barrier(
+            (own_static, ensemble, innovation, precision)
         )
         (smoothed,) = call(
             fold_smooth,
@@ -475,6 +502,28 @@
         up = [(at, at + 1) for at in range(bands - 1)]
         below = lax.ppermute(smoothed, "band", up)
         above = lax.ppermute(smoothed, "band", [(target, source) for source, target in up])
+
+        ring, above = lax.optimization_barrier((ring_kernel(width, padded), above))
+        total, weighted, image_first, fields = call(
+            first_half,
+            [
+                ((members, per_member, kept), bf16),
+                ((slots, per_member, padded), f32),
+                ((slots, per_member, kept), f32),
+                ((arrays, per_member, kept), f32),
+            ],
+            [here, member_weight],
+            [stacked, ring, taper, factor, *blocks],
+            scratch=[((bands,) + block, bf16)],
+        )
+        total = lax.all_to_all(total, "member", 0, 0, tiled=True)
+        grad, image_second = call(
+            second_half,
+            [((members * bands, own, kept), bf16), ((slots, per_member, kept), f32)],
+            [member_weight],
+            [stacked, ring, taper, factor, weighted],
+            flops=10**9,
+        )
 
         results = call(
             combine,
@@ -483,7 +532,8 @@
             [total, grad, image_first, image_second, fields, mixing],
             scratch=[((bands, traded, kept), bf16)],
         )
-        back = lax.all_to_all(results[-1], BOTH, 0, 0, tiled=True)
+        gradients, below = lax.optimization_barrier((results[-1], below))
+        back = lax.all_to_all(gradients, BOTH, 0, 0, tiled=True)
         blocks = trade(results[:-1])
         pulled_second, images = call(
             join,

time: 68.3 us -> 60.6 us (0.89)
  waiting for transfers between devices: 21.5 us -> 12.3 us
  starting transfers between devices: 28.6 us -> 32.3 us
  local copies, waits for them, and re-layouts: 3.65 us -> 0.63 us
  Pallas kernels: 12.4 us -> 13.3 us
    all_to_all x1, waiting for transfers between devices: 5.05 us -> 0.01 us  [shards(): stacked = lax.all_to_all(pieces, BOTH, 0, 0, tiled=True)]
    all_to_all x1, waiting for transfers between devices: 7.08 us -> 3.29 us  [shards(): total = lax.all_to_all(total, 'member', 0, 0, tiled=True)]
    ppermute x1, waiting for transfers between devices: 0.01 us -> 3.03 us  [shards(): lax.ppermute(smoothed, 'band', [(target, source) for source, target in up])]
    ppermute x6, waiting for transfers between devices: 8.67 us -> 5.99 us  [trade(): lax.ppermute(blocks[shift], 'band', [(at, (at + shift) % bands) for at in...]
    unnamed x26 -> x28, local copies, waits for them, and re-layouts: 3.08 us -> 0.63 us
    ppermute x6, starting transfers between devices: 9.37 us -> 11.6 us  [trade(): lax.ppermute(blocks[shift], 'band', [(at, (at + shift) % bands) for at in...]
    pallas_call x0 -> x1, Pallas kernels: none -> 2.02 us  [shards(): pl.pallas_call(pack, out_shape=jax.ShapeDtypeStruct(block, bf16), in_spec...]
    all_to_all x1, starting transfers between devices: 2.71 us -> 4.4 us  [shards(): back = lax.all_to_all(gradients, BOTH, 0, 0, tiled=True)]
  transfers between devices with their start and end apart: 11 -> 11, of which waited for: 9 -> 5; matrix products, arithmetic and copies ran while one was open for 1% -> 0% of each run, Pallas kernels for 8% -> 13%
where the time goes in v6:
time: 60.6 us; the launch traced here: 60.1 us
  starting transfers between devices  32.3 us (53%)
  Pallas kernels  13.3 us (22%)
  waiting for transfers between devices  12.3 us (20%)
  between operations  1.51 us (2%)
  local copies, waits for them, and re-layouts  0.63 us (1%)
    ppermute x6, starting transfers between devices, trade(): lax.ppermute(blocks[shift], 'band', [(at, (at + shift) % bands) for at in...  11.6 us
    pallas_call x8, Pallas kernels, call(): pl.pallas_call(body, out_shape=tuple((jax.ShapeDtypeStruct(shape, kind) f...  11.3 us
    all_to_all x1, starting transfers between devices, shards(): stacked = lax.all_to_all(pieces, BOTH, 0, 0, tiled=True)  7.3 us
    ppermute x6, waiting for transfers between devices, trade(): lax.ppermute(blocks[shift], 'band', [(at, (at + shift) % bands) for at in...  5.99 us
    all_to_all x1, starting transfers between devices, shards(): back = lax.all_to_all(gradients, BOTH, 0, 0, tiled=True)  4.4 us
    all_to_all x1, starting transfers between devices, shards(): total = lax.all_to_all(total, 'member', 0, 0, tiled=True)  4.26 us
    ppermute x1, starting transfers between devices, shards(): below = lax.ppermute(smoothed, 'band', up)  3.44 us
    all_to_all x1, waiting for transfers between devices, shards(): total = lax.all_to_all(total, 'member', 0, 0, tiled=True)  3.29 us
  transfers between devices with their start and end apart: 11, of which 5 were waited for; matrix products, arithmetic and copies ran while one was open for 0% of the time, Pallas kernels for 13%

profile of v6, /device:TPU:0, one launch (start us, length us, event | category | flops | bytes accessed | tf_op | source)
XLA Modules:
  0.0 60.1 jit_solution(4591815066789071009)
XLA Ops:
  1.3 2.0 %pack.1 = bf16[32,16,512]{2,1,0:T(8,128)(2,1)} custom-call(s32[1]{0:T(128)S(6)} %copy.18.marks, bf16[1,2,16,4,1440]{4,3,2,1,0:T(4,128)(2,1)} %ensemble.2), custom_call_target="tpu_custom_call" | custom-call | tf_op jit(solution)/shard_map/pack/pallas_call | solution.py:453
  3.3 0.0 copy-start.1
  3.3 0.0 copy-start.2
  3.3 0.0 copy-start.5
  3.3 0.0 copy-start.6
  3.3 0.0 copy-start.9
  3.4 0.0 copy-start.10
  3.4 7.3 %all-to-all-start = ((bf16[32,16,512]{2,1,0:T(8,128)(2,1)}), bf16[32,16,512]{2,1,0:T(8,128)(2,1)S(1)}, u32[]{:S(2)}, u32[]{:S(2)}) async-start(bf16[32,16,512]{2,1,0:T(8,128)(2,1)} %pack.1), calls=%async_computation | async-start | bytes 1048576 | tf_op jit(solution)/shard_map/all_to_all | solution.py:470
  10.7 0.0 copy-start.11
  10.7 0.0 copy-start.12
  10.7 0.0 copy-start.13
  10.7 0.1 pad_add_fusion.here
  10.8 0.0 copy-done.1
  10.8 0.0 copy-done.2
  10.8 0.0 copy-done.5
  10.8 0.0 copy-done.6
  10.8 0.0 copy-done.9
  10.8 0.0 copy-done.10
  10.8 0.6 copy-done.11
  11.4 0.0 copy-done.12
  11.4 0.0 copy-done.13
  11.4 0.0 copy-start
  11.4 0.0 copy-start.4
  11.4 1.9 %observe.1 = (bf16[32,512]{1,0:T(8,128)(2,1)S(1)}, bf16[32,512]{1,0:T(8,128)(2,1)S(1)}, bf16[32,512]{1,0:T(8,128)(2,1)S(1)}, bf16[32,512]{1,0:T(8,128)(2,1)S(1)}...) custom-call(s32[2]{0:T(128)S(1)} %pad_add_fusion.here, ...), custom_call_target="tpu_custom_call" | custom-call | tf_op jit(solution)/shard_map/observe/pallas_call | solution.py:150
  13.3 0.0 copy-done
  13.3 0.0 copy-done.4
  13.3 0.0 copy-start.3
  13.3 1.0 %fold_smooth.1.middle = bf16[64,1440]{1,0:T(8,128)(2,1)S(1)} custom-call(s32[1]{0:T(128)S(6)} %copy.18.marks, f32[8]{0:T(128)S(1)} %copy-done.12, bf16[1,2,16,4,1440]{4,3,2,1,0:T(4,128)(2,1)S(1)} %copy-done, bf16[2,16,4,1440]{3,2,1,0:T(4,128)(2,1)S(1)} %copy-done.1, bf16[16,4,1440]{2,1,0:T(4,128)(2,1)S(1)} %copy-done.2, bf16[512,256]{1,0:T(8,128)(2,1)S(1)} %copy-done.4), custom_call_target="tpu_custom_call" | custom-call | tf_op jit(solution)/shard_map/fold_smooth/pallas_call | solution.py:150
  14.4 1.3 %collective-permute-start = (bf16[64,1440]{1,0:T(8,128)(2,1)S(1)}, bf16[64,1440]{1,0:T(8,128)(2,1)S(1)}, u32[]{:S(2)}, u32[]{:S(2)}) collective-permute-start(bf16[64,1440]{1,0:T(8,128)(2,1)S(1)} %fold_smooth.1.middle), channel_id=1, source_target_pairs={{1,0},{2,1},{3,2},{5,4},{6,5},{7,6},{9,8},{10,9},{11,10},{13,12},{... | collective-permute-start | bytes 552968 | tf_op jit(solution)/shard_map/ppermute | solution.py:504
  15.7 2.7 %collective-permute-start.1 = (bf16[32,512]{1,0:T(8,128)(2,1)S(1)}, bf16[32,512]{1,0:T(8,128)(2,1)S(1)}, u32[]{:S(2)}, u32[]{:S(2)}) collective-permute-start(bf16[32,512]{1,0:T(8,128)(2,1)S(1)} %get-tuple-element.52), channel_id=1, source_target_pairs={{0,1},{1,2},{2,3},{3,0},{4,5},{5,6},{6,7},{7,4},{8,9},{9,10},{10,1... | collective-permute-start | bytes 98312 | tf_op jit(solution)/shard_map/ppermute | solution.py:443
  18.3 1.8 %collective-permute-start.2 = (bf16[32,512]{1,0:T(8,128)(2,1)S(1)}, bf16[32,512]{1,0:T(8,128)(2,1)S(1)}, u32[]{:S(2)}, u32[]{:S(2)}) collective-permute-start(bf16[32,512]{1,0:T(8,128)(2,1)S(1)} %get-tuple-element.53), channel_id=1, source_target_pairs={{0,2},{1,3},{2,0},{3,1},{4,6},{5,7},{6,4},{7,5},{8,10},{9,11},{10,... | collective-permute-start | bytes 98312 | tf_op jit(solution)/shard_map/ppermute | solution.py:443
  20.1 2.4 %collective-permute-start.3 = (bf16[32,512]{1,0:T(8,128)(2,1)S(1)}, bf16[32,512]{1,0:T(8,128)(2,1)S(1)}, u32[]{:S(2)}, u32[]{:S(2)}) collective-permute-start(bf16[32,512]{1,0:T(8,128)(2,1)S(1)} %get-tuple-element.54), channel_id=1, source_target_pairs={{0,3},{1,0},{2,1},{3,2},{4,7},{5,4},{6,5},{7,6},{8,11},{9,8},{10,9... | collective-permute-start | bytes 98312 | tf_op jit(solution)/shard_map/ppermute | solution.py:443
  22.5 3.0 %collective-permute-done.above = bf16[64,1440]{1,0:T(8,128)(2,1)S(1)} collective-permute-done((bf16[64,1440]{1,0:T(8,128)(2,1)S(1)}, bf16[64,1440]{1,0:T(8,128)(2,1)S(1)}, u32[]{:S(2)}, u32[]{:S(2)}) %collective-permute-start) | collective-permute-done | bytes 184352 | tf_op jit(solution)/shard_map/ppermute | solution.py:504
  25.5 1.7 %collective-permute-done.1.refs_1_ = bf16[32,512]{1,0:T(8,128)(2,1)S(1)} collective-permute-done((bf16[32,512]{1,0:T(8,128)(2,1)S(1)}, bf16[32,512]{1,0:T(8,128)(2,1)S(1)}, u32[]{:S(2)}, u32[]{:S(2)}) %collective-permute-start.1) | collective-permute-done | bytes 32800 | tf_op jit(solution)/shard_map/ppermute | solution.py:443
  27.2 0.0 collective-permute-done.2.refs_2_
  27.2 0.0 collective-permute-done.3.refs_3_
  27.2 0.0 all-to-all-done.stacked
  27.2 0.0 copy-done.3
  27.2 2.3 %first_half.1 = (bf16[8,32,384]{2,1,0:T(8,128)(2,1)}, f32[2,32,512]{2,1,0:T(8,128)S(1)}, f32[2,32,384]{2,1,0:T(8,128)S(1)}, f32[4,32,384]{2,1,0:T(8,128)S(1)}) custom-call(s32[2]{0:T(128)S(1)} %pad_add_fusion.here, f32[8]{0:T(128)S(1)} %copy-done.12, bf16[32,16,512]{2,1,0:T(8,128)(2,1)S(1)} %all-to-all-done.stacked, bf16[512,512]{1,0:T(8,128)(2,1)S(1)} %copy-done.3, ...), custom_call_target="tpu_custom_call" | custom-call | tf_op jit(solution)/shard_map/first_half/pallas_call | solution.py:150
  29.5 4.3 %all-to-all-start.1 = ((bf16[8,32,384]{2,1,0:T(8,128)(2,1)}), bf16[8,32,384]{2,1,0:T(8,128)(2,1)S(1)}, u32[]{:S(2)}, u32[]{:S(2)}) async-start(bf16[8,32,384]{2,1,0:T(8,128)(2,1)} %get-tuple-element.55), calls=%async_computation.1 | async-start | bytes 393216 | tf_op jit(solution)/shard_map/all_to_all | solution.py:519
  33.8 3.4 %collective-permute-start.4 = (bf16[64,1440]{1,0:T(8,128)(2,1)S(1)}, bf16[64,1440]{1,0:T(8,128)(2,1)S(1)}, u32[]{:S(2)}, u32[]{:S(2)}) collective-permute-start(bf16[64,1440]{1,0:T(8,128)(2,1)S(1)} %fold_smooth.1.middle), channel_id=1, source_target_pairs={{0,1},{1,2},{2,3},{4,5},{5,6},{6,7},{8,9},{9,10},{10,11},{12,13},{... | collective-permute-start | bytes 552968 | tf_op jit(solution)/shard_map/ppermute | solution.py:503
  37.3 1.6 %second_half.1 = (bf16[32,8,384]{2,1,0:T(8,128)(2,1)S(1)}, f32[2,32,384]{2,1,0:T(8,128)S(1)}) custom-call(f32[8]{0:T(128)S(1)} %copy-done.12, bf16[32,16,512]{2,1,0:T(8,128)(2,1)S(1)} %all-to-all-done.stacked, bf16[512,512]{1,0:T(8,128)(2,1)S(1)} %copy-done.3, bf16[256,256]{1,0:T(8,128)(2,1)S(1)} %get-tuple-element.49.taper, ...), custom_call_target="tpu_custom_call" | custom-call | flops 1000000000 | tf_op jit(solution)/shard_map/second_half/pallas_call | solution.py:150
  38.9 3.3 %all-to-all-done.1.total = bf16[8,32,384]{2,1,0:T(8,128)(2,1)S(1)} async-done(((bf16[8,32,384]{2,1,0:T(8,128)(2,1)}), bf16[8,32,384]{2,1,0:T(8,128)(2,1)S(1)}, u32[]{:S(2)}, u32[]{:S(2)}) %all-to-all-start.1) | async-done | bytes 196640 | tf_op jit(solution)/shard_map/all_to_all | solution.py:519
  42.1 1.5 %combine.1 = (bf16[128,384]{1,0:T(8,128)(2,1)S(1)}, bf16[128,384]{1,0:T(8,128)(2,1)S(1)}, bf16[128,384]{1,0:T(8,128)(2,1)S(1)}, bf16[128,384]{1,0:T(8,128)(2,1)S(1)}, bf16[32,8,384]{2,1,0:T(8,128)(2,1)}) custom-call(s32[2]{0:T(128)S(1)} %pad_add_fusion.here, bf16[8,32,384]{2,1,0:T(8,128)(2,1)S(1)} %all-to-all-done.1.total, ...), custom_call_target="tpu_custom_call" | custom-call | tf_op jit(solution)/shard_map/combine/pallas_call | solution.py:150
  43.7 0.0 collective-permute-done.4.below
  43.7 0.0 copy-start.7
  43.7 0.0 copy-start.8
  43.7 4.4 %all-to-all-start.2 = ((bf16[32,8,384]{2,1,0:T(8,128)(2,1)}), bf16[32,8,384]{2,1,0:T(8,128)(2,1)S(1)}, u32[]{:S(2)}, u32[]{:S(2)}) async-start(bf16[32,8,384]{2,1,0:T(8,128)(2,1)} %get-tuple-element.63), calls=%async_computation.2 | async-start | bytes 393216 | tf_op jit(solution)/shard_map/all_to_all | solution.py:536
  48.1 1.8 %collective-permute-start.5 = (bf16[128,384]{1,0:T(8,128)(2,1)S(1)}, bf16[128,384]{1,0:T(8,128)(2,1)S(1)}, u32[]{:S(2)}, u32[]{:S(2)}) collective-permute-start(bf16[128,384]{1,0:T(8,128)(2,1)S(1)} %get-tuple-element.70), channel_id=1, source_target_pairs={{0,1},{1,2},{2,3},{3,0},{4,5},{5,6},{6,7},{7,4},{8,9},{9,10},{10,1... | collective-permute-start | bytes 294920 | tf_op jit(solution)/shard_map/ppermute | solution.py:443
  49.9 1.5 %collective-permute-start.6 = (bf16[128,384]{1,0:T(8,128)(2,1)S(1)}, bf16[128,384]{1,0:T(8,128)(2,1)S(1)}, u32[]{:S(2)}, u32[]{:S(2)}) collective-permute-start(bf16[128,384]{1,0:T(8,128)(2,1)S(1)} %get-tuple-element.71), channel_id=1, source_target_pairs={{0,2},{1,3},{2,0},{3,1},{4,6},{5,7},{6,4},{7,5},{8,10},{9,11},{10,... | collective-permute-start | bytes 294920 | tf_op jit(solution)/shard_map/ppermute | solution.py:443
  51.4 1.5 %collective-permute-start.7 = (bf16[128,384]{1,0:T(8,128)(2,1)S(1)}, bf16[128,384]{1,0:T(8,128)(2,1)S(1)}, u32[]{:S(2)}, u32[]{:S(2)}) collective-permute-start(bf16[128,384]{1,0:T(8,128)(2,1)S(1)} %get-tuple-element.72), channel_id=1, source_target_pairs={{0,3},{1,0},{2,1},{3,2},{4,7},{5,4},{6,5},{7,6},{8,11},{9,8},{10,9... | collective-permute-start | bytes 294920 | tf_op jit(solution)/shard_map/ppermute | solution.py:443
  52.8 0.0 copy-done.7
  52.8 0.0 copy-done.8
  52.8 0.8 %first_gradient.1.grad_first = f32[64,1440]{1,0:T(8,128)S(1)} custom-call(s32[16]{0:T(128)S(1)} %copy-done.13, bf16[64,1440]{1,0:T(8,128)(2,1)S(1)} %collective-permute-done.4.below, bf16[64,1440]{1,0:T(8,128)(2,1)S(1)} %fold_smooth.1.middle, bf16[64,1440]{1,0:T(8,128)(2,1)S(1)} %collective-permute-done.above, f32[64,192]{1,0:T(8,128)S(1)} %copy-done.7, ...), custom_call_target="tpu_custom_call" | custom-call | tf_op jit(solution)/shard_map/first_gradient/pallas_call | solution.py:150
  53.7 2.4 %collective-permute-done.5.refs_1_ = bf16[128,384]{1,0:T(8,128)(2,1)S(1)} collective-permute-done((bf16[128,384]{1,0:T(8,128)(2,1)S(1)}, bf16[128,384]{1,0:T(8,128)(2,1)S(1)}, u32[]{:S(2)}, u32[]{:S(2)}) %collective-permute-start.5) | collective-permute-done | bytes 98336 | tf_op jit(solution)/shard_map/ppermute | solution.py:443
  56.1 1.8 %collective-permute-done.6.refs_2_ = bf16[128,384]{1,0:T(8,128)(2,1)S(1)} collective-permute-done((bf16[128,384]{1,0:T(8,128)(2,1)S(1)}, bf16[128,384]{1,0:T(8,128)(2,1)S(1)}, u32[]{:S(2)}, u32[]{:S(2)}) %collective-permute-start.6) | collective-permute-done | bytes 98336 | tf_op jit(solution)/shard_map/ppermute | solution.py:443
  58.0 0.0 collective-permute-done.7.refs_3_
  58.0 0.9 %join.1 = (f32[64,1440]{1,0:T(8,128)S(1)}, f32[32,1440]{1,0:T(8,128)S(1)}) custom-call(s32[2]{0:T(128)S(1)} %pad_add_fusion.here, f32[4,8,384]{2,1,0:T(8,128)S(1)} %get-tuple-element.67.own_static, f32[64,64]{1,0:T(8,128)S(1)} %get-tuple-element.68.pulling, bf16[128,384]{1,0:T(8,128)(2,1)S(1)} %get-tuple-element.69.refs_0_, ...), custom_call_target="tpu_custom_call" | custom-call | tf_op jit(solution)/shard_map/join/pallas_call | solution.py:150
  58.9 0.0 all-to-all-done.2.back
  58.9 1.2 %finish.1 = (f32[1,16,4,1440]{3,2,1,0:T(4,128)}, f32[16,4,1440]{2,1,0:T(4,128)}, f32[2,2,4,1440]{3,2,1,0:T(4,128)}) custom-call(bf16[32,8,384]{2,1,0:T(8,128)(2,1)S(1)} %all-to-all-done.2.back, f32[64,1440]{1,0:T(8,128)S(1)} %first_gradient.1.grad_first, f32[64,1440]{1,0:T(8,128)S(1)} %get-tuple-element.66.pulled_first, ...), custom_call_target="tpu_custom_call" | custom-call | tf_op jit(solution)/shard_map/finish/pallas_call | solution.py:150
Async XLA Ops:
  3.3 7.5 %copy-start.1 = (bf16[2,16,4,1440]{3,2,1,0:T(4,128)(2,1)S(1)}, bf16[2,16,4,1440]{3,2,1,0:T(4,128)(2,1)}, u32[]{:S(2)}) copy-start(bf16[2,16,4,1440]{3,2,1,0:T(4,128)(2,1)} %innovation.1) | copy-start | bytes 1105924
  3.3 7.5 %copy-start.2 = (bf16[16,4,1440]{2,1,0:T(4,128)(2,1)S(1)}, bf16[16,4,1440]{2,1,0:T(4,128)(2,1)}, u32[]{:S(2)}) copy-start(bf16[16,4,1440]{2,1,0:T(4,128)(2,1)} %precision.1) | copy-start | bytes 552964
  3.3 7.5 %copy-start.5 = (f32[256,256]{1,0:T(8,128)S(1)}, f32[256,256]{1,0:T(8,128)}, u32[]{:S(2)}) copy-start(f32[256,256]{1,0:T(8,128)} %constant.27.clone.apart) | copy-start | bytes 786436
  3.3 7.5 %copy-start.6 = (f32[256,1]{1,0:T(8,128)S(1)}, f32[256,1]{1,0:T(8,128)}, u32[]{:S(2)}) copy-start(f32[256,1]{1,0:T(8,128)} %constant.28.clone.level) | copy-start | bytes 3076
  3.3 7.5 %copy-start.9 = (f32[64,16]{1,0:T(8,128)S(1)}, f32[64,16]{1,0:T(8,128)}, u32[]{:S(2)}) copy-start(f32[64,16]{1,0:T(8,128)} %constant.25.clone.of_level) | copy-start | bytes 12292
  3.4 7.5 %copy-start.10 = (f32[64,64]{1,0:T(8,128)S(1)}, f32[64,64]{1,0:T(8,128)}, u32[]{:S(2)}) copy-start(f32[64,64]{1,0:T(8,128)} %constant.26.clone.same) | copy-start | bytes 49156
  3.4 23.8 %all-to-all-start = ((bf16[32,16,512]{2,1,0:T(8,128)(2,1)}), bf16[32,16,512]{2,1,0:T(8,128)(2,1)S(1)}, u32[]{:S(2)}, u32[]{:S(2)}) async-start(bf16[32,16,512]{2,1,0:T(8,128)(2,1)} %pack.1), calls=%async_computation | async-start | bytes 1048576 | tf_op jit(solution)/shard_map/all_to_all | solution.py:470
  10.7 0.7 %copy-start.11 = (f32[16,16]{1,0:T(8,128)S(1)}, f32[16,16]{1,0:T(8,128)}, u32[]{:S(2)}) copy-start(f32[16,16]{1,0:T(8,128)} %root) | copy-start | bytes 3076
  10.7 0.7 %copy-start.12 = (f32[8]{0:T(128)S(1)}, f32[8]{0:T(128)}, u32[]{:S(2)}) copy-start(f32[8]{0:T(128)} %weight.7) | copy-start | bytes 100
  10.7 0.7 %copy-start.13 = (s32[16]{0:T(128)S(1)}, s32[16]{0:T(128)}, u32[]{:S(2)}) copy-start(s32[16]{0:T(128)} %widths.3) | copy-start | bytes 196
  11.4 1.9 %copy-start = (bf16[1,2,16,4,1440]{4,3,2,1,0:T(4,128)(2,1)S(1)}, bf16[1,2,16,4,1440]{4,3,2,1,0:T(4,128)(2,1)}, u32[]{:S(2)}) copy-start(bf16[1,2,16,4,1440]{4,3,2,1,0:T(4,128)(2,1)} %ensemble.2) | copy-start | bytes 1105924
  11.4 1.9 %copy-start.4 = (bf16[512,256]{1,0:T(8,128)(2,1)S(1)}, bf16[512,256]{1,0:T(8,128)(2,1)}, u32[]{:S(2)}) copy-start(bf16[512,256]{1,0:T(8,128)(2,1)} %constant.29.clone.kernel) | copy-start | bytes 786436
  13.3 13.9 %copy-start.3 = (bf16[512,512]{1,0:T(8,128)(2,1)S(1)}, bf16[512,512]{1,0:T(8,128)(2,1)}, u32[]{:S(2)}) copy-start(bf16[512,512]{1,0:T(8,128)(2,1)} %constant.30.clone.ring) | copy-start | bytes 1572868
  14.4 11.2 %collective-permute-start = (bf16[64,1440]{1,0:T(8,128)(2,1)S(1)}, bf16[64,1440]{1,0:T(8,128)(2,1)S(1)}, u32[]{:S(2)}, u32[]{:S(2)}) collective-permute-start(bf16[64,1440]{1,0:T(8,128)(2,1)S(1)} %fold_smooth.1.middle), channel_id=1, source_target_pairs={{1,0},{2,1},{3,2},{5,4},{6,5},{7,6},{9,8},{10,9},{11,10},{13,12},{... | collective-permute-start | bytes 552968 | tf_op jit(solution)/shard_map/ppermute | solution.py:504
  15.7 11.6 %collective-permute-start.1 = (bf16[32,512]{1,0:T(8,128)(2,1)S(1)}, bf16[32,512]{1,0:T(8,128)(2,1)S(1)}, u32[]{:S(2)}, u32[]{:S(2)}) collective-permute-start(bf16[32,512]{1,0:T(8,128)(2,1)S(1)} %get-tuple-element.52), channel_id=1, source_target_pairs={{0,1},{1,2},{2,3},{3,0},{4,5},{5,6},{6,7},{7,4},{8,9},{9,10},{10,1... | collective-permute-start | bytes 98312 | tf_op jit(solution)/shard_map/ppermute | solution.py:443
  18.3 8.9 %collective-permute-start.2 = (bf16[32,512]{1,0:T(8,128)(2,1)S(1)}, bf16[32,512]{1,0:T(8,128)(2,1)S(1)}, u32[]{:S(2)}, u32[]{:S(2)}) collective-permute-start(bf16[32,512]{1,0:T(8,128)(2,1)S(1)} %get-tuple-element.53), channel_id=1, source_target_pairs={{0,2},{1,3},{2,0},{3,1},{4,6},{5,7},{6,4},{7,5},{8,10},{9,11},{10,... | collective-permute-start | bytes 98312 | tf_op jit(solution)/shard_map/ppermute | solution.py:443
  20.1 7.1 %collective-permute-start.3 = (bf16[32,512]{1,0:T(8,128)(2,1)S(1)}, bf16[32,512]{1,0:T(8,128)(2,1)S(1)}, u32[]{:S(2)}, u32[]{:S(2)}) collective-permute-start(bf16[32,512]{1,0:T(8,128)(2,1)S(1)} %get-tuple-element.54), channel_id=1, source_target_pairs={{0,3},{1,0},{2,1},{3,2},{4,7},{5,4},{6,5},{7,6},{8,11},{9,8},{10,9... | collective-permute-start | bytes 98312 | tf_op jit(solution)/shard_map/ppermute | solution.py:443
  29.5 12.6 %all-to-all-start.1 = ((bf16[8,32,384]{2,1,0:T(8,128)(2,1)}), bf16[8,32,384]{2,1,0:T(8,128)(2,1)S(1)}, u32[]{:S(2)}, u32[]{:S(2)}) async-start(bf16[8,32,384]{2,1,0:T(8,128)(2,1)} %get-tuple-element.55), calls=%async_computation.1 | async-start | bytes 393216 | tf_op jit(solution)/shard_map/all_to_all | solution.py:519
  33.8 9.9 %collective-permute-start.4 = (bf16[64,1440]{1,0:T(8,128)(2,1)S(1)}, bf16[64,1440]{1,0:T(8,128)(2,1)S(1)}, u32[]{:S(2)}, u32[]{:S(2)}) collective-permute-start(bf16[64,1440]{1,0:T(8,128)(2,1)S(1)} %fold_smooth.1.middle), channel_id=1, source_target_pairs={{0,1},{1,2},{2,3},{4,5},{5,6},{6,7},{8,9},{9,10},{10,11},{12,13},{... | collective-permute-start | bytes 552968 | tf_op jit(solution)/shard_map/ppermute | solution.py:503
  43.7 9.2 %copy-start.7 = (f32[64,192]{1,0:T(8,128)S(1)}, f32[64,192]{1,0:T(8,128)}, u32[]{:S(2)}) copy-start(f32[64,192]{1,0:T(8,128)} %constant.31.clone.apart) | copy-start | bytes 147460
  43.7 9.2 %copy-start.8 = (f32[64,1]{1,0:T(8,128)S(1)}, f32[64,1]{1,0:T(8,128)}, u32[]{:S(2)}) copy-start(f32[64,1]{1,0:T(8,128)} %constant.32.clone.level) | copy-start | bytes 772
  43.7 15.2 %all-to-all-start.2 = ((bf16[32,8,384]{2,1,0:T(8,128)(2,1)}), bf16[32,8,384]{2,1,0:T(8,128)(2,1)S(1)}, u32[]{:S(2)}, u32[]{:S(2)}) async-start(bf16[32,8,384]{2,1,0:T(8,128)(2,1)} %get-tuple-element.63), calls=%async_computation.2 | async-start | bytes 393216 | tf_op jit(solution)/shard_map/all_to_all | solution.py:536
  48.1 8.1 %collective-permute-start.5 = (bf16[128,384]{1,0:T(8,128)(2,1)S(1)}, bf16[128,384]{1,0:T(8,128)(2,1)S(1)}, u32[]{:S(2)}, u32[]{:S(2)}) collective-permute-start(bf16[128,384]{1,0:T(8,128)(2,1)S(1)} %get-tuple-element.70), channel_id=1, source_target_pairs={{0,1},{1,2},{2,3},{3,0},{4,5},{5,6},{6,7},{7,4},{8,9},{9,10},{10,1... | collective-permute-start | bytes 294920 | tf_op jit(solution)/shard_map/ppermute | solution.py:443
  49.9 8.1 %collective-permute-start.6 = (bf16[128,384]{1,0:T(8,128)(2,1)S(1)}, bf16[128,384]{1,0:T(8,128)(2,1)S(1)}, u32[]{:S(2)}, u32[]{:S(2)}) collective-permute-start(bf16[128,384]{1,0:T(8,128)(2,1)S(1)} %get-tuple-element.71), channel_id=1, source_target_pairs={{0,2},{1,3},{2,0},{3,1},{4,6},{5,7},{6,4},{7,5},{8,10},{9,11},{10,... | collective-permute-start | bytes 294920 | tf_op jit(solution)/shard_map/ppermute | solution.py:443
  51.4 6.6 %collective-permute-start.7 = (bf16[128,384]{1,0:T(8,128)(2,1)S(1)}, bf16[128,384]{1,0:T(8,128)(2,1)S(1)}, u32[]{:S(2)}, u32[]{:S(2)}) collective-permute-start(bf16[128,384]{1,0:T(8,128)(2,1)S(1)} %get-tuple-element.72), channel_id=1, source_target_pairs={{0,3},{1,0},{2,1},{3,2},{4,7},{5,4},{6,5},{7,6},{8,11},{9,8},{10,9... | collective-permute-start | bytes 294920 | tf_op jit(solution)/shard_map/ppermute | solution.py:443

commit v7 on v6

--- a/solution.py
+++ b/solution.py
@@ -33,19 +33,10 @@
     return jnp.asarray(np.where(distance <= LREACH, values, 0.0), jnp.bfloat16)
 
 
-def lon_kernel(reach, width):
-    return lon_weights(np.abs(np.arange(width + 2 * reach)[:, None] - reach - np.arange(width)[None]))
-
-
 def ring_kernel(width, padded):
     apart = np.abs(np.arange(padded)[:, None] - np.arange(padded)[None])
     inside = (np.arange(padded)[:, None] < width) & (np.arange(padded)[None] < width)
     return lon_weights(np.where(inside, np.minimum(apart, width - apart), 2 * LREACH))
-
-
-def halves(full):
-    high = full.astype(jnp.bfloat16)
-    return high, (full - high.astype(jnp.float32)).astype(jnp.bfloat16)
 
 
 def near(apart, spans):
@@ -60,15 +51,6 @@
     same = (copy[:, None] == copy[None]) & (level[:, None] == level[None])
     apart = np.where(same, np.abs(latitude[:, None] - latitude[None]), 1000)
     return apart.astype(np.float32), level[:, None].astype(np.float32)
-
-
-def halo_apart(levels, rows):
-    own = levels * rows
-    target, source = np.arange(own)[:, None], np.arange(3 * own)[None]
-    shift = (source // own - 1) * rows + source % rows - target % rows
-    same = source // rows % levels == target // rows
-    level = (target // rows).astype(np.float32)
-    return np.where(same, np.abs(shift), 1000).astype(np.float32), level
 
 
 def row_levels(levels, rows):
@@ -141,7 +123,7 @@
             copies -= 1
         arrays = slots + 2
         everything = levels * rows
-        traded = everything + 4 * slots * own
+        traded = everything + 2 * slots * own
         vmem = pl.BlockSpec(memory_space=pltpu.VMEM)
         smem = pl.BlockSpec(memory_space=pltpu.SMEM)
         limit = min(48, max(14, 24 * members * bands * slots * own * padded // 2**20)) * 2**20
@@ -258,7 +240,7 @@
             factor[...] = ensemble_share / (span * span)
 
         def first_half(here, weight, stacked, ring, taper, factor, *refs):
-            blocks, (total_out, weighted_out, image_out, fields, spans) = refs[:-5], refs[-5:]
+            blocks, (total_out, weighted_out, grad_out, image_out, fields, spans) = refs[:-6], refs[-6:]
             if few:
                 for shift in range(bands):
                     spans[shifted(here[1], -shift)] = blocks[shift][...]
@@ -275,6 +257,7 @@
             scaled = load_members(weight, stacked)
             weighted = [precise * field[t] for t in range(slots)]
             grad = spread(fold(scaled, weighted), ring[...], taper[...], factor[...])
+            grad_out[...] = grad[:, :kept]
             total = jnp.zeros((per_member, padded), f32)
             for t, image in enumerate(images_of(scaled, grad, ring[...], taper[...], factor[...])):
                 image_out[t] = image[:, :kept]
@@ -285,11 +268,15 @@
             for member in range(members):
                 total_out[member] = total
 
-        def store_halves(spans, start, slot, values):
-            for half, part in enumerate(halves(values)):
-                at = start + (half * slots + slot) * own
-                for band in range(bands):
-                    spans[band, at : at + own] = part[band * own : (band + 1) * own]
+        def inner(first, second):
+            inside = lax.broadcasted_iota(jnp.int32, first.shape, 1) < lon_share
+            product = jnp.where(inside, first * second, 0.0)
+            return jnp.sum(jnp.sum(product, axis=0, keepdims=True), axis=1, keepdims=True)
+
+        def closest(first, second):
+            norm = inner(first, first)
+            ratio = inner(first, second) / jnp.where(norm > 0.0, norm, 1.0)
+            return ratio.astype(bf16).astype(f32)
 
         def deal(here, spans, outs):
             for shift in range(bands):
@@ -298,16 +285,24 @@
                 else:
                     outs[0][shift] = spans[shift]
 
-        def second_half(weight, stacked, ring, taper, factor, weighted, grad_out, image_out):
+        def second_half(weight, stacked, ring, taper, factor, weighted, first, pair_out, image_out):
             scaled = load_members(weight, stacked)
             grad = fold(scaled, [weighted[t] for t in range(slots)])
-            grad = spread(grad, ring[...], taper[...], factor[...]).astype(bf16)
-            grad_out[...] = grad[:, :kept].reshape(members * bands, own, kept)
+            grad = spread(grad, ring[...], taper[...], factor[...])
             for t, image in enumerate(images_of(scaled, grad, ring[...], taper[...], factor[...])):
                 image_out[t] = image[:, :kept]
-
-        def combine(here, total, grad, first, second, fields, mixing, *refs):
+            first, second = first[...], grad[:, :kept]
+            ratio = closest(first, second)
+            shape = (members * bands, own, kept)
+            second = (second - ratio * first).reshape(shape)
+            lane = lax.broadcasted_iota(jnp.int32, shape, 2)
+            second = jnp.where(lane < lon_share, second, ratio.reshape(1, 1, 1))
+            pair_out[:, :own] = first.reshape(shape).astype(bf16)
+            pair_out[:, own:] = second.astype(bf16)
+
+        def combine(here, total, pairs, first, second, fields, mixing, *refs):
             outs, (out, spans) = refs[:-2], refs[-2:]
+            lane = lax.broadcasted_iota(jnp.int32, (1, kept), 1) - lon_share
             mixed, precise, static = [], fields[slots], fields[slots + 1]
             for band in range(bands):
                 place = slice(band * own, (band + 1) * own)
@@ -316,64 +311,41 @@
                 mixed.append(parts_dot(mixing[...], every))
                 spans[band, :everything] = every
             mixed = jnp.concatenate(mixed, axis=0)
+            images = [second[t] + mixed for t in range(slots)]
             sums = [jnp.zeros((per_member, kept), f32) for _ in range(SUMS)]
-            for t in range(slots):
-                image = second[t] + mixed
+            for t, image in enumerate(images):
                 whole = first[t] + static
                 weighted = precise * whole
                 sums[0] = sums[0] + precise * fields[t] * whole
                 sums[1] = sums[1] + weighted * whole
                 sums[2] = sums[2] + weighted * image
                 sums[3] = sums[3] + precise * image * image
-                store_halves(spans, everything, t, first[t])
-                store_halves(spans, everything + 2 * slots * own, t, image)
+            ratio = closest(
+                jnp.concatenate([first[t] for t in range(slots)], axis=0), jnp.concatenate(images, axis=0)
+            )
+            for which in range(2):
+                for t, image in enumerate(images):
+                    image = jnp.where(lane < 0, image - ratio * first[t], ratio) if which else first[t]
+                    image = image.astype(bf16)
+                    at = everything + (which * slots + t) * own
+                    for band in range(bands):
+                        spans[band, at : at + own] = image[band * own : (band + 1) * own]
             deal(here, spans, outs)
-            inside = lax.broadcasted_iota(jnp.int32, (per_member, kept), 1) < lon_share
-            lane = lax.broadcasted_iota(jnp.int32, (1, kept), 1) - lon_share
             row = jnp.zeros((1, kept), f32)
             for index, part in enumerate(sums):
-                part = jnp.where(inside, part, 0.0)
+                part = jnp.where(lane < 0, part, 0.0)
                 part = jnp.sum(jnp.sum(part, axis=0, keepdims=True), axis=1, keepdims=True)
                 for piece in range(PARTS):
                     high = part.astype(bf16).astype(f32)
                     row = row + jnp.where(lane == PARTS * index + piece, high, 0.0)
                     part = part - high
-            shape = (own, kept)
+            shape = (2 * own, kept)
             lane = lax.broadcasted_iota(jnp.int32, shape, 1)
+            sender = lax.broadcasted_iota(jnp.int32, shape, 0) < own
             row = jnp.broadcast_to(row, shape)
             for block in range(members * bands):
-                out[block] = jnp.where(lane < lon_share, grad[block].astype(f32), row).astype(bf16)
-
-        def fold_smooth(marks, weight, ensemble, innovation, precision, kernel, out):
-            total = []
-            for at in range(levels):
-                precise = precision[at].astype(f32)
-                part = jnp.zeros((rows, lon), f32)
-                for t in range(slots):
-                    weighted = precise * innovation[t, at].astype(f32)
-                    part = part + ensemble[0, t, at].astype(f32) * weighted
-                total.append(part)
-            total = weight[marks[0]] * jnp.concatenate(total, axis=0)
-            step = kernel.shape[1]
-            margin = (kernel.shape[0] - step) // 2
-            steps = -(-lon // step)
-            after = steps * step + margin - lon
-            ring = jnp.concatenate([total[:, lon - margin :], total, total[:, :after]], axis=1)
-            ring = ring.astype(bf16)
-            for start in range(0, lon, step):
-                stop = min(lon, start + step)
-                piece = jnp.dot(
-                    ring[:, start : start + kernel.shape[0]], kernel[...], preferred_element_type=f32
-                )
-                out[:, start:stop] = piece[:, : stop - start].astype(bf16)
-
-        def first_gradient(widths, below, middle, above, apart, level, grad):
-            span = jnp.ones(level.shape, f32)
-            for at in range(levels):
-                span = span + jnp.where(level[...] == at, widths[at].astype(f32), 0.0)
-            stacked = jnp.concatenate([below[...], middle[...], above[...]], axis=0)
-            summed = jnp.dot(near(apart[...], span), stacked, preferred_element_type=f32)
-            grad[...] = ensemble_share / (span * span) * summed
+                values = pairs[block].astype(f32)
+                out[block] = jnp.where((lane >= lon_share) & sender, row, values).astype(bf16)
 
         def join(here, own_static, pulling, *refs):
             blocks, (pulled, images, spans) = refs[:-3], refs[-3:]
@@ -387,16 +359,16 @@
                 place = slice(band * lon_share, (band + 1) * lon_share)
                 pulled[:, place] = parts_dot(pulling[...], spans[band, :everything])[:, :lon_share]
                 parts = spans[band, everything:].astype(f32)
-                first = parts[:size] + parts[size : 2 * size]
-                second = parts[2 * size : 3 * size] + parts[3 * size :]
+                first = parts[:size]
+                second = parts[size:] + parts[size : size + 1, lon_share : lon_share + 1] * first
                 static = own_static[band]
                 for t in range(slots):
                     at = slice(t * own, (t + 1) * own)
                     images[at, place] = (first[at] + static)[:, :lon_share]
                 images[size:, place] = second[:, :lon_share]
 
-        def finish(back, grad_first, pulled_first, pulled_second, images, *refs):
-            member_out, static_out, image_out, second = refs
+        def finish(back, pulled_first, pulled_second, images, *refs):
+            member_out, static_out, image_out, member = refs
             total = back[0, :1].astype(f32)
             for block in range(1, members * bands):
                 total = total + back[block, :1].astype(f32)
@@ -419,11 +391,14 @@
             on_first = alpha + alpha_next * (1.0 - alpha + beta)
             on_second = -alpha * alpha_next
             for band in range(bands):
-                grad = jnp.concatenate(
-                    [back[member * bands + band].astype(f32) for member in range(members)], axis=0
-                )
-                second[:, band * lon_share : (band + 1) * lon_share] = grad[:, :lon_share]
-            member = on_first * grad_first[...] + on_second * second[...]
+                parts = []
+                for source in range(members):
+                    first = back[source * bands + band, :own].astype(f32)
+                    second = back[source * bands + band, own:].astype(f32)
+                    ratio = second[:1, lon_share : lon_share + 1]
+                    parts.append((on_first + on_second * ratio) * first + on_second * second)
+                piece = jnp.concatenate(parts, axis=0)
+                member[:, band * lon_share : (band + 1) * lon_share] = piece[:, :lon_share]
             static = on_first * pulled_first[...] + on_second * pulled_second[...]
             for level in range(levels):
                 place = slice(level * rows, (level + 1) * rows)
@@ -464,8 +439,8 @@
             compiler_params=pltpu.CompilerParams(vmem_limit_bytes=60 * 2**20),
             name="pack",
         )(member_of_slot, ensemble)
-        pieces, ensemble, innovation, precision, static_root = lax.optimization_barrier(
-            (pieces, ensemble, innovation, precision, static_root)
+        pieces, innovation, precision, static_root = lax.optimization_barrier(
+            (pieces, innovation, precision, static_root)
         )
         stacked = lax.all_to_all(pieces, BOTH, 0, 0, tiled=True)
 
@@ -490,25 +465,14 @@
         )
         blocks = trade(results[:-6])
         own_static, pulled, mixing, pulling, taper, factor = results[-6:]
-        own_static, ensemble, innovation, precision = lax.optimization_barrier(
-            (own_static, ensemble, innovation, precision)
-        )
-        (smoothed,) = call(
-            fold_smooth,
-            [((everything, lon), bf16)],
-            [member_of_slot, member_weight],
-            [ensemble, innovation, precision, lon_kernel(LANES, 2 * LANES)],
-        )
-        up = [(at, at + 1) for at in range(bands - 1)]
-        below = lax.ppermute(smoothed, "band", up)
-        above = lax.ppermute(smoothed, "band", [(target, source) for source, target in up])
-
-        ring, above = lax.optimization_barrier((ring_kernel(width, padded), above))
-        total, weighted, image_first, fields = call(
+        ring = ring_kernel(width, padded)
+
+        total, weighted, grad_first, image_first, fields = call(
             first_half,
             [
                 ((members, per_member, kept), bf16),
                 ((slots, per_member, padded), f32),
+                ((members * per_member, kept), f32),
                 ((slots, per_member, kept), f32),
                 ((arrays, per_member, kept), f32),
             ],
@@ -517,23 +481,22 @@
             scratch=[((bands,) + block, bf16)],
         )
         total = lax.all_to_all(total, "member", 0, 0, tiled=True)
-        grad, image_second = call(
+        pairs, image_second = call(
             second_half,
-            [((members * bands, own, kept), bf16), ((slots, per_member, kept), f32)],
+            [((members * bands, 2 * own, kept), bf16), ((slots, per_member, kept), f32)],
             [member_weight],
-            [stacked, ring, taper, factor, weighted],
+            [stacked, ring, taper, factor, weighted, grad_first],
             flops=10**9,
         )
 
         results = call(
             combine,
-            tradable((traded, kept), bf16) + [((members * bands, own, kept), bf16)],
+            tradable((traded, kept), bf16) + [((members * bands, 2 * own, kept), bf16)],
             [here],
-            [total, grad, image_first, image_second, fields, mixing],
+            [total, pairs, image_first, image_second, fields, mixing],
             scratch=[((bands, traded, kept), bf16)],
         )
-        gradients, below = lax.optimization_barrier((results[-1], below))
-        back = lax.all_to_all(gradients, BOTH, 0, 0, tiled=True)
+        back = lax.all_to_all(results[-1], BOTH, 0, 0, tiled=True)
         blocks = trade(results[:-1])
         pulled_second, images = call(
             join,
@@ -541,13 +504,6 @@
             [here],
             [own_static, pulling, *blocks],
             scratch=[((bands, traded, kept), bf16)],
-        )
-        apart, level = halo_apart(levels, rows)
-        (grad_first,) = call(
-            first_gradient,
-            [((everything, lon), f32)],
-            [halfwidth],
-            [below, smoothed, above, jnp.asarray(apart), jnp.asarray(level)],
         )
         return call(
             finish,
@@ -557,7 +513,7 @@
                 ((slots, level_share, rows, lon), f32),
             ],
             [],
-            [back, grad_first, pulled, pulled_second, images],
+            [back, pulled, pulled_second, images],
             scratch=[((everything, lon), f32)],
         )
 

time: 60.6 us -> 60.4 us (level)
  waiting for transfers between devices: 12.3 us -> 23.6 us
  starting transfers between devices: 32.3 us -> 22.7 us
  Pallas kernels: 13.3 us -> 11.6 us
    all_to_all x1, waiting for transfers between devices: 0.01 us -> 6.34 us  [shards(): stacked = lax.all_to_all(pieces, BOTH, 0, 0, tiled=True)]
    ppermute x2 -> x0, starting transfers between devices: 4.73 us -> none  [the longest x1 3.44 us: shards(): below = lax.ppermute(smoothed, 'band', up)]
    all_to_all x1, waiting for transfers between devices: 3.29 us -> 6.65 us  [shards(): total = lax.all_to_all(total, 'member', 0, 0, tiled=True)]
    ppermute x2 -> x0, waiting for transfers between devices: 3.03 us -> none  [the longest x1 3.03 us: shards(): lax.ppermute(smoothed, 'band', [(target, source) for source, target in up])]
    all_to_all x1, waiting for transfers between devices: 0.01 us -> 2.81 us  [shards(): back = lax.all_to_all(results[-1], BOTH, 0, 0, tiled=True)]
    ppermute x6, starting transfers between devices: 11.6 us -> 9.38 us  [trade(): lax.ppermute(blocks[shift], 'band', [(at, (at + shift) % bands) for at in...]
    all_to_all x1, starting transfers between devices: 4.4 us -> 2.6 us  [shards(): back = lax.all_to_all(results[-1], BOTH, 0, 0, tiled=True)]
    ppermute x6, waiting for transfers between devices: 5.99 us -> 7.79 us  [trade(): lax.ppermute(blocks[shift], 'band', [(at, (at + shift) % bands) for at in...]
  transfers between devices with their start and end apart: 11 -> 9, of which waited for: 5 -> 8; matrix products, arithmetic and copies ran while one was open for 0% -> 0% of each run, Pallas kernels for 13% -> 7%
where the time goes in v7:
time: 60.4 us; the launch traced here: 60 us
  waiting for transfers between devices  23.6 us (39%)
  starting transfers between devices  22.7 us (38%)
  Pallas kernels  11.6 us (19%)
  between operations  1.44 us (2%)
  local copies, waits for them, and re-layouts  0.61 us (1%)
    pallas_call x6, Pallas kernels, call(): pl.pallas_call(body, out_shape=tuple((jax.ShapeDtypeStruct(shape, kind) f...  9.63 us
    ppermute x6, starting transfers between devices, trade(): lax.ppermute(blocks[shift], 'band', [(at, (at + shift) % bands) for at in...  9.38 us
    ppermute x6, waiting for transfers between devices, trade(): lax.ppermute(blocks[shift], 'band', [(at, (at + shift) % bands) for at in...  7.79 us
    all_to_all x1, starting transfers between devices, shards(): stacked = lax.all_to_all(pieces, BOTH, 0, 0, tiled=True)  7.3 us
    all_to_all x1, waiting for transfers between devices, shards(): total = lax.all_to_all(total, 'member', 0, 0, tiled=True)  6.65 us
    all_to_all x1, waiting for transfers between devices, shards(): stacked = lax.all_to_all(pieces, BOTH, 0, 0, tiled=True)  6.34 us
    all_to_all x1, starting transfers between devices, shards(): total = lax.all_to_all(total, 'member', 0, 0, tiled=True)  3.39 us
    all_to_all x1, waiting for transfers between devices, shards(): back = lax.all_to_all(results[-1], BOTH, 0, 0, tiled=True)  2.81 us
  transfers between devices with their start and end apart: 9, of which 8 were waited for; matrix products, arithmetic and copies ran while one was open for 0% of the time, Pallas kernels for 7%

profile of v7, /device:TPU:0, one launch (start us, length us, event | category | flops | bytes accessed | tf_op | source)
XLA Modules:
  0.0 60.0 jit_solution(9281138206332092711)
XLA Ops:
  1.3 2.0 %pack.1 = bf16[32,16,512]{2,1,0:T(8,128)(2,1)} custom-call(s32[1]{0:T(128)S(6)} %copy.15.marks, bf16[1,2,16,4,1440]{4,3,2,1,0:T(4,128)(2,1)} %ensemble.1), custom_call_target="tpu_custom_call" | custom-call | tf_op jit(solution)/shard_map/pack/pallas_call | solution.py:428
  3.3 0.0 copy-start.1
  3.3 0.0 copy-start.2
  3.3 0.0 copy-start.3
  3.3 0.0 copy-start.4
  3.3 0.0 copy-start.5
  3.3 0.0 copy-start.6
  3.4 7.3 %all-to-all-start = ((bf16[32,16,512]{2,1,0:T(8,128)(2,1)}), bf16[32,16,512]{2,1,0:T(8,128)(2,1)S(1)}, u32[]{:S(2)}, u32[]{:S(2)}) async-start(bf16[32,16,512]{2,1,0:T(8,128)(2,1)} %pack.1), calls=%async_computation | async-start | bytes 1048576 | tf_op jit(solution)/shard_map/all_to_all | solution.py:445
  10.7 0.0 copy-start.7
  10.7 0.0 copy-start.8
  10.7 0.0 copy-start.9
  10.7 0.1 pad_add_fusion.here
  10.8 0.0 copy-done.1
  10.8 0.0 copy-done.2
  10.8 0.0 copy-done.3
  10.8 0.0 copy-done.4
  10.8 0.0 copy-done.5
  10.8 0.0 copy-done.6
  10.8 0.6 copy-done.7
  11.4 0.0 copy-done.8
  11.4 0.0 copy-done.9
  11.4 0.0 copy-start
  11.4 1.9 %observe.1 = (bf16[32,512]{1,0:T(8,128)(2,1)S(1)}, bf16[32,512]{1,0:T(8,128)(2,1)S(1)}, bf16[32,512]{1,0:T(8,128)(2,1)S(1)}, bf16[32,512]{1,0:T(8,128)(2,1)S(1)}...) custom-call(s32[2]{0:T(128)S(1)} %pad_add_fusion.here, ...), custom_call_target="tpu_custom_call" | custom-call | tf_op jit(solution)/shard_map/observe/pallas_call | solution.py:132
  13.3 1.8 %collective-permute-start = (bf16[32,512]{1,0:T(8,128)(2,1)S(1)}, bf16[32,512]{1,0:T(8,128)(2,1)S(1)}, u32[]{:S(2)}, u32[]{:S(2)}) collective-permute-start(bf16[32,512]{1,0:T(8,128)(2,1)S(1)} %get-tuple-element.38), channel_id=1, source_target_pairs={{0,1},{1,2},{2,3},{3,0},{4,5},{5,6},{6,7},{7,4},{8,9},{9,10},{10,1... | collective-permute-start | bytes 98312 | tf_op jit(solution)/shard_map/ppermute | solution.py:418
  15.1 1.5 %collective-permute-start.1 = (bf16[32,512]{1,0:T(8,128)(2,1)S(1)}, bf16[32,512]{1,0:T(8,128)(2,1)S(1)}, u32[]{:S(2)}, u32[]{:S(2)}) collective-permute-start(bf16[32,512]{1,0:T(8,128)(2,1)S(1)} %get-tuple-element.39), channel_id=1, source_target_pairs={{0,2},{1,3},{2,0},{3,1},{4,6},{5,7},{6,4},{7,5},{8,10},{9,11},{10,... | collective-permute-start | bytes 98312 | tf_op jit(solution)/shard_map/ppermute | solution.py:418
  16.6 1.5 %collective-permute-start.2 = (bf16[32,512]{1,0:T(8,128)(2,1)S(1)}, bf16[32,512]{1,0:T(8,128)(2,1)S(1)}, u32[]{:S(2)}, u32[]{:S(2)}) collective-permute-start(bf16[32,512]{1,0:T(8,128)(2,1)S(1)} %get-tuple-element.40), channel_id=1, source_target_pairs={{0,3},{1,0},{2,1},{3,2},{4,7},{5,4},{6,5},{7,6},{8,11},{9,8},{10,9... | collective-permute-start | bytes 98312 | tf_op jit(solution)/shard_map/ppermute | solution.py:418
  18.0 0.9 %collective-permute-done.refs_1_ = bf16[32,512]{1,0:T(8,128)(2,1)S(1)} collective-permute-done((bf16[32,512]{1,0:T(8,128)(2,1)S(1)}, bf16[32,512]{1,0:T(8,128)(2,1)S(1)}, u32[]{:S(2)}, u32[]{:S(2)}) %collective-permute-start) | collective-permute-done | bytes 32800 | tf_op jit(solution)/shard_map/ppermute | solution.py:418
  18.9 1.3 %collective-permute-done.1.refs_2_ = bf16[32,512]{1,0:T(8,128)(2,1)S(1)} collective-permute-done((bf16[32,512]{1,0:T(8,128)(2,1)S(1)}, bf16[32,512]{1,0:T(8,128)(2,1)S(1)}, u32[]{:S(2)}, u32[]{:S(2)}) %collective-permute-start.1) | collective-permute-done | bytes 32800 | tf_op jit(solution)/shard_map/ppermute | solution.py:418
  20.3 0.3 collective-permute-done.2.refs_3_
  20.6 6.3 %all-to-all-done.stacked = bf16[32,16,512]{2,1,0:T(8,128)(2,1)S(1)} async-done(((bf16[32,16,512]{2,1,0:T(8,128)(2,1)}), bf16[32,16,512]{2,1,0:T(8,128)(2,1)S(1)}, u32[]{:S(2)}, u32[]{:S(2)}) %all-to-all-start) | async-done | bytes 524320 | tf_op jit(solution)/shard_map/all_to_all | solution.py:445
  26.9 0.0 copy-done
  26.9 2.3 %first_half.1 = (bf16[8,32,384]{2,1,0:T(8,128)(2,1)}, f32[2,32,512]{2,1,0:T(8,128)S(1)}, f32[256,384]{1,0:T(8,128)S(1)}, f32[2,32,384]{2,1,0:T(8,128)S(1)}, f32[4,32,384]{2,1,0:T(8,128)S(1)}) custom-call(s32[2]{0:T(128)S(1)} %pad_add_fusion.here, f32[8]{0:T(128)S(1)} %copy-done.8, bf16[32,16,512]{2,1,0:T(8,128)(2,1)S(1)} %all-to-all-done.stacked, ...), custom_call_target="tpu_custom_call" | custom-call | tf_op jit(solution)/shard_map/first_half/pallas_call | solution.py:132
  29.2 3.4 %all-to-all-start.1 = ((bf16[8,32,384]{2,1,0:T(8,128)(2,1)}), bf16[8,32,384]{2,1,0:T(8,128)(2,1)S(1)}, u32[]{:S(2)}, u32[]{:S(2)}) async-start(bf16[8,32,384]{2,1,0:T(8,128)(2,1)} %get-tuple-element.41), calls=%async_computation.1 | async-start | bytes 393216 | tf_op jit(solution)/shard_map/all_to_all | solution.py:483
  32.6 1.6 %second_half.1 = (bf16[32,16,384]{2,1,0:T(8,128)(2,1)S(1)}, f32[2,32,384]{2,1,0:T(8,128)S(1)}) custom-call(f32[8]{0:T(128)S(1)} %copy-done.8, bf16[32,16,512]{2,1,0:T(8,128)(2,1)S(1)} %all-to-all-done.stacked, bf16[512,512]{1,0:T(8,128)(2,1)S(1)} %copy-done, bf16[256,256]{1,0:T(8,128)(2,1)S(1)} %get-tuple-element.35.taper, ...), custom_call_target="tpu_custom_call" | custom-call | flops 1000000000 | tf_op jit(solution)/shard_map/second_half/pallas_call | solution.py:132
  34.2 6.7 %all-to-all-done.1.total = bf16[8,32,384]{2,1,0:T(8,128)(2,1)S(1)} async-done(((bf16[8,32,384]{2,1,0:T(8,128)(2,1)}), bf16[8,32,384]{2,1,0:T(8,128)(2,1)S(1)}, u32[]{:S(2)}, u32[]{:S(2)}) %all-to-all-start.1) | async-done | bytes 196640 | tf_op jit(solution)/shard_map/all_to_all | solution.py:483
  40.9 1.6 %combine.1 = (bf16[96,384]{1,0:T(8,128)(2,1)S(1)}, bf16[96,384]{1,0:T(8,128)(2,1)S(1)}, bf16[96,384]{1,0:T(8,128)(2,1)S(1)}, bf16[96,384]{1,0:T(8,128)(2,1)S(1)}, bf16[32,16,384]{2,1,0:T(8,128)(2,1)}) custom-call(s32[2]{0:T(128)S(1)} %pad_add_fusion.here, bf16[8,32,384]{2,1,0:T(8,128)(2,1)S(1)} %all-to-all-done.1.total, ...), custom_call_target="tpu_custom_call" | custom-call | tf_op jit(solution)/shard_map/combine/pallas_call | solution.py:132
  42.5 2.6 %all-to-all-start.2 = ((bf16[32,16,384]{2,1,0:T(8,128)(2,1)}), bf16[32,16,384]{2,1,0:T(8,128)(2,1)S(1)}, u32[]{:S(2)}, u32[]{:S(2)}) async-start(bf16[32,16,384]{2,1,0:T(8,128)(2,1)} %get-tuple-element.49), calls=%async_computation.2 | async-start | bytes 786432 | tf_op jit(solution)/shard_map/all_to_all | solution.py:499
  45.1 1.7 %collective-permute-start.3 = (bf16[96,384]{1,0:T(8,128)(2,1)S(1)}, bf16[96,384]{1,0:T(8,128)(2,1)S(1)}, u32[]{:S(2)}, u32[]{:S(2)}) collective-permute-start(bf16[96,384]{1,0:T(8,128)(2,1)S(1)} %get-tuple-element.54), channel_id=1, source_target_pairs={{0,1},{1,2},{2,3},{3,0},{4,5},{5,6},{6,7},{7,4},{8,9},{9,10},{10,1... | collective-permute-start | bytes 221192 | tf_op jit(solution)/shard_map/ppermute | solution.py:418
  46.8 1.5 %collective-permute-start.4 = (bf16[96,384]{1,0:T(8,128)(2,1)S(1)}, bf16[96,384]{1,0:T(8,128)(2,1)S(1)}, u32[]{:S(2)}, u32[]{:S(2)}) collective-permute-start(bf16[96,384]{1,0:T(8,128)(2,1)S(1)} %get-tuple-element.55), channel_id=1, source_target_pairs={{0,2},{1,3},{2,0},{3,1},{4,6},{5,7},{6,4},{7,5},{8,10},{9,11},{10,... | collective-permute-start | bytes 221192 | tf_op jit(solution)/shard_map/ppermute | solution.py:418
  48.3 1.4 %collective-permute-start.5 = (bf16[96,384]{1,0:T(8,128)(2,1)S(1)}, bf16[96,384]{1,0:T(8,128)(2,1)S(1)}, u32[]{:S(2)}, u32[]{:S(2)}) collective-permute-start(bf16[96,384]{1,0:T(8,128)(2,1)S(1)} %get-tuple-element.56), channel_id=1, source_target_pairs={{0,3},{1,0},{2,1},{3,2},{4,7},{5,4},{6,5},{7,6},{8,11},{9,8},{10,9... | collective-permute-start | bytes 221192 | tf_op jit(solution)/shard_map/ppermute | solution.py:418
  49.7 3.8 %collective-permute-done.3.refs_1_ = bf16[96,384]{1,0:T(8,128)(2,1)S(1)} collective-permute-done((bf16[96,384]{1,0:T(8,128)(2,1)S(1)}, bf16[96,384]{1,0:T(8,128)(2,1)S(1)}, u32[]{:S(2)}, u32[]{:S(2)}) %collective-permute-start.3) | collective-permute-done | bytes 73760 | tf_op jit(solution)/shard_map/ppermute | solution.py:418
  53.6 1.4 %collective-permute-done.4.refs_2_ = bf16[96,384]{1,0:T(8,128)(2,1)S(1)} collective-permute-done((bf16[96,384]{1,0:T(8,128)(2,1)S(1)}, bf16[96,384]{1,0:T(8,128)(2,1)S(1)}, u32[]{:S(2)}, u32[]{:S(2)}) %collective-permute-start.4) | collective-permute-done | bytes 73760 | tf_op jit(solution)/shard_map/ppermute | solution.py:418
  54.9 0.0 collective-permute-done.5.refs_3_
  54.9 1.0 %join.1 = (f32[64,1440]{1,0:T(8,128)S(1)}, f32[32,1440]{1,0:T(8,128)S(1)}) custom-call(s32[2]{0:T(128)S(1)} %pad_add_fusion.here, f32[4,8,384]{2,1,0:T(8,128)S(1)} %get-tuple-element.51.own_static, f32[64,64]{1,0:T(8,128)S(1)} %get-tuple-element.52.pulling, bf16[96,384]{1,0:T(8,128)(2,1)S(1)} %get-tuple-element.53.refs_0_, ...), custom_call_target="tpu_custom_call" | custom-call | tf_op jit(solution)/shard_map/join/pallas_call | solution.py:132
  55.9 2.8 %all-to-all-done.2.back = bf16[32,16,384]{2,1,0:T(8,128)(2,1)S(1)} async-done(((bf16[32,16,384]{2,1,0:T(8,128)(2,1)}), bf16[32,16,384]{2,1,0:T(8,128)(2,1)S(1)}, u32[]{:S(2)}, u32[]{:S(2)}) %all-to-all-start.2) | async-done | bytes 393248 | tf_op jit(solution)/shard_map/all_to_all | solution.py:499
  58.7 1.3 %finish.1 = (f32[1,16,4,1440]{3,2,1,0:T(4,128)}, f32[16,4,1440]{2,1,0:T(4,128)}, f32[2,2,4,1440]{3,2,1,0:T(4,128)}) custom-call(bf16[32,16,384]{2,1,0:T(8,128)(2,1)S(1)} %all-to-all-done.2.back, f32[64,1440]{1,0:T(8,128)S(1)} %get-tuple-element.50.pulled_first, f32[64,1440]{1,0:T(8,128)S(1)} %get-tuple-element.57.pulled_second, ...), custom_call_target="tpu_custom_call" | custom-call | tf_op jit(solution)/shard_map/finish/pallas_call | solution.py:132
Async XLA Ops:
  3.3 7.5 %copy-start.1 = (bf16[2,16,4,1440]{3,2,1,0:T(4,128)(2,1)S(1)}, bf16[2,16,4,1440]{3,2,1,0:T(4,128)(2,1)}, u32[]{:S(2)}) copy-start(bf16[2,16,4,1440]{3,2,1,0:T(4,128)(2,1)} %innovation) | copy-start | bytes 1105924
  3.3 7.5 %copy-start.2 = (f32[256,256]{1,0:T(8,128)S(1)}, f32[256,256]{1,0:T(8,128)}, u32[]{:S(2)}) copy-start(f32[256,256]{1,0:T(8,128)} %constant.21.clone.apart) | copy-start | bytes 786436
  3.3 7.5 %copy-start.3 = (bf16[16,4,1440]{2,1,0:T(4,128)(2,1)S(1)}, bf16[16,4,1440]{2,1,0:T(4,128)(2,1)}, u32[]{:S(2)}) copy-start(bf16[16,4,1440]{2,1,0:T(4,128)(2,1)} %precision) | copy-start | bytes 552964
  3.3 7.5 %copy-start.4 = (f32[256,1]{1,0:T(8,128)S(1)}, f32[256,1]{1,0:T(8,128)}, u32[]{:S(2)}) copy-start(f32[256,1]{1,0:T(8,128)} %constant.22.clone.level) | copy-start | bytes 3076
  3.3 7.5 %copy-start.5 = (f32[64,64]{1,0:T(8,128)S(1)}, f32[64,64]{1,0:T(8,128)}, u32[]{:S(2)}) copy-start(f32[64,64]{1,0:T(8,128)} %constant.20.clone.same) | copy-start | bytes 49156
  3.3 7.5 %copy-start.6 = (f32[64,16]{1,0:T(8,128)S(1)}, f32[64,16]{1,0:T(8,128)}, u32[]{:S(2)}) copy-start(f32[64,16]{1,0:T(8,128)} %constant.19.clone.of_level) | copy-start | bytes 12292
  3.4 23.6 %all-to-all-start = ((bf16[32,16,512]{2,1,0:T(8,128)(2,1)}), bf16[32,16,512]{2,1,0:T(8,128)(2,1)S(1)}, u32[]{:S(2)}, u32[]{:S(2)}) async-start(bf16[32,16,512]{2,1,0:T(8,128)(2,1)} %pack.1), calls=%async_computation | async-start | bytes 1048576 | tf_op jit(solution)/shard_map/all_to_all | solution.py:445
  10.7 0.7 %copy-start.7 = (f32[16,16]{1,0:T(8,128)S(1)}, f32[16,16]{1,0:T(8,128)}, u32[]{:S(2)}) copy-start(f32[16,16]{1,0:T(8,128)} %root) | copy-start | bytes 3076
  10.7 0.7 %copy-start.8 = (f32[8]{0:T(128)S(1)}, f32[8]{0:T(128)}, u32[]{:S(2)}) copy-start(f32[8]{0:T(128)} %weight.5) | copy-start | bytes 100
  10.7 0.7 %copy-start.9 = (s32[16]{0:T(128)S(1)}, s32[16]{0:T(128)}, u32[]{:S(2)}) copy-start(s32[16]{0:T(128)} %widths.1) | copy-start | bytes 196
  11.4 15.5 %copy-start = (bf16[512,512]{1,0:T(8,128)(2,1)S(1)}, bf16[512,512]{1,0:T(8,128)(2,1)}, u32[]{:S(2)}) copy-start(bf16[512,512]{1,0:T(8,128)(2,1)} %constant.23.clone.ring) | copy-start | bytes 1572868
  13.3 5.7 %collective-permute-start = (bf16[32,512]{1,0:T(8,128)(2,1)S(1)}, bf16[32,512]{1,0:T(8,128)(2,1)S(1)}, u32[]{:S(2)}, u32[]{:S(2)}) collective-permute-start(bf16[32,512]{1,0:T(8,128)(2,1)S(1)} %get-tuple-element.38), channel_id=1, source_target_pairs={{0,1},{1,2},{2,3},{3,0},{4,5},{5,6},{6,7},{7,4},{8,9},{9,10},{10,1... | collective-permute-start | bytes 98312 | tf_op jit(solution)/shard_map/ppermute | solution.py:418
  15.1 5.2 %collective-permute-start.1 = (bf16[32,512]{1,0:T(8,128)(2,1)S(1)}, bf16[32,512]{1,0:T(8,128)(2,1)S(1)}, u32[]{:S(2)}, u32[]{:S(2)}) collective-permute-start(bf16[32,512]{1,0:T(8,128)(2,1)S(1)} %get-tuple-element.39), channel_id=1, source_target_pairs={{0,2},{1,3},{2,0},{3,1},{4,6},{5,7},{6,4},{7,5},{8,10},{9,11},{10,... | collective-permute-start | bytes 98312 | tf_op jit(solution)/shard_map/ppermute | solution.py:418
  16.6 4.0 %collective-permute-start.2 = (bf16[32,512]{1,0:T(8,128)(2,1)S(1)}, bf16[32,512]{1,0:T(8,128)(2,1)S(1)}, u32[]{:S(2)}, u32[]{:S(2)}) collective-permute-start(bf16[32,512]{1,0:T(8,128)(2,1)S(1)} %get-tuple-element.40), channel_id=1, source_target_pairs={{0,3},{1,0},{2,1},{3,2},{4,7},{5,4},{6,5},{7,6},{8,11},{9,8},{10,9... | collective-permute-start | bytes 98312 | tf_op jit(solution)/shard_map/ppermute | solution.py:418
  29.2 11.7 %all-to-all-start.1 = ((bf16[8,32,384]{2,1,0:T(8,128)(2,1)}), bf16[8,32,384]{2,1,0:T(8,128)(2,1)S(1)}, u32[]{:S(2)}, u32[]{:S(2)}) async-start(bf16[8,32,384]{2,1,0:T(8,128)(2,1)} %get-tuple-element.41), calls=%async_computation.1 | async-start | bytes 393216 | tf_op jit(solution)/shard_map/all_to_all | solution.py:483
  42.5 16.2 %all-to-all-start.2 = ((bf16[32,16,384]{2,1,0:T(8,128)(2,1)}), bf16[32,16,384]{2,1,0:T(8,128)(2,1)S(1)}, u32[]{:S(2)}, u32[]{:S(2)}) async-start(bf16[32,16,384]{2,1,0:T(8,128)(2,1)} %get-tuple-element.49), calls=%async_computation.2 | async-start | bytes 786432 | tf_op jit(solution)/shard_map/all_to_all | solution.py:499
  45.1 8.5 %collective-permute-start.3 = (bf16[96,384]{1,0:T(8,128)(2,1)S(1)}, bf16[96,384]{1,0:T(8,128)(2,1)S(1)}, u32[]{:S(2)}, u32[]{:S(2)}) collective-permute-start(bf16[96,384]{1,0:T(8,128)(2,1)S(1)} %get-tuple-element.54), channel_id=1, source_target_pairs={{0,1},{1,2},{2,3},{3,0},{4,5},{5,6},{6,7},{7,4},{8,9},{9,10},{10,1... | collective-permute-start | bytes 221192 | tf_op jit(solution)/shard_map/ppermute | solution.py:418
  46.8 8.2 %collective-permute-start.4 = (bf16[96,384]{1,0:T(8,128)(2,1)S(1)}, bf16[96,384]{1,0:T(8,128)(2,1)S(1)}, u32[]{:S(2)}, u32[]{:S(2)}) collective-permute-start(bf16[96,384]{1,0:T(8,128)(2,1)S(1)} %get-tuple-element.55), channel_id=1, source_target_pairs={{0,2},{1,3},{2,0},{3,1},{4,6},{5,7},{6,4},{7,5},{8,10},{9,11},{10,... | collective-permute-start | bytes 221192 | tf_op jit(solution)/shard_map/ppermute | solution.py:418
  48.3 6.7 %collective-permute-start.5 = (bf16[96,384]{1,0:T(8,128)(2,1)S(1)}, bf16[96,384]{1,0:T(8,128)(2,1)S(1)}, u32[]{:S(2)}, u32[]{:S(2)}) collective-permute-start(bf16[96,384]{1,0:T(8,128)(2,1)S(1)} %get-tuple-element.56), channel_id=1, source_target_pairs={{0,3},{1,0},{2,1},{3,2},{4,7},{5,4},{6,5},{7,6},{8,11},{9,8},{10,9... | collective-permute-start | bytes 221192 | tf_op jit(solution)/shard_map/ppermute | solution.py:418

commit v8 on v7

v8 whole, which is shorter than its diff:
```python
import math

import jax
import jax.numpy as jnp
import numpy as np
from jax import lax
from jax.experimental import pallas as pl
from jax.experimental.pallas import tpu as pltpu
from jax.sharding import PartitionSpec as P

HMAX = 4
LREACH = 18
REACHES = 4
LANES = 128
FEW = 8
SUMS = 4
PARTS = 3
BOTH = ("member", "band")

ensemble_share = 0.8
static_share = 0.6
length_scale = 6.0


def round_up(value, step):
    return -(-value // step) * step


def lon_weights(distance):
    distance = distance.astype(np.float32)
    values = np.exp(np.float32(-0.5) * (distance / np.float32(length_scale)) ** 2)
    values = values / np.float32(length_scale * math.sqrt(2.0 * math.pi))
    return jnp.asarray(np.where(distance <= LREACH, values, 0.0), jnp.bfloat16)


def ring_kernel(width, padded):
    apart = np.abs(np.arange(padded)[:, None] - np.arange(padded)[None])
    inside = (np.arange(padded)[:, None] < width) & (np.arange(padded)[None] < width)
    return lon_weights(np.where(inside, np.minimum(apart, width - apart), 2 * LREACH))


def near(apart, spans):
    return jnp.maximum(spans - apart, 0.0).astype(jnp.bfloat16)


def row_apart(bands, held, rows, copies):
    index = np.arange(copies * bands * held * rows)
    latitude = index // (held * rows) % bands * rows + index % rows
    level = index // rows % held
    copy = index // (bands * held * rows)
    same = (copy[:, None] == copy[None]) & (level[:, None] == level[None])
    apart = np.where(same, np.abs(latitude[:, None] - latitude[None]), 1000)
    return apart.astype(np.float32), level[:, None].astype(np.float32)


def row_levels(levels, rows):
    index = np.arange(levels * rows)
    level = index[:, None] // rows == np.arange(levels)[None]
    place = index[:, None] % rows == index[None] % rows
    return level.astype(np.float32), place.astype(np.float32)


def exact_dot(matrix, field):
    return jnp.dot(
        matrix, field, precision=lax.Precision.HIGHEST, preferred_element_type=jnp.float32
    )


def parts_dot(matrix, field):
    count, parts = matrix.shape[0], []
    for _ in range(PARTS):
        part = matrix.astype(jnp.bfloat16).astype(jnp.float32)
        parts.append(part)
        matrix = matrix - part
    stacked = jnp.concatenate(parts, axis=0).astype(jnp.bfloat16)
    products = jnp.dot(stacked, field, preferred_element_type=jnp.float32)
    total = products[:count]
    for index in range(1, PARTS):
        total = total + products[index * count : (index + 1) * count]
    return total


def window(values, band, share, halo, tail):
    lon = values.shape[1]
    start = band * share
    stop = start + share + halo
    parts = [values[:, start : min(lon, stop)]]
    if stop > lon:
        parts.append(values[:, : stop - lon])
    if start < halo:
        parts.append(values[:, lon - halo + start :])
    if start:
        parts.append(values[:, max(start - halo, 0) : start])
    return jnp.concatenate(parts + [tail], axis=1)


def spread(field, ring, taper, factor):
    copies = taper.shape[0]
    smoothed = jnp.dot(field.astype(jnp.bfloat16), ring, preferred_element_type=jnp.float32)
    smoothed = smoothed.astype(jnp.bfloat16)
    parts = []
    for start in range(0, field.shape[0], copies):
        part = smoothed[start : start + copies]
        parts.append(jnp.dot(taper, part, preferred_element_type=jnp.float32))
    return factor * (parts[0] if len(parts) == 1 else jnp.concatenate(parts, axis=0))


def solution(mesh):
    members, bands = mesh.shape["member"], mesh.shape["band"]
    few = bands <= FEW
    paired = members % 2 == 0 and members // 2 <= FEW

    def shards(ensemble, member_weight, member_of_slot, halfwidth, static_root, innovation, precision):
        _, slots, levels, rows, lon = ensemble.shape
        level_share, lon_share = levels // members, lon // bands
        own = level_share * rows
        halo = REACHES * LREACH
        width = lon_share + 2 * halo
        padded = round_up(width + 1, LANES)
        kept = round_up(lon_share + SUMS * PARTS, LANES)
        per_member = bands * own
        copies = members
        while copies > 1 and (copies * per_member > 256 or members % copies):
            copies -= 1
        arrays = slots + 2
        everything = levels * rows
        traded = everything + 2 * slots * own
        vmem = pl.BlockSpec(memory_space=pltpu.VMEM)
        smem = pl.BlockSpec(memory_space=pltpu.SMEM)
        limit = min(48, max(14, 24 * members * bands * slots * own * padded // 2**20)) * 2**20

        def call(body, shapes, scalars, operands, scratch=(), flops=0):
            return pl.pallas_call(
                body,
                out_shape=tuple(jax.ShapeDtypeStruct(shape, kind) for shape, kind in shapes),
                in_specs=[smem] * len(scalars) + [vmem] * len(operands),
                out_specs=(vmem,) * len(shapes),
                scratch_shapes=[pltpu.VMEM(shape, kind) for shape, kind in scratch],
                compiler_params=pltpu.CompilerParams(vmem_limit_bytes=limit),
                cost_estimate=pl.CostEstimate(flops=flops, bytes_accessed=0, transcendentals=0),
                name=body.__name__,
            )(*scalars, *operands)

        f32, bf16 = jnp.float32, jnp.bfloat16

        def chosen(turn, blocks, sign):
            if not few:
                return [blocks[0][band] for band in range(bands)]
            turned = []
            for band in range(bands):
                value = blocks[0]
                for shift in range(1, bands):
                    value = jnp.where(turn == (band - sign * shift) % bands, blocks[shift], value)
                turned.append(value)
            return turned

        def load_members(weights, stacked, factor):
            shape = (members, per_member, padded)
            values = stacked[...].astype(f32)
            ensemble = [
                values[:, slot * own : (slot + 1) * own].reshape(shape) for slot in range(slots)
            ]
            which = ensemble[0][:, :1, width : width + 1]
            scale = jnp.zeros(which.shape, f32)
            for member in range(members):
                weight = weights[member : member + 1, :1].reshape(1, 1, 1)
                scale = scale + jnp.where(which == member, weight, 0.0)
            scale = jnp.broadcast_to(scale, (members, per_member, 1))
            return ensemble, scale.reshape(members * per_member, 1) * factor

        def fold(ensemble, weighted):
            total = ensemble[0] * weighted[0][None]
            for slot in range(1, slots):
                total = total + ensemble[slot] * weighted[slot][None]
            return total.reshape(members * per_member, padded)

        def images_of(ensemble, grad, ring, taper, factor):
            local = spread(grad, ring, taper, factor).reshape(members, per_member, padded)
            return [jnp.sum(ensemble[t] * local, axis=0) for t in range(slots)]

        def pack(slot, ensemble, out, marks, arrived, packed, mark_sem, in_sems, out_sems):
            def incoming(t):
                return pltpu.make_async_copy(ensemble.at[0, t], arrived.at[t], in_sems.at[t])

            def outgoing(member):
                place = pl.ds(member * bands, bands)
                return pltpu.make_async_copy(packed.at[place], out.at[place], out_sems.at[member])

            mark = pltpu.make_async_copy(slot, marks, mark_sem)
            mark.start()
            for t in range(slots):
                incoming(t).start()
            mark.wait()
            tail = jnp.full((slots * own, padded - width), marks[0], jnp.int32).astype(f32).astype(bf16)
            for t in range(slots):
                incoming(t).wait()
            for member in range(members):
                picked = range(member * level_share, (member + 1) * level_share)
                values = [arrived[t, at].astype(f32) for t in range(slots) for at in picked]
                values = jnp.concatenate(values, axis=0).astype(bf16)
                for band in range(bands):
                    packed[member * bands + band] = window(values, band, lon_share, halo, tail)
                outgoing(member).start()
            for member in range(members):
                outgoing(member).wait()

        def observe(here, widths, weight, innovation, precision, root, of_level, same, apart, level, *refs):
            outs, results, (static, mixed, pulls) = refs[:-11], refs[-11:-3], refs[-3:]
            own_static, pulled, mixing, pulling, taper, factor, weights, turn = results
            turn[...] = jnp.full((1, LANES), here[1], jnp.int32)
            for member in range(members):
                weights[member : member + 1] = jnp.full((1, LANES), weight[member], f32)
            total = []
            for at in range(levels):
                precise = precision[at].astype(f32)
                part = precise * innovation[0, at].astype(f32)
                for t in range(1, slots):
                    part = part + precise * innovation[t, at].astype(f32)
                total.append(part)
            out_of = lax.dot_general(
                exact_dot(of_level[...], static_share * root[...]),
                of_level[...],
                (((1,), (1,)), ((), ())),
                precision=lax.Precision.HIGHEST,
                preferred_element_type=f32,
            )
            out_of = out_of * same[...]
            into = out_of.T
            back = exact_dot(into, jnp.concatenate(total, axis=0))
            pulled[...] = back
            forth = exact_dot(out_of, back)
            both = exact_dot(out_of, into)
            for at in range(levels):
                static[at] = forth[at * rows : (at + 1) * rows]
                mixed[at] = both[at * rows : (at + 1) * rows]
                pulls[at] = out_of[at * rows : (at + 1) * rows]
            picked = [here[0] * level_share + share for share in range(level_share)]
            arriving = [
                member * level_share + share
                for _, _, member in arrivals(here[0])
                for share in range(level_share)
            ]
            pulling[...] = jnp.concatenate([pulls[at] for at in arriving], axis=0).T
            column = lax.broadcasted_iota(jnp.int32, (everything, own), 0)
            own_column = here[0] * own + lax.broadcasted_iota(jnp.int32, (everything, own), 1)
            mixing[...] = exact_dot(
                jnp.concatenate([mixed[at] for at in arriving], axis=0), (column == own_column).astype(f32)
            ).T
            parts = [innovation[t, at].astype(f32) for t in range(slots) for at in picked]
            parts += [precision[at].astype(f32) for at in picked] + [static[at] for at in picked]
            values = jnp.concatenate(parts, axis=0)
            tail = jnp.zeros((values.shape[0], padded - width), f32)
            pieces = [window(values, band, lon_share, halo, tail) for band in range(bands)]
            for band, piece in enumerate(pieces):
                own_static[band] = piece[(slots + 1) * own :, :kept]
            deal(turn[:, :1], pieces, outs)
            span = jnp.ones(level.shape, f32)
            for at, which in enumerate(picked):
                span = span + jnp.where(level[...] == at, widths[which].astype(f32), 0.0)
            taper[...] = near(apart[...], span[: apart.shape[0]])
            factor[...] = ensemble_share / (span * span)

        def first_half(weights, turn, stacked, ring, taper, factor, *refs):
            blocks, (total_out, weighted_out, grad_out, image_out, fields) = refs[:-5], refs[-5:]
            if few:
                blocks = [block[...].astype(f32) for block in blocks]
            values = jnp.stack(chosen(turn[:, :1], blocks, -1)).astype(f32)
            field = []
            for index in range(arrays):
                piece = values[:, index * own : (index + 1) * own].reshape(per_member, padded)
                fields[index] = piece[:, :kept]
                field.append(piece)
            precise, static = field[slots], field[slots + 1]
            ensemble, factors = load_members(weights, stacked, factor[...])
            weighted = [precise * field[t] for t in range(slots)]
            grad = spread(fold(ensemble, weighted), ring[...], taper[...], factors)
            grad_out[...] = grad[:, :kept]
            total = jnp.zeros((per_member, padded), f32)
            for t, image in enumerate(images_of(ensemble, grad, ring[...], taper[...], factors)):
                image_out[t] = image[:, :kept]
                image = precise * (image + static)
                weighted_out[t] = image
                total = total + image
            total_out[...] = total[:, :kept].astype(bf16)

        def inner(first, second):
            inside = lax.broadcasted_iota(jnp.int32, first.shape, 1) < lon_share
            product = jnp.where(inside, first * second, 0.0)
            return jnp.sum(jnp.sum(product, axis=0, keepdims=True), axis=1, keepdims=True)

        def closest(first, second):
            norm = inner(first, first)
            ratio = inner(first, second) / jnp.where(norm > 0.0, norm, 1.0)
            return ratio.astype(bf16).astype(f32)

        def deal(turn, pieces, outs):
            if not few:
                for band, piece in enumerate(pieces):
                    outs[0][band] = piece.astype(bf16)
                return
            for shift in range(bands):
                value = pieces[0]
                for band in range(1, bands):
                    value = jnp.where(turn == (band - shift) % bands, pieces[band], value)
                outs[shift][...] = value.astype(bf16)

        def second_half(weights, stacked, ring, taper, factor, weighted, first, pair_out, image_out):
            ensemble, factors = load_members(weights, stacked, factor[...])
            grad = fold(ensemble, [weighted[t] for t in range(slots)])
            grad = spread(grad, ring[...], taper[...], factors)
            for t, image in enumerate(images_of(ensemble, grad, ring[...], taper[...], factors)):
                image_out[t] = image[:, :kept]
            first, second = first[...], grad[:, :kept]
            ratio = closest(first, second)
            shape = (members * bands, own, kept)
            second = (second - ratio * first).reshape(shape)
            lane = lax.broadcasted_iota(jnp.int32, shape, 2)
            second = jnp.where(lane < lon_share, second, ratio.reshape(1, 1, 1))
            pair_out[:, :own] = first.reshape(shape).astype(bf16)
            pair_out[:, own:] = second.astype(bf16)

        def combine(pairs, first, second, fields, mixing, *refs):
            blocks, (out, image_out) = refs[:-2], refs[-2:]
            lane = lax.broadcasted_iota(jnp.int32, (1, kept), 1) - lon_share
            every = [
                jnp.concatenate(
                    [
                        blocks[block][shift, band * own : (band + 1) * own].astype(f32)
                        for block, shift, _ in arrivals(0)
                    ],
                    axis=0,
                )
                for band in range(bands)
            ]
            mixed = parts_dot(mixing[...], jnp.concatenate(every, axis=1).astype(bf16))
            mixed = jnp.concatenate(
                [mixed[:, band * kept : (band + 1) * kept] for band in range(bands)], axis=0
            )
            precise, static = fields[slots], fields[slots + 1]
            sums = [jnp.zeros((per_member, kept), f32) for _ in range(SUMS)]
            for t in range(slots):
                image = second[t] + mixed
                image_out[t] = image
                whole = first[t] + static
                weighted = precise * whole
                sums[0] = sums[0] + precise * fields[t] * whole
                sums[1] = sums[1] + weighted * whole
                sums[2] = sums[2] + weighted * image
                sums[3] = sums[3] + precise * image * image
            row = jnp.zeros((1, kept), f32)
            for index, part in enumerate(sums):
                part = jnp.sum(jnp.where(lane < 0, part, 0.0), axis=0, keepdims=True)
                part = jnp.sum(part, axis=1, keepdims=True)
                for piece in range(PARTS):
                    high = part.astype(bf16).astype(f32)
                    row = row + jnp.where(lane == PARTS * index + piece, high, 0.0)
                    part = part - high
            row = jnp.broadcast_to(row, (own, kept))
            lane = lax.broadcasted_iota(jnp.int32, (own, kept), 1)
            for block in range(members * bands):
                values = pairs[block].astype(f32)
                values = [jnp.where(lane < lon_share, values[:own], row), values[own:]]
                out[block] = jnp.concatenate(values, axis=0).astype(bf16)

        def hand_out(turn, first, second, *refs):
            blocks, outs = refs[: len(totals)], refs[len(totals) :]
            lane = lax.broadcasted_iota(jnp.int32, (1, kept), 1)
            ratio = closest(
                jnp.concatenate([first[t] for t in range(slots)], axis=0),
                jnp.concatenate([second[t] for t in range(slots)], axis=0),
            )
            rest = [
                jnp.where(lane < lon_share, second[t] - ratio * first[t], ratio) for t in range(slots)
            ]
            images = [first[t] for t in range(slots)] + rest
            pieces = []
            for band in range(bands):
                place = slice(band * own, (band + 1) * own)
                parts = [blocks[block][shift, place].astype(f32) for block, shift, _ in arrivals(0)]
                pieces.append(jnp.concatenate(parts + [image[place] for image in images], axis=0))
            deal(turn[:, :1], pieces, outs)

        def join(turn, own_static, pulling, *refs):
            blocks, (pulled, images) = refs[:-2], refs[-2:]
            if few:
                blocks = [block[...].astype(f32) for block in blocks]
            pieces = chosen(turn[:, :1], blocks, -1)
            size = slots * own
            for band in range(bands):
                place = slice(band * lon_share, (band + 1) * lon_share)
                piece = pieces[band].astype(f32)
                every = piece[:everything].astype(bf16)
                pulled[:, place] = parts_dot(pulling[...], every)[:, :lon_share]
                parts = piece[everything:]
                first = parts[:size]
                second = parts[size:] + parts[size : size + 1, lon_share : lon_share + 1] * first
                static = own_static[band]
                for t in range(slots):
                    at = slice(t * own, (t + 1) * own)
                    images[at, place] = (first[at] + static)[:, :lon_share]
                images[size:, place] = second[:, :lon_share]

        def finish(back, pulled_first, pulled_second, images, *refs):
            (member_out, static_out, image_out), (member, static, image, sems) = refs[:3], refs[3:]

            def outgoing(index, source, target):
                return pltpu.make_async_copy(source, target, sems.at[index])

            def outgoing_member(index):
                place = pl.ds(index * level_share, level_share)
                return outgoing(index, member.at[place], member_out.at[0, place])

            static_copy = outgoing(members, static, static_out)
            image_copy = outgoing(members + 1, image, image_out)
            total = back[0, :1].astype(f32)
            for block in range(1, members * bands):
                total = total + back[block, :1].astype(f32)
            lane = lax.broadcasted_iota(jnp.int32, total.shape, 1) - lon_share
            first_norm, first_image, cross, second_image = [
                jnp.sum(
                    jnp.where((lane >= PARTS * index) & (lane < PARTS * (index + 1)), total, 0.0),
                    axis=1,
                    keepdims=True,
                )
                for index in range(SUMS)
            ]
            alpha = first_norm / (first_norm + first_image)
            ratio = first_image / first_norm
            next_norm = alpha * alpha * jnp.maximum(cross - ratio * first_image, 0.0)
            beta = next_norm / first_norm
            apart = second_image - 2.0 * ratio * cross + ratio * ratio * first_image
            curvature = next_norm + alpha * alpha * apart - beta * next_norm / alpha
            alpha_next = jnp.clip(next_norm / curvature, 0.0, 1.0)
            on_first = alpha + alpha_next * (1.0 - alpha + beta)
            on_second = -alpha * alpha_next
            values = on_first * pulled_first[...] + on_second * pulled_second[...]
            for level in range(levels):
                static[level] = values[level * rows : (level + 1) * rows]
            static_copy.start()
            half = slots * own
            values = on_first * images[:half] + on_second * images[half:]
            for t in range(slots):
                for level in range(level_share):
                    start = (t * level_share + level) * rows
                    image[t, level] = values[start : start + rows]
            image_copy.start()
            for source in range(members):
                parts = []
                for band in range(bands):
                    both = back[source * bands + band].astype(f32)
                    first, second = both[:own], both[own:]
                    ratio = second[:1, lon_share : lon_share + 1]
                    values = (on_first + on_second * ratio) * first + on_second * second
                    parts.append(values[:, :lon_share])
                values = jnp.concatenate(parts, axis=1)
                for share in range(level_share):
                    member[source * level_share + share] = values[share * rows : (share + 1) * rows]
                outgoing_member(source).start()
            static_copy.wait()
            image_copy.wait()
            for source in range(members):
                outgoing_member(source).wait()

        def trade(blocks):
            if not few:
                return [lax.all_to_all(blocks[0], "band", 0, 0, tiled=True)]
            return [blocks[0]] + [
                lax.ppermute(blocks[shift], "band", [(at, (at + shift) % bands) for at in range(bands)])
                for shift in range(1, bands)
            ]

        def around(block, beside):
            if not paired:
                return [lax.all_gather(block, "member")], beside
            here = [block] + [
                lax.ppermute(block, "member", [(at, (at + 2 * shift) % members) for at in range(members)])
                for shift in range(1, members // 2)
            ]
            here, beside = lax.optimization_barrier((jnp.stack(here), beside))
            return [here, lax.ppermute(here, "member", [(at, at ^ 1) for at in range(members)])], beside

        def arrivals(here):
            if not paired:
                return [(0, member, member) for member in range(members)]
            other = here + 1 - 2 * lax.rem(here, 2)
            return [
                (block, shift, lax.rem(source + members - 2 * shift, members))
                for block, source in enumerate((here, other))
                for shift in range(members // 2)
            ]

        def tradable(shape, kind):
            return [(shape, kind)] * bands if few else [((bands,) + shape, kind)]

        here = jnp.stack([lax.axis_index("member"), lax.axis_index("band")]).astype(jnp.int32)

        block = (members * bands, slots * own, padded)
        pieces = pl.pallas_call(
            pack,
            out_shape=jax.ShapeDtypeStruct(block, bf16),
            in_specs=[pl.BlockSpec(memory_space=pltpu.HBM)] * 2,
            out_specs=pl.BlockSpec(memory_space=pltpu.HBM),
            scratch_shapes=[
                pltpu.SMEM((1,), jnp.int32),
                pltpu.VMEM((slots, levels, rows, lon), bf16),
                pltpu.VMEM(block, bf16),
                pltpu.SemaphoreType.DMA,
                pltpu.SemaphoreType.DMA((slots,)),
                pltpu.SemaphoreType.DMA((members,)),
            ],
            compiler_params=pltpu.CompilerParams(vmem_limit_bytes=60 * 2**20),
            name="pack",
        )(member_of_slot, ensemble)
        pieces, innovation, precision, static_root = lax.optimization_barrier(
            (pieces, innovation, precision, static_root)
        )
        stacked = lax.all_to_all(pieces, BOTH, 0, 0, tiled=True)

        of_level, same = row_levels(levels, rows)
        apart, level = row_apart(bands, level_share, rows, copies)
        every_level = np.tile(level, (members // copies, 1))
        block = (arrays * own, padded)
        results = call(
            observe,
            tradable(block, bf16)
            + [
                ((bands, own, kept), f32),
                ((everything, lon), f32),
                ((own, everything), f32),
                ((everything, everything), f32),
                (apart.shape, bf16),
                (every_level.shape, f32),
                ((members, LANES), f32),
                ((1, LANES), jnp.int32),
            ],
            [here, halfwidth, member_weight],
            [innovation, precision, static_root]
            + [jnp.asarray(table) for table in (of_level, same, apart, every_level)],
            scratch=[((levels, rows, lon), f32)] + [((levels, rows, everything), f32)] * 2,
        )
        blocks = trade(results[:-8])
        own_static, pulled, mixing, pulling, taper, factor, weights, turn = results[-8:]
        ring = ring_kernel(width, padded)

        total, weighted, grad_first, image_first, fields = call(
            first_half,
            [
                ((per_member, kept), bf16),
                ((slots, per_member, padded), f32),
                ((members * per_member, kept), f32),
                ((slots, per_member, kept), f32),
                ((arrays, per_member, kept), f32),
            ],
            [],
            [weights, turn, stacked, ring, taper, factor, *blocks],
        )
        pairs, image_second = call(
            second_half,
            [((members * bands, 2 * own, kept), bf16), ((slots, per_member, kept), f32)],
            [],
            [weights, stacked, ring, taper, factor, weighted, grad_first],
            flops=10**9,
        )
        totals, image_second = around(total, image_second)

        pairs, image_second = call(
            combine,
            [((members * bands, 2 * own, kept), bf16), ((slots, per_member, kept), f32)],
            [],
            [pairs, image_first, image_second, fields, mixing, *totals],
        )
        back = lax.all_to_all(pairs, BOTH, 0, 0, tiled=True)
        blocks = call(
            hand_out,
            tradable((traded, kept), bf16),
            [],
            [turn, image_first, image_second, *totals],
        )
        blocks = trade(blocks)
        pulled_second, images = call(
            join,
            [((everything, lon), f32), ((2 * slots * own, lon), f32)],
            [],
            [turn, own_static, pulling, *blocks],
        )
        return pl.pallas_call(
            finish,
            out_shape=(
                jax.ShapeDtypeStruct((1, levels, rows, lon), f32),
                jax.ShapeDtypeStruct((levels, rows, lon), f32),
                jax.ShapeDtypeStruct((slots, level_share, rows, lon), f32),
            ),
            in_specs=[vmem] * 4,
            out_specs=(pl.BlockSpec(memory_space=pltpu.HBM),) * 3,
            scratch_shapes=[
                pltpu.VMEM((levels, rows, lon), f32),
                pltpu.VMEM((levels, rows, lon), f32),
                pltpu.VMEM((slots, level_share, rows, lon), f32),
                pltpu.SemaphoreType.DMA((members + 2,)),
            ],
            compiler_params=pltpu.CompilerParams(vmem_limit_bytes=limit),
            name="finish",
        )(back, pulled, pulled_second, images)

    return jax.shard_map(
        shards,
        mesh=mesh,
        in_specs=(
            P("member", None, None, "band", None),
            P(),
            P("member"),
            P(),
            P(),
            P(None, None, "band", None),
            P(None, "band", None),
        ),
        out_specs=(
            P("member", None, "band", None),
            P(None, "band", None),
            P(None, "member", "band", None),
        ),
        check_vma=False,
    )
```

time: 60.4 us -> 56.5 us (0.935)
  Pallas kernels: 11.6 us -> 9 us
  starting transfers between devices: 22.7 us -> 21.8 us
    all_to_all x2 -> x1, waiting for transfers between devices: 9.46 us -> 3.29 us  [shards(): back = lax.all_to_all(pairs, BOTH, 0, 0, tiled=True)]
    ppermute x0 -> x4, waiting for transfers between devices: none -> 5.96 us  [the longest x3 4.67 us: around(): lax.ppermute(block, 'member', [(at, (at + 2 * shift) % members) for at in...]
    pallas_call x6, Pallas kernels: 9.63 us -> 5.7 us  [call(): pl.pallas_call(body, out_shape=tuple((jax.ShapeDtypeStruct(shape, kind) f...]
    all_to_all x2 -> x1, starting transfers between devices: 5.99 us -> 2.6 us  [shards(): back = lax.all_to_all(pairs, BOTH, 0, 0, tiled=True)]
    ppermute x0 -> x4, starting transfers between devices: none -> 2.57 us  [the longest x3 2.49 us: around(): lax.ppermute(block, 'member', [(at, (at + 2 * shift) % members) for at in...]
    pallas_call x0 -> x1, Pallas kernels: none -> 1.28 us  [shards(): pl.pallas_call(finish, out_shape=(jax.ShapeDtypeStruct((1, levels, rows,...]
  transfers between devices with their start and end apart: 9 -> 12, of which waited for: 8 -> 11; matrix products, arithmetic and copies ran while one was open for 0% -> 0% of each run, Pallas kernels for 7% -> 7%
where the time goes in v8:
time: 56.5 us; the launch traced here: 56 us
  waiting for transfers between devices  23 us (41%)
  starting transfers between devices  21.8 us (39%)
  Pallas kernels  9 us (16%)
  between operations  1.45 us (3%)
  local copies, waits for them, and re-layouts  0.61 us (1%)
    ppermute x6, starting transfers between devices, trade(): lax.ppermute(blocks[shift], 'band', [(at, (at + shift) % bands) for at in...  9.36 us
    ppermute x6, waiting for transfers between devices, trade(): lax.ppermute(blocks[shift], 'band', [(at, (at + shift) % bands) for at in...  7.51 us
    all_to_all x1, starting transfers between devices, shards(): stacked = lax.all_to_all(pieces, BOTH, 0, 0, tiled=True)  7.3 us
    all_to_all x1, waiting for transfers between devices, shards(): stacked = lax.all_to_all(pieces, BOTH, 0, 0, tiled=True)  6.28 us
    pallas_call x6, Pallas kernels, call(): pl.pallas_call(body, out_shape=tuple((jax.ShapeDtypeStruct(shape, kind) f...  5.7 us
    ppermute x3, waiting for transfers between devices, around(): lax.ppermute(block, 'member', [(at, (at + 2 * shift) % members) for at in...  4.67 us
    all_to_all x1, waiting for transfers between devices, shards(): back = lax.all_to_all(pairs, BOTH, 0, 0, tiled=True)  3.29 us
    all_to_all x1, starting transfers between devices, shards(): back = lax.all_to_all(pairs, BOTH, 0, 0, tiled=True)  2.6 us
  transfers between devices with their start and end apart: 12, of which 11 were waited for; matrix products, arithmetic and copies ran while one was open for 0% of the time, Pallas kernels for 7%

profile of v8, /device:TPU:0, one launch (start us, length us, event | category | flops | bytes accessed | tf_op | source)
XLA Modules:
  0.0 56.0 jit_solution(551002571737729451)
XLA Ops:
  1.3 2.0 %pack.1 = bf16[32,16,512]{2,1,0:T(8,128)(2,1)} custom-call(s32[1]{0:T(128)S(6)} %copy.15.slot, bf16[1,2,16,4,1440]{4,3,2,1,0:T(4,128)(2,1)} %ensemble.1), custom_call_target="tpu_custom_call" | custom-call | tf_op jit(solution)/shard_map/pack/pallas_call | solution.py:498
  3.3 0.0 copy-start.1
  3.3 0.0 copy-start.2
  3.3 0.0 copy-start.3
  3.3 0.0 copy-start.4
  3.4 0.0 copy-start.5
  3.4 0.0 copy-start.6
  3.4 7.3 %all-to-all-start = ((bf16[32,16,512]{2,1,0:T(8,128)(2,1)}), bf16[32,16,512]{2,1,0:T(8,128)(2,1)S(1)}, u32[]{:S(2)}, u32[]{:S(2)}) async-start(bf16[32,16,512]{2,1,0:T(8,128)(2,1)} %pack.1), calls=%async_computation | async-start | bytes 1048576 | tf_op jit(solution)/shard_map/all_to_all | solution.py:517
  10.7 0.0 copy-start.7
  10.7 0.0 copy-start.8
  10.7 0.0 copy-start.9
  10.7 0.1 pad_add_fusion.here
  10.8 0.0 copy-done.1
  10.8 0.0 copy-done.2
  10.8 0.0 copy-done.3
  10.8 0.0 copy-done.4
  10.8 0.0 copy-done.5
  10.8 0.0 copy-done.6
  10.8 0.6 copy-done.7
  11.4 0.0 copy-done.8
  11.4 0.0 copy-done.9
  11.4 0.0 copy-start
  11.4 2.0 %observe.1 = (bf16[32,512]{1,0:T(8,128)(2,1)S(1)}, bf16[32,512]{1,0:T(8,128)(2,1)S(1)}, bf16[32,512]{1,0:T(8,128)(2,1)S(1)}, bf16[32,512]{1,0:T(8,128)(2,1)S(1)}...) custom-call(s32[2]{0:T(128)S(1)} %pad_add_fusion.here, ...), custom_call_target="tpu_custom_call" | custom-call | tf_op jit(solution)/shard_map/observe/pallas_call | solution.py:133
  13.4 1.8 %collective-permute-start = (bf16[32,512]{1,0:T(8,128)(2,1)S(1)}, bf16[32,512]{1,0:T(8,128)(2,1)S(1)}, u32[]{:S(2)}, u32[]{:S(2)}) collective-permute-start(bf16[32,512]{1,0:T(8,128)(2,1)S(1)} %get-tuple-element.45), channel_id=1, source_target_pairs={{0,1},{1,2},{2,3},{3,0},{4,5},{5,6},{6,7},{7,4},{8,9},{9,10},{10,1... | collective-permute-start | bytes 98312 | tf_op jit(solution)/shard_map/ppermute | solution.py:468
  15.2 1.5 %collective-permute-start.1 = (bf16[32,512]{1,0:T(8,128)(2,1)S(1)}, bf16[32,512]{1,0:T(8,128)(2,1)S(1)}, u32[]{:S(2)}, u32[]{:S(2)}) collective-permute-start(bf16[32,512]{1,0:T(8,128)(2,1)S(1)} %get-tuple-element.46), channel_id=1, source_target_pairs={{0,2},{1,3},{2,0},{3,1},{4,6},{5,7},{6,4},{7,5},{8,10},{9,11},{10,... | collective-permute-start | bytes 98312 | tf_op jit(solution)/shard_map/ppermute | solution.py:468
  16.7 1.5 %collective-permute-start.2 = (bf16[32,512]{1,0:T(8,128)(2,1)S(1)}, bf16[32,512]{1,0:T(8,128)(2,1)S(1)}, u32[]{:S(2)}, u32[]{:S(2)}) collective-permute-start(bf16[32,512]{1,0:T(8,128)(2,1)S(1)} %get-tuple-element.47), channel_id=1, source_target_pairs={{0,3},{1,0},{2,1},{3,2},{4,7},{5,4},{6,5},{7,6},{8,11},{9,8},{10,9... | collective-permute-start | bytes 98312 | tf_op jit(solution)/shard_map/ppermute | solution.py:468
  18.2 0.9 %collective-permute-done.refs_1_ = bf16[32,512]{1,0:T(8,128)(2,1)S(1)} collective-permute-done((bf16[32,512]{1,0:T(8,128)(2,1)S(1)}, bf16[32,512]{1,0:T(8,128)(2,1)S(1)}, u32[]{:S(2)}, u32[]{:S(2)}) %collective-permute-start) | collective-permute-done | bytes 32800 | tf_op jit(solution)/shard_map/ppermute | solution.py:468
  19.1 1.3 %collective-permute-done.1.refs_2_ = bf16[32,512]{1,0:T(8,128)(2,1)S(1)} collective-permute-done((bf16[32,512]{1,0:T(8,128)(2,1)S(1)}, bf16[32,512]{1,0:T(8,128)(2,1)S(1)}, u32[]{:S(2)}, u32[]{:S(2)}) %collective-permute-start.1) | collective-permute-done | bytes 32800 | tf_op jit(solution)/shard_map/ppermute | solution.py:468
  20.4 0.3 collective-permute-done.2.refs_3_
  20.7 6.3 %all-to-all-done.stacked = bf16[32,16,512]{2,1,0:T(8,128)(2,1)S(1)} async-done(((bf16[32,16,512]{2,1,0:T(8,128)(2,1)}), bf16[32,16,512]{2,1,0:T(8,128)(2,1)S(1)}, u32[]{:S(2)}, u32[]{:S(2)}) %all-to-all-start) | async-done | bytes 524320 | tf_op jit(solution)/shard_map/all_to_all | solution.py:517
  26.9 0.0 copy-done
  26.9 1.0 %first_half.1 = (bf16[32,384]{1,0:T(8,128)(2,1)S(1)}, f32[2,32,512]{2,1,0:T(8,128)S(1)}, f32[256,384]{1,0:T(8,128)S(1)}, f32[2,32,384]{2,1,0:T(8,128)S(1)}, f32[4,32,384]{2,1,0:T(8,128)S(1)}) custom-call(f32[8,128]{1,0:T(8,128)S(1)} %get-tuple-element.39.weights, s32[1,128]{1,0:T(1,128)S(1)} %get-tuple-element.43.turn, ...), custom_call_target="tpu_custom_call" | custom-call | tf_op jit(solution)/shard_map/first_half/pallas_call | solution.py:133
  28.0 1.5 %collective-permute-start.5 = (bf16[32,384]{1,0:T(8,128)(2,1)S(1)}, bf16[32,384]{1,0:T(8,128)(2,1)S(1)}, u32[]{:S(2)}, u32[]{:S(2)}) collective-permute-start(bf16[32,384]{1,0:T(8,128)(2,1)S(1)} %get-tuple-element.52), channel_id=1, source_target_pairs={{0,24},{4,28},{8,0},{12,4},{16,8},{20,12},{24,16},{28,20},{1,25},{... | collective-permute-start | bytes 73736 | tf_op jit(solution)/shard_map/ppermute | solution.py:476
  29.5 1.0 %collective-permute-start.4 = (bf16[32,384]{1,0:T(8,128)(2,1)S(1)}, bf16[32,384]{1,0:T(8,128)(2,1)S(1)}, u32[]{:S(2)}, u32[]{:S(2)}) collective-permute-start(bf16[32,384]{1,0:T(8,128)(2,1)S(1)} %get-tuple-element.52), channel_id=1, source_target_pairs={{0,16},{4,20},{8,24},{12,28},{16,0},{20,4},{24,8},{28,12},{1,17},{... | collective-permute-start | bytes 73736 | tf_op jit(solution)/shard_map/ppermute | solution.py:476
  30.5 0.0 collective-permute-start.3
  30.5 0.9 %second_half.1 = (bf16[32,16,384]{2,1,0:T(8,128)(2,1)S(1)}, f32[2,32,384]{2,1,0:T(8,128)S(1)}) custom-call(f32[8,128]{1,0:T(8,128)S(1)} %get-tuple-element.39.weights, bf16[32,16,512]{2,1,0:T(8,128)(2,1)S(1)} %all-to-all-done.stacked, bf16[512,512]{1,0:T(8,128)(2,1)S(1)} %copy-done, bf16[256,256]{1,0:T(8,128)(2,1)S(1)} %get-tuple-element.41.taper, ...), custom_call_target="tpu_custom_call" | custom-call | flops 1000000000 | tf_op jit(solution)/shard_map/second_half/pallas_call | solution.py:133
  31.4 0.4 collective-permute-done.5
  31.9 2.6 %collective-permute-done.4 = bf16[32,384]{1,0:T(8,128)(2,1)S(1)} collective-permute-done((bf16[32,384]{1,0:T(8,128)(2,1)S(1)}, bf16[32,384]{1,0:T(8,128)(2,1)S(1)}, u32[]{:S(2)}, u32[]{:S(2)}) %collective-permute-start.4) | collective-permute-done | bytes 24608 | tf_op jit(solution)/shard_map/ppermute | solution.py:476
  34.5 1.6 %collective-permute-done.3 = bf16[32,384]{1,0:T(8,128)(2,1)S(1)} collective-permute-done((bf16[32,384]{1,0:T(8,128)(2,1)S(1)}, bf16[32,384]{1,0:T(8,128)(2,1)S(1)}, u32[]{:S(2)}, u32[]{:S(2)}) %collective-permute-start.3) | collective-permute-done | bytes 24608 | tf_op jit(solution)/shard_map/ppermute | solution.py:476
  36.1 0.1 collective-permute-start.6
  36.2 1.3 %collective-permute-done.6.refs_1_ = bf16[4,32,384]{2,1,0:T(8,128)(2,1)S(1)} collective-permute-done((bf16[4,32,384]{2,1,0:T(8,128)(2,1)S(1)}, bf16[4,32,384]{2,1,0:T(8,128)(2,1)S(1)}, u32[]{:S(2)}, u32[]{:S(2)}) %collective-permute-start.6) | collective-permute-done | bytes 98336 | tf_op jit(solution)/shard_map/ppermute | solution.py:480
  37.5 1.0 %combine.1 = (bf16[32,16,384]{2,1,0:T(8,128)(2,1)}, f32[2,32,384]{2,1,0:T(8,128)S(1)}) custom-call(bf16[32,16,384]{2,1,0:T(8,128)(2,1)S(1)} %get-tuple-element.50.pairs, f32[2,32,384]{2,1,0:T(8,128)S(1)} %get-tuple-element.51.first, f32[2,32,384]{2,1,0:T(8,128)S(1)} %get-tuple-element.54.second, f32[4,32,384]{2,1,0:T(8,128)S(1)} %get-tuple-element.55.fields, ...), custom_call_target="tpu_custom_call" | custom-call | tf_op jit(solution)/shard_map/combine/pallas_call | solution.py:133
  38.5 2.6 %all-to-all-start.1 = ((bf16[32,16,384]{2,1,0:T(8,128)(2,1)}), bf16[32,16,384]{2,1,0:T(8,128)(2,1)S(1)}, u32[]{:S(2)}, u32[]{:S(2)}) async-start(bf16[32,16,384]{2,1,0:T(8,128)(2,1)} %get-tuple-element.58), calls=%async_computation.1 | async-start | bytes 786432 | tf_op jit(solution)/shard_map/all_to_all | solution.py:572
  41.1 0.2 hand_out.1
  41.3 1.7 %collective-permute-start.7 = (bf16[96,384]{1,0:T(8,128)(2,1)S(1)}, bf16[96,384]{1,0:T(8,128)(2,1)S(1)}, u32[]{:S(2)}, u32[]{:S(2)}) collective-permute-start(bf16[96,384]{1,0:T(8,128)(2,1)S(1)} %get-tuple-element.64), channel_id=1, source_target_pairs={{0,1},{1,2},{2,3},{3,0},{4,5},{5,6},{6,7},{7,4},{8,9},{9,10},{10,1... | collective-permute-start | bytes 221192 | tf_op jit(solution)/shard_map/ppermute | solution.py:468
  43.0 1.5 %collective-permute-start.8 = (bf16[96,384]{1,0:T(8,128)(2,1)S(1)}, bf16[96,384]{1,0:T(8,128)(2,1)S(1)}, u32[]{:S(2)}, u32[]{:S(2)}) collective-permute-start(bf16[96,384]{1,0:T(8,128)(2,1)S(1)} %get-tuple-element.65), channel_id=1, source_target_pairs={{0,2},{1,3},{2,0},{3,1},{4,6},{5,7},{6,4},{7,5},{8,10},{9,11},{10,... | collective-permute-start | bytes 221192 | tf_op jit(solution)/shard_map/ppermute | solution.py:468
  44.5 1.4 %collective-permute-start.9 = (bf16[96,384]{1,0:T(8,128)(2,1)S(1)}, bf16[96,384]{1,0:T(8,128)(2,1)S(1)}, u32[]{:S(2)}, u32[]{:S(2)}) collective-permute-start(bf16[96,384]{1,0:T(8,128)(2,1)S(1)} %get-tuple-element.66), channel_id=1, source_target_pairs={{0,3},{1,0},{2,1},{3,2},{4,7},{5,4},{6,5},{7,6},{8,11},{9,8},{10,9... | collective-permute-start | bytes 221192 | tf_op jit(solution)/shard_map/ppermute | solution.py:468
  46.0 3.6 %collective-permute-done.7.refs_1_ = bf16[96,384]{1,0:T(8,128)(2,1)S(1)} collective-permute-done((bf16[96,384]{1,0:T(8,128)(2,1)S(1)}, bf16[96,384]{1,0:T(8,128)(2,1)S(1)}, u32[]{:S(2)}, u32[]{:S(2)}) %collective-permute-start.7) | collective-permute-done | bytes 73760 | tf_op jit(solution)/shard_map/ppermute | solution.py:468
  49.6 1.4 %collective-permute-done.8.refs_2_ = bf16[96,384]{1,0:T(8,128)(2,1)S(1)} collective-permute-done((bf16[96,384]{1,0:T(8,128)(2,1)S(1)}, bf16[96,384]{1,0:T(8,128)(2,1)S(1)}, u32[]{:S(2)}, u32[]{:S(2)}) %collective-permute-start.8) | collective-permute-done | bytes 73760 | tf_op jit(solution)/shard_map/ppermute | solution.py:468
  51.0 0.0 collective-permute-done.9.refs_3_
  51.0 0.5 join.1
  51.4 3.3 %all-to-all-done.1.back = bf16[32,16,384]{2,1,0:T(8,128)(2,1)S(1)} async-done(((bf16[32,16,384]{2,1,0:T(8,128)(2,1)}), bf16[32,16,384]{2,1,0:T(8,128)(2,1)S(1)}, u32[]{:S(2)}, u32[]{:S(2)}) %all-to-all-start.1) | async-done | bytes 393248 | tf_op jit(solution)/shard_map/all_to_all | solution.py:572
  54.7 1.3 %finish.1 = (f32[1,16,4,1440]{3,2,1,0:T(4,128)}, f32[16,4,1440]{2,1,0:T(4,128)}, f32[2,2,4,1440]{3,2,1,0:T(4,128)}) custom-call(bf16[32,16,384]{2,1,0:T(8,128)(2,1)S(1)} %all-to-all-done.1.back, f32[64,1440]{1,0:T(8,128)S(1)} %get-tuple-element.59.pulled_first, f32[64,1440]{1,0:T(8,128)S(1)} %get-tuple-element.67.pulled_second, ...), custom_call_target="tpu_custom_call" | custom-call | tf_op jit(solution)/shard_map/finish/pallas_call | solution.py:586
  (1 shorter events, 0.0 us)
Async XLA Ops:
  3.3 7.5 %copy-start.1 = (bf16[2,16,4,1440]{3,2,1,0:T(4,128)(2,1)S(1)}, bf16[2,16,4,1440]{3,2,1,0:T(4,128)(2,1)}, u32[]{:S(2)}) copy-start(bf16[2,16,4,1440]{3,2,1,0:T(4,128)(2,1)} %innovation) | copy-start | bytes 1105924
  3.3 7.5 %copy-start.2 = (f32[256,256]{1,0:T(8,128)S(1)}, f32[256,256]{1,0:T(8,128)}, u32[]{:S(2)}) copy-start(f32[256,256]{1,0:T(8,128)} %constant.21.clone.apart) | copy-start | bytes 786436
  3.3 7.5 %copy-start.3 = (bf16[16,4,1440]{2,1,0:T(4,128)(2,1)S(1)}, bf16[16,4,1440]{2,1,0:T(4,128)(2,1)}, u32[]{:S(2)}) copy-start(bf16[16,4,1440]{2,1,0:T(4,128)(2,1)} %precision) | copy-start | bytes 552964
  3.3 7.5 %copy-start.4 = (f32[256,1]{1,0:T(8,128)S(1)}, f32[256,1]{1,0:T(8,128)}, u32[]{:S(2)}) copy-start(f32[256,1]{1,0:T(8,128)} %constant.22.clone.level) | copy-start | bytes 3076
  3.4 7.5 %copy-start.5 = (f32[64,64]{1,0:T(8,128)S(1)}, f32[64,64]{1,0:T(8,128)}, u32[]{:S(2)}) copy-start(f32[64,64]{1,0:T(8,128)} %constant.20.clone.same) | copy-start | bytes 49156
  3.4 7.5 %copy-start.6 = (f32[64,16]{1,0:T(8,128)S(1)}, f32[64,16]{1,0:T(8,128)}, u32[]{:S(2)}) copy-start(f32[64,16]{1,0:T(8,128)} %constant.19.clone.of_level) | copy-start | bytes 12292
  3.4 23.6 %all-to-all-start = ((bf16[32,16,512]{2,1,0:T(8,128)(2,1)}), bf16[32,16,512]{2,1,0:T(8,128)(2,1)S(1)}, u32[]{:S(2)}, u32[]{:S(2)}) async-start(bf16[32,16,512]{2,1,0:T(8,128)(2,1)} %pack.1), calls=%async_computation | async-start | bytes 1048576 | tf_op jit(solution)/shard_map/all_to_all | solution.py:517
  10.7 0.7 %copy-start.7 = (f32[16,16]{1,0:T(8,128)S(1)}, f32[16,16]{1,0:T(8,128)}, u32[]{:S(2)}) copy-start(f32[16,16]{1,0:T(8,128)} %root) | copy-start | bytes 3076
  10.7 0.7 %copy-start.8 = (s32[16]{0:T(128)S(1)}, s32[16]{0:T(128)}, u32[]{:S(2)}) copy-start(s32[16]{0:T(128)} %widths.1) | copy-start | bytes 196
  10.7 0.7 %copy-start.9 = (f32[8]{0:T(128)S(1)}, f32[8]{0:T(128)}, u32[]{:S(2)}) copy-start(f32[8]{0:T(128)} %weight.1) | copy-start | bytes 100
  11.4 15.5 %copy-start = (bf16[512,512]{1,0:T(8,128)(2,1)S(1)}, bf16[512,512]{1,0:T(8,128)(2,1)}, u32[]{:S(2)}) copy-start(bf16[512,512]{1,0:T(8,128)(2,1)} %constant.23.clone.ring) | copy-start | bytes 1572868
  13.4 5.6 %collective-permute-start = (bf16[32,512]{1,0:T(8,128)(2,1)S(1)}, bf16[32,512]{1,0:T(8,128)(2,1)S(1)}, u32[]{:S(2)}, u32[]{:S(2)}) collective-permute-start(bf16[32,512]{1,0:T(8,128)(2,1)S(1)} %get-tuple-element.45), channel_id=1, source_target_pairs={{0,1},{1,2},{2,3},{3,0},{4,5},{5,6},{6,7},{7,4},{8,9},{9,10},{10,1... | collective-permute-start | bytes 98312 | tf_op jit(solution)/shard_map/ppermute | solution.py:468
  15.2 5.2 %collective-permute-start.1 = (bf16[32,512]{1,0:T(8,128)(2,1)S(1)}, bf16[32,512]{1,0:T(8,128)(2,1)S(1)}, u32[]{:S(2)}, u32[]{:S(2)}) collective-permute-start(bf16[32,512]{1,0:T(8,128)(2,1)S(1)} %get-tuple-element.46), channel_id=1, source_target_pairs={{0,2},{1,3},{2,0},{3,1},{4,6},{5,7},{6,4},{7,5},{8,10},{9,11},{10,... | collective-permute-start | bytes 98312 | tf_op jit(solution)/shard_map/ppermute | solution.py:468
  16.7 4.0 %collective-permute-start.2 = (bf16[32,512]{1,0:T(8,128)(2,1)S(1)}, bf16[32,512]{1,0:T(8,128)(2,1)S(1)}, u32[]{:S(2)}, u32[]{:S(2)}) collective-permute-start(bf16[32,512]{1,0:T(8,128)(2,1)S(1)} %get-tuple-element.47), channel_id=1, source_target_pairs={{0,3},{1,0},{2,1},{3,2},{4,7},{5,4},{6,5},{7,6},{8,11},{9,8},{10,9... | collective-permute-start | bytes 98312 | tf_op jit(solution)/shard_map/ppermute | solution.py:468
  28.0 3.9 %collective-permute-start.5 = (bf16[32,384]{1,0:T(8,128)(2,1)S(1)}, bf16[32,384]{1,0:T(8,128)(2,1)S(1)}, u32[]{:S(2)}, u32[]{:S(2)}) collective-permute-start(bf16[32,384]{1,0:T(8,128)(2,1)S(1)} %get-tuple-element.52), channel_id=1, source_target_pairs={{0,24},{4,28},{8,0},{12,4},{16,8},{20,12},{24,16},{28,20},{1,25},{... | collective-permute-start | bytes 73736 | tf_op jit(solution)/shard_map/ppermute | solution.py:476
  29.5 5.0 %collective-permute-start.4 = (bf16[32,384]{1,0:T(8,128)(2,1)S(1)}, bf16[32,384]{1,0:T(8,128)(2,1)S(1)}, u32[]{:S(2)}, u32[]{:S(2)}) collective-permute-start(bf16[32,384]{1,0:T(8,128)(2,1)S(1)} %get-tuple-element.52), channel_id=1, source_target_pairs={{0,16},{4,20},{8,24},{12,28},{16,0},{20,4},{24,8},{28,12},{1,17},{... | collective-permute-start | bytes 73736 | tf_op jit(solution)/shard_map/ppermute | solution.py:476
  30.5 5.6 %collective-permute-start.3 = (bf16[32,384]{1,0:T(8,128)(2,1)S(1)}, bf16[32,384]{1,0:T(8,128)(2,1)S(1)}, u32[]{:S(2)}, u32[]{:S(2)}) collective-permute-start(bf16[32,384]{1,0:T(8,128)(2,1)S(1)} %get-tuple-element.52), channel_id=1, source_target_pairs={{0,8},{4,12},{8,16},{12,20},{16,24},{20,28},{24,0},{28,4},{1,9},{5... | collective-permute-start | bytes 73736 | tf_op jit(solution)/shard_map/ppermute | solution.py:476
  36.1 1.4 %collective-permute-start.6 = (bf16[4,32,384]{2,1,0:T(8,128)(2,1)S(1)}, bf16[4,32,384]{2,1,0:T(8,128)(2,1)S(1)}, u32[]{:S(2)}, u32[]{:S(2)}) collective-permute-start(bf16[4,32,384]{2,1,0:T(8,128)(2,1)S(1)} %pad_maximum_fusion.refs_0_), channel_id=1, source_target_pairs={{0,4},{4,0},{8,12},{12,8},{16,20},{20,16},{24,28},{28,24},{1,5},{5... | collective-permute-start | bytes 294920 | tf_op jit(solution)/shard_map/ppermute | solution.py:480
  38.5 16.2 %all-to-all-start.1 = ((bf16[32,16,384]{2,1,0:T(8,128)(2,1)}), bf16[32,16,384]{2,1,0:T(8,128)(2,1)S(1)}, u32[]{:S(2)}, u32[]{:S(2)}) async-start(bf16[32,16,384]{2,1,0:T(8,128)(2,1)} %get-tuple-element.58), calls=%async_computation.1 | async-start | bytes 786432 | tf_op jit(solution)/shard_map/all_to_all | solution.py:572
  41.3 8.3 %collective-permute-start.7 = (bf16[96,384]{1,0:T(8,128)(2,1)S(1)}, bf16[96,384]{1,0:T(8,128)(2,1)S(1)}, u32[]{:S(2)}, u32[]{:S(2)}) collective-permute-start(bf16[96,384]{1,0:T(8,128)(2,1)S(1)} %get-tuple-element.64), channel_id=1, source_target_pairs={{0,1},{1,2},{2,3},{3,0},{4,5},{5,6},{6,7},{7,4},{8,9},{9,10},{10,1... | collective-permute-start | bytes 221192 | tf_op jit(solution)/shard_map/ppermute | solution.py:468
  43.0 8.0 %collective-permute-start.8 = (bf16[96,384]{1,0:T(8,128)(2,1)S(1)}, bf16[96,384]{1,0:T(8,128)(2,1)S(1)}, u32[]{:S(2)}, u32[]{:S(2)}) collective-permute-start(bf16[96,384]{1,0:T(8,128)(2,1)S(1)} %get-tuple-element.65), channel_id=1, source_target_pairs={{0,2},{1,3},{2,0},{3,1},{4,6},{5,7},{6,4},{7,5},{8,10},{9,11},{10,... | collective-permute-start | bytes 221192 | tf_op jit(solution)/shard_map/ppermute | solution.py:468
  44.5 6.5 %collective-permute-start.9 = (bf16[96,384]{1,0:T(8,128)(2,1)S(1)}, bf16[96,384]{1,0:T(8,128)(2,1)S(1)}, u32[]{:S(2)}, u32[]{:S(2)}) collective-permute-start(bf16[96,384]{1,0:T(8,128)(2,1)S(1)} %get-tuple-element.66), channel_id=1, source_target_pairs={{0,3},{1,0},{2,1},{3,2},{4,7},{5,4},{6,5},{7,6},{8,11},{9,8},{10,9... | collective-permute-start | bytes 221192 | tf_op jit(solution)/shard_map/ppermute | solution.py:468

commit v9 on v8

--- a/solution.py
+++ b/solution.py
@@ -154,7 +154,7 @@
                 turned.append(value)
             return turned
 
-        def load_members(weights, stacked, factor):
+        def load_members(weights, stacked):
             shape = (members, per_member, padded)
             values = stacked[...].astype(f32)
             ensemble = [
@@ -166,13 +166,13 @@
                 weight = weights[member : member + 1, :1].reshape(1, 1, 1)
                 scale = scale + jnp.where(which == member, weight, 0.0)
             scale = jnp.broadcast_to(scale, (members, per_member, 1))
-            return ensemble, scale.reshape(members * per_member, 1) * factor
-
-        def fold(ensemble, weighted):
+            return ensemble, scale.reshape(members * per_member, 1)
+
+        def fold(ensemble, scale, weighted):
             total = ensemble[0] * weighted[0][None]
             for slot in range(1, slots):
                 total = total + ensemble[slot] * weighted[slot][None]
-            return total.reshape(members * per_member, padded)
+            return scale * total.reshape(members * per_member, padded)
 
         def images_of(ensemble, grad, ring, taper, factor):
             local = spread(grad, ring, taper, factor).reshape(members, per_member, padded)
@@ -271,12 +271,12 @@
                 fields[index] = piece[:, :kept]
                 field.append(piece)
             precise, static = field[slots], field[slots + 1]
-            ensemble, factors = load_members(weights, stacked, factor[...])
+            ensemble, scale = load_members(weights, stacked)
             weighted = [precise * field[t] for t in range(slots)]
-            grad = spread(fold(ensemble, weighted), ring[...], taper[...], factors)
+            grad = spread(fold(ensemble, scale, weighted), ring[...], taper[...], factor[...])
             grad_out[...] = grad[:, :kept]
             total = jnp.zeros((per_member, padded), f32)
-            for t, image in enumerate(images_of(ensemble, grad, ring[...], taper[...], factors)):
+            for t, image in enumerate(images_of(ensemble, grad, ring[...], taper[...], scale * factor[...])):
                 image_out[t] = image[:, :kept]
                 image = precise * (image + static)
                 weighted_out[t] = image
@@ -305,10 +305,10 @@
                 outs[shift][...] = value.astype(bf16)
 
         def second_half(weights, stacked, ring, taper, factor, weighted, first, pair_out, image_out):
-            ensemble, factors = load_members(weights, stacked, factor[...])
-            grad = fold(ensemble, [weighted[t] for t in range(slots)])
-            grad = spread(grad, ring[...], taper[...], factors)
-            for t, image in enumerate(images_of(ensemble, grad, ring[...], taper[...], factors)):
+            ensemble, scale = load_members(weights, stacked)
+            grad = fold(ensemble, scale, [weighted[t] for t in range(slots)])
+            grad = spread(grad, ring[...], taper[...], factor[...])
+            for t, image in enumerate(images_of(ensemble, grad, ring[...], taper[...], scale * factor[...])):
                 image_out[t] = image[:, :kept]
             first, second = first[...], grad[:, :kept]
             ratio = closest(first, second)

time: 56.5 us -> 56.5 us (level)
  no operation moved by 1% of the time
where the time goes in v9:
time: 56.5 us; the launch traced here: 56.1 us
  waiting for transfers between devices  22.9 us (41%)
  starting transfers between devices  21.8 us (39%)
  Pallas kernels  9.23 us (16%)
  between operations  1.45 us (3%)
  local copies, waits for them, and re-layouts  0.61 us (1%)
    ppermute x6, starting transfers between devices, trade(): lax.ppermute(blocks[shift], 'band', [(at, (at + shift) % bands) for at in...  9.36 us
    ppermute x6, waiting for transfers between devices, trade(): lax.ppermute(blocks[shift], 'band', [(at, (at + shift) % bands) for at in...  7.51 us
    all_to_all x1, starting transfers between devices, shards(): stacked = lax.all_to_all(pieces, BOTH, 0, 0, tiled=True)  7.3 us
    all_to_all x1, waiting for transfers between devices, shards(): stacked = lax.all_to_all(pieces, BOTH, 0, 0, tiled=True)  6.28 us
    pallas_call x6, Pallas kernels, call(): pl.pallas_call(body, out_shape=tuple((jax.ShapeDtypeStruct(shape, kind) f...  5.92 us
    ppermute x3, waiting for transfers between devices, around(): lax.ppermute(block, 'member', [(at, (at + 2 * shift) % members) for at in...  4.52 us
    all_to_all x1, waiting for transfers between devices, shards(): back = lax.all_to_all(pairs, BOTH, 0, 0, tiled=True)  3.29 us
    all_to_all x1, starting transfers between devices, shards(): back = lax.all_to_all(pairs, BOTH, 0, 0, tiled=True)  2.6 us
  transfers between devices with their start and end apart: 12, of which 11 were waited for; matrix products, arithmetic and copies ran while one was open for 0% of the time, Pallas kernels for 7%

profile of v9, /device:TPU:0, one launch (start us, length us, event | category | flops | bytes accessed | tf_op | source)
XLA Modules:
  0.0 56.1 jit_solution(13594220985461582800)
XLA Ops:
  1.3 2.0 %pack.1 = bf16[32,16,512]{2,1,0:T(8,128)(2,1)} custom-call(s32[1]{0:T(128)S(6)} %copy.15.slot, bf16[1,2,16,4,1440]{4,3,2,1,0:T(4,128)(2,1)} %ensemble.1), custom_call_target="tpu_custom_call" | custom-call | tf_op jit(solution)/shard_map/pack/pallas_call | solution.py:498
  3.3 0.0 copy-start.1
  3.3 0.0 copy-start.2
  3.3 0.0 copy-start.3
  3.3 0.0 copy-start.4
  3.4 0.0 copy-start.5
  3.4 0.0 copy-start.6
  3.4 7.3 %all-to-all-start = ((bf16[32,16,512]{2,1,0:T(8,128)(2,1)}), bf16[32,16,512]{2,1,0:T(8,128)(2,1)S(1)}, u32[]{:S(2)}, u32[]{:S(2)}) async-start(bf16[32,16,512]{2,1,0:T(8,128)(2,1)} %pack.1), calls=%async_computation | async-start | bytes 1048576 | tf_op jit(solution)/shard_map/all_to_all | solution.py:517
  10.7 0.0 copy-start.7
  10.7 0.0 copy-start.8
  10.7 0.0 copy-start.9
  10.7 0.1 pad_add_fusion.here
  10.8 0.0 copy-done.1
  10.8 0.0 copy-done.2
  10.8 0.0 copy-done.3
  10.8 0.0 copy-done.4
  10.8 0.0 copy-done.5
  10.8 0.0 copy-done.6
  10.8 0.6 copy-done.7
  11.4 0.0 copy-done.8
  11.4 0.0 copy-done.9
  11.4 0.0 copy-start
  11.4 2.0 %observe.1 = (bf16[32,512]{1,0:T(8,128)(2,1)S(1)}, bf16[32,512]{1,0:T(8,128)(2,1)S(1)}, bf16[32,512]{1,0:T(8,128)(2,1)S(1)}, bf16[32,512]{1,0:T(8,128)(2,1)S(1)}...) custom-call(s32[2]{0:T(128)S(1)} %pad_add_fusion.here, ...), custom_call_target="tpu_custom_call" | custom-call | tf_op jit(solution)/shard_map/observe/pallas_call | solution.py:133
  13.4 1.8 %collective-permute-start = (bf16[32,512]{1,0:T(8,128)(2,1)S(1)}, bf16[32,512]{1,0:T(8,128)(2,1)S(1)}, u32[]{:S(2)}, u32[]{:S(2)}) collective-permute-start(bf16[32,512]{1,0:T(8,128)(2,1)S(1)} %get-tuple-element.45), channel_id=1, source_target_pairs={{0,1},{1,2},{2,3},{3,0},{4,5},{5,6},{6,7},{7,4},{8,9},{9,10},{10,1... | collective-permute-start | bytes 98312 | tf_op jit(solution)/shard_map/ppermute | solution.py:468
  15.2 1.5 %collective-permute-start.1 = (bf16[32,512]{1,0:T(8,128)(2,1)S(1)}, bf16[32,512]{1,0:T(8,128)(2,1)S(1)}, u32[]{:S(2)}, u32[]{:S(2)}) collective-permute-start(bf16[32,512]{1,0:T(8,128)(2,1)S(1)} %get-tuple-element.46), channel_id=1, source_target_pairs={{0,2},{1,3},{2,0},{3,1},{4,6},{5,7},{6,4},{7,5},{8,10},{9,11},{10,... | collective-permute-start | bytes 98312 | tf_op jit(solution)/shard_map/ppermute | solution.py:468
  16.7 1.5 %collective-permute-start.2 = (bf16[32,512]{1,0:T(8,128)(2,1)S(1)}, bf16[32,512]{1,0:T(8,128)(2,1)S(1)}, u32[]{:S(2)}, u32[]{:S(2)}) collective-permute-start(bf16[32,512]{1,0:T(8,128)(2,1)S(1)} %get-tuple-element.47), channel_id=1, source_target_pairs={{0,3},{1,0},{2,1},{3,2},{4,7},{5,4},{6,5},{7,6},{8,11},{9,8},{10,9... | collective-permute-start | bytes 98312 | tf_op jit(solution)/shard_map/ppermute | solution.py:468
  18.2 0.9 %collective-permute-done.refs_1_ = bf16[32,512]{1,0:T(8,128)(2,1)S(1)} collective-permute-done((bf16[32,512]{1,0:T(8,128)(2,1)S(1)}, bf16[32,512]{1,0:T(8,128)(2,1)S(1)}, u32[]{:S(2)}, u32[]{:S(2)}) %collective-permute-start) | collective-permute-done | bytes 32800 | tf_op jit(solution)/shard_map/ppermute | solution.py:468
  19.1 1.3 %collective-permute-done.1.refs_2_ = bf16[32,512]{1,0:T(8,128)(2,1)S(1)} collective-permute-done((bf16[32,512]{1,0:T(8,128)(2,1)S(1)}, bf16[32,512]{1,0:T(8,128)(2,1)S(1)}, u32[]{:S(2)}, u32[]{:S(2)}) %collective-permute-start.1) | collective-permute-done | bytes 32800 | tf_op jit(solution)/shard_map/ppermute | solution.py:468
  20.4 0.3 collective-permute-done.2.refs_3_
  20.7 6.3 %all-to-all-done.stacked = bf16[32,16,512]{2,1,0:T(8,128)(2,1)S(1)} async-done(((bf16[32,16,512]{2,1,0:T(8,128)(2,1)}), bf16[32,16,512]{2,1,0:T(8,128)(2,1)S(1)}, u32[]{:S(2)}, u32[]{:S(2)}) %all-to-all-start) | async-done | bytes 524320 | tf_op jit(solution)/shard_map/all_to_all | solution.py:517
  26.9 0.0 copy-done
  26.9 1.1 %first_half.1 = (bf16[32,384]{1,0:T(8,128)(2,1)S(1)}, f32[2,32,512]{2,1,0:T(8,128)S(1)}, f32[256,384]{1,0:T(8,128)S(1)}, f32[2,32,384]{2,1,0:T(8,128)S(1)}, f32[4,32,384]{2,1,0:T(8,128)S(1)}) custom-call(f32[8,128]{1,0:T(8,128)S(1)} %get-tuple-element.39.weights, s32[1,128]{1,0:T(1,128)S(1)} %get-tuple-element.43.turn, ...), custom_call_target="tpu_custom_call" | custom-call | tf_op jit(solution)/shard_map/first_half/pallas_call | solution.py:133
  28.0 1.5 %collective-permute-start.5 = (bf16[32,384]{1,0:T(8,128)(2,1)S(1)}, bf16[32,384]{1,0:T(8,128)(2,1)S(1)}, u32[]{:S(2)}, u32[]{:S(2)}) collective-permute-start(bf16[32,384]{1,0:T(8,128)(2,1)S(1)} %get-tuple-element.52), channel_id=1, source_target_pairs={{0,24},{4,28},{8,0},{12,4},{16,8},{20,12},{24,16},{28,20},{1,25},{... | collective-permute-start | bytes 73736 | tf_op jit(solution)/shard_map/ppermute | solution.py:476
  29.6 1.0 %collective-permute-start.4 = (bf16[32,384]{1,0:T(8,128)(2,1)S(1)}, bf16[32,384]{1,0:T(8,128)(2,1)S(1)}, u32[]{:S(2)}, u32[]{:S(2)}) collective-permute-start(bf16[32,384]{1,0:T(8,128)(2,1)S(1)} %get-tuple-element.52), channel_id=1, source_target_pairs={{0,16},{4,20},{8,24},{12,28},{16,0},{20,4},{24,8},{28,12},{1,17},{... | collective-permute-start | bytes 73736 | tf_op jit(solution)/shard_map/ppermute | solution.py:476
  30.5 0.0 collective-permute-start.3
  30.5 1.1 %second_half.1 = (bf16[32,16,384]{2,1,0:T(8,128)(2,1)S(1)}, f32[2,32,384]{2,1,0:T(8,128)S(1)}) custom-call(f32[8,128]{1,0:T(8,128)S(1)} %get-tuple-element.39.weights, bf16[32,16,512]{2,1,0:T(8,128)(2,1)S(1)} %all-to-all-done.stacked, bf16[512,512]{1,0:T(8,128)(2,1)S(1)} %copy-done, bf16[256,256]{1,0:T(8,128)(2,1)S(1)} %get-tuple-element.41.taper, ...), custom_call_target="tpu_custom_call" | custom-call | flops 1000000000 | tf_op jit(solution)/shard_map/second_half/pallas_call | solution.py:133
  31.6 0.3 collective-permute-done.5
  31.9 2.6 %collective-permute-done.4 = bf16[32,384]{1,0:T(8,128)(2,1)S(1)} collective-permute-done((bf16[32,384]{1,0:T(8,128)(2,1)S(1)}, bf16[32,384]{1,0:T(8,128)(2,1)S(1)}, u32[]{:S(2)}, u32[]{:S(2)}) %collective-permute-start.4) | collective-permute-done | bytes 24608 | tf_op jit(solution)/shard_map/ppermute | solution.py:476
  34.6 1.6 %collective-permute-done.3 = bf16[32,384]{1,0:T(8,128)(2,1)S(1)} collective-permute-done((bf16[32,384]{1,0:T(8,128)(2,1)S(1)}, bf16[32,384]{1,0:T(8,128)(2,1)S(1)}, u32[]{:S(2)}, u32[]{:S(2)}) %collective-permute-start.3) | collective-permute-done | bytes 24608 | tf_op jit(solution)/shard_map/ppermute | solution.py:476
  36.2 0.1 collective-permute-start.6
  36.3 1.3 %collective-permute-done.6.refs_1_ = bf16[4,32,384]{2,1,0:T(8,128)(2,1)S(1)} collective-permute-done((bf16[4,32,384]{2,1,0:T(8,128)(2,1)S(1)}, bf16[4,32,384]{2,1,0:T(8,128)(2,1)S(1)}, u32[]{:S(2)}, u32[]{:S(2)}) %collective-permute-start.6) | collective-permute-done | bytes 98336 | tf_op jit(solution)/shard_map/ppermute | solution.py:480
  37.5 1.0 %combine.1 = (bf16[32,16,384]{2,1,0:T(8,128)(2,1)}, f32[2,32,384]{2,1,0:T(8,128)S(1)}) custom-call(bf16[32,16,384]{2,1,0:T(8,128)(2,1)S(1)} %get-tuple-element.50.pairs, f32[2,32,384]{2,1,0:T(8,128)S(1)} %get-tuple-element.51.first, f32[2,32,384]{2,1,0:T(8,128)S(1)} %get-tuple-element.54.second, f32[4,32,384]{2,1,0:T(8,128)S(1)} %get-tuple-element.55.fields, ...), custom_call_target="tpu_custom_call" | custom-call | tf_op jit(solution)/shard_map/combine/pallas_call | solution.py:133
  38.6 2.6 %all-to-all-start.1 = ((bf16[32,16,384]{2,1,0:T(8,128)(2,1)}), bf16[32,16,384]{2,1,0:T(8,128)(2,1)S(1)}, u32[]{:S(2)}, u32[]{:S(2)}) async-start(bf16[32,16,384]{2,1,0:T(8,128)(2,1)} %get-tuple-element.58), calls=%async_computation.1 | async-start | bytes 786432 | tf_op jit(solution)/shard_map/all_to_all | solution.py:572
  41.2 0.2 hand_out.1
  41.4 1.7 %collective-permute-start.7 = (bf16[96,384]{1,0:T(8,128)(2,1)S(1)}, bf16[96,384]{1,0:T(8,128)(2,1)S(1)}, u32[]{:S(2)}, u32[]{:S(2)}) collective-permute-start(bf16[96,384]{1,0:T(8,128)(2,1)S(1)} %get-tuple-element.64), channel_id=1, source_target_pairs={{0,1},{1,2},{2,3},{3,0},{4,5},{5,6},{6,7},{7,4},{8,9},{9,10},{10,1... | collective-permute-start | bytes 221192 | tf_op jit(solution)/shard_map/ppermute | solution.py:468
  43.1 1.5 %collective-permute-start.8 = (bf16[96,384]{1,0:T(8,128)(2,1)S(1)}, bf16[96,384]{1,0:T(8,128)(2,1)S(1)}, u32[]{:S(2)}, u32[]{:S(2)}) collective-permute-start(bf16[96,384]{1,0:T(8,128)(2,1)S(1)} %get-tuple-element.65), channel_id=1, source_target_pairs={{0,2},{1,3},{2,0},{3,1},{4,6},{5,7},{6,4},{7,5},{8,10},{9,11},{10,... | collective-permute-start | bytes 221192 | tf_op jit(solution)/shard_map/ppermute | solution.py:468
  44.6 1.4 %collective-permute-start.9 = (bf16[96,384]{1,0:T(8,128)(2,1)S(1)}, bf16[96,384]{1,0:T(8,128)(2,1)S(1)}, u32[]{:S(2)}, u32[]{:S(2)}) collective-permute-start(bf16[96,384]{1,0:T(8,128)(2,1)S(1)} %get-tuple-element.66), channel_id=1, source_target_pairs={{0,3},{1,0},{2,1},{3,2},{4,7},{5,4},{6,5},{7,6},{8,11},{9,8},{10,9... | collective-permute-start | bytes 221192 | tf_op jit(solution)/shard_map/ppermute | solution.py:468
  46.0 3.6 %collective-permute-done.7.refs_1_ = bf16[96,384]{1,0:T(8,128)(2,1)S(1)} collective-permute-done((bf16[96,384]{1,0:T(8,128)(2,1)S(1)}, bf16[96,384]{1,0:T(8,128)(2,1)S(1)}, u32[]{:S(2)}, u32[]{:S(2)}) %collective-permute-start.7) | collective-permute-done | bytes 73760 | tf_op jit(solution)/shard_map/ppermute | solution.py:468
  49.7 1.4 %collective-permute-done.8.refs_2_ = bf16[96,384]{1,0:T(8,128)(2,1)S(1)} collective-permute-done((bf16[96,384]{1,0:T(8,128)(2,1)S(1)}, bf16[96,384]{1,0:T(8,128)(2,1)S(1)}, u32[]{:S(2)}, u32[]{:S(2)}) %collective-permute-start.8) | collective-permute-done | bytes 73760 | tf_op jit(solution)/shard_map/ppermute | solution.py:468
  51.0 0.0 collective-permute-done.9.refs_3_
  51.0 0.5 join.1
  51.5 3.3 %all-to-all-done.1.back = bf16[32,16,384]{2,1,0:T(8,128)(2,1)S(1)} async-done(((bf16[32,16,384]{2,1,0:T(8,128)(2,1)}), bf16[32,16,384]{2,1,0:T(8,128)(2,1)S(1)}, u32[]{:S(2)}, u32[]{:S(2)}) %all-to-all-start.1) | async-done | bytes 393248 | tf_op jit(solution)/shard_map/all_to_all | solution.py:572
  54.8 1.3 %finish.1 = (f32[1,16,4,1440]{3,2,1,0:T(4,128)}, f32[16,4,1440]{2,1,0:T(4,128)}, f32[2,2,4,1440]{3,2,1,0:T(4,128)}) custom-call(bf16[32,16,384]{2,1,0:T(8,128)(2,1)S(1)} %all-to-all-done.1.back, f32[64,1440]{1,0:T(8,128)S(1)} %get-tuple-element.59.pulled_first, f32[64,1440]{1,0:T(8,128)S(1)} %get-tuple-element.67.pulled_second, ...), custom_call_target="tpu_custom_call" | custom-call | tf_op jit(solution)/shard_map/finish/pallas_call | solution.py:586
  (1 shorter events, 0.0 us)
Async XLA Ops:
  3.3 7.5 %copy-start.1 = (bf16[2,16,4,1440]{3,2,1,0:T(4,128)(2,1)S(1)}, bf16[2,16,4,1440]{3,2,1,0:T(4,128)(2,1)}, u32[]{:S(2)}) copy-start(bf16[2,16,4,1440]{3,2,1,0:T(4,128)(2,1)} %innovation) | copy-start | bytes 1105924
  3.3 7.5 %copy-start.2 = (f32[256,256]{1,0:T(8,128)S(1)}, f32[256,256]{1,0:T(8,128)}, u32[]{:S(2)}) copy-start(f32[256,256]{1,0:T(8,128)} %constant.21.clone.apart) | copy-start | bytes 786436
  3.3 7.5 %copy-start.3 = (bf16[16,4,1440]{2,1,0:T(4,128)(2,1)S(1)}, bf16[16,4,1440]{2,1,0:T(4,128)(2,1)}, u32[]{:S(2)}) copy-start(bf16[16,4,1440]{2,1,0:T(4,128)(2,1)} %precision) | copy-start | bytes 552964
  3.3 7.5 %copy-start.4 = (f32[256,1]{1,0:T(8,128)S(1)}, f32[256,1]{1,0:T(8,128)}, u32[]{:S(2)}) copy-start(f32[256,1]{1,0:T(8,128)} %constant.22.clone.level) | copy-start | bytes 3076
  3.4 7.5 %copy-start.5 = (f32[64,64]{1,0:T(8,128)S(1)}, f32[64,64]{1,0:T(8,128)}, u32[]{:S(2)}) copy-start(f32[64,64]{1,0:T(8,128)} %constant.20.clone.same) | copy-start | bytes 49156
  3.4 7.5 %copy-start.6 = (f32[64,16]{1,0:T(8,128)S(1)}, f32[64,16]{1,0:T(8,128)}, u32[]{:S(2)}) copy-start(f32[64,16]{1,0:T(8,128)} %constant.19.clone.of_level) | copy-start | bytes 12292
  3.4 23.6 %all-to-all-start = ((bf16[32,16,512]{2,1,0:T(8,128)(2,1)}), bf16[32,16,512]{2,1,0:T(8,128)(2,1)S(1)}, u32[]{:S(2)}, u32[]{:S(2)}) async-start(bf16[32,16,512]{2,1,0:T(8,128)(2,1)} %pack.1), calls=%async_computation | async-start | bytes 1048576 | tf_op jit(solution)/shard_map/all_to_all | solution.py:517
  10.7 0.7 %copy-start.7 = (f32[16,16]{1,0:T(8,128)S(1)}, f32[16,16]{1,0:T(8,128)}, u32[]{:S(2)}) copy-start(f32[16,16]{1,0:T(8,128)} %root) | copy-start | bytes 3076
  10.7 0.7 %copy-start.8 = (s32[16]{0:T(128)S(1)}, s32[16]{0:T(128)}, u32[]{:S(2)}) copy-start(s32[16]{0:T(128)} %widths.1) | copy-start | bytes 196
  10.7 0.7 %copy-start.9 = (f32[8]{0:T(128)S(1)}, f32[8]{0:T(128)}, u32[]{:S(2)}) copy-start(f32[8]{0:T(128)} %weight.1) | copy-start | bytes 100
  11.4 15.5 %copy-start = (bf16[512,512]{1,0:T(8,128)(2,1)S(1)}, bf16[512,512]{1,0:T(8,128)(2,1)}, u32[]{:S(2)}) copy-start(bf16[512,512]{1,0:T(8,128)(2,1)} %constant.23.clone.ring) | copy-start | bytes 1572868
  13.4 5.6 %collective-permute-start = (bf16[32,512]{1,0:T(8,128)(2,1)S(1)}, bf16[32,512]{1,0:T(8,128)(2,1)S(1)}, u32[]{:S(2)}, u32[]{:S(2)}) collective-permute-start(bf16[32,512]{1,0:T(8,128)(2,1)S(1)} %get-tuple-element.45), channel_id=1, source_target_pairs={{0,1},{1,2},{2,3},{3,0},{4,5},{5,6},{6,7},{7,4},{8,9},{9,10},{10,1... | collective-permute-start | bytes 98312 | tf_op jit(solution)/shard_map/ppermute | solution.py:468
  15.2 5.2 %collective-permute-start.1 = (bf16[32,512]{1,0:T(8,128)(2,1)S(1)}, bf16[32,512]{1,0:T(8,128)(2,1)S(1)}, u32[]{:S(2)}, u32[]{:S(2)}) collective-permute-start(bf16[32,512]{1,0:T(8,128)(2,1)S(1)} %get-tuple-element.46), channel_id=1, source_target_pairs={{0,2},{1,3},{2,0},{3,1},{4,6},{5,7},{6,4},{7,5},{8,10},{9,11},{10,... | collective-permute-start | bytes 98312 | tf_op jit(solution)/shard_map/ppermute | solution.py:468
  16.7 4.0 %collective-permute-start.2 = (bf16[32,512]{1,0:T(8,128)(2,1)S(1)}, bf16[32,512]{1,0:T(8,128)(2,1)S(1)}, u32[]{:S(2)}, u32[]{:S(2)}) collective-permute-start(bf16[32,512]{1,0:T(8,128)(2,1)S(1)} %get-tuple-element.47), channel_id=1, source_target_pairs={{0,3},{1,0},{2,1},{3,2},{4,7},{5,4},{6,5},{7,6},{8,11},{9,8},{10,9... | collective-permute-start | bytes 98312 | tf_op jit(solution)/shard_map/ppermute | solution.py:468
  28.0 3.9 %collective-permute-start.5 = (bf16[32,384]{1,0:T(8,128)(2,1)S(1)}, bf16[32,384]{1,0:T(8,128)(2,1)S(1)}, u32[]{:S(2)}, u32[]{:S(2)}) collective-permute-start(bf16[32,384]{1,0:T(8,128)(2,1)S(1)} %get-tuple-element.52), channel_id=1, source_target_pairs={{0,24},{4,28},{8,0},{12,4},{16,8},{20,12},{24,16},{28,20},{1,25},{... | collective-permute-start | bytes 73736 | tf_op jit(solution)/shard_map/ppermute | solution.py:476
  29.6 5.0 %collective-permute-start.4 = (bf16[32,384]{1,0:T(8,128)(2,1)S(1)}, bf16[32,384]{1,0:T(8,128)(2,1)S(1)}, u32[]{:S(2)}, u32[]{:S(2)}) collective-permute-start(bf16[32,384]{1,0:T(8,128)(2,1)S(1)} %get-tuple-element.52), channel_id=1, source_target_pairs={{0,16},{4,20},{8,24},{12,28},{16,0},{20,4},{24,8},{28,12},{1,17},{... | collective-permute-start | bytes 73736 | tf_op jit(solution)/shard_map/ppermute | solution.py:476
  30.5 5.6 %collective-permute-start.3 = (bf16[32,384]{1,0:T(8,128)(2,1)S(1)}, bf16[32,384]{1,0:T(8,128)(2,1)S(1)}, u32[]{:S(2)}, u32[]{:S(2)}) collective-permute-start(bf16[32,384]{1,0:T(8,128)(2,1)S(1)} %get-tuple-element.52), channel_id=1, source_target_pairs={{0,8},{4,12},{8,16},{12,20},{16,24},{20,28},{24,0},{28,4},{1,9},{5... | collective-permute-start | bytes 73736 | tf_op jit(solution)/shard_map/ppermute | solution.py:476
  36.2 1.4 %collective-permute-start.6 = (bf16[4,32,384]{2,1,0:T(8,128)(2,1)S(1)}, bf16[4,32,384]{2,1,0:T(8,128)(2,1)S(1)}, u32[]{:S(2)}, u32[]{:S(2)}) collective-permute-start(bf16[4,32,384]{2,1,0:T(8,128)(2,1)S(1)} %pad_maximum_fusion.refs_0_), channel_id=1, source_target_pairs={{0,4},{4,0},{8,12},{12,8},{16,20},{20,16},{24,28},{28,24},{1,5},{5... | collective-permute-start | bytes 294920 | tf_op jit(solution)/shard_map/ppermute | solution.py:480
  38.6 16.2 %all-to-all-start.1 = ((bf16[32,16,384]{2,1,0:T(8,128)(2,1)}), bf16[32,16,384]{2,1,0:T(8,128)(2,1)S(1)}, u32[]{:S(2)}, u32[]{:S(2)}) async-start(bf16[32,16,384]{2,1,0:T(8,128)(2,1)} %get-tuple-element.58), calls=%async_computation.1 | async-start | bytes 786432 | tf_op jit(solution)/shard_map/all_to_all | solution.py:572
  41.4 8.3 %collective-permute-start.7 = (bf16[96,384]{1,0:T(8,128)(2,1)S(1)}, bf16[96,384]{1,0:T(8,128)(2,1)S(1)}, u32[]{:S(2)}, u32[]{:S(2)}) collective-permute-start(bf16[96,384]{1,0:T(8,128)(2,1)S(1)} %get-tuple-element.64), channel_id=1, source_target_pairs={{0,1},{1,2},{2,3},{3,0},{4,5},{5,6},{6,7},{7,4},{8,9},{9,10},{10,1... | collective-permute-start | bytes 221192 | tf_op jit(solution)/shard_map/ppermute | solution.py:468
  43.1 8.0 %collective-permute-start.8 = (bf16[96,384]{1,0:T(8,128)(2,1)S(1)}, bf16[96,384]{1,0:T(8,128)(2,1)S(1)}, u32[]{:S(2)}, u32[]{:S(2)}) collective-permute-start(bf16[96,384]{1,0:T(8,128)(2,1)S(1)} %get-tuple-element.65), channel_id=1, source_target_pairs={{0,2},{1,3},{2,0},{3,1},{4,6},{5,7},{6,4},{7,5},{8,10},{9,11},{10,... | collective-permute-start | bytes 221192 | tf_op jit(solution)/shard_map/ppermute | solution.py:468
  44.6 6.5 %collective-permute-start.9 = (bf16[96,384]{1,0:T(8,128)(2,1)S(1)}, bf16[96,384]{1,0:T(8,128)(2,1)S(1)}, u32[]{:S(2)}, u32[]{:S(2)}) collective-permute-start(bf16[96,384]{1,0:T(8,128)(2,1)S(1)} %get-tuple-element.66), channel_id=1, source_target_pairs={{0,3},{1,0},{2,1},{3,2},{4,7},{5,4},{6,5},{7,6},{8,11},{9,8},{10,9... | collective-permute-start | bytes 221192 | tf_op jit(solution)/shard_map/ppermute | solution.py:468

commit v10 on v9

--- a/solution.py
+++ b/solution.py
@@ -33,6 +33,10 @@
     return jnp.asarray(np.where(distance <= LREACH, values, 0.0), jnp.bfloat16)
 
 
+def lon_kernel(reach, width):
+    return lon_weights(np.abs(np.arange(width + 2 * reach)[:, None] - reach - np.arange(width)[None]))
+
+
 def ring_kernel(width, padded):
     apart = np.abs(np.arange(padded)[:, None] - np.arange(padded)[None])
     inside = (np.arange(padded)[:, None] < width) & (np.arange(padded)[None] < width)
@@ -53,11 +57,25 @@
     return apart.astype(np.float32), level[:, None].astype(np.float32)
 
 
+def halo_apart(levels, rows):
+    own = levels * rows
+    target, source = np.arange(own)[:, None], np.arange(3 * own)[None]
+    shift = (source // own - 1) * rows + source % rows - target % rows
+    same = source // rows % levels == target // rows
+    return np.where(same, np.abs(shift), 1000).astype(np.float32)
+
+
 def row_levels(levels, rows):
     index = np.arange(levels * rows)
     level = index[:, None] // rows == np.arange(levels)[None]
     place = index[:, None] % rows == index[None] % rows
     return level.astype(np.float32), place.astype(np.float32)
+
+
+def partner(at, step, count, sign):
+    if count & (count - 1):
+        return (at + sign * step) % count
+    return at ^ step
 
 
 def exact_dot(matrix, field):
@@ -143,6 +161,39 @@
 
         f32, bf16 = jnp.float32, jnp.bfloat16
 
+        def fold_smooth(own_weight, ensemble, innovation, precision, kernel, out):
+            total = []
+            for at in range(levels):
+                precise = precision[at].astype(f32)
+                part = jnp.zeros((rows, lon), f32)
+                for t in range(slots):
+                    weighted = precise * innovation[t, at].astype(f32)
+                    part = part + ensemble[0, t, at].astype(f32) * weighted
+                total.append(part)
+            total = own_weight[:, :1] * jnp.concatenate(total, axis=0)
+            step = kernel.shape[1]
+            margin = (kernel.shape[0] - step) // 2
+            steps = -(-lon // step)
+            after = steps * step + margin - lon
+            ring = jnp.concatenate([total[:, lon - margin :], total, total[:, :after]], axis=1)
+            ring = ring.astype(bf16)
+            for start in range(0, lon, step):
+                stop = min(lon, start + step)
+                piece = jnp.dot(
+                    ring[:, start : start + kernel.shape[0]], kernel[...], preferred_element_type=f32
+                )
+                out[:, start:stop] = piece[:, : stop - start].astype(bf16)
+
+        def first_gradient(turn, row_span, below, middle, above, apart, grad):
+            span = row_span[:, :1]
+            odd = jnp.full((everything, 1), 1, jnp.int32) * lax.rem(turn[:, :1], 2) == 1
+            even_pair, odd_pair = below[...].astype(f32), above[...].astype(f32)
+            low = jnp.where(odd, even_pair, odd_pair).astype(bf16)
+            high = jnp.where(odd, odd_pair, even_pair).astype(bf16)
+            stacked = jnp.concatenate([low, middle[...], high], axis=0)
+            summed = jnp.dot(near(apart[...], span), stacked, preferred_element_type=f32)
+            grad[...] = ensemble_share / (span * span) * summed
+
         def chosen(turn, blocks, sign):
             if not few:
                 return [blocks[0][band] for band in range(bands)]
@@ -150,7 +201,7 @@
             for band in range(bands):
                 value = blocks[0]
                 for shift in range(1, bands):
-                    value = jnp.where(turn == (band - sign * shift) % bands, blocks[shift], value)
+                    value = jnp.where(turn == partner(band, shift, bands, -sign), blocks[shift], value)
                 turned.append(value)
             return turned
 
@@ -204,9 +255,12 @@
             for member in range(members):
                 outgoing(member).wait()
 
-        def observe(here, widths, weight, innovation, precision, root, of_level, same, apart, level, *refs):
-            outs, results, (static, mixed, pulls) = refs[:-11], refs[-11:-3], refs[-3:]
-            own_static, pulled, mixing, pulling, taper, factor, weights, turn = results
+        def observe(here, widths, weight, marks, innovation, precision, root, of_level, same, apart, level, *refs):
+            outs, results, (static, mixed, pulls) = refs[:-13], refs[-13:-3], refs[-3:]
+            own_static, pulled, mixing, pulling, taper, factor, weights, turn, own_weight, row_span = results
+            own_weight[...] = jnp.full((1, LANES), weight[marks[0]], f32)
+            for at in range(levels):
+                row_span[at * rows : (at + 1) * rows] = jnp.full((rows, LANES), widths[at].astype(f32) + 1.0, f32)
             turn[...] = jnp.full((1, LANES), here[1], jnp.int32)
             for member in range(members):
                 weights[member : member + 1] = jnp.full((1, LANES), weight[member], f32)
@@ -261,7 +315,7 @@
             factor[...] = ensemble_share / (span * span)
 
         def first_half(weights, turn, stacked, ring, taper, factor, *refs):
-            blocks, (total_out, weighted_out, grad_out, image_out, fields) = refs[:-5], refs[-5:]
+            blocks, (total_out, weighted_out, image_out, fields) = refs[:-4], refs[-4:]
             if few:
                 blocks = [block[...].astype(f32) for block in blocks]
             values = jnp.stack(chosen(turn[:, :1], blocks, -1)).astype(f32)
@@ -274,7 +328,6 @@
             ensemble, scale = load_members(weights, stacked)
             weighted = [precise * field[t] for t in range(slots)]
             grad = spread(fold(ensemble, scale, weighted), ring[...], taper[...], factor[...])
-            grad_out[...] = grad[:, :kept]
             total = jnp.zeros((per_member, padded), f32)
             for t, image in enumerate(images_of(ensemble, grad, ring[...], taper[...], scale * factor[...])):
                 image_out[t] = image[:, :kept]
@@ -301,25 +354,18 @@
             for shift in range(bands):
                 value = pieces[0]
                 for band in range(1, bands):
-                    value = jnp.where(turn == (band - shift) % bands, pieces[band], value)
+                    value = jnp.where(turn == partner(band, shift, bands, -1), pieces[band], value)
                 outs[shift][...] = value.astype(bf16)
 
-        def second_half(weights, stacked, ring, taper, factor, weighted, first, pair_out, image_out):
+        def second_half(weights, stacked, ring, taper, factor, weighted, grad_out, image_out):
             ensemble, scale = load_members(weights, stacked)
             grad = fold(ensemble, scale, [weighted[t] for t in range(slots)])
             grad = spread(grad, ring[...], taper[...], factor[...])
             for t, image in enumerate(images_of(ensemble, grad, ring[...], taper[...], scale * factor[...])):
                 image_out[t] = image[:, :kept]
-            first, second = first[...], grad[:, :kept]
-            ratio = closest(first, second)
-            shape = (members * bands, own, kept)
-            second = (second - ratio * first).reshape(shape)
-            lane = lax.broadcasted_iota(jnp.int32, shape, 2)
-            second = jnp.where(lane < lon_share, second, ratio.reshape(1, 1, 1))
-            pair_out[:, :own] = first.reshape(shape).astype(bf16)
-            pair_out[:, own:] = second.astype(bf16)
-
-        def combine(pairs, first, second, fields, mixing, *refs):
+            grad_out[...] = grad[:, :kept].reshape(members * bands, own, kept).astype(bf16)
+
+        def combine(grad, first, second, fields, mixing, *refs):
             blocks, (out, image_out) = refs[:-2], refs[-2:]
             lane = lax.broadcasted_iota(jnp.int32, (1, kept), 1) - lon_share
             every = [
@@ -358,9 +404,7 @@
             row = jnp.broadcast_to(row, (own, kept))
             lane = lax.broadcasted_iota(jnp.int32, (own, kept), 1)
             for block in range(members * bands):
-                values = pairs[block].astype(f32)
-                values = [jnp.where(lane < lon_share, values[:own], row), values[own:]]
-                out[block] = jnp.concatenate(values, axis=0).astype(bf16)
+                out[block] = jnp.where(lane < lon_share, grad[block].astype(f32), row).astype(bf16)
 
         def hand_out(turn, first, second, *refs):
             blocks, outs = refs[: len(totals)], refs[len(totals) :]
@@ -400,7 +444,7 @@
                     images[at, place] = (first[at] + static)[:, :lon_share]
                 images[size:, place] = second[:, :lon_share]
 
-        def finish(back, pulled_first, pulled_second, images, *refs):
+        def finish(back, grad_first, pulled_first, pulled_second, images, *refs):
             (member_out, static_out, image_out), (member, static, image, sems) = refs[:3], refs[3:]
 
             def outgoing(index, source, target):
@@ -445,14 +489,11 @@
                     image[t, level] = values[start : start + rows]
             image_copy.start()
             for source in range(members):
-                parts = []
-                for band in range(bands):
-                    both = back[source * bands + band].astype(f32)
-                    first, second = both[:own], both[own:]
-                    ratio = second[:1, lon_share : lon_share + 1]
-                    values = (on_first + on_second * ratio) * first + on_second * second
-                    parts.append(values[:, :lon_share])
-                values = jnp.concatenate(parts, axis=1)
+                parts = [
+                    back[source * bands + band].astype(f32)[:, :lon_share] for band in range(bands)
+                ]
+                values = on_second * jnp.concatenate(parts, axis=1)
+                values = values + on_first * grad_first[source * own : (source + 1) * own]
                 for share in range(level_share):
                     member[source * level_share + share] = values[share * rows : (share + 1) * rows]
                 outgoing_member(source).start()
@@ -465,7 +506,9 @@
             if not few:
                 return [lax.all_to_all(blocks[0], "band", 0, 0, tiled=True)]
             return [blocks[0]] + [
-                lax.ppermute(blocks[shift], "band", [(at, (at + shift) % bands) for at in range(bands)])
+                lax.ppermute(
+                    blocks[shift], "band", [(at, partner(at, shift, bands, 1)) for at in range(bands)]
+                )
                 for shift in range(1, bands)
             ]
 
@@ -473,7 +516,11 @@
             if not paired:
                 return [lax.all_gather(block, "member")], beside
             here = [block] + [
-                lax.ppermute(block, "member", [(at, (at + 2 * shift) % members) for at in range(members)])
+                lax.ppermute(
+                    block,
+                    "member",
+                    [(at, 2 * partner(at // 2, shift, members // 2, 1) + at % 2) for at in range(members)],
+                )
                 for shift in range(1, members // 2)
             ]
             here, beside = lax.optimization_barrier((jnp.stack(here), beside))
@@ -482,10 +529,15 @@
         def arrivals(here):
             if not paired:
                 return [(0, member, member) for member in range(members)]
-            other = here + 1 - 2 * lax.rem(here, 2)
+            chip, core = lax.div(here, 2), lax.rem(here, 2)
+            ring = (members // 2) & (members // 2 - 1)
             return [
-                (block, shift, lax.rem(source + members - 2 * shift, members))
-                for block, source in enumerate((here, other))
+                (
+                    block,
+                    shift,
+                    2 * (lax.rem(chip + members // 2 - shift, members // 2) if ring else chip ^ shift) + side,
+                )
+                for block, side in enumerate((core, 1 - core))
                 for shift in range(members // 2)
             ]
 
@@ -511,8 +563,8 @@
             compiler_params=pltpu.CompilerParams(vmem_limit_bytes=60 * 2**20),
             name="pack",
         )(member_of_slot, ensemble)
-        pieces, innovation, precision, static_root = lax.optimization_barrier(
-            (pieces, innovation, precision, static_root)
+        pieces, ensemble, innovation, precision, static_root = lax.optimization_barrier(
+            (pieces, ensemble, innovation, precision, static_root)
         )
         stacked = lax.all_to_all(pieces, BOTH, 0, 0, tiled=True)
 
@@ -532,44 +584,59 @@
                 (every_level.shape, f32),
                 ((members, LANES), f32),
                 ((1, LANES), jnp.int32),
+                ((1, LANES), f32),
+                ((everything, LANES), f32),
             ],
-            [here, halfwidth, member_weight],
+            [here, halfwidth, member_weight, member_of_slot],
             [innovation, precision, static_root]
             + [jnp.asarray(table) for table in (of_level, same, apart, every_level)],
             scratch=[((levels, rows, lon), f32)] + [((levels, rows, everything), f32)] * 2,
         )
-        blocks = trade(results[:-8])
-        own_static, pulled, mixing, pulling, taper, factor, weights, turn = results[-8:]
+        blocks = trade(results[:-10])
+        own_static, pulled, mixing, pulling, taper, factor, weights, turn, own_weight, row_span = results[-10:]
+        blocks, ensemble, innovation, precision = lax.optimization_barrier(
+            (blocks, ensemble, innovation, precision)
+        )
+        (smoothed,) = call(
+            fold_smooth,
+            [((everything, lon), bf16)],
+            [],
+            [own_weight, ensemble, innovation, precision, lon_kernel(LANES, 2 * LANES)],
+        )
+        pairs = [(at, at + 1) for at in range(bands - 1)]
+        below, above = [
+            lax.ppermute(smoothed, "band", pairs[start::2] + [(to, at) for at, to in pairs[start::2]])
+            for start in range(2)
+        ]
         ring = ring_kernel(width, padded)
 
-        total, weighted, grad_first, image_first, fields = call(
+        total, weighted, image_first, fields = call(
             first_half,
             [
                 ((per_member, kept), bf16),
                 ((slots, per_member, padded), f32),
-                ((members * per_member, kept), f32),
                 ((slots, per_member, kept), f32),
                 ((arrays, per_member, kept), f32),
             ],
             [],
             [weights, turn, stacked, ring, taper, factor, *blocks],
         )
-        pairs, image_second = call(
+        grad, image_second = call(
             second_half,
-            [((members * bands, 2 * own, kept), bf16), ((slots, per_member, kept), f32)],
+            [((members * bands, own, kept), bf16), ((slots, per_member, kept), f32)],
             [],
-            [weights, stacked, ring, taper, factor, weighted, grad_first],
+            [weights, stacked, ring, taper, factor, weighted],
             flops=10**9,
         )
-        totals, image_second = around(total, image_second)
-
-        pairs, image_second = call(
+        totals, (image_second, below, above) = around(total, (image_second, below, above))
+
+        grad, image_second = call(
             combine,
-            [((members * bands, 2 * own, kept), bf16), ((slots, per_member, kept), f32)],
+            [((members * bands, own, kept), bf16), ((slots, per_member, kept), f32)],
             [],
-            [pairs, image_first, image_second, fields, mixing, *totals],
-        )
-        back = lax.all_to_all(pairs, BOTH, 0, 0, tiled=True)
+            [grad, image_first, image_second, fields, mixing, *totals],
+        )
+        back = lax.all_to_all(grad, BOTH, 0, 0, tiled=True)
         blocks = call(
             hand_out,
             tradable((traded, kept), bf16),
@@ -582,6 +649,12 @@
             [((everything, lon), f32), ((2 * slots * own, lon), f32)],
             [],
             [turn, own_static, pulling, *blocks],
+        )
+        (grad_first,) = call(
+            first_gradient,
+            [((everything, lon), f32)],
+            [],
+            [turn, row_span, below, smoothed, above, jnp.asarray(halo_apart(levels, rows))],
         )
         return pl.pallas_call(
             finish,
@@ -590,7 +663,7 @@
                 jax.ShapeDtypeStruct((levels, rows, lon), f32),
                 jax.ShapeDtypeStruct((slots, level_share, rows, lon), f32),
             ),
-            in_specs=[vmem] * 4,
+            in_specs=[vmem] * 5,
             out_specs=(pl.BlockSpec(memory_space=pltpu.HBM),) * 3,
             scratch_shapes=[
                 pltpu.VMEM((levels, rows, lon), f32),
@@ -600,7 +673,7 @@
             ],
             compiler_params=pltpu.CompilerParams(vmem_limit_bytes=limit),
             name="finish",
-        )(back, pulled, pulled_second, images)
+        )(back, grad_first, pulled, pulled_second, images)
 
     return jax.shard_map(
         shards,

time: 56.5 us -> 52.5 us (0.929)
  waiting for transfers between devices: 22.9 us -> 15.5 us
  starting transfers between devices: 21.8 us -> 24.4 us
  Pallas kernels: 9.23 us -> 9.93 us
    all_to_all x1, waiting for transfers between devices: 3.29 us -> 0.01 us  [shards(): back = lax.all_to_all(grad, BOTH, 0, 0, tiled=True)]
    all_to_all x1, waiting for transfers between devices: 6.28 us -> 3.49 us  [shards(): stacked = lax.all_to_all(pieces, BOTH, 0, 0, tiled=True)]
    all_to_all x1, starting transfers between devices: 2.6 us -> 4.26 us  [shards(): back = lax.all_to_all(grad, BOTH, 0, 0, tiled=True)]
    ppermute x9 -> x11, waiting for transfers between devices: 12 us -> 10.8 us  [the longest x6 9.73 us: trade(): lax.ppermute(blocks[shift], 'band', [(at, partner(at, shift, bands, 1)) f...]
    ppermute x9 -> x11, starting transfers between devices: 11.8 us -> 12.7 us  [the longest x6 7.08 us: trade(): lax.ppermute(blocks[shift], 'band', [(at, partner(at, shift, bands, 1)) f...]
    pallas_call x6 -> x8, Pallas kernels: 5.92 us -> 6.65 us  [call(): pl.pallas_call(body, out_shape=tuple((jax.ShapeDtypeStruct(shape, kind) f...]
  transfers between devices with their start and end apart: 12 -> 14, of which waited for: 11 -> 11; matrix products, arithmetic and copies ran while one was open for 0% -> 0% of each run, Pallas kernels for 7% -> 11%
where the time goes in v10:
time: 52.5 us; the launch traced here: 52.1 us
  starting transfers between devices  24.4 us (46%)
  waiting for transfers between devices  15.5 us (30%)
  Pallas kernels  9.93 us (19%)
  between operations  1.51 us (3%)
  local copies, waits for them, and re-layouts  0.63 us (1%)
    ppermute x6, waiting for transfers between devices, trade(): lax.ppermute(blocks[shift], 'band', [(at, partner(at, shift, bands, 1)) f...  9.73 us
    all_to_all x1, starting transfers between devices, shards(): stacked = lax.all_to_all(pieces, BOTH, 0, 0, tiled=True)  7.3 us
    ppermute x6, starting transfers between devices, trade(): lax.ppermute(blocks[shift], 'band', [(at, partner(at, shift, bands, 1)) f...  7.08 us
    pallas_call x8, Pallas kernels, call(): pl.pallas_call(body, out_shape=tuple((jax.ShapeDtypeStruct(shape, kind) f...  6.65 us
    ppermute x3, starting transfers between devices, around(): lax.ppermute(block, 'member', [(at, 2 * partner(at // 2, shift, members /...  4.45 us
    all_to_all x1, starting transfers between devices, shards(): back = lax.all_to_all(grad, BOTH, 0, 0, tiled=True)  4.26 us
    all_to_all x1, waiting for transfers between devices, shards(): stacked = lax.all_to_all(pieces, BOTH, 0, 0, tiled=True)  3.49 us
    pallas_call x1, Pallas kernels, shards(): pl.pallas_call(pack, out_shape=jax.ShapeDtypeStruct(block, bf16), in_spec...  2.01 us
  transfers between devices with their start and end apart: 14, of which 11 were waited for; matrix products, arithmetic and copies ran while one was open for 0% of the time, Pallas kernels for 11%

profile of v10, /device:TPU:0, one launch (start us, length us, event | category | flops | bytes accessed | tf_op | source)
XLA Modules:
  0.0 52.1 jit_solution(15024170420079166065)
XLA Ops:
  1.3 2.0 %pack.1 = bf16[32,16,512]{2,1,0:T(8,128)(2,1)} custom-call(s32[1]{0:T(128)S(6)} %copy.17.slot.marks, bf16[1,2,16,4,1440]{4,3,2,1,0:T(4,128)(2,1)} %ensemble.2), custom_call_target="tpu_custom_call" | custom-call | tf_op jit(solution)/shard_map/pack/pallas_call | solution.py:550
  3.3 0.0 copy-start
  3.3 0.0 copy-start.2
  3.3 0.0 copy-start.5
  3.3 0.0 copy-start.6
  3.3 0.0 copy-start.8
  3.4 0.0 copy-start.9
  3.4 7.3 %all-to-all-start = ((bf16[32,16,512]{2,1,0:T(8,128)(2,1)}), bf16[32,16,512]{2,1,0:T(8,128)(2,1)S(1)}, u32[]{:S(2)}, u32[]{:S(2)}) async-start(bf16[32,16,512]{2,1,0:T(8,128)(2,1)} %pack.1), calls=%async_computation | async-start | bytes 1048576 | tf_op jit(solution)/shard_map/all_to_all | solution.py:569
  10.7 0.0 copy-start.10
  10.7 0.0 copy-start.11
  10.7 0.0 copy-start.12
  10.7 0.1 pad_add_fusion.here
  10.8 0.0 copy-done
  10.8 0.0 copy-done.2
  10.8 0.0 copy-done.5
  10.8 0.0 copy-done.6
  10.8 0.0 copy-done.8
  10.8 0.0 copy-done.9
  10.8 0.6 %copy-done.10 = f32[16,16]{1,0:T(8,128)S(1)} copy-done((f32[16,16]{1,0:T(8,128)S(1)}, f32[16,16]{1,0:T(8,128)}, u32[]{:S(2)}) %copy-start.10) | copy-done | bytes 1048
  11.4 0.0 copy-done.11
  11.4 0.0 copy-done.12
  11.4 0.0 copy-start.1
  11.4 0.0 copy-start.4
  11.4 2.0 %observe.1 = (bf16[32,512]{1,0:T(8,128)(2,1)S(1)}, bf16[32,512]{1,0:T(8,128)(2,1)S(1)}, bf16[32,512]{1,0:T(8,128)(2,1)S(1)}, bf16[32,512]{1,0:T(8,128)(2,1)S(1)}...) custom-call(s32[2]{0:T(128)S(1)} %pad_add_fusion.here, ...), custom_call_target="tpu_custom_call" | custom-call | tf_op jit(solution)/shard_map/observe/pallas_call | solution.py:151
  13.4 1.8 %collective-permute-start = (bf16[32,512]{1,0:T(8,128)(2,1)S(1)}, bf16[32,512]{1,0:T(8,128)(2,1)S(1)}, u32[]{:S(2)}, u32[]{:S(2)}) collective-permute-start(bf16[32,512]{1,0:T(8,128)(2,1)S(1)} %get-tuple-element.56), channel_id=1, source_target_pairs={{0,1},{1,0},{2,3},{3,2},{4,5},{5,4},{6,7},{7,6},{8,9},{9,8},{10,11... | collective-permute-start | bytes 98312 | tf_op jit(solution)/shard_map/ppermute | solution.py:509
  15.3 1.5 %collective-permute-start.1 = (bf16[32,512]{1,0:T(8,128)(2,1)S(1)}, bf16[32,512]{1,0:T(8,128)(2,1)S(1)}, u32[]{:S(2)}, u32[]{:S(2)}) collective-permute-start(bf16[32,512]{1,0:T(8,128)(2,1)S(1)} %get-tuple-element.57), channel_id=1, source_target_pairs={{0,2},{1,3},{2,0},{3,1},{4,6},{5,7},{6,4},{7,5},{8,10},{9,11},{10,... | collective-permute-start | bytes 98312 | tf_op jit(solution)/shard_map/ppermute | solution.py:509
  16.7 0.3 collective-permute-start.2
  17.0 1.3 %collective-permute-done.refs_1_ = bf16[32,512]{1,0:T(8,128)(2,1)S(1)} collective-permute-done((bf16[32,512]{1,0:T(8,128)(2,1)S(1)}, bf16[32,512]{1,0:T(8,128)(2,1)S(1)}, u32[]{:S(2)}, u32[]{:S(2)}) %collective-permute-start) | collective-permute-done | bytes 32800 | tf_op jit(solution)/shard_map/ppermute | solution.py:509
  18.3 1.2 %collective-permute-done.1.refs_2_ = bf16[32,512]{1,0:T(8,128)(2,1)S(1)} collective-permute-done((bf16[32,512]{1,0:T(8,128)(2,1)S(1)}, bf16[32,512]{1,0:T(8,128)(2,1)S(1)}, u32[]{:S(2)}, u32[]{:S(2)}) %collective-permute-start.1) | collective-permute-done | bytes 32800 | tf_op jit(solution)/shard_map/ppermute | solution.py:509
  19.5 2.2 %collective-permute-done.2.refs_3_ = bf16[32,512]{1,0:T(8,128)(2,1)S(1)} collective-permute-done((bf16[32,512]{1,0:T(8,128)(2,1)S(1)}, bf16[32,512]{1,0:T(8,128)(2,1)S(1)}, u32[]{:S(2)}, u32[]{:S(2)}) %collective-permute-start.2) | collective-permute-done | bytes 32800 | tf_op jit(solution)/shard_map/ppermute | solution.py:509
  21.7 0.0 copy-done.1
  21.7 0.0 copy-done.4
  21.7 0.5 fold_smooth.1.middle
  22.2 0.5 %collective-permute-start.6 = (bf16[64,1440]{1,0:T(8,128)(2,1)S(1)}, bf16[64,1440]{1,0:T(8,128)(2,1)S(1)}, u32[]{:S(2)}, u32[]{:S(2)}) collective-permute-start(bf16[64,1440]{1,0:T(8,128)(2,1)S(1)} %fold_smooth.1.middle), channel_id=1, source_target_pairs={{0,1},{2,3},{1,0},{3,2},{4,5},{6,7},{5,4},{7,6},{8,9},{10,11},{9,8... | collective-permute-start | bytes 552968 | tf_op jit(solution)/shard_map/ppermute | solution.py:608
  22.8 0.7 %collective-permute-start.7 = (bf16[64,1440]{1,0:T(8,128)(2,1)S(1)}, bf16[64,1440]{1,0:T(8,128)(2,1)S(1)}, u32[]{:S(2)}, u32[]{:S(2)}) collective-permute-start(bf16[64,1440]{1,0:T(8,128)(2,1)S(1)} %fold_smooth.1.middle), channel_id=1, source_target_pairs={{1,2},{2,1},{5,6},{6,5},{9,10},{10,9},{13,14},{14,13},{17,18},{18,... | collective-permute-start | bytes 552968 | tf_op jit(solution)/shard_map/ppermute | solution.py:608
  23.4 3.5 %all-to-all-done.stacked = bf16[32,16,512]{2,1,0:T(8,128)(2,1)S(1)} async-done(((bf16[32,16,512]{2,1,0:T(8,128)(2,1)}), bf16[32,16,512]{2,1,0:T(8,128)(2,1)S(1)}, u32[]{:S(2)}, u32[]{:S(2)}) %all-to-all-start) | async-done | bytes 524320 | tf_op jit(solution)/shard_map/all_to_all | solution.py:569
  26.9 0.0 copy-done.3
  26.9 1.1 %first_half.1 = (bf16[32,384]{1,0:T(8,128)(2,1)S(1)}, f32[2,32,512]{2,1,0:T(8,128)S(1)}, f32[2,32,384]{2,1,0:T(8,128)S(1)}, f32[4,32,384]{2,1,0:T(8,128)S(1)}) custom-call(f32[8,128]{1,0:T(8,128)S(1)} %get-tuple-element.50.weights, s32[1,128]{1,0:T(1,128)S(1)} %get-tuple-element.54.turn, bf16[32,16,512]{2,1,0:T(8,128)(2,1)S(1)} %all-to-all-done.stacked, ...), custom_call_target="tpu_custom_call" | custom-call | tf_op jit(solution)/shard_map/first_half/pallas_call | solution.py:151
  28.0 1.6 %collective-permute-start.5 = (bf16[32,384]{1,0:T(8,128)(2,1)S(1)}, bf16[32,384]{1,0:T(8,128)(2,1)S(1)}, u32[]{:S(2)}, u32[]{:S(2)}) collective-permute-start(bf16[32,384]{1,0:T(8,128)(2,1)S(1)} %get-tuple-element.67), channel_id=1, source_target_pairs={{0,24},{4,28},{8,16},{12,20},{16,8},{20,12},{24,0},{28,4},{1,25},{... | collective-permute-start | bytes 73736 | tf_op jit(solution)/shard_map/ppermute | solution.py:519
  29.6 1.1 %collective-permute-start.4 = (bf16[32,384]{1,0:T(8,128)(2,1)S(1)}, bf16[32,384]{1,0:T(8,128)(2,1)S(1)}, u32[]{:S(2)}, u32[]{:S(2)}) collective-permute-start(bf16[32,384]{1,0:T(8,128)(2,1)S(1)} %get-tuple-element.67), channel_id=1, source_target_pairs={{0,16},{4,20},{8,24},{12,28},{16,0},{20,4},{24,8},{28,12},{1,17},{... | collective-permute-start | bytes 73736 | tf_op jit(solution)/shard_map/ppermute | solution.py:519
  30.6 1.9 %collective-permute-start.3 = (bf16[32,384]{1,0:T(8,128)(2,1)S(1)}, bf16[32,384]{1,0:T(8,128)(2,1)S(1)}, u32[]{:S(2)}, u32[]{:S(2)}) collective-permute-start(bf16[32,384]{1,0:T(8,128)(2,1)S(1)} %get-tuple-element.67), channel_id=1, source_target_pairs={{0,8},{4,12},{8,0},{12,4},{16,24},{20,28},{24,16},{28,20},{1,9},{5... | collective-permute-start | bytes 73736 | tf_op jit(solution)/shard_map/ppermute | solution.py:519
  32.5 1.1 %second_half.1 = (bf16[32,8,384]{2,1,0:T(8,128)(2,1)S(1)}, f32[2,32,384]{2,1,0:T(8,128)S(1)}) custom-call(f32[8,128]{1,0:T(8,128)S(1)} %get-tuple-element.50.weights, bf16[32,16,512]{2,1,0:T(8,128)(2,1)S(1)} %all-to-all-done.stacked, bf16[512,512]{1,0:T(8,128)(2,1)S(1)} %copy-done.3, bf16[256,256]{1,0:T(8,128)(2,1)S(1)} %get-tuple-element.52.taper, ...), custom_call_target="tpu_custom_call" | custom-call | flops 1000000000 | tf_op jit(solution)/shard_map/second_half/pallas_call | solution.py:151
  33.6 0.2 collective-permute-done.5
  33.7 0.6 %collective-permute-done.4 = bf16[32,384]{1,0:T(8,128)(2,1)S(1)} collective-permute-done((bf16[32,384]{1,0:T(8,128)(2,1)S(1)}, bf16[32,384]{1,0:T(8,128)(2,1)S(1)}, u32[]{:S(2)}, u32[]{:S(2)}) %collective-permute-start.4) | collective-permute-done | bytes 24608 | tf_op jit(solution)/shard_map/ppermute | solution.py:519
  34.3 0.3 collective-permute-done.3
  34.6 0.0 collective-permute-done.6.below
  34.6 0.0 collective-permute-done.7.above
  34.6 0.1 collective-permute-start.8
  34.7 1.3 %collective-permute-done.8.refs_1_ = bf16[4,32,384]{2,1,0:T(8,128)(2,1)S(1)} collective-permute-done((bf16[4,32,384]{2,1,0:T(8,128)(2,1)S(1)}, bf16[4,32,384]{2,1,0:T(8,128)(2,1)S(1)}, u32[]{:S(2)}, u32[]{:S(2)}) %collective-permute-start.8) | collective-permute-done | bytes 98336 | tf_op jit(solution)/shard_map/ppermute | solution.py:527
  36.0 1.0 %combine.1 = (bf16[32,8,384]{2,1,0:T(8,128)(2,1)}, f32[2,32,384]{2,1,0:T(8,128)S(1)}) custom-call(bf16[32,8,384]{2,1,0:T(8,128)(2,1)S(1)} %get-tuple-element.65.grad, f32[2,32,384]{2,1,0:T(8,128)S(1)} %get-tuple-element.66.first, f32[2,32,384]{2,1,0:T(8,128)S(1)} %get-tuple-element.73.second, f32[4,32,384]{2,1,0:T(8,128)S(1)} %get-tuple-element.74.fields, ...), custom_call_target="tpu_custom_call" | custom-call | tf_op jit(solution)/shard_map/combine/pallas_call | solution.py:151
  36.9 4.3 %all-to-all-start.1 = ((bf16[32,8,384]{2,1,0:T(8,128)(2,1)}), bf16[32,8,384]{2,1,0:T(8,128)(2,1)S(1)}, u32[]{:S(2)}, u32[]{:S(2)}) async-start(bf16[32,8,384]{2,1,0:T(8,128)(2,1)} %get-tuple-element.77), calls=%async_computation.1 | async-start | bytes 393216 | tf_op jit(solution)/shard_map/all_to_all | solution.py:639
  41.2 0.0 copy-start.7
  41.2 0.2 hand_out.1
  41.4 1.8 %collective-permute-start.9 = (bf16[96,384]{1,0:T(8,128)(2,1)S(1)}, bf16[96,384]{1,0:T(8,128)(2,1)S(1)}, u32[]{:S(2)}, u32[]{:S(2)}) collective-permute-start(bf16[96,384]{1,0:T(8,128)(2,1)S(1)} %get-tuple-element.86), channel_id=1, source_target_pairs={{0,1},{1,0},{2,3},{3,2},{4,5},{5,4},{6,7},{7,6},{8,9},{9,8},{10,11... | collective-permute-start | bytes 221192 | tf_op jit(solution)/shard_map/ppermute | solution.py:509
  43.3 1.5 %collective-permute-start.10 = (bf16[96,384]{1,0:T(8,128)(2,1)S(1)}, bf16[96,384]{1,0:T(8,128)(2,1)S(1)}, u32[]{:S(2)}, u32[]{:S(2)}) collective-permute-start(bf16[96,384]{1,0:T(8,128)(2,1)S(1)} %get-tuple-element.87), channel_id=1, source_target_pairs={{0,2},{1,3},{2,0},{3,1},{4,6},{5,7},{6,4},{7,5},{8,10},{9,11},{10,... | collective-permute-start | bytes 221192 | tf_op jit(solution)/shard_map/ppermute | solution.py:509
  44.7 0.3 collective-permute-start.11
  45.0 0.0 copy-done.7
  45.0 0.3 first_gradient.1.grad_first
  45.3 1.6 %collective-permute-done.9.refs_1_ = bf16[96,384]{1,0:T(8,128)(2,1)S(1)} collective-permute-done((bf16[96,384]{1,0:T(8,128)(2,1)S(1)}, bf16[96,384]{1,0:T(8,128)(2,1)S(1)}, u32[]{:S(2)}, u32[]{:S(2)}) %collective-permute-start.9) | collective-permute-done | bytes 73760 | tf_op jit(solution)/shard_map/ppermute | solution.py:509
  47.0 1.9 %collective-permute-done.10.refs_2_ = bf16[96,384]{1,0:T(8,128)(2,1)S(1)} collective-permute-done((bf16[96,384]{1,0:T(8,128)(2,1)S(1)}, bf16[96,384]{1,0:T(8,128)(2,1)S(1)}, u32[]{:S(2)}, u32[]{:S(2)}) %collective-permute-start.10) | collective-permute-done | bytes 73760 | tf_op jit(solution)/shard_map/ppermute | solution.py:509
  48.8 1.5 %collective-permute-done.11.refs_3_ = bf16[96,384]{1,0:T(8,128)(2,1)S(1)} collective-permute-done((bf16[96,384]{1,0:T(8,128)(2,1)S(1)}, bf16[96,384]{1,0:T(8,128)(2,1)S(1)}, u32[]{:S(2)}, u32[]{:S(2)}) %collective-permute-start.11) | collective-permute-done | bytes 73760 | tf_op jit(solution)/shard_map/ppermute | solution.py:509
  50.3 0.5 join.1
  50.8 0.0 all-to-all-done.1.back
  50.8 1.3 %finish.1 = (f32[1,16,4,1440]{3,2,1,0:T(4,128)}, f32[16,4,1440]{2,1,0:T(4,128)}, f32[2,2,4,1440]{3,2,1,0:T(4,128)}) custom-call(bf16[32,8,384]{2,1,0:T(8,128)(2,1)S(1)} %all-to-all-done.1.back, f32[64,1440]{1,0:T(8,128)S(1)} %first_gradient.1.grad_first, f32[64,1440]{1,0:T(8,128)S(1)} %get-tuple-element.81.pulled_first, ...), custom_call_target="tpu_custom_call" | custom-call | tf_op jit(solution)/shard_map/finish/pallas_call | solution.py:659
  (2 shorter events, 0.0 us)
Async XLA Ops:
  3.3 7.5 %copy-start = (bf16[2,16,4,1440]{3,2,1,0:T(4,128)(2,1)S(1)}, bf16[2,16,4,1440]{3,2,1,0:T(4,128)(2,1)}, u32[]{:S(2)}) copy-start(bf16[2,16,4,1440]{3,2,1,0:T(4,128)(2,1)} %innovation.1) | copy-start | bytes 1105924
  3.3 7.5 %copy-start.2 = (bf16[16,4,1440]{2,1,0:T(4,128)(2,1)S(1)}, bf16[16,4,1440]{2,1,0:T(4,128)(2,1)}, u32[]{:S(2)}) copy-start(bf16[16,4,1440]{2,1,0:T(4,128)(2,1)} %precision.1) | copy-start | bytes 552964
  3.3 7.5 %copy-start.5 = (f32[256,256]{1,0:T(8,128)S(1)}, f32[256,256]{1,0:T(8,128)}, u32[]{:S(2)}) copy-start(f32[256,256]{1,0:T(8,128)} %constant.25.clone.apart) | copy-start | bytes 786436
  3.3 7.5 %copy-start.6 = (f32[256,1]{1,0:T(8,128)S(1)}, f32[256,1]{1,0:T(8,128)}, u32[]{:S(2)}) copy-start(f32[256,1]{1,0:T(8,128)} %constant.26.clone.level) | copy-start | bytes 3076
  3.3 7.5 %copy-start.8 = (f32[64,16]{1,0:T(8,128)S(1)}, f32[64,16]{1,0:T(8,128)}, u32[]{:S(2)}) copy-start(f32[64,16]{1,0:T(8,128)} %constant.23.clone.of_level) | copy-start | bytes 12292
  3.4 7.5 %copy-start.9 = (f32[64,64]{1,0:T(8,128)S(1)}, f32[64,64]{1,0:T(8,128)}, u32[]{:S(2)}) copy-start(f32[64,64]{1,0:T(8,128)} %constant.24.clone.same) | copy-start | bytes 49156
  3.4 23.6 %all-to-all-start = ((bf16[32,16,512]{2,1,0:T(8,128)(2,1)}), bf16[32,16,512]{2,1,0:T(8,128)(2,1)S(1)}, u32[]{:S(2)}, u32[]{:S(2)}) async-start(bf16[32,16,512]{2,1,0:T(8,128)(2,1)} %pack.1), calls=%async_computation | async-start | bytes 1048576 | tf_op jit(solution)/shard_map/all_to_all | solution.py:569
  10.7 0.7 %copy-start.10 = (f32[16,16]{1,0:T(8,128)S(1)}, f32[16,16]{1,0:T(8,128)}, u32[]{:S(2)}) copy-start(f32[16,16]{1,0:T(8,128)} %root) | copy-start | bytes 3076
  10.7 0.7 %copy-start.11 = (s32[16]{0:T(128)S(1)}, s32[16]{0:T(128)}, u32[]{:S(2)}) copy-start(s32[16]{0:T(128)} %widths.1) | copy-start | bytes 196
  10.7 0.7 %copy-start.12 = (f32[8]{0:T(128)S(1)}, f32[8]{0:T(128)}, u32[]{:S(2)}) copy-start(f32[8]{0:T(128)} %weight.1) | copy-start | bytes 100
  11.4 10.3 %copy-start.1 = (bf16[1,2,16,4,1440]{4,3,2,1,0:T(4,128)(2,1)S(1)}, bf16[1,2,16,4,1440]{4,3,2,1,0:T(4,128)(2,1)}, u32[]{:S(2)}) copy-start(bf16[1,2,16,4,1440]{4,3,2,1,0:T(4,128)(2,1)} %ensemble.2) | copy-start | bytes 1105924
  11.4 10.3 %copy-start.4 = (bf16[512,256]{1,0:T(8,128)(2,1)S(1)}, bf16[512,256]{1,0:T(8,128)(2,1)}, u32[]{:S(2)}) copy-start(bf16[512,256]{1,0:T(8,128)(2,1)} %constant.27.clone.kernel) | copy-start | bytes 786436
  13.4 4.9 %collective-permute-start = (bf16[32,512]{1,0:T(8,128)(2,1)S(1)}, bf16[32,512]{1,0:T(8,128)(2,1)S(1)}, u32[]{:S(2)}, u32[]{:S(2)}) collective-permute-start(bf16[32,512]{1,0:T(8,128)(2,1)S(1)} %get-tuple-element.56), channel_id=1, source_target_pairs={{0,1},{1,0},{2,3},{3,2},{4,5},{5,4},{6,7},{7,6},{8,9},{9,8},{10,11... | collective-permute-start | bytes 98312 | tf_op jit(solution)/shard_map/ppermute | solution.py:509
  15.3 4.3 %collective-permute-start.1 = (bf16[32,512]{1,0:T(8,128)(2,1)S(1)}, bf16[32,512]{1,0:T(8,128)(2,1)S(1)}, u32[]{:S(2)}, u32[]{:S(2)}) collective-permute-start(bf16[32,512]{1,0:T(8,128)(2,1)S(1)} %get-tuple-element.57), channel_id=1, source_target_pairs={{0,2},{1,3},{2,0},{3,1},{4,6},{5,7},{6,4},{7,5},{8,10},{9,11},{10,... | collective-permute-start | bytes 98312 | tf_op jit(solution)/shard_map/ppermute | solution.py:509
  16.7 5.0 %collective-permute-start.2 = (bf16[32,512]{1,0:T(8,128)(2,1)S(1)}, bf16[32,512]{1,0:T(8,128)(2,1)S(1)}, u32[]{:S(2)}, u32[]{:S(2)}) collective-permute-start(bf16[32,512]{1,0:T(8,128)(2,1)S(1)} %get-tuple-element.58), channel_id=1, source_target_pairs={{0,3},{1,2},{2,1},{3,0},{4,7},{5,6},{6,5},{7,4},{8,11},{9,10},{10,... | collective-permute-start | bytes 98312 | tf_op jit(solution)/shard_map/ppermute | solution.py:509
  21.7 5.2 %copy-start.3 = (bf16[512,512]{1,0:T(8,128)(2,1)S(1)}, bf16[512,512]{1,0:T(8,128)(2,1)}, u32[]{:S(2)}) copy-start(bf16[512,512]{1,0:T(8,128)(2,1)} %constant.28.clone.ring) | copy-start | bytes 1572868
  22.2 12.4 %collective-permute-start.6 = (bf16[64,1440]{1,0:T(8,128)(2,1)S(1)}, bf16[64,1440]{1,0:T(8,128)(2,1)S(1)}, u32[]{:S(2)}, u32[]{:S(2)}) collective-permute-start(bf16[64,1440]{1,0:T(8,128)(2,1)S(1)} %fold_smooth.1.middle), channel_id=1, source_target_pairs={{0,1},{2,3},{1,0},{3,2},{4,5},{6,7},{5,4},{7,6},{8,9},{10,11},{9,8... | collective-permute-start | bytes 552968 | tf_op jit(solution)/shard_map/ppermute | solution.py:608
  22.8 11.8 %collective-permute-start.7 = (bf16[64,1440]{1,0:T(8,128)(2,1)S(1)}, bf16[64,1440]{1,0:T(8,128)(2,1)S(1)}, u32[]{:S(2)}, u32[]{:S(2)}) collective-permute-start(bf16[64,1440]{1,0:T(8,128)(2,1)S(1)} %fold_smooth.1.middle), channel_id=1, source_target_pairs={{1,2},{2,1},{5,6},{6,5},{9,10},{10,9},{13,14},{14,13},{17,18},{18,... | collective-permute-start | bytes 552968 | tf_op jit(solution)/shard_map/ppermute | solution.py:608
  28.0 5.7 %collective-permute-start.5 = (bf16[32,384]{1,0:T(8,128)(2,1)S(1)}, bf16[32,384]{1,0:T(8,128)(2,1)S(1)}, u32[]{:S(2)}, u32[]{:S(2)}) collective-permute-start(bf16[32,384]{1,0:T(8,128)(2,1)S(1)} %get-tuple-element.67), channel_id=1, source_target_pairs={{0,24},{4,28},{8,16},{12,20},{16,8},{20,12},{24,0},{28,4},{1,25},{... | collective-permute-start | bytes 73736 | tf_op jit(solution)/shard_map/ppermute | solution.py:519
  29.6 4.7 %collective-permute-start.4 = (bf16[32,384]{1,0:T(8,128)(2,1)S(1)}, bf16[32,384]{1,0:T(8,128)(2,1)S(1)}, u32[]{:S(2)}, u32[]{:S(2)}) collective-permute-start(bf16[32,384]{1,0:T(8,128)(2,1)S(1)} %get-tuple-element.67), channel_id=1, source_target_pairs={{0,16},{4,20},{8,24},{12,28},{16,0},{20,4},{24,8},{28,12},{1,17},{... | collective-permute-start | bytes 73736 | tf_op jit(solution)/shard_map/ppermute | solution.py:519
  30.6 3.9 %collective-permute-start.3 = (bf16[32,384]{1,0:T(8,128)(2,1)S(1)}, bf16[32,384]{1,0:T(8,128)(2,1)S(1)}, u32[]{:S(2)}, u32[]{:S(2)}) collective-permute-start(bf16[32,384]{1,0:T(8,128)(2,1)S(1)} %get-tuple-element.67), channel_id=1, source_target_pairs={{0,8},{4,12},{8,0},{12,4},{16,24},{20,28},{24,16},{28,20},{1,9},{5... | collective-permute-start | bytes 73736 | tf_op jit(solution)/shard_map/ppermute | solution.py:519
  34.6 1.4 %collective-permute-start.8 = (bf16[4,32,384]{2,1,0:T(8,128)(2,1)S(1)}, bf16[4,32,384]{2,1,0:T(8,128)(2,1)S(1)}, u32[]{:S(2)}, u32[]{:S(2)}) collective-permute-start(bf16[4,32,384]{2,1,0:T(8,128)(2,1)S(1)} %pad_maximum_fusion.refs_0_), channel_id=1, source_target_pairs={{0,4},{4,0},{8,12},{12,8},{16,20},{20,16},{24,28},{28,24},{1,5},{5... | collective-permute-start | bytes 294920 | tf_op jit(solution)/shard_map/ppermute | solution.py:527
  36.9 13.8 %all-to-all-start.1 = ((bf16[32,8,384]{2,1,0:T(8,128)(2,1)}), bf16[32,8,384]{2,1,0:T(8,128)(2,1)S(1)}, u32[]{:S(2)}, u32[]{:S(2)}) async-start(bf16[32,8,384]{2,1,0:T(8,128)(2,1)} %get-tuple-element.77), calls=%async_computation.1 | async-start | bytes 393216 | tf_op jit(solution)/shard_map/all_to_all | solution.py:639
  41.2 3.8 %copy-start.7 = (f32[64,192]{1,0:T(8,128)S(1)}, f32[64,192]{1,0:T(8,128)}, u32[]{:S(2)}) copy-start(f32[64,192]{1,0:T(8,128)} %constant.29.clone.apart) | copy-start | bytes 147460
  41.4 5.5 %collective-permute-start.9 = (bf16[96,384]{1,0:T(8,128)(2,1)S(1)}, bf16[96,384]{1,0:T(8,128)(2,1)S(1)}, u32[]{:S(2)}, u32[]{:S(2)}) collective-permute-start(bf16[96,384]{1,0:T(8,128)(2,1)S(1)} %get-tuple-element.86), channel_id=1, source_target_pairs={{0,1},{1,0},{2,3},{3,2},{4,5},{5,4},{6,7},{7,6},{8,9},{9,8},{10,11... | collective-permute-start | bytes 221192 | tf_op jit(solution)/shard_map/ppermute | solution.py:509
  43.3 5.6 %collective-permute-start.10 = (bf16[96,384]{1,0:T(8,128)(2,1)S(1)}, bf16[96,384]{1,0:T(8,128)(2,1)S(1)}, u32[]{:S(2)}, u32[]{:S(2)}) collective-permute-start(bf16[96,384]{1,0:T(8,128)(2,1)S(1)} %get-tuple-element.87), channel_id=1, source_target_pairs={{0,2},{1,3},{2,0},{3,1},{4,6},{5,7},{6,4},{7,5},{8,10},{9,11},{10,... | collective-permute-start | bytes 221192 | tf_op jit(solution)/shard_map/ppermute | solution.py:509
  44.7 5.6 %collective-permute-start.11 = (bf16[96,384]{1,0:T(8,128)(2,1)S(1)}, bf16[96,384]{1,0:T(8,128)(2,1)S(1)}, u32[]{:S(2)}, u32[]{:S(2)}) collective-permute-start(bf16[96,384]{1,0:T(8,128)(2,1)S(1)} %get-tuple-element.88), channel_id=1, source_target_pairs={{0,3},{1,2},{2,1},{3,0},{4,7},{5,6},{6,5},{7,4},{8,11},{9,10},{10,... | collective-permute-start | bytes 221192 | tf_op jit(solution)/shard_map/ppermute | solution.py:509

commit v11 on v10

--- a/solution.py
+++ b/solution.py
@@ -255,40 +255,61 @@
             for member in range(members):
                 outgoing(member).wait()
 
-        def observe(here, widths, weight, marks, innovation, precision, root, of_level, same, apart, level, *refs):
-            outs, results, (static, mixed, pulls) = refs[:-13], refs[-13:-3], refs[-3:]
-            own_static, pulled, mixing, pulling, taper, factor, weights, turn, own_weight, row_span = results
-            own_weight[...] = jnp.full((1, LANES), weight[marks[0]], f32)
-            for at in range(levels):
-                row_span[at * rows : (at + 1) * rows] = jnp.full((rows, LANES), widths[at].astype(f32) + 1.0, f32)
-            turn[...] = jnp.full((1, LANES), here[1], jnp.int32)
-            for member in range(members):
-                weights[member : member + 1] = jnp.full((1, LANES), weight[member], f32)
-            total = []
-            for at in range(levels):
-                precise = precision[at].astype(f32)
-                part = precise * innovation[0, at].astype(f32)
-                for t in range(1, slots):
-                    part = part + precise * innovation[t, at].astype(f32)
-                total.append(part)
-            out_of = lax.dot_general(
-                exact_dot(of_level[...], static_share * root[...]),
-                of_level[...],
+        def rows_between(root, of_level, same):
+            wide = lax.dot_general(
+                exact_dot(of_level, static_share * root),
+                of_level,
                 (((1,), (1,)), ((), ())),
                 precision=lax.Precision.HIGHEST,
                 preferred_element_type=f32,
             )
-            out_of = out_of * same[...]
+            return wide * same
+
+        def observe(place, turn, innovation, precision, root, of_level, same, *refs):
+            outs, (own_static, pulled) = refs[:-2], refs[-2:]
+            out_of = rows_between(root[...], of_level[...], same[...])
+            row = lax.broadcasted_iota(jnp.int32, (own, everything), 0)
+            column = lax.broadcasted_iota(jnp.int32, (own, everything), 1)
+            picker = (column == place[:, :1] * own + row).astype(f32)
+            out_of_own = exact_dot(picker, out_of)
+            precise = jnp.concatenate([precision[at].astype(f32) for at in range(levels)], axis=0)
+            innovations = [
+                jnp.concatenate([innovation[t, at].astype(f32) for at in range(levels)], axis=0)
+                for t in range(slots)
+            ]
+            total = precise * innovations[0]
+            for t in range(1, slots):
+                total = total + precise * innovations[t]
+            high = total.astype(bf16)
+            low = (total - high.astype(f32)).astype(bf16)
             into = out_of.T
-            back = exact_dot(into, jnp.concatenate(total, axis=0))
+            back = parts_dot(into, high) + jnp.dot(into.astype(bf16), low, preferred_element_type=f32)
             pulled[...] = back
-            forth = exact_dot(out_of, back)
-            both = exact_dot(out_of, into)
+            values = [
+                jnp.dot(picker.astype(bf16), field.astype(bf16), preferred_element_type=f32)
+                for field in innovations + [precise]
+            ]
+            values = jnp.concatenate(values + [exact_dot(out_of_own, back)], axis=0)
+            tail = jnp.zeros((values.shape[0], padded - width), f32)
+            pieces = [window(values, band, lon_share, halo, tail) for band in range(bands)]
+            for band, piece in enumerate(pieces):
+                own_static[band] = piece[(slots + 1) * own :, :kept]
+            deal(turn[:, :1], pieces, outs)
+
+        def prepare(here, widths, weight, marks, root, of_level, same, apart, level, *refs):
+            mixing, pulling, taper, factor, weights, own_weight, row_span, mixed, pulls = refs
+            for member in range(members):
+                weights[member : member + 1] = jnp.full((1, LANES), weight[member], f32)
+            own_weight[...] = jnp.full((1, LANES), weight[marks[0]], f32)
             for at in range(levels):
-                static[at] = forth[at * rows : (at + 1) * rows]
+                row_span[at * rows : (at + 1) * rows] = jnp.full(
+                    (rows, LANES), widths[at].astype(f32) + 1.0, f32
+                )
+            out_of = rows_between(root[...], of_level[...], same[...])
+            both = exact_dot(out_of, out_of.T)
+            for at in range(levels):
                 mixed[at] = both[at * rows : (at + 1) * rows]
                 pulls[at] = out_of[at * rows : (at + 1) * rows]
-            picked = [here[0] * level_share + share for share in range(level_share)]
             arriving = [
                 member * level_share + share
                 for _, _, member in arrivals(here[0])
@@ -300,17 +321,10 @@
             mixing[...] = exact_dot(
                 jnp.concatenate([mixed[at] for at in arriving], axis=0), (column == own_column).astype(f32)
             ).T
-            parts = [innovation[t, at].astype(f32) for t in range(slots) for at in picked]
-            parts += [precision[at].astype(f32) for at in picked] + [static[at] for at in picked]
-            values = jnp.concatenate(parts, axis=0)
-            tail = jnp.zeros((values.shape[0], padded - width), f32)
-            pieces = [window(values, band, lon_share, halo, tail) for band in range(bands)]
-            for band, piece in enumerate(pieces):
-                own_static[band] = piece[(slots + 1) * own :, :kept]
-            deal(turn[:, :1], pieces, outs)
             span = jnp.ones(level.shape, f32)
-            for at, which in enumerate(picked):
-                span = span + jnp.where(level[...] == at, widths[which].astype(f32), 0.0)
+            for share in range(level_share):
+                which = here[0] * level_share + share
+                span = span + jnp.where(level[...] == share, widths[which].astype(f32), 0.0)
             taper[...] = near(apart[...], span[: apart.shape[0]])
             factor[...] = ensemble_share / (span * span)
 
@@ -544,7 +558,9 @@
         def tradable(shape, kind):
             return [(shape, kind)] * bands if few else [((bands,) + shape, kind)]
 
-        here = jnp.stack([lax.axis_index("member"), lax.axis_index("band")]).astype(jnp.int32)
+        place = jnp.full((1, LANES), lax.axis_index("member"), jnp.int32)
+        turn = jnp.full((1, LANES), lax.axis_index("band"), jnp.int32)
+        here = lax.axis_index("member").astype(jnp.int32).reshape(1)
 
         block = (members * bands, slots * own, padded)
         pieces = pl.pallas_call(
@@ -572,28 +588,30 @@
         apart, level = row_apart(bands, level_share, rows, copies)
         every_level = np.tile(level, (members // copies, 1))
         block = (arrays * own, padded)
+        between = [static_root] + [jnp.asarray(table) for table in (of_level, same)]
         results = call(
             observe,
-            tradable(block, bf16)
-            + [
-                ((bands, own, kept), f32),
-                ((everything, lon), f32),
+            tradable(block, bf16) + [((bands, own, kept), f32), ((everything, lon), f32)],
+            [],
+            [place, turn, innovation, precision, *between],
+        )
+        blocks, (own_static, pulled) = trade(results[:-2]), results[-2:]
+        own_static, between = lax.optimization_barrier((own_static, between))
+        mixing, pulling, taper, factor, weights, own_weight, row_span = call(
+            prepare,
+            [
                 ((own, everything), f32),
                 ((everything, everything), f32),
                 (apart.shape, bf16),
                 (every_level.shape, f32),
                 ((members, LANES), f32),
-                ((1, LANES), jnp.int32),
                 ((1, LANES), f32),
                 ((everything, LANES), f32),
             ],
             [here, halfwidth, member_weight, member_of_slot],
-            [innovation, precision, static_root]
-            + [jnp.asarray(table) for table in (of_level, same, apart, every_level)],
-            scratch=[((levels, rows, lon), f32)] + [((levels, rows, everything), f32)] * 2,
-        )
-        blocks = trade(results[:-10])
-        own_static, pulled, mixing, pulling, taper, factor, weights, turn, own_weight, row_span = results[-10:]
+            [*between, jnp.asarray(apart), jnp.asarray(every_level)],
+            scratch=[((levels, rows, everything), f32)] * 2,
+        )
         blocks, ensemble, innovation, precision = lax.optimization_barrier(
             (blocks, ensemble, innovation, precision)
         )

time: 52.5 us -> 51.6 us (0.983)
  waiting for transfers between devices: 15.5 us -> 14.8 us
  starting transfers between devices: 24.4 us -> 23.8 us
    ppermute x6, waiting for transfers between devices: 9.73 us -> 8.31 us  [trade(): lax.ppermute(blocks[shift], 'band', [(at, partner(at, shift, bands, 1)) f...]
    all_to_all x1, starting transfers between devices: 4.26 us -> 3.44 us  [shards(): back = lax.all_to_all(grad, BOTH, 0, 0, tiled=True)]
    all_to_all x1, waiting for transfers between devices: 3.49 us -> 4.19 us  [shards(): stacked = lax.all_to_all(pieces, BOTH, 0, 0, tiled=True)]
    pallas_call x8 -> x9, Pallas kernels: 6.65 us -> 7.13 us  [call(): pl.pallas_call(body, out_shape=tuple((jax.ShapeDtypeStruct(shape, kind) f...]
  transfers between devices with their start and end apart: 14 -> 14, of which waited for: 11 -> 10; matrix products, arithmetic and copies ran while one was open for 0% -> 0% of each run, Pallas kernels for 11% -> 12%
where the time goes in v11:
time: 51.6 us; the launch traced here: 51.2 us
  starting transfers between devices  23.8 us (46%)
  waiting for transfers between devices  14.8 us (29%)
  Pallas kernels  10.4 us (20%)
  between operations  1.53 us (3%)
  local copies, waits for them, and re-layouts  0.7 us (1%)
    ppermute x6, waiting for transfers between devices, trade(): lax.ppermute(blocks[shift], 'band', [(at, partner(at, shift, bands, 1)) f...  8.31 us
    all_to_all x1, starting transfers between devices, shards(): stacked = lax.all_to_all(pieces, BOTH, 0, 0, tiled=True)  7.3 us
    pallas_call x9, Pallas kernels, call(): pl.pallas_call(body, out_shape=tuple((jax.ShapeDtypeStruct(shape, kind) f...  7.13 us
    ppermute x6, starting transfers between devices, trade(): lax.ppermute(blocks[shift], 'band', [(at, partner(at, shift, bands, 1)) f...  7.11 us
    ppermute x3, starting transfers between devices, around(): lax.ppermute(block, 'member', [(at, 2 * partner(at // 2, shift, members /...  4.45 us
    all_to_all x1, waiting for transfers between devices, shards(): stacked = lax.all_to_all(pieces, BOTH, 0, 0, tiled=True)  4.19 us
    all_to_all x1, starting transfers between devices, shards(): back = lax.all_to_all(grad, BOTH, 0, 0, tiled=True)  3.44 us
    pallas_call x1, Pallas kernels, shards(): pl.pallas_call(pack, out_shape=jax.ShapeDtypeStruct(block, bf16), in_spec...  2 us
  transfers between devices with their start and end apart: 14, of which 10 were waited for; matrix products, arithmetic and copies ran while one was open for 0% of the time, Pallas kernels for 12%

profile of v11, /device:TPU:0, one launch (start us, length us, event | category | flops | bytes accessed | tf_op | source)
XLA Modules:
  0.0 51.2 jit_solution(16233015220474377652)
XLA Ops:
  1.3 2.0 %pack.1 = bf16[32,16,512]{2,1,0:T(8,128)(2,1)} custom-call(s32[1]{0:T(128)S(6)} %copy.17.slot.marks, bf16[1,2,16,4,1440]{4,3,2,1,0:T(4,128)(2,1)} %ensemble.2), custom_call_target="tpu_custom_call" | custom-call | tf_op jit(solution)/shard_map/pack/pallas_call | solution.py:566
  3.3 0.0 copy-start.1
  3.3 0.0 copy-start.2
  3.3 0.0 copy-start.7
  3.3 0.0 copy-start.8
  3.3 7.3 %all-to-all-start = ((bf16[32,16,512]{2,1,0:T(8,128)(2,1)}), bf16[32,16,512]{2,1,0:T(8,128)(2,1)S(1)}, u32[]{:S(2)}, u32[]{:S(2)}) async-start(bf16[32,16,512]{2,1,0:T(8,128)(2,1)} %pack.1), calls=%async_computation | async-start | bytes 1048576 | tf_op jit(solution)/shard_map/all_to_all | solution.py:585
  10.6 0.0 copy-start.10
  10.7 0.0 copy-done.1
  10.7 0.0 copy-done.2
  10.7 0.0 copy-done.7
  10.7 0.0 copy-done.8
  10.7 0.6 %copy-done.10 = f32[16,16]{1,0:T(8,128)S(1)} copy-done((f32[16,16]{1,0:T(8,128)S(1)}, f32[16,16]{1,0:T(8,128)}, u32[]{:S(2)}) %copy-start.10) | copy-done | bytes 1048
  11.3 0.0 copy-start.4
  11.3 0.0 copy-start.6
  11.3 0.0 copy-start.11
  11.4 0.0 copy-start.12
  11.4 0.0 copy-start.5
  11.4 1.1 %observe.1 = (bf16[32,512]{1,0:T(8,128)(2,1)S(1)}, bf16[32,512]{1,0:T(8,128)(2,1)S(1)}, bf16[32,512]{1,0:T(8,128)(2,1)S(1)}, bf16[32,512]{1,0:T(8,128)(2,1)S(1)}...) custom-call(s32[1,128]{1,0:T(1,128)S(1)} %broadcast_in_dim.6.place, s32[1,128]{1,0:T(1,128)S(1)} %broadcast_in_dim.7.turn, ...), custom_call_target="tpu_custom_call" | custom-call | tf_op jit(solution)/shard_map/observe/pallas_call | solution.py:151
  12.5 0.0 copy-start
  12.5 1.8 %collective-permute-start = (bf16[32,512]{1,0:T(8,128)(2,1)S(1)}, bf16[32,512]{1,0:T(8,128)(2,1)S(1)}, u32[]{:S(2)}, u32[]{:S(2)}) collective-permute-start(bf16[32,512]{1,0:T(8,128)(2,1)S(1)} %get-tuple-element.62), channel_id=1, source_target_pairs={{0,1},{1,0},{2,3},{3,2},{4,5},{5,4},{6,7},{7,6},{8,9},{9,8},{10,11... | collective-permute-start | bytes 98312 | tf_op jit(solution)/shard_map/ppermute | solution.py:523
  14.4 1.5 %collective-permute-start.1 = (bf16[32,512]{1,0:T(8,128)(2,1)S(1)}, bf16[32,512]{1,0:T(8,128)(2,1)S(1)}, u32[]{:S(2)}, u32[]{:S(2)}) collective-permute-start(bf16[32,512]{1,0:T(8,128)(2,1)S(1)} %get-tuple-element.63), channel_id=1, source_target_pairs={{0,2},{1,3},{2,0},{3,1},{4,6},{5,7},{6,4},{7,5},{8,10},{9,11},{10,... | collective-permute-start | bytes 98312 | tf_op jit(solution)/shard_map/ppermute | solution.py:523
  15.8 0.3 collective-permute-start.2
  16.1 0.0 copy-done.4
  16.1 0.0 copy-done.6
  16.1 0.0 copy-done.11
  16.1 0.0 copy-done.12
  16.1 1.4 %prepare.1 = (f32[8,64]{1,0:T(8,128)S(1)}, f32[64,64]{1,0:T(8,128)S(1)}, bf16[256,256]{1,0:T(8,128)(2,1)S(1)}, f32[256,1]{1,0:T(8,128)S(1)}, f32[8,128]{1,0:T(8,...) custom-call(s32[1]{0:T(128)} %bitcast.here, s32[16]{0:T(128)S(1)} %copy-done.11, f32[8]{0:T(128)S(1)} %copy-done.12, ...), custom_call_target="tpu_custom_call" | custom-call | tf_op jit(solution)/shard_map/prepare/pallas_call | solution.py:151
  17.5 0.0 collective-permute-done.refs_1_
  17.5 1.4 %collective-permute-done.1.refs_2_ = bf16[32,512]{1,0:T(8,128)(2,1)S(1)} collective-permute-done((bf16[32,512]{1,0:T(8,128)(2,1)S(1)}, bf16[32,512]{1,0:T(8,128)(2,1)S(1)}, u32[]{:S(2)}, u32[]{:S(2)}) %collective-permute-start.1) | collective-permute-done | bytes 32800 | tf_op jit(solution)/shard_map/ppermute | solution.py:523
  18.8 2.0 %collective-permute-done.2.refs_3_ = bf16[32,512]{1,0:T(8,128)(2,1)S(1)} collective-permute-done((bf16[32,512]{1,0:T(8,128)(2,1)S(1)}, bf16[32,512]{1,0:T(8,128)(2,1)S(1)}, u32[]{:S(2)}, u32[]{:S(2)}) %collective-permute-start.2) | collective-permute-done | bytes 32800 | tf_op jit(solution)/shard_map/ppermute | solution.py:523
  20.8 0.0 copy-done.5
  20.8 0.0 copy-done
  20.8 0.5 fold_smooth.1.middle
  21.3 0.7 %collective-permute-start.6 = (bf16[64,1440]{1,0:T(8,128)(2,1)S(1)}, bf16[64,1440]{1,0:T(8,128)(2,1)S(1)}, u32[]{:S(2)}, u32[]{:S(2)}) collective-permute-start(bf16[64,1440]{1,0:T(8,128)(2,1)S(1)} %fold_smooth.1.middle), channel_id=1, source_target_pairs={{0,1},{2,3},{1,0},{3,2},{4,5},{6,7},{5,4},{7,6},{8,9},{10,11},{9,8... | collective-permute-start | bytes 552968 | tf_op jit(solution)/shard_map/ppermute | solution.py:626
  22.0 0.7 %collective-permute-start.7 = (bf16[64,1440]{1,0:T(8,128)(2,1)S(1)}, bf16[64,1440]{1,0:T(8,128)(2,1)S(1)}, u32[]{:S(2)}, u32[]{:S(2)}) collective-permute-start(bf16[64,1440]{1,0:T(8,128)(2,1)S(1)} %fold_smooth.1.middle), channel_id=1, source_target_pairs={{1,2},{2,1},{5,6},{6,5},{9,10},{10,9},{13,14},{14,13},{17,18},{18,... | collective-permute-start | bytes 552968 | tf_op jit(solution)/shard_map/ppermute | solution.py:626
  22.7 4.2 %all-to-all-done.stacked = bf16[32,16,512]{2,1,0:T(8,128)(2,1)S(1)} async-done(((bf16[32,16,512]{2,1,0:T(8,128)(2,1)}), bf16[32,16,512]{2,1,0:T(8,128)(2,1)S(1)}, u32[]{:S(2)}, u32[]{:S(2)}) %all-to-all-start) | async-done | bytes 524320 | tf_op jit(solution)/shard_map/all_to_all | solution.py:585
  26.9 0.0 copy-done.3
  26.9 1.1 %first_half.1 = (bf16[32,384]{1,0:T(8,128)(2,1)S(1)}, f32[2,32,512]{2,1,0:T(8,128)S(1)}, f32[2,32,384]{2,1,0:T(8,128)S(1)}, f32[4,32,384]{2,1,0:T(8,128)S(1)}) custom-call(f32[8,128]{1,0:T(8,128)S(1)} %get-tuple-element.57.weights, s32[1,128]{1,0:T(1,128)S(1)} %broadcast_in_dim.7.turn, bf16[32,16,512]{2,1,0:T(8,128)(2,1)S(1)} %all-to-all-done.stacked, ...), custom_call_target="tpu_custom_call" | custom-call | tf_op jit(solution)/shard_map/first_half/pallas_call | solution.py:151
  28.0 1.5 %collective-permute-start.5 = (bf16[32,384]{1,0:T(8,128)(2,1)S(1)}, bf16[32,384]{1,0:T(8,128)(2,1)S(1)}, u32[]{:S(2)}, u32[]{:S(2)}) collective-permute-start(bf16[32,384]{1,0:T(8,128)(2,1)S(1)} %get-tuple-element.73), channel_id=1, source_target_pairs={{0,24},{4,28},{8,16},{12,20},{16,8},{20,12},{24,0},{28,4},{1,25},{... | collective-permute-start | bytes 73736 | tf_op jit(solution)/shard_map/ppermute | solution.py:533
  29.6 1.1 %collective-permute-start.4 = (bf16[32,384]{1,0:T(8,128)(2,1)S(1)}, bf16[32,384]{1,0:T(8,128)(2,1)S(1)}, u32[]{:S(2)}, u32[]{:S(2)}) collective-permute-start(bf16[32,384]{1,0:T(8,128)(2,1)S(1)} %get-tuple-element.73), channel_id=1, source_target_pairs={{0,16},{4,20},{8,24},{12,28},{16,0},{20,4},{24,8},{28,12},{1,17},{... | collective-permute-start | bytes 73736 | tf_op jit(solution)/shard_map/ppermute | solution.py:533
  30.6 1.9 %collective-permute-start.3 = (bf16[32,384]{1,0:T(8,128)(2,1)S(1)}, bf16[32,384]{1,0:T(8,128)(2,1)S(1)}, u32[]{:S(2)}, u32[]{:S(2)}) collective-permute-start(bf16[32,384]{1,0:T(8,128)(2,1)S(1)} %get-tuple-element.73), channel_id=1, source_target_pairs={{0,8},{4,12},{8,0},{12,4},{16,24},{20,28},{24,16},{28,20},{1,9},{5... | collective-permute-start | bytes 73736 | tf_op jit(solution)/shard_map/ppermute | solution.py:533
  32.5 1.1 %second_half.1 = (bf16[32,8,384]{2,1,0:T(8,128)(2,1)S(1)}, f32[2,32,384]{2,1,0:T(8,128)S(1)}) custom-call(f32[8,128]{1,0:T(8,128)S(1)} %get-tuple-element.57.weights, bf16[32,16,512]{2,1,0:T(8,128)(2,1)S(1)} %all-to-all-done.stacked, bf16[512,512]{1,0:T(8,128)(2,1)S(1)} %copy-done.3, bf16[256,256]{1,0:T(8,128)(2,1)S(1)} %get-tuple-element.59.taper, ...), custom_call_target="tpu_custom_call" | custom-call | flops 1000000000 | tf_op jit(solution)/shard_map/second_half/pallas_call | solution.py:151
  33.5 0.2 collective-permute-done.5
  33.7 0.6 %collective-permute-done.4 = bf16[32,384]{1,0:T(8,128)(2,1)S(1)} collective-permute-done((bf16[32,384]{1,0:T(8,128)(2,1)S(1)}, bf16[32,384]{1,0:T(8,128)(2,1)S(1)}, u32[]{:S(2)}, u32[]{:S(2)}) %collective-permute-start.4) | collective-permute-done | bytes 24608 | tf_op jit(solution)/shard_map/ppermute | solution.py:533
  34.3 0.3 collective-permute-done.3
  34.6 0.0 collective-permute-done.6.below
  34.6 0.0 collective-permute-done.7.above
  34.6 0.1 collective-permute-start.8
  34.7 1.3 %collective-permute-done.8.refs_1_ = bf16[4,32,384]{2,1,0:T(8,128)(2,1)S(1)} collective-permute-done((bf16[4,32,384]{2,1,0:T(8,128)(2,1)S(1)}, bf16[4,32,384]{2,1,0:T(8,128)(2,1)S(1)}, u32[]{:S(2)}, u32[]{:S(2)}) %collective-permute-start.8) | collective-permute-done | bytes 98336 | tf_op jit(solution)/shard_map/ppermute | solution.py:541
  36.0 1.0 %combine.1 = (bf16[32,8,384]{2,1,0:T(8,128)(2,1)}, f32[2,32,384]{2,1,0:T(8,128)S(1)}) custom-call(bf16[32,8,384]{2,1,0:T(8,128)(2,1)S(1)} %get-tuple-element.71.grad, f32[2,32,384]{2,1,0:T(8,128)S(1)} %get-tuple-element.72.first, f32[2,32,384]{2,1,0:T(8,128)S(1)} %get-tuple-element.79.second, f32[4,32,384]{2,1,0:T(8,128)S(1)} %get-tuple-element.80.fields, ...), custom_call_target="tpu_custom_call" | custom-call | tf_op jit(solution)/shard_map/combine/pallas_call | solution.py:151
  36.9 3.4 %all-to-all-start.1 = ((bf16[32,8,384]{2,1,0:T(8,128)(2,1)}), bf16[32,8,384]{2,1,0:T(8,128)(2,1)S(1)}, u32[]{:S(2)}, u32[]{:S(2)}) async-start(bf16[32,8,384]{2,1,0:T(8,128)(2,1)} %get-tuple-element.83), calls=%async_computation.1 | async-start | bytes 393216 | tf_op jit(solution)/shard_map/all_to_all | solution.py:657
  40.4 0.0 copy-start.9
  40.4 0.2 hand_out.1
  40.6 1.8 %collective-permute-start.9 = (bf16[96,384]{1,0:T(8,128)(2,1)S(1)}, bf16[96,384]{1,0:T(8,128)(2,1)S(1)}, u32[]{:S(2)}, u32[]{:S(2)}) collective-permute-start(bf16[96,384]{1,0:T(8,128)(2,1)S(1)} %get-tuple-element.92), channel_id=1, source_target_pairs={{0,1},{1,0},{2,3},{3,2},{4,5},{5,4},{6,7},{7,6},{8,9},{9,8},{10,11... | collective-permute-start | bytes 221192 | tf_op jit(solution)/shard_map/ppermute | solution.py:523
  42.4 1.5 %collective-permute-start.10 = (bf16[96,384]{1,0:T(8,128)(2,1)S(1)}, bf16[96,384]{1,0:T(8,128)(2,1)S(1)}, u32[]{:S(2)}, u32[]{:S(2)}) collective-permute-start(bf16[96,384]{1,0:T(8,128)(2,1)S(1)} %get-tuple-element.93), channel_id=1, source_target_pairs={{0,2},{1,3},{2,0},{3,1},{4,6},{5,7},{6,4},{7,5},{8,10},{9,11},{10,... | collective-permute-start | bytes 221192 | tf_op jit(solution)/shard_map/ppermute | solution.py:523
  43.9 0.3 collective-permute-start.11
  44.1 0.0 copy-done.9
  44.1 0.3 first_gradient.1.grad_first
  44.5 1.6 %collective-permute-done.9.refs_1_ = bf16[96,384]{1,0:T(8,128)(2,1)S(1)} collective-permute-done((bf16[96,384]{1,0:T(8,128)(2,1)S(1)}, bf16[96,384]{1,0:T(8,128)(2,1)S(1)}, u32[]{:S(2)}, u32[]{:S(2)}) %collective-permute-start.9) | collective-permute-done | bytes 73760 | tf_op jit(solution)/shard_map/ppermute | solution.py:523
  46.1 1.9 %collective-permute-done.10.refs_2_ = bf16[96,384]{1,0:T(8,128)(2,1)S(1)} collective-permute-done((bf16[96,384]{1,0:T(8,128)(2,1)S(1)}, bf16[96,384]{1,0:T(8,128)(2,1)S(1)}, u32[]{:S(2)}, u32[]{:S(2)}) %collective-permute-start.10) | collective-permute-done | bytes 73760 | tf_op jit(solution)/shard_map/ppermute | solution.py:523
  48.0 1.5 %collective-permute-done.11.refs_3_ = bf16[96,384]{1,0:T(8,128)(2,1)S(1)} collective-permute-done((bf16[96,384]{1,0:T(8,128)(2,1)S(1)}, bf16[96,384]{1,0:T(8,128)(2,1)S(1)}, u32[]{:S(2)}, u32[]{:S(2)}) %collective-permute-start.11) | collective-permute-done | bytes 73760 | tf_op jit(solution)/shard_map/ppermute | solution.py:523
  49.4 0.5 join.1
  49.9 0.0 all-to-all-done.1.back
  49.9 1.3 %finish.1 = (f32[1,16,4,1440]{3,2,1,0:T(4,128)}, f32[16,4,1440]{2,1,0:T(4,128)}, f32[2,2,4,1440]{3,2,1,0:T(4,128)}) custom-call(bf16[32,8,384]{2,1,0:T(8,128)(2,1)S(1)} %all-to-all-done.1.back, f32[64,1440]{1,0:T(8,128)S(1)} %first_gradient.1.grad_first, f32[64,1440]{1,0:T(8,128)S(1)} %get-tuple-element.87.pulled_first, ...), custom_call_target="tpu_custom_call" | custom-call | tf_op jit(solution)/shard_map/finish/pallas_call | solution.py:677
  (4 shorter events, 0.0 us)
Async XLA Ops:
  3.3 7.4 %copy-start.1 = (bf16[2,16,4,1440]{3,2,1,0:T(4,128)(2,1)S(1)}, bf16[2,16,4,1440]{3,2,1,0:T(4,128)(2,1)}, u32[]{:S(2)}) copy-start(bf16[2,16,4,1440]{3,2,1,0:T(4,128)(2,1)} %innovation.1) | copy-start | bytes 1105924
  3.3 7.4 %copy-start.2 = (bf16[16,4,1440]{2,1,0:T(4,128)(2,1)S(1)}, bf16[16,4,1440]{2,1,0:T(4,128)(2,1)}, u32[]{:S(2)}) copy-start(bf16[16,4,1440]{2,1,0:T(4,128)(2,1)} %precision.1) | copy-start | bytes 552964
  3.3 7.4 %copy-start.7 = (f32[64,16]{1,0:T(8,128)S(1)}, f32[64,16]{1,0:T(8,128)}, u32[]{:S(2)}) copy-start(f32[64,16]{1,0:T(8,128)} %constant.23.clone.of_level) | copy-start | bytes 12292
  3.3 7.4 %copy-start.8 = (f32[64,64]{1,0:T(8,128)S(1)}, f32[64,64]{1,0:T(8,128)}, u32[]{:S(2)}) copy-start(f32[64,64]{1,0:T(8,128)} %constant.24.clone.same) | copy-start | bytes 49156
  3.3 23.6 %all-to-all-start = ((bf16[32,16,512]{2,1,0:T(8,128)(2,1)}), bf16[32,16,512]{2,1,0:T(8,128)(2,1)S(1)}, u32[]{:S(2)}, u32[]{:S(2)}) async-start(bf16[32,16,512]{2,1,0:T(8,128)(2,1)} %pack.1), calls=%async_computation | async-start | bytes 1048576 | tf_op jit(solution)/shard_map/all_to_all | solution.py:585
  10.6 0.7 %copy-start.10 = (f32[16,16]{1,0:T(8,128)S(1)}, f32[16,16]{1,0:T(8,128)}, u32[]{:S(2)}) copy-start(f32[16,16]{1,0:T(8,128)} %root.1) | copy-start | bytes 3076
  11.3 4.8 %copy-start.4 = (f32[256,256]{1,0:T(8,128)S(1)}, f32[256,256]{1,0:T(8,128)}, u32[]{:S(2)}) copy-start(f32[256,256]{1,0:T(8,128)} %constant.25.clone.apart) | copy-start | bytes 786436
  11.3 4.8 %copy-start.6 = (f32[256,1]{1,0:T(8,128)S(1)}, f32[256,1]{1,0:T(8,128)}, u32[]{:S(2)}) copy-start(f32[256,1]{1,0:T(8,128)} %constant.26.clone.level) | copy-start | bytes 3076
  11.3 4.8 %copy-start.11 = (s32[16]{0:T(128)S(1)}, s32[16]{0:T(128)}, u32[]{:S(2)}) copy-start(s32[16]{0:T(128)} %widths.1) | copy-start | bytes 196
  11.4 4.8 %copy-start.12 = (f32[8]{0:T(128)S(1)}, f32[8]{0:T(128)}, u32[]{:S(2)}) copy-start(f32[8]{0:T(128)} %weight.1) | copy-start | bytes 100
  11.4 9.4 %copy-start.5 = (bf16[512,256]{1,0:T(8,128)(2,1)S(1)}, bf16[512,256]{1,0:T(8,128)(2,1)}, u32[]{:S(2)}) copy-start(bf16[512,256]{1,0:T(8,128)(2,1)} %constant.27.clone.kernel) | copy-start | bytes 786436
  12.5 8.3 %copy-start = (bf16[1,2,16,4,1440]{4,3,2,1,0:T(4,128)(2,1)S(1)}, bf16[1,2,16,4,1440]{4,3,2,1,0:T(4,128)(2,1)}, u32[]{:S(2)}) copy-start(bf16[1,2,16,4,1440]{4,3,2,1,0:T(4,128)(2,1)} %ensemble.2) | copy-start | bytes 1105924
  12.5 4.9 %collective-permute-start = (bf16[32,512]{1,0:T(8,128)(2,1)S(1)}, bf16[32,512]{1,0:T(8,128)(2,1)S(1)}, u32[]{:S(2)}, u32[]{:S(2)}) collective-permute-start(bf16[32,512]{1,0:T(8,128)(2,1)S(1)} %get-tuple-element.62), channel_id=1, source_target_pairs={{0,1},{1,0},{2,3},{3,2},{4,5},{5,4},{6,7},{7,6},{8,9},{9,8},{10,11... | collective-permute-start | bytes 98312 | tf_op jit(solution)/shard_map/ppermute | solution.py:523
  14.4 4.4 %collective-permute-start.1 = (bf16[32,512]{1,0:T(8,128)(2,1)S(1)}, bf16[32,512]{1,0:T(8,128)(2,1)S(1)}, u32[]{:S(2)}, u32[]{:S(2)}) collective-permute-start(bf16[32,512]{1,0:T(8,128)(2,1)S(1)} %get-tuple-element.63), channel_id=1, source_target_pairs={{0,2},{1,3},{2,0},{3,1},{4,6},{5,7},{6,4},{7,5},{8,10},{9,11},{10,... | collective-permute-start | bytes 98312 | tf_op jit(solution)/shard_map/ppermute | solution.py:523
  15.8 5.0 %collective-permute-start.2 = (bf16[32,512]{1,0:T(8,128)(2,1)S(1)}, bf16[32,512]{1,0:T(8,128)(2,1)S(1)}, u32[]{:S(2)}, u32[]{:S(2)}) collective-permute-start(bf16[32,512]{1,0:T(8,128)(2,1)S(1)} %get-tuple-element.64), channel_id=1, source_target_pairs={{0,3},{1,2},{2,1},{3,0},{4,7},{5,6},{6,5},{7,4},{8,11},{9,10},{10,... | collective-permute-start | bytes 98312 | tf_op jit(solution)/shard_map/ppermute | solution.py:523
  20.8 6.1 %copy-start.3 = (bf16[512,512]{1,0:T(8,128)(2,1)S(1)}, bf16[512,512]{1,0:T(8,128)(2,1)}, u32[]{:S(2)}) copy-start(bf16[512,512]{1,0:T(8,128)(2,1)} %constant.28.clone.ring) | copy-start | bytes 1572868
  21.3 13.2 %collective-permute-start.6 = (bf16[64,1440]{1,0:T(8,128)(2,1)S(1)}, bf16[64,1440]{1,0:T(8,128)(2,1)S(1)}, u32[]{:S(2)}, u32[]{:S(2)}) collective-permute-start(bf16[64,1440]{1,0:T(8,128)(2,1)S(1)} %fold_smooth.1.middle), channel_id=1, source_target_pairs={{0,1},{2,3},{1,0},{3,2},{4,5},{6,7},{5,4},{7,6},{8,9},{10,11},{9,8... | collective-permute-start | bytes 552968 | tf_op jit(solution)/shard_map/ppermute | solution.py:626
  22.0 12.5 %collective-permute-start.7 = (bf16[64,1440]{1,0:T(8,128)(2,1)S(1)}, bf16[64,1440]{1,0:T(8,128)(2,1)S(1)}, u32[]{:S(2)}, u32[]{:S(2)}) collective-permute-start(bf16[64,1440]{1,0:T(8,128)(2,1)S(1)} %fold_smooth.1.middle), channel_id=1, source_target_pairs={{1,2},{2,1},{5,6},{6,5},{9,10},{10,9},{13,14},{14,13},{17,18},{18,... | collective-permute-start | bytes 552968 | tf_op jit(solution)/shard_map/ppermute | solution.py:626
  28.0 5.7 %collective-permute-start.5 = (bf16[32,384]{1,0:T(8,128)(2,1)S(1)}, bf16[32,384]{1,0:T(8,128)(2,1)S(1)}, u32[]{:S(2)}, u32[]{:S(2)}) collective-permute-start(bf16[32,384]{1,0:T(8,128)(2,1)S(1)} %get-tuple-element.73), channel_id=1, source_target_pairs={{0,24},{4,28},{8,16},{12,20},{16,8},{20,12},{24,0},{28,4},{1,25},{... | collective-permute-start | bytes 73736 | tf_op jit(solution)/shard_map/ppermute | solution.py:533
  29.6 4.7 %collective-permute-start.4 = (bf16[32,384]{1,0:T(8,128)(2,1)S(1)}, bf16[32,384]{1,0:T(8,128)(2,1)S(1)}, u32[]{:S(2)}, u32[]{:S(2)}) collective-permute-start(bf16[32,384]{1,0:T(8,128)(2,1)S(1)} %get-tuple-element.73), channel_id=1, source_target_pairs={{0,16},{4,20},{8,24},{12,28},{16,0},{20,4},{24,8},{28,12},{1,17},{... | collective-permute-start | bytes 73736 | tf_op jit(solution)/shard_map/ppermute | solution.py:533
  30.6 3.9 %collective-permute-start.3 = (bf16[32,384]{1,0:T(8,128)(2,1)S(1)}, bf16[32,384]{1,0:T(8,128)(2,1)S(1)}, u32[]{:S(2)}, u32[]{:S(2)}) collective-permute-start(bf16[32,384]{1,0:T(8,128)(2,1)S(1)} %get-tuple-element.73), channel_id=1, source_target_pairs={{0,8},{4,12},{8,0},{12,4},{16,24},{20,28},{24,16},{28,20},{1,9},{5... | collective-permute-start | bytes 73736 | tf_op jit(solution)/shard_map/ppermute | solution.py:533
  34.6 1.4 %collective-permute-start.8 = (bf16[4,32,384]{2,1,0:T(8,128)(2,1)S(1)}, bf16[4,32,384]{2,1,0:T(8,128)(2,1)S(1)}, u32[]{:S(2)}, u32[]{:S(2)}) collective-permute-start(bf16[4,32,384]{2,1,0:T(8,128)(2,1)S(1)} %pad_maximum_fusion.refs_0_), channel_id=1, source_target_pairs={{0,4},{4,0},{8,12},{12,8},{16,20},{20,16},{24,28},{28,24},{1,5},{5... | collective-permute-start | bytes 294920 | tf_op jit(solution)/shard_map/ppermute | solution.py:541
  36.9 13.0 %all-to-all-start.1 = ((bf16[32,8,384]{2,1,0:T(8,128)(2,1)}), bf16[32,8,384]{2,1,0:T(8,128)(2,1)S(1)}, u32[]{:S(2)}, u32[]{:S(2)}) async-start(bf16[32,8,384]{2,1,0:T(8,128)(2,1)} %get-tuple-element.83), calls=%async_computation.1 | async-start | bytes 393216 | tf_op jit(solution)/shard_map/all_to_all | solution.py:657
  40.4 3.8 %copy-start.9 = (f32[64,192]{1,0:T(8,128)S(1)}, f32[64,192]{1,0:T(8,128)}, u32[]{:S(2)}) copy-start(f32[64,192]{1,0:T(8,128)} %constant.29.clone.apart) | copy-start | bytes 147460
  40.6 5.5 %collective-permute-start.9 = (bf16[96,384]{1,0:T(8,128)(2,1)S(1)}, bf16[96,384]{1,0:T(8,128)(2,1)S(1)}, u32[]{:S(2)}, u32[]{:S(2)}) collective-permute-start(bf16[96,384]{1,0:T(8,128)(2,1)S(1)} %get-tuple-element.92), channel_id=1, source_target_pairs={{0,1},{1,0},{2,3},{3,2},{4,5},{5,4},{6,7},{7,6},{8,9},{9,8},{10,11... | collective-permute-start | bytes 221192 | tf_op jit(solution)/shard_map/ppermute | solution.py:523
  42.4 5.6 %collective-permute-start.10 = (bf16[96,384]{1,0:T(8,128)(2,1)S(1)}, bf16[96,384]{1,0:T(8,128)(2,1)S(1)}, u32[]{:S(2)}, u32[]{:S(2)}) collective-permute-start(bf16[96,384]{1,0:T(8,128)(2,1)S(1)} %get-tuple-element.93), channel_id=1, source_target_pairs={{0,2},{1,3},{2,0},{3,1},{4,6},{5,7},{6,4},{7,5},{8,10},{9,11},{10,... | collective-permute-start | bytes 221192 | tf_op jit(solution)/shard_map/ppermute | solution.py:523
  43.9 5.6 %collective-permute-start.11 = (bf16[96,384]{1,0:T(8,128)(2,1)S(1)}, bf16[96,384]{1,0:T(8,128)(2,1)S(1)}, u32[]{:S(2)}, u32[]{:S(2)}) collective-permute-start(bf16[96,384]{1,0:T(8,128)(2,1)S(1)} %get-tuple-element.94), channel_id=1, source_target_pairs={{0,3},{1,2},{2,1},{3,0},{4,7},{5,6},{6,5},{7,4},{8,11},{9,10},{10,... | collective-permute-start | bytes 221192 | tf_op jit(solution)/shard_map/ppermute | solution.py:523

commit v12 on v11

--- a/solution.py
+++ b/solution.py
@@ -612,8 +612,9 @@
             [*between, jnp.asarray(apart), jnp.asarray(every_level)],
             scratch=[((levels, rows, everything), f32)] * 2,
         )
-        blocks, ensemble, innovation, precision = lax.optimization_barrier(
-            (blocks, ensemble, innovation, precision)
+        awaited = bands // 2 if few else 0
+        blocks[awaited], ensemble, innovation, precision = lax.optimization_barrier(
+            (blocks[awaited], ensemble, innovation, precision)
         )
         (smoothed,) = call(
             fold_smooth,

time: 51.6 us -> 51.2 us (level)
  waiting for transfers between devices: 14.8 us -> 13.4 us
  starting transfers between devices: 23.8 us -> 24.7 us
    ppermute x6, waiting for transfers between devices: 8.31 us -> 4.98 us  [trade(): lax.ppermute(blocks[shift], 'band', [(at, partner(at, shift, bands, 1)) f...]
    all_to_all x1, waiting for transfers between devices: 4.19 us -> 6.07 us  [shards(): stacked = lax.all_to_all(pieces, BOTH, 0, 0, tiled=True)]
    ppermute x2, starting transfers between devices: 1.38 us -> 2.75 us  [shards(): lax.ppermute(smoothed, 'band', pairs[start::2] + [(to, at) for at, to in...]
  transfers between devices with their start and end apart: 14 -> 14, of which waited for: 10 -> 8; matrix products, arithmetic and copies ran while one was open for 0% -> 0% of each run, Pallas kernels for 12% -> 12%
where the time goes in v12:
time: 51.2 us; the launch traced here: 50.8 us
  starting transfers between devices  24.7 us (48%)
  waiting for transfers between devices  13.4 us (26%)
  Pallas kernels  10.4 us (20%)
  between operations  1.59 us (3%)
  local copies, waits for them, and re-layouts  0.72 us (1%)
    all_to_all x1, starting transfers between devices, shards(): stacked = lax.all_to_all(pieces, BOTH, 0, 0, tiled=True)  7.3 us
    pallas_call x9, Pallas kernels, call(): pl.pallas_call(body, out_shape=tuple((jax.ShapeDtypeStruct(shape, kind) f...  7.14 us
    ppermute x6, starting transfers between devices, trade(): lax.ppermute(blocks[shift], 'band', [(at, partner(at, shift, bands, 1)) f...  7.11 us
    all_to_all x1, waiting for transfers between devices, shards(): stacked = lax.all_to_all(pieces, BOTH, 0, 0, tiled=True)  6.07 us
    ppermute x6, waiting for transfers between devices, trade(): lax.ppermute(blocks[shift], 'band', [(at, partner(at, shift, bands, 1)) f...  4.98 us
    ppermute x3, starting transfers between devices, around(): lax.ppermute(block, 'member', [(at, 2 * partner(at // 2, shift, members /...  4.45 us
    all_to_all x1, starting transfers between devices, shards(): back = lax.all_to_all(grad, BOTH, 0, 0, tiled=True)  3.03 us
    ppermute x2, starting transfers between devices, shards(): lax.ppermute(smoothed, 'band', pairs[start::2] + [(to, at) for at, to in...  2.75 us
  transfers between devices with their start and end apart: 14, of which 8 were waited for; matrix products, arithmetic and copies ran while one was open for 0% of the time, Pallas kernels for 12%

profile of v12, /device:TPU:0, one launch (start us, length us, event | category | flops | bytes accessed | tf_op | source)
XLA Modules:
  0.0 50.8 jit_solution(11993858012472767432)
XLA Ops:
  1.3 2.0 %pack.1 = bf16[32,16,512]{2,1,0:T(8,128)(2,1)} custom-call(s32[1]{0:T(128)S(6)} %copy.17.slot.marks, bf16[1,2,16,4,1440]{4,3,2,1,0:T(4,128)(2,1)} %ensemble.2), custom_call_target="tpu_custom_call" | custom-call | tf_op jit(solution)/shard_map/pack/pallas_call | solution.py:566
  3.3 0.0 copy-start.1
  3.3 0.0 copy-start.2
  3.3 0.0 copy-start.7
  3.3 0.0 copy-start.8
  3.3 7.3 %all-to-all-start = ((bf16[32,16,512]{2,1,0:T(8,128)(2,1)}), bf16[32,16,512]{2,1,0:T(8,128)(2,1)S(1)}, u32[]{:S(2)}, u32[]{:S(2)}) async-start(bf16[32,16,512]{2,1,0:T(8,128)(2,1)} %pack.1), calls=%async_computation | async-start | bytes 1048576 | tf_op jit(solution)/shard_map/all_to_all | solution.py:585
  10.6 0.0 copy-start.10
  10.7 0.0 copy-done.1
  10.7 0.0 copy-done.2
  10.7 0.0 copy-done.7
  10.7 0.0 copy-done.8
  10.7 0.6 %copy-done.10 = f32[16,16]{1,0:T(8,128)S(1)} copy-done((f32[16,16]{1,0:T(8,128)S(1)}, f32[16,16]{1,0:T(8,128)}, u32[]{:S(2)}) %copy-start.10) | copy-done | bytes 1048
  11.3 0.0 copy-start.4
  11.3 0.0 copy-start.6
  11.3 0.0 copy-start.11
  11.4 0.0 copy-start.5
  11.4 1.1 %observe.1 = (bf16[32,512]{1,0:T(8,128)(2,1)S(1)}, bf16[32,512]{1,0:T(8,128)(2,1)S(1)}, bf16[32,512]{1,0:T(8,128)(2,1)S(1)}, bf16[32,512]{1,0:T(8,128)(2,1)S(1)}...) custom-call(s32[1,128]{1,0:T(1,128)S(1)} %broadcast_in_dim.6.place, s32[1,128]{1,0:T(1,128)S(1)} %broadcast_in_dim.7.turn, ...), custom_call_target="tpu_custom_call" | custom-call | tf_op jit(solution)/shard_map/observe/pallas_call | solution.py:151
  12.5 0.0 copy-start
  12.5 1.8 %collective-permute-start.1 = (bf16[32,512]{1,0:T(8,128)(2,1)S(1)}, bf16[32,512]{1,0:T(8,128)(2,1)S(1)}, u32[]{:S(2)}, u32[]{:S(2)}) collective-permute-start(bf16[32,512]{1,0:T(8,128)(2,1)S(1)} %get-tuple-element.60), channel_id=1, source_target_pairs={{0,2},{1,3},{2,0},{3,1},{4,6},{5,7},{6,4},{7,5},{8,10},{9,11},{10,... | collective-permute-start | bytes 98312 | tf_op jit(solution)/shard_map/ppermute | solution.py:523
  14.4 1.5 %collective-permute-start = (bf16[32,512]{1,0:T(8,128)(2,1)S(1)}, bf16[32,512]{1,0:T(8,128)(2,1)S(1)}, u32[]{:S(2)}, u32[]{:S(2)}) collective-permute-start(bf16[32,512]{1,0:T(8,128)(2,1)S(1)} %get-tuple-element.59), channel_id=1, source_target_pairs={{0,1},{1,0},{2,3},{3,2},{4,5},{5,4},{6,7},{7,6},{8,9},{9,8},{10,11... | collective-permute-start | bytes 98312 | tf_op jit(solution)/shard_map/ppermute | solution.py:523
  15.8 0.3 collective-permute-start.2
  16.1 0.0 copy-done.4
  16.1 0.0 copy-done.6
  16.1 0.0 copy-done.11
  16.1 0.0 copy-done.12
  16.1 1.4 %prepare.1 = (f32[8,64]{1,0:T(8,128)S(1)}, f32[64,64]{1,0:T(8,128)S(1)}, bf16[256,256]{1,0:T(8,128)(2,1)S(1)}, f32[256,1]{1,0:T(8,128)S(1)}, f32[8,128]{1,0:T(8,...) custom-call(s32[1]{0:T(128)} %bitcast.here, s32[16]{0:T(128)S(1)} %copy-done.11, f32[8]{0:T(128)S(1)} %copy-done.12, ...), custom_call_target="tpu_custom_call" | custom-call | tf_op jit(solution)/shard_map/prepare/pallas_call | solution.py:151
  17.5 0.0 collective-permute-done.1.refs_2_
  17.5 0.0 copy-done.5
  17.5 0.0 copy-done
  17.5 0.0 copy-start.3
  17.5 0.5 fold_smooth.1.middle
  18.0 2.1 %collective-permute-start.6 = (bf16[64,1440]{1,0:T(8,128)(2,1)S(1)}, bf16[64,1440]{1,0:T(8,128)(2,1)S(1)}, u32[]{:S(2)}, u32[]{:S(2)}) collective-permute-start(bf16[64,1440]{1,0:T(8,128)(2,1)S(1)} %fold_smooth.1.middle), channel_id=1, source_target_pairs={{0,1},{2,3},{1,0},{3,2},{4,5},{6,7},{5,4},{7,6},{8,9},{10,11},{9,8... | collective-permute-start | bytes 552968 | tf_op jit(solution)/shard_map/ppermute | solution.py:627
  20.1 0.7 %collective-permute-start.7 = (bf16[64,1440]{1,0:T(8,128)(2,1)S(1)}, bf16[64,1440]{1,0:T(8,128)(2,1)S(1)}, u32[]{:S(2)}, u32[]{:S(2)}) collective-permute-start(bf16[64,1440]{1,0:T(8,128)(2,1)S(1)} %fold_smooth.1.middle), channel_id=1, source_target_pairs={{1,2},{2,1},{5,6},{6,5},{9,10},{10,9},{13,14},{14,13},{17,18},{18,... | collective-permute-start | bytes 552968 | tf_op jit(solution)/shard_map/ppermute | solution.py:627
  20.8 0.0 collective-permute-done.refs_1_
  20.8 0.0 collective-permute-done.2.refs_3_
  20.8 6.1 %all-to-all-done.stacked = bf16[32,16,512]{2,1,0:T(8,128)(2,1)S(1)} async-done(((bf16[32,16,512]{2,1,0:T(8,128)(2,1)}), bf16[32,16,512]{2,1,0:T(8,128)(2,1)S(1)}, u32[]{:S(2)}, u32[]{:S(2)}) %all-to-all-start) | async-done | bytes 524320 | tf_op jit(solution)/shard_map/all_to_all | solution.py:585
  26.9 0.0 copy-done.3
  26.9 1.1 %first_half.1 = (bf16[32,384]{1,0:T(8,128)(2,1)S(1)}, f32[2,32,512]{2,1,0:T(8,128)S(1)}, f32[2,32,384]{2,1,0:T(8,128)S(1)}, f32[4,32,384]{2,1,0:T(8,128)S(1)}) custom-call(f32[8,128]{1,0:T(8,128)S(1)} %get-tuple-element.54.weights, s32[1,128]{1,0:T(1,128)S(1)} %broadcast_in_dim.7.turn, bf16[32,16,512]{2,1,0:T(8,128)(2,1)S(1)} %all-to-all-done.stacked, ...), custom_call_target="tpu_custom_call" | custom-call | tf_op jit(solution)/shard_map/first_half/pallas_call | solution.py:151
  28.0 1.5 %collective-permute-start.5 = (bf16[32,384]{1,0:T(8,128)(2,1)S(1)}, bf16[32,384]{1,0:T(8,128)(2,1)S(1)}, u32[]{:S(2)}, u32[]{:S(2)}) collective-permute-start(bf16[32,384]{1,0:T(8,128)(2,1)S(1)} %get-tuple-element.67), channel_id=1, source_target_pairs={{0,24},{4,28},{8,16},{12,20},{16,8},{20,12},{24,0},{28,4},{1,25},{... | collective-permute-start | bytes 73736 | tf_op jit(solution)/shard_map/ppermute | solution.py:533
  29.6 1.1 %collective-permute-start.4 = (bf16[32,384]{1,0:T(8,128)(2,1)S(1)}, bf16[32,384]{1,0:T(8,128)(2,1)S(1)}, u32[]{:S(2)}, u32[]{:S(2)}) collective-permute-start(bf16[32,384]{1,0:T(8,128)(2,1)S(1)} %get-tuple-element.67), channel_id=1, source_target_pairs={{0,16},{4,20},{8,24},{12,28},{16,0},{20,4},{24,8},{28,12},{1,17},{... | collective-permute-start | bytes 73736 | tf_op jit(solution)/shard_map/ppermute | solution.py:533
  30.6 1.8 %collective-permute-start.3 = (bf16[32,384]{1,0:T(8,128)(2,1)S(1)}, bf16[32,384]{1,0:T(8,128)(2,1)S(1)}, u32[]{:S(2)}, u32[]{:S(2)}) collective-permute-start(bf16[32,384]{1,0:T(8,128)(2,1)S(1)} %get-tuple-element.67), channel_id=1, source_target_pairs={{0,8},{4,12},{8,0},{12,4},{16,24},{20,28},{24,16},{28,20},{1,9},{5... | collective-permute-start | bytes 73736 | tf_op jit(solution)/shard_map/ppermute | solution.py:533
  32.5 1.1 %second_half.1 = (bf16[32,8,384]{2,1,0:T(8,128)(2,1)S(1)}, f32[2,32,384]{2,1,0:T(8,128)S(1)}) custom-call(f32[8,128]{1,0:T(8,128)S(1)} %get-tuple-element.54.weights, bf16[32,16,512]{2,1,0:T(8,128)(2,1)S(1)} %all-to-all-done.stacked, bf16[512,512]{1,0:T(8,128)(2,1)S(1)} %copy-done.3, bf16[256,256]{1,0:T(8,128)(2,1)S(1)} %get-tuple-element.56.taper, ...), custom_call_target="tpu_custom_call" | custom-call | flops 1000000000 | tf_op jit(solution)/shard_map/second_half/pallas_call | solution.py:151
  33.5 0.2 collective-permute-done.5
  33.7 0.6 %collective-permute-done.4 = bf16[32,384]{1,0:T(8,128)(2,1)S(1)} collective-permute-done((bf16[32,384]{1,0:T(8,128)(2,1)S(1)}, bf16[32,384]{1,0:T(8,128)(2,1)S(1)}, u32[]{:S(2)}, u32[]{:S(2)}) %collective-permute-start.4) | collective-permute-done | bytes 24608 | tf_op jit(solution)/shard_map/ppermute | solution.py:533
  34.3 0.3 collective-permute-done.3
  34.6 0.0 collective-permute-done.6.below
  34.6 0.0 collective-permute-done.7.above
  34.6 0.1 collective-permute-start.8
  34.7 1.3 %collective-permute-done.8.refs_1_ = bf16[4,32,384]{2,1,0:T(8,128)(2,1)S(1)} collective-permute-done((bf16[4,32,384]{2,1,0:T(8,128)(2,1)S(1)}, bf16[4,32,384]{2,1,0:T(8,128)(2,1)S(1)}, u32[]{:S(2)}, u32[]{:S(2)}) %collective-permute-start.8) | collective-permute-done | bytes 98336 | tf_op jit(solution)/shard_map/ppermute | solution.py:541
  36.0 1.0 %combine.1 = (bf16[32,8,384]{2,1,0:T(8,128)(2,1)}, f32[2,32,384]{2,1,0:T(8,128)S(1)}) custom-call(bf16[32,8,384]{2,1,0:T(8,128)(2,1)S(1)} %get-tuple-element.65.grad, f32[2,32,384]{2,1,0:T(8,128)S(1)} %get-tuple-element.66.first, f32[2,32,384]{2,1,0:T(8,128)S(1)} %get-tuple-element.73.second, f32[4,32,384]{2,1,0:T(8,128)S(1)} %get-tuple-element.74.fields, ...), custom_call_target="tpu_custom_call" | custom-call | tf_op jit(solution)/shard_map/combine/pallas_call | solution.py:151
  36.9 3.0 %all-to-all-start.1 = ((bf16[32,8,384]{2,1,0:T(8,128)(2,1)}), bf16[32,8,384]{2,1,0:T(8,128)(2,1)S(1)}, u32[]{:S(2)}, u32[]{:S(2)}) async-start(bf16[32,8,384]{2,1,0:T(8,128)(2,1)} %get-tuple-element.77), calls=%async_computation.1 | async-start | bytes 393216 | tf_op jit(solution)/shard_map/all_to_all | solution.py:658
  39.9 0.0 copy-start.9
  40.0 0.2 hand_out.1
  40.2 1.8 %collective-permute-start.9 = (bf16[96,384]{1,0:T(8,128)(2,1)S(1)}, bf16[96,384]{1,0:T(8,128)(2,1)S(1)}, u32[]{:S(2)}, u32[]{:S(2)}) collective-permute-start(bf16[96,384]{1,0:T(8,128)(2,1)S(1)} %get-tuple-element.86), channel_id=1, source_target_pairs={{0,1},{1,0},{2,3},{3,2},{4,5},{5,4},{6,7},{7,6},{8,9},{9,8},{10,11... | collective-permute-start | bytes 221192 | tf_op jit(solution)/shard_map/ppermute | solution.py:523
  42.0 1.5 %collective-permute-start.10 = (bf16[96,384]{1,0:T(8,128)(2,1)S(1)}, bf16[96,384]{1,0:T(8,128)(2,1)S(1)}, u32[]{:S(2)}, u32[]{:S(2)}) collective-permute-start(bf16[96,384]{1,0:T(8,128)(2,1)S(1)} %get-tuple-element.87), channel_id=1, source_target_pairs={{0,2},{1,3},{2,0},{3,1},{4,6},{5,7},{6,4},{7,5},{8,10},{9,11},{10,... | collective-permute-start | bytes 221192 | tf_op jit(solution)/shard_map/ppermute | solution.py:523
  43.5 0.3 collective-permute-start.11
  43.7 0.0 copy-done.9
  43.7 0.3 first_gradient.1.grad_first
  44.1 1.7 %collective-permute-done.9.refs_1_ = bf16[96,384]{1,0:T(8,128)(2,1)S(1)} collective-permute-done((bf16[96,384]{1,0:T(8,128)(2,1)S(1)}, bf16[96,384]{1,0:T(8,128)(2,1)S(1)}, u32[]{:S(2)}, u32[]{:S(2)}) %collective-permute-start.9) | collective-permute-done | bytes 73760 | tf_op jit(solution)/shard_map/ppermute | solution.py:523
  45.7 1.9 %collective-permute-done.10.refs_2_ = bf16[96,384]{1,0:T(8,128)(2,1)S(1)} collective-permute-done((bf16[96,384]{1,0:T(8,128)(2,1)S(1)}, bf16[96,384]{1,0:T(8,128)(2,1)S(1)}, u32[]{:S(2)}, u32[]{:S(2)}) %collective-permute-start.10) | collective-permute-done | bytes 73760 | tf_op jit(solution)/shard_map/ppermute | solution.py:523
  47.6 1.5 %collective-permute-done.11.refs_3_ = bf16[96,384]{1,0:T(8,128)(2,1)S(1)} collective-permute-done((bf16[96,384]{1,0:T(8,128)(2,1)S(1)}, bf16[96,384]{1,0:T(8,128)(2,1)S(1)}, u32[]{:S(2)}, u32[]{:S(2)}) %collective-permute-start.11) | collective-permute-done | bytes 73760 | tf_op jit(solution)/shard_map/ppermute | solution.py:523
  49.0 0.5 join.1
  49.5 0.0 all-to-all-done.1.back
  49.5 1.3 %finish.1 = (f32[1,16,4,1440]{3,2,1,0:T(4,128)}, f32[16,4,1440]{2,1,0:T(4,128)}, f32[2,2,4,1440]{3,2,1,0:T(4,128)}) custom-call(bf16[32,8,384]{2,1,0:T(8,128)(2,1)S(1)} %all-to-all-done.1.back, f32[64,1440]{1,0:T(8,128)S(1)} %first_gradient.1.grad_first, f32[64,1440]{1,0:T(8,128)S(1)} %get-tuple-element.81.pulled_first, ...), custom_call_target="tpu_custom_call" | custom-call | tf_op jit(solution)/shard_map/finish/pallas_call | solution.py:678
  (4 shorter events, 0.0 us)
Async XLA Ops:
  3.3 7.4 %copy-start.1 = (bf16[2,16,4,1440]{3,2,1,0:T(4,128)(2,1)S(1)}, bf16[2,16,4,1440]{3,2,1,0:T(4,128)(2,1)}, u32[]{:S(2)}) copy-start(bf16[2,16,4,1440]{3,2,1,0:T(4,128)(2,1)} %innovation.1) | copy-start | bytes 1105924
  3.3 7.4 %copy-start.2 = (bf16[16,4,1440]{2,1,0:T(4,128)(2,1)S(1)}, bf16[16,4,1440]{2,1,0:T(4,128)(2,1)}, u32[]{:S(2)}) copy-start(bf16[16,4,1440]{2,1,0:T(4,128)(2,1)} %precision.1) | copy-start | bytes 552964
  3.3 7.4 %copy-start.7 = (f32[64,16]{1,0:T(8,128)S(1)}, f32[64,16]{1,0:T(8,128)}, u32[]{:S(2)}) copy-start(f32[64,16]{1,0:T(8,128)} %constant.23.clone.of_level) | copy-start | bytes 12292
  3.3 7.4 %copy-start.8 = (f32[64,64]{1,0:T(8,128)S(1)}, f32[64,64]{1,0:T(8,128)}, u32[]{:S(2)}) copy-start(f32[64,64]{1,0:T(8,128)} %constant.24.clone.same) | copy-start | bytes 49156
  3.3 23.6 %all-to-all-start = ((bf16[32,16,512]{2,1,0:T(8,128)(2,1)}), bf16[32,16,512]{2,1,0:T(8,128)(2,1)S(1)}, u32[]{:S(2)}, u32[]{:S(2)}) async-start(bf16[32,16,512]{2,1,0:T(8,128)(2,1)} %pack.1), calls=%async_computation | async-start | bytes 1048576 | tf_op jit(solution)/shard_map/all_to_all | solution.py:585
  10.6 0.7 %copy-start.10 = (f32[16,16]{1,0:T(8,128)S(1)}, f32[16,16]{1,0:T(8,128)}, u32[]{:S(2)}) copy-start(f32[16,16]{1,0:T(8,128)} %root.1) | copy-start | bytes 3076
  11.3 4.8 %copy-start.4 = (f32[256,256]{1,0:T(8,128)S(1)}, f32[256,256]{1,0:T(8,128)}, u32[]{:S(2)}) copy-start(f32[256,256]{1,0:T(8,128)} %constant.25.clone.apart) | copy-start | bytes 786436
  11.3 4.8 %copy-start.6 = (f32[256,1]{1,0:T(8,128)S(1)}, f32[256,1]{1,0:T(8,128)}, u32[]{:S(2)}) copy-start(f32[256,1]{1,0:T(8,128)} %constant.26.clone.level) | copy-start | bytes 3076
  11.3 4.8 %copy-start.11 = (s32[16]{0:T(128)S(1)}, s32[16]{0:T(128)}, u32[]{:S(2)}) copy-start(s32[16]{0:T(128)} %widths.1) | copy-start | bytes 196
  11.4 4.8 %copy-start.12 = (f32[8]{0:T(128)S(1)}, f32[8]{0:T(128)}, u32[]{:S(2)}) copy-start(f32[8]{0:T(128)} %weight.1) | copy-start | bytes 100
  11.4 6.1 %copy-start.5 = (bf16[512,256]{1,0:T(8,128)(2,1)S(1)}, bf16[512,256]{1,0:T(8,128)(2,1)}, u32[]{:S(2)}) copy-start(bf16[512,256]{1,0:T(8,128)(2,1)} %constant.27.clone.kernel) | copy-start | bytes 786436
  12.5 5.0 %copy-start = (bf16[1,2,16,4,1440]{4,3,2,1,0:T(4,128)(2,1)S(1)}, bf16[1,2,16,4,1440]{4,3,2,1,0:T(4,128)(2,1)}, u32[]{:S(2)}) copy-start(bf16[1,2,16,4,1440]{4,3,2,1,0:T(4,128)(2,1)} %ensemble.2) | copy-start | bytes 1105924
  12.5 4.9 %collective-permute-start.1 = (bf16[32,512]{1,0:T(8,128)(2,1)S(1)}, bf16[32,512]{1,0:T(8,128)(2,1)S(1)}, u32[]{:S(2)}, u32[]{:S(2)}) collective-permute-start(bf16[32,512]{1,0:T(8,128)(2,1)S(1)} %get-tuple-element.60), channel_id=1, source_target_pairs={{0,2},{1,3},{2,0},{3,1},{4,6},{5,7},{6,4},{7,5},{8,10},{9,11},{10,... | collective-permute-start | bytes 98312 | tf_op jit(solution)/shard_map/ppermute | solution.py:523
  14.4 6.4 %collective-permute-start = (bf16[32,512]{1,0:T(8,128)(2,1)S(1)}, bf16[32,512]{1,0:T(8,128)(2,1)S(1)}, u32[]{:S(2)}, u32[]{:S(2)}) collective-permute-start(bf16[32,512]{1,0:T(8,128)(2,1)S(1)} %get-tuple-element.59), channel_id=1, source_target_pairs={{0,1},{1,0},{2,3},{3,2},{4,5},{5,4},{6,7},{7,6},{8,9},{9,8},{10,11... | collective-permute-start | bytes 98312 | tf_op jit(solution)/shard_map/ppermute | solution.py:523
  15.8 5.0 %collective-permute-start.2 = (bf16[32,512]{1,0:T(8,128)(2,1)S(1)}, bf16[32,512]{1,0:T(8,128)(2,1)S(1)}, u32[]{:S(2)}, u32[]{:S(2)}) collective-permute-start(bf16[32,512]{1,0:T(8,128)(2,1)S(1)} %get-tuple-element.63), channel_id=1, source_target_pairs={{0,3},{1,2},{2,1},{3,0},{4,7},{5,6},{6,5},{7,4},{8,11},{9,10},{10,... | collective-permute-start | bytes 98312 | tf_op jit(solution)/shard_map/ppermute | solution.py:523
  17.5 9.4 %copy-start.3 = (bf16[512,512]{1,0:T(8,128)(2,1)S(1)}, bf16[512,512]{1,0:T(8,128)(2,1)}, u32[]{:S(2)}) copy-start(bf16[512,512]{1,0:T(8,128)(2,1)} %constant.28.clone.ring) | copy-start | bytes 1572868
  18.0 16.5 %collective-permute-start.6 = (bf16[64,1440]{1,0:T(8,128)(2,1)S(1)}, bf16[64,1440]{1,0:T(8,128)(2,1)S(1)}, u32[]{:S(2)}, u32[]{:S(2)}) collective-permute-start(bf16[64,1440]{1,0:T(8,128)(2,1)S(1)} %fold_smooth.1.middle), channel_id=1, source_target_pairs={{0,1},{2,3},{1,0},{3,2},{4,5},{6,7},{5,4},{7,6},{8,9},{10,11},{9,8... | collective-permute-start | bytes 552968 | tf_op jit(solution)/shard_map/ppermute | solution.py:627
  20.1 14.4 %collective-permute-start.7 = (bf16[64,1440]{1,0:T(8,128)(2,1)S(1)}, bf16[64,1440]{1,0:T(8,128)(2,1)S(1)}, u32[]{:S(2)}, u32[]{:S(2)}) collective-permute-start(bf16[64,1440]{1,0:T(8,128)(2,1)S(1)} %fold_smooth.1.middle), channel_id=1, source_target_pairs={{1,2},{2,1},{5,6},{6,5},{9,10},{10,9},{13,14},{14,13},{17,18},{18,... | collective-permute-start | bytes 552968 | tf_op jit(solution)/shard_map/ppermute | solution.py:627
  28.0 5.7 %collective-permute-start.5 = (bf16[32,384]{1,0:T(8,128)(2,1)S(1)}, bf16[32,384]{1,0:T(8,128)(2,1)S(1)}, u32[]{:S(2)}, u32[]{:S(2)}) collective-permute-start(bf16[32,384]{1,0:T(8,128)(2,1)S(1)} %get-tuple-element.67), channel_id=1, source_target_pairs={{0,24},{4,28},{8,16},{12,20},{16,8},{20,12},{24,0},{28,4},{1,25},{... | collective-permute-start | bytes 73736 | tf_op jit(solution)/shard_map/ppermute | solution.py:533
  29.6 4.7 %collective-permute-start.4 = (bf16[32,384]{1,0:T(8,128)(2,1)S(1)}, bf16[32,384]{1,0:T(8,128)(2,1)S(1)}, u32[]{:S(2)}, u32[]{:S(2)}) collective-permute-start(bf16[32,384]{1,0:T(8,128)(2,1)S(1)} %get-tuple-element.67), channel_id=1, source_target_pairs={{0,16},{4,20},{8,24},{12,28},{16,0},{20,4},{24,8},{28,12},{1,17},{... | collective-permute-start | bytes 73736 | tf_op jit(solution)/shard_map/ppermute | solution.py:533
  30.6 3.9 %collective-permute-start.3 = (bf16[32,384]{1,0:T(8,128)(2,1)S(1)}, bf16[32,384]{1,0:T(8,128)(2,1)S(1)}, u32[]{:S(2)}, u32[]{:S(2)}) collective-permute-start(bf16[32,384]{1,0:T(8,128)(2,1)S(1)} %get-tuple-element.67), channel_id=1, source_target_pairs={{0,8},{4,12},{8,0},{12,4},{16,24},{20,28},{24,16},{28,20},{1,9},{5... | collective-permute-start | bytes 73736 | tf_op jit(solution)/shard_map/ppermute | solution.py:533
  34.6 1.4 %collective-permute-start.8 = (bf16[4,32,384]{2,1,0:T(8,128)(2,1)S(1)}, bf16[4,32,384]{2,1,0:T(8,128)(2,1)S(1)}, u32[]{:S(2)}, u32[]{:S(2)}) collective-permute-start(bf16[4,32,384]{2,1,0:T(8,128)(2,1)S(1)} %pad_maximum_fusion.refs_0_), channel_id=1, source_target_pairs={{0,4},{4,0},{8,12},{12,8},{16,20},{20,16},{24,28},{28,24},{1,5},{5... | collective-permute-start | bytes 294920 | tf_op jit(solution)/shard_map/ppermute | solution.py:541
  36.9 12.6 %all-to-all-start.1 = ((bf16[32,8,384]{2,1,0:T(8,128)(2,1)}), bf16[32,8,384]{2,1,0:T(8,128)(2,1)S(1)}, u32[]{:S(2)}, u32[]{:S(2)}) async-start(bf16[32,8,384]{2,1,0:T(8,128)(2,1)} %get-tuple-element.77), calls=%async_computation.1 | async-start | bytes 393216 | tf_op jit(solution)/shard_map/all_to_all | solution.py:658
  39.9 3.8 %copy-start.9 = (f32[64,192]{1,0:T(8,128)S(1)}, f32[64,192]{1,0:T(8,128)}, u32[]{:S(2)}) copy-start(f32[64,192]{1,0:T(8,128)} %constant.29.clone.apart) | copy-start | bytes 147460
  40.2 5.5 %collective-permute-start.9 = (bf16[96,384]{1,0:T(8,128)(2,1)S(1)}, bf16[96,384]{1,0:T(8,128)(2,1)S(1)}, u32[]{:S(2)}, u32[]{:S(2)}) collective-permute-start(bf16[96,384]{1,0:T(8,128)(2,1)S(1)} %get-tuple-element.86), channel_id=1, source_target_pairs={{0,1},{1,0},{2,3},{3,2},{4,5},{5,4},{6,7},{7,6},{8,9},{9,8},{10,11... | collective-permute-start | bytes 221192 | tf_op jit(solution)/shard_map/ppermute | solution.py:523
  42.0 5.6 %collective-permute-start.10 = (bf16[96,384]{1,0:T(8,128)(2,1)S(1)}, bf16[96,384]{1,0:T(8,128)(2,1)S(1)}, u32[]{:S(2)}, u32[]{:S(2)}) collective-permute-start(bf16[96,384]{1,0:T(8,128)(2,1)S(1)} %get-tuple-element.87), channel_id=1, source_target_pairs={{0,2},{1,3},{2,0},{3,1},{4,6},{5,7},{6,4},{7,5},{8,10},{9,11},{10,... | collective-permute-start | bytes 221192 | tf_op jit(solution)/shard_map/ppermute | solution.py:523
  43.5 5.6 %collective-permute-start.11 = (bf16[96,384]{1,0:T(8,128)(2,1)S(1)}, bf16[96,384]{1,0:T(8,128)(2,1)S(1)}, u32[]{:S(2)}, u32[]{:S(2)}) collective-permute-start(bf16[96,384]{1,0:T(8,128)(2,1)S(1)} %get-tuple-element.88), channel_id=1, source_target_pairs={{0,3},{1,2},{2,1},{3,0},{4,7},{5,6},{6,5},{7,4},{8,11},{9,10},{10,... | collective-permute-start | bytes 221192 | tf_op jit(solution)/shard_map/ppermute | solution.py:523

commit v13 on v12

--- a/solution.py
+++ b/solution.py
@@ -15,6 +15,7 @@
 FEW = 8
 SUMS = 4
 PARTS = 3
+HALVES = 2
 BOTH = ("member", "band")
 
 ensemble_share = 0.8
@@ -86,14 +87,14 @@
 
 def parts_dot(matrix, field):
     count, parts = matrix.shape[0], []
-    for _ in range(PARTS):
+    for _ in range(HALVES):
         part = matrix.astype(jnp.bfloat16).astype(jnp.float32)
         parts.append(part)
         matrix = matrix - part
     stacked = jnp.concatenate(parts, axis=0).astype(jnp.bfloat16)
     products = jnp.dot(stacked, field, preferred_element_type=jnp.float32)
     total = products[:count]
-    for index in range(1, PARTS):
+    for index in range(1, HALVES):
         total = total + products[index * count : (index + 1) * count]
     return total
 
@@ -470,10 +471,11 @@
 
             static_copy = outgoing(members, static, static_out)
             image_copy = outgoing(members + 1, image, image_out)
-            total = back[0, :1].astype(f32)
+            tile = lon_share // LANES * LANES
+            total = back[0, :1, tile:].astype(f32)
             for block in range(1, members * bands):
-                total = total + back[block, :1].astype(f32)
-            lane = lax.broadcasted_iota(jnp.int32, total.shape, 1) - lon_share
+                total = total + back[block, :1, tile:].astype(f32)
+            lane = lax.broadcasted_iota(jnp.int32, total.shape, 1) + tile - lon_share
             first_norm, first_image, cross, second_image = [
                 jnp.sum(
                     jnp.where((lane >= PARTS * index) & (lane < PARTS * (index + 1)), total, 0.0),

time: 51.2 us -> 51.1 us (level)
  no operation moved by 1% of the time
where the time goes in v13:
time: 51.1 us; the launch traced here: 50.7 us
  starting transfers between devices  24.7 us (48%)
  waiting for transfers between devices  13.4 us (26%)
  Pallas kernels  10.3 us (20%)
  between operations  1.59 us (3%)
  local copies, waits for them, and re-layouts  0.72 us (1%)
    all_to_all x1, starting transfers between devices, shards(): stacked = lax.all_to_all(pieces, BOTH, 0, 0, tiled=True)  7.3 us
    ppermute x6, starting transfers between devices, trade(): lax.ppermute(blocks[shift], 'band', [(at, partner(at, shift, bands, 1)) f...  7.11 us
    pallas_call x9, Pallas kernels, call(): pl.pallas_call(body, out_shape=tuple((jax.ShapeDtypeStruct(shape, kind) f...  7.04 us
    all_to_all x1, waiting for transfers between devices, shards(): stacked = lax.all_to_all(pieces, BOTH, 0, 0, tiled=True)  6.1 us
    ppermute x6, waiting for transfers between devices, trade(): lax.ppermute(blocks[shift], 'band', [(at, partner(at, shift, bands, 1)) f...  4.98 us
    ppermute x3, starting transfers between devices, around(): lax.ppermute(block, 'member', [(at, 2 * partner(at // 2, shift, members /...  4.45 us
    all_to_all x1, starting transfers between devices, shards(): back = lax.all_to_all(grad, BOTH, 0, 0, tiled=True)  3.03 us
    ppermute x2, starting transfers between devices, shards(): lax.ppermute(smoothed, 'band', pairs[start::2] + [(to, at) for at, to in...  2.75 us
  transfers between devices with their start and end apart: 14, of which 8 were waited for; matrix products, arithmetic and copies ran while one was open for 0% of the time, Pallas kernels for 12%

profile of v13, /device:TPU:0, one launch (start us, length us, event | category | flops | bytes accessed | tf_op | source)
XLA Modules:
  0.0 50.7 jit_solution(232298461285455167)
XLA Ops:
  1.3 2.0 %pack.1 = bf16[32,16,512]{2,1,0:T(8,128)(2,1)} custom-call(s32[1]{0:T(128)S(6)} %copy.17.slot.marks, bf16[1,2,16,4,1440]{4,3,2,1,0:T(4,128)(2,1)} %ensemble.2), custom_call_target="tpu_custom_call" | custom-call | tf_op jit(solution)/shard_map/pack/pallas_call | solution.py:568
  3.3 0.0 copy-start.1
  3.3 0.0 copy-start.2
  3.3 0.0 copy-start.7
  3.3 0.0 copy-start.8
  3.3 7.3 %all-to-all-start = ((bf16[32,16,512]{2,1,0:T(8,128)(2,1)}), bf16[32,16,512]{2,1,0:T(8,128)(2,1)S(1)}, u32[]{:S(2)}, u32[]{:S(2)}) async-start(bf16[32,16,512]{2,1,0:T(8,128)(2,1)} %pack.1), calls=%async_computation | async-start | bytes 1048576 | tf_op jit(solution)/shard_map/all_to_all | solution.py:587
  10.6 0.0 copy-start.10
  10.7 0.0 copy-done.1
  10.7 0.0 copy-done.2
  10.7 0.0 copy-done.7
  10.7 0.0 copy-done.8
  10.7 0.6 %copy-done.10 = f32[16,16]{1,0:T(8,128)S(1)} copy-done((f32[16,16]{1,0:T(8,128)S(1)}, f32[16,16]{1,0:T(8,128)}, u32[]{:S(2)}) %copy-start.10) | copy-done | bytes 1048
  11.3 0.0 copy-start.4
  11.3 0.0 copy-start.6
  11.3 0.0 copy-start.11
  11.4 0.0 copy-start.5
  11.4 1.1 %observe.1 = (bf16[32,512]{1,0:T(8,128)(2,1)S(1)}, bf16[32,512]{1,0:T(8,128)(2,1)S(1)}, bf16[32,512]{1,0:T(8,128)(2,1)S(1)}, bf16[32,512]{1,0:T(8,128)(2,1)S(1)}...) custom-call(s32[1,128]{1,0:T(1,128)S(1)} %broadcast_in_dim.6.place, s32[1,128]{1,0:T(1,128)S(1)} %broadcast_in_dim.7.turn, ...), custom_call_target="tpu_custom_call" | custom-call | tf_op jit(solution)/shard_map/observe/pallas_call | solution.py:152
  12.5 0.0 copy-start
  12.5 1.8 %collective-permute-start.1 = (bf16[32,512]{1,0:T(8,128)(2,1)S(1)}, bf16[32,512]{1,0:T(8,128)(2,1)S(1)}, u32[]{:S(2)}, u32[]{:S(2)}) collective-permute-start(bf16[32,512]{1,0:T(8,128)(2,1)S(1)} %get-tuple-element.60), channel_id=1, source_target_pairs={{0,2},{1,3},{2,0},{3,1},{4,6},{5,7},{6,4},{7,5},{8,10},{9,11},{10,... | collective-permute-start | bytes 98312 | tf_op jit(solution)/shard_map/ppermute | solution.py:525
  14.3 1.5 %collective-permute-start = (bf16[32,512]{1,0:T(8,128)(2,1)S(1)}, bf16[32,512]{1,0:T(8,128)(2,1)S(1)}, u32[]{:S(2)}, u32[]{:S(2)}) collective-permute-start(bf16[32,512]{1,0:T(8,128)(2,1)S(1)} %get-tuple-element.59), channel_id=1, source_target_pairs={{0,1},{1,0},{2,3},{3,2},{4,5},{5,4},{6,7},{7,6},{8,9},{9,8},{10,11... | collective-permute-start | bytes 98312 | tf_op jit(solution)/shard_map/ppermute | solution.py:525
  15.8 0.3 collective-permute-start.2
  16.1 0.0 copy-done.4
  16.1 0.0 copy-done.6
  16.1 0.0 copy-done.11
  16.1 0.0 copy-done.12
  16.1 1.4 %prepare.1 = (f32[8,64]{1,0:T(8,128)S(1)}, f32[64,64]{1,0:T(8,128)S(1)}, bf16[256,256]{1,0:T(8,128)(2,1)S(1)}, f32[256,1]{1,0:T(8,128)S(1)}, f32[8,128]{1,0:T(8,...) custom-call(s32[1]{0:T(128)} %bitcast.here, s32[16]{0:T(128)S(1)} %copy-done.11, f32[8]{0:T(128)S(1)} %copy-done.12, ...), custom_call_target="tpu_custom_call" | custom-call | tf_op jit(solution)/shard_map/prepare/pallas_call | solution.py:152
  17.4 0.0 collective-permute-done.1.refs_2_
  17.4 0.0 copy-done.5
  17.5 0.0 copy-done
  17.5 0.0 copy-start.3
  17.5 0.5 fold_smooth.1.middle
  18.0 2.1 %collective-permute-start.6 = (bf16[64,1440]{1,0:T(8,128)(2,1)S(1)}, bf16[64,1440]{1,0:T(8,128)(2,1)S(1)}, u32[]{:S(2)}, u32[]{:S(2)}) collective-permute-start(bf16[64,1440]{1,0:T(8,128)(2,1)S(1)} %fold_smooth.1.middle), channel_id=1, source_target_pairs={{0,1},{2,3},{1,0},{3,2},{4,5},{6,7},{5,4},{7,6},{8,9},{10,11},{9,8... | collective-permute-start | bytes 552968 | tf_op jit(solution)/shard_map/ppermute | solution.py:629
  20.1 0.7 %collective-permute-start.7 = (bf16[64,1440]{1,0:T(8,128)(2,1)S(1)}, bf16[64,1440]{1,0:T(8,128)(2,1)S(1)}, u32[]{:S(2)}, u32[]{:S(2)}) collective-permute-start(bf16[64,1440]{1,0:T(8,128)(2,1)S(1)} %fold_smooth.1.middle), channel_id=1, source_target_pairs={{1,2},{2,1},{5,6},{6,5},{9,10},{10,9},{13,14},{14,13},{17,18},{18,... | collective-permute-start | bytes 552968 | tf_op jit(solution)/shard_map/ppermute | solution.py:629
  20.8 0.0 collective-permute-done.refs_1_
  20.8 0.0 collective-permute-done.2.refs_3_
  20.8 6.1 %all-to-all-done.stacked = bf16[32,16,512]{2,1,0:T(8,128)(2,1)S(1)} async-done(((bf16[32,16,512]{2,1,0:T(8,128)(2,1)}), bf16[32,16,512]{2,1,0:T(8,128)(2,1)S(1)}, u32[]{:S(2)}, u32[]{:S(2)}) %all-to-all-start) | async-done | bytes 524320 | tf_op jit(solution)/shard_map/all_to_all | solution.py:587
  26.9 0.0 copy-done.3
  26.9 1.1 %first_half.1 = (bf16[32,384]{1,0:T(8,128)(2,1)S(1)}, f32[2,32,512]{2,1,0:T(8,128)S(1)}, f32[2,32,384]{2,1,0:T(8,128)S(1)}, f32[4,32,384]{2,1,0:T(8,128)S(1)}) custom-call(f32[8,128]{1,0:T(8,128)S(1)} %get-tuple-element.54.weights, s32[1,128]{1,0:T(1,128)S(1)} %broadcast_in_dim.7.turn, bf16[32,16,512]{2,1,0:T(8,128)(2,1)S(1)} %all-to-all-done.stacked, ...), custom_call_target="tpu_custom_call" | custom-call | tf_op jit(solution)/shard_map/first_half/pallas_call | solution.py:152
  28.0 1.5 %collective-permute-start.5 = (bf16[32,384]{1,0:T(8,128)(2,1)S(1)}, bf16[32,384]{1,0:T(8,128)(2,1)S(1)}, u32[]{:S(2)}, u32[]{:S(2)}) collective-permute-start(bf16[32,384]{1,0:T(8,128)(2,1)S(1)} %get-tuple-element.67), channel_id=1, source_target_pairs={{0,24},{4,28},{8,16},{12,20},{16,8},{20,12},{24,0},{28,4},{1,25},{... | collective-permute-start | bytes 73736 | tf_op jit(solution)/shard_map/ppermute | solution.py:535
  29.6 1.1 %collective-permute-start.4 = (bf16[32,384]{1,0:T(8,128)(2,1)S(1)}, bf16[32,384]{1,0:T(8,128)(2,1)S(1)}, u32[]{:S(2)}, u32[]{:S(2)}) collective-permute-start(bf16[32,384]{1,0:T(8,128)(2,1)S(1)} %get-tuple-element.67), channel_id=1, source_target_pairs={{0,16},{4,20},{8,24},{12,28},{16,0},{20,4},{24,8},{28,12},{1,17},{... | collective-permute-start | bytes 73736 | tf_op jit(solution)/shard_map/ppermute | solution.py:535
  30.6 1.8 %collective-permute-start.3 = (bf16[32,384]{1,0:T(8,128)(2,1)S(1)}, bf16[32,384]{1,0:T(8,128)(2,1)S(1)}, u32[]{:S(2)}, u32[]{:S(2)}) collective-permute-start(bf16[32,384]{1,0:T(8,128)(2,1)S(1)} %get-tuple-element.67), channel_id=1, source_target_pairs={{0,8},{4,12},{8,0},{12,4},{16,24},{20,28},{24,16},{28,20},{1,9},{5... | collective-permute-start | bytes 73736 | tf_op jit(solution)/shard_map/ppermute | solution.py:535
  32.5 1.1 %second_half.1 = (bf16[32,8,384]{2,1,0:T(8,128)(2,1)S(1)}, f32[2,32,384]{2,1,0:T(8,128)S(1)}) custom-call(f32[8,128]{1,0:T(8,128)S(1)} %get-tuple-element.54.weights, bf16[32,16,512]{2,1,0:T(8,128)(2,1)S(1)} %all-to-all-done.stacked, bf16[512,512]{1,0:T(8,128)(2,1)S(1)} %copy-done.3, bf16[256,256]{1,0:T(8,128)(2,1)S(1)} %get-tuple-element.56.taper, ...), custom_call_target="tpu_custom_call" | custom-call | flops 1000000000 | tf_op jit(solution)/shard_map/second_half/pallas_call | solution.py:152
  33.5 0.2 collective-permute-done.5
  33.7 0.6 %collective-permute-done.4 = bf16[32,384]{1,0:T(8,128)(2,1)S(1)} collective-permute-done((bf16[32,384]{1,0:T(8,128)(2,1)S(1)}, bf16[32,384]{1,0:T(8,128)(2,1)S(1)}, u32[]{:S(2)}, u32[]{:S(2)}) %collective-permute-start.4) | collective-permute-done | bytes 24608 | tf_op jit(solution)/shard_map/ppermute | solution.py:535
  34.3 0.3 collective-permute-done.3
  34.6 0.0 collective-permute-done.6.below
  34.6 0.0 collective-permute-done.7.above
  34.6 0.1 collective-permute-start.8
  34.7 1.3 %collective-permute-done.8.refs_1_ = bf16[4,32,384]{2,1,0:T(8,128)(2,1)S(1)} collective-permute-done((bf16[4,32,384]{2,1,0:T(8,128)(2,1)S(1)}, bf16[4,32,384]{2,1,0:T(8,128)(2,1)S(1)}, u32[]{:S(2)}, u32[]{:S(2)}) %collective-permute-start.8) | collective-permute-done | bytes 98336 | tf_op jit(solution)/shard_map/ppermute | solution.py:543
  36.0 0.9 %combine.1 = (bf16[32,8,384]{2,1,0:T(8,128)(2,1)}, f32[2,32,384]{2,1,0:T(8,128)S(1)}) custom-call(bf16[32,8,384]{2,1,0:T(8,128)(2,1)S(1)} %get-tuple-element.65.grad, f32[2,32,384]{2,1,0:T(8,128)S(1)} %get-tuple-element.66.first, f32[2,32,384]{2,1,0:T(8,128)S(1)} %get-tuple-element.73.second, f32[4,32,384]{2,1,0:T(8,128)S(1)} %get-tuple-element.74.fields, ...), custom_call_target="tpu_custom_call" | custom-call | tf_op jit(solution)/shard_map/combine/pallas_call | solution.py:152
  36.9 3.0 %all-to-all-start.1 = ((bf16[32,8,384]{2,1,0:T(8,128)(2,1)}), bf16[32,8,384]{2,1,0:T(8,128)(2,1)S(1)}, u32[]{:S(2)}, u32[]{:S(2)}) async-start(bf16[32,8,384]{2,1,0:T(8,128)(2,1)} %get-tuple-element.77), calls=%async_computation.1 | async-start | bytes 393216 | tf_op jit(solution)/shard_map/all_to_all | solution.py:660
  39.9 0.0 copy-start.9
  39.9 0.2 hand_out.1
  40.2 1.8 %collective-permute-start.9 = (bf16[96,384]{1,0:T(8,128)(2,1)S(1)}, bf16[96,384]{1,0:T(8,128)(2,1)S(1)}, u32[]{:S(2)}, u32[]{:S(2)}) collective-permute-start(bf16[96,384]{1,0:T(8,128)(2,1)S(1)} %get-tuple-element.86), channel_id=1, source_target_pairs={{0,1},{1,0},{2,3},{3,2},{4,5},{5,4},{6,7},{7,6},{8,9},{9,8},{10,11... | collective-permute-start | bytes 221192 | tf_op jit(solution)/shard_map/ppermute | solution.py:525
  42.0 1.5 %collective-permute-start.10 = (bf16[96,384]{1,0:T(8,128)(2,1)S(1)}, bf16[96,384]{1,0:T(8,128)(2,1)S(1)}, u32[]{:S(2)}, u32[]{:S(2)}) collective-permute-start(bf16[96,384]{1,0:T(8,128)(2,1)S(1)} %get-tuple-element.87), channel_id=1, source_target_pairs={{0,2},{1,3},{2,0},{3,1},{4,6},{5,7},{6,4},{7,5},{8,10},{9,11},{10,... | collective-permute-start | bytes 221192 | tf_op jit(solution)/shard_map/ppermute | solution.py:525
  43.5 0.3 collective-permute-start.11
  43.7 0.0 copy-done.9
  43.7 0.3 first_gradient.1.grad_first
  44.1 1.6 %collective-permute-done.9.refs_1_ = bf16[96,384]{1,0:T(8,128)(2,1)S(1)} collective-permute-done((bf16[96,384]{1,0:T(8,128)(2,1)S(1)}, bf16[96,384]{1,0:T(8,128)(2,1)S(1)}, u32[]{:S(2)}, u32[]{:S(2)}) %collective-permute-start.9) | collective-permute-done | bytes 73760 | tf_op jit(solution)/shard_map/ppermute | solution.py:525
  45.7 1.9 %collective-permute-done.10.refs_2_ = bf16[96,384]{1,0:T(8,128)(2,1)S(1)} collective-permute-done((bf16[96,384]{1,0:T(8,128)(2,1)S(1)}, bf16[96,384]{1,0:T(8,128)(2,1)S(1)}, u32[]{:S(2)}, u32[]{:S(2)}) %collective-permute-start.10) | collective-permute-done | bytes 73760 | tf_op jit(solution)/shard_map/ppermute | solution.py:525
  47.6 1.5 %collective-permute-done.11.refs_3_ = bf16[96,384]{1,0:T(8,128)(2,1)S(1)} collective-permute-done((bf16[96,384]{1,0:T(8,128)(2,1)S(1)}, bf16[96,384]{1,0:T(8,128)(2,1)S(1)}, u32[]{:S(2)}, u32[]{:S(2)}) %collective-permute-start.11) | collective-permute-done | bytes 73760 | tf_op jit(solution)/shard_map/ppermute | solution.py:525
  49.0 0.4 join.1
  49.5 0.0 all-to-all-done.1.back
  49.5 1.3 %finish.1 = (f32[1,16,4,1440]{3,2,1,0:T(4,128)}, f32[16,4,1440]{2,1,0:T(4,128)}, f32[2,2,4,1440]{3,2,1,0:T(4,128)}) custom-call(bf16[32,8,384]{2,1,0:T(8,128)(2,1)S(1)} %all-to-all-done.1.back, f32[64,1440]{1,0:T(8,128)S(1)} %first_gradient.1.grad_first, f32[64,1440]{1,0:T(8,128)S(1)} %get-tuple-element.81.pulled_first, ...), custom_call_target="tpu_custom_call" | custom-call | tf_op jit(solution)/shard_map/finish/pallas_call | solution.py:680
  (4 shorter events, 0.0 us)
Async XLA Ops:
  3.3 7.4 %copy-start.1 = (bf16[2,16,4,1440]{3,2,1,0:T(4,128)(2,1)S(1)}, bf16[2,16,4,1440]{3,2,1,0:T(4,128)(2,1)}, u32[]{:S(2)}) copy-start(bf16[2,16,4,1440]{3,2,1,0:T(4,128)(2,1)} %innovation.1) | copy-start | bytes 1105924
  3.3 7.4 %copy-start.2 = (bf16[16,4,1440]{2,1,0:T(4,128)(2,1)S(1)}, bf16[16,4,1440]{2,1,0:T(4,128)(2,1)}, u32[]{:S(2)}) copy-start(bf16[16,4,1440]{2,1,0:T(4,128)(2,1)} %precision.1) | copy-start | bytes 552964
  3.3 7.4 %copy-start.7 = (f32[64,16]{1,0:T(8,128)S(1)}, f32[64,16]{1,0:T(8,128)}, u32[]{:S(2)}) copy-start(f32[64,16]{1,0:T(8,128)} %constant.23.clone.of_level) | copy-start | bytes 12292
  3.3 7.4 %copy-start.8 = (f32[64,64]{1,0:T(8,128)S(1)}, f32[64,64]{1,0:T(8,128)}, u32[]{:S(2)}) copy-start(f32[64,64]{1,0:T(8,128)} %constant.24.clone.same) | copy-start | bytes 49156
  3.3 23.6 %all-to-all-start = ((bf16[32,16,512]{2,1,0:T(8,128)(2,1)}), bf16[32,16,512]{2,1,0:T(8,128)(2,1)S(1)}, u32[]{:S(2)}, u32[]{:S(2)}) async-start(bf16[32,16,512]{2,1,0:T(8,128)(2,1)} %pack.1), calls=%async_computation | async-start | bytes 1048576 | tf_op jit(solution)/shard_map/all_to_all | solution.py:587
  10.6 0.7 %copy-start.10 = (f32[16,16]{1,0:T(8,128)S(1)}, f32[16,16]{1,0:T(8,128)}, u32[]{:S(2)}) copy-start(f32[16,16]{1,0:T(8,128)} %root.1) | copy-start | bytes 3076
  11.3 4.7 %copy-start.4 = (f32[256,256]{1,0:T(8,128)S(1)}, f32[256,256]{1,0:T(8,128)}, u32[]{:S(2)}) copy-start(f32[256,256]{1,0:T(8,128)} %constant.25.clone.apart) | copy-start | bytes 786436
  11.3 4.7 %copy-start.6 = (f32[256,1]{1,0:T(8,128)S(1)}, f32[256,1]{1,0:T(8,128)}, u32[]{:S(2)}) copy-start(f32[256,1]{1,0:T(8,128)} %constant.26.clone.level) | copy-start | bytes 3076
  11.3 4.7 %copy-start.11 = (s32[16]{0:T(128)S(1)}, s32[16]{0:T(128)}, u32[]{:S(2)}) copy-start(s32[16]{0:T(128)} %widths.1) | copy-start | bytes 196
  11.4 4.7 %copy-start.12 = (f32[8]{0:T(128)S(1)}, f32[8]{0:T(128)}, u32[]{:S(2)}) copy-start(f32[8]{0:T(128)} %weight.1) | copy-start | bytes 100
  11.4 6.1 %copy-start.5 = (bf16[512,256]{1,0:T(8,128)(2,1)S(1)}, bf16[512,256]{1,0:T(8,128)(2,1)}, u32[]{:S(2)}) copy-start(bf16[512,256]{1,0:T(8,128)(2,1)} %constant.27.clone.kernel) | copy-start | bytes 786436
  12.5 5.0 %copy-start = (bf16[1,2,16,4,1440]{4,3,2,1,0:T(4,128)(2,1)S(1)}, bf16[1,2,16,4,1440]{4,3,2,1,0:T(4,128)(2,1)}, u32[]{:S(2)}) copy-start(bf16[1,2,16,4,1440]{4,3,2,1,0:T(4,128)(2,1)} %ensemble.2) | copy-start | bytes 1105924
  12.5 4.9 %collective-permute-start.1 = (bf16[32,512]{1,0:T(8,128)(2,1)S(1)}, bf16[32,512]{1,0:T(8,128)(2,1)S(1)}, u32[]{:S(2)}, u32[]{:S(2)}) collective-permute-start(bf16[32,512]{1,0:T(8,128)(2,1)S(1)} %get-tuple-element.60), channel_id=1, source_target_pairs={{0,2},{1,3},{2,0},{3,1},{4,6},{5,7},{6,4},{7,5},{8,10},{9,11},{10,... | collective-permute-start | bytes 98312 | tf_op jit(solution)/shard_map/ppermute | solution.py:525
  14.3 6.4 %collective-permute-start = (bf16[32,512]{1,0:T(8,128)(2,1)S(1)}, bf16[32,512]{1,0:T(8,128)(2,1)S(1)}, u32[]{:S(2)}, u32[]{:S(2)}) collective-permute-start(bf16[32,512]{1,0:T(8,128)(2,1)S(1)} %get-tuple-element.59), channel_id=1, source_target_pairs={{0,1},{1,0},{2,3},{3,2},{4,5},{5,4},{6,7},{7,6},{8,9},{9,8},{10,11... | collective-permute-start | bytes 98312 | tf_op jit(solution)/shard_map/ppermute | solution.py:525
  15.8 5.0 %collective-permute-start.2 = (bf16[32,512]{1,0:T(8,128)(2,1)S(1)}, bf16[32,512]{1,0:T(8,128)(2,1)S(1)}, u32[]{:S(2)}, u32[]{:S(2)}) collective-permute-start(bf16[32,512]{1,0:T(8,128)(2,1)S(1)} %get-tuple-element.63), channel_id=1, source_target_pairs={{0,3},{1,2},{2,1},{3,0},{4,7},{5,6},{6,5},{7,4},{8,11},{9,10},{10,... | collective-permute-start | bytes 98312 | tf_op jit(solution)/shard_map/ppermute | solution.py:525
  17.5 9.4 %copy-start.3 = (bf16[512,512]{1,0:T(8,128)(2,1)S(1)}, bf16[512,512]{1,0:T(8,128)(2,1)}, u32[]{:S(2)}) copy-start(bf16[512,512]{1,0:T(8,128)(2,1)} %constant.28.clone.ring) | copy-start | bytes 1572868
  18.0 16.5 %collective-permute-start.6 = (bf16[64,1440]{1,0:T(8,128)(2,1)S(1)}, bf16[64,1440]{1,0:T(8,128)(2,1)S(1)}, u32[]{:S(2)}, u32[]{:S(2)}) collective-permute-start(bf16[64,1440]{1,0:T(8,128)(2,1)S(1)} %fold_smooth.1.middle), channel_id=1, source_target_pairs={{0,1},{2,3},{1,0},{3,2},{4,5},{6,7},{5,4},{7,6},{8,9},{10,11},{9,8... | collective-permute-start | bytes 552968 | tf_op jit(solution)/shard_map/ppermute | solution.py:629
  20.1 14.5 %collective-permute-start.7 = (bf16[64,1440]{1,0:T(8,128)(2,1)S(1)}, bf16[64,1440]{1,0:T(8,128)(2,1)S(1)}, u32[]{:S(2)}, u32[]{:S(2)}) collective-permute-start(bf16[64,1440]{1,0:T(8,128)(2,1)S(1)} %fold_smooth.1.middle), channel_id=1, source_target_pairs={{1,2},{2,1},{5,6},{6,5},{9,10},{10,9},{13,14},{14,13},{17,18},{18,... | collective-permute-start | bytes 552968 | tf_op jit(solution)/shard_map/ppermute | solution.py:629
  28.0 5.7 %collective-permute-start.5 = (bf16[32,384]{1,0:T(8,128)(2,1)S(1)}, bf16[32,384]{1,0:T(8,128)(2,1)S(1)}, u32[]{:S(2)}, u32[]{:S(2)}) collective-permute-start(bf16[32,384]{1,0:T(8,128)(2,1)S(1)} %get-tuple-element.67), channel_id=1, source_target_pairs={{0,24},{4,28},{8,16},{12,20},{16,8},{20,12},{24,0},{28,4},{1,25},{... | collective-permute-start | bytes 73736 | tf_op jit(solution)/shard_map/ppermute | solution.py:535
  29.6 4.7 %collective-permute-start.4 = (bf16[32,384]{1,0:T(8,128)(2,1)S(1)}, bf16[32,384]{1,0:T(8,128)(2,1)S(1)}, u32[]{:S(2)}, u32[]{:S(2)}) collective-permute-start(bf16[32,384]{1,0:T(8,128)(2,1)S(1)} %get-tuple-element.67), channel_id=1, source_target_pairs={{0,16},{4,20},{8,24},{12,28},{16,0},{20,4},{24,8},{28,12},{1,17},{... | collective-permute-start | bytes 73736 | tf_op jit(solution)/shard_map/ppermute | solution.py:535
  30.6 3.9 %collective-permute-start.3 = (bf16[32,384]{1,0:T(8,128)(2,1)S(1)}, bf16[32,384]{1,0:T(8,128)(2,1)S(1)}, u32[]{:S(2)}, u32[]{:S(2)}) collective-permute-start(bf16[32,384]{1,0:T(8,128)(2,1)S(1)} %get-tuple-element.67), channel_id=1, source_target_pairs={{0,8},{4,12},{8,0},{12,4},{16,24},{20,28},{24,16},{28,20},{1,9},{5... | collective-permute-start | bytes 73736 | tf_op jit(solution)/shard_map/ppermute | solution.py:535
  34.6 1.4 %collective-permute-start.8 = (bf16[4,32,384]{2,1,0:T(8,128)(2,1)S(1)}, bf16[4,32,384]{2,1,0:T(8,128)(2,1)S(1)}, u32[]{:S(2)}, u32[]{:S(2)}) collective-permute-start(bf16[4,32,384]{2,1,0:T(8,128)(2,1)S(1)} %pad_maximum_fusion.refs_0_), channel_id=1, source_target_pairs={{0,4},{4,0},{8,12},{12,8},{16,20},{20,16},{24,28},{28,24},{1,5},{5... | collective-permute-start | bytes 294920 | tf_op jit(solution)/shard_map/ppermute | solution.py:543
  36.9 12.6 %all-to-all-start.1 = ((bf16[32,8,384]{2,1,0:T(8,128)(2,1)}), bf16[32,8,384]{2,1,0:T(8,128)(2,1)S(1)}, u32[]{:S(2)}, u32[]{:S(2)}) async-start(bf16[32,8,384]{2,1,0:T(8,128)(2,1)} %get-tuple-element.77), calls=%async_computation.1 | async-start | bytes 393216 | tf_op jit(solution)/shard_map/all_to_all | solution.py:660
  39.9 3.8 %copy-start.9 = (f32[64,192]{1,0:T(8,128)S(1)}, f32[64,192]{1,0:T(8,128)}, u32[]{:S(2)}) copy-start(f32[64,192]{1,0:T(8,128)} %constant.29.clone.apart) | copy-start | bytes 147460
  40.2 5.5 %collective-permute-start.9 = (bf16[96,384]{1,0:T(8,128)(2,1)S(1)}, bf16[96,384]{1,0:T(8,128)(2,1)S(1)}, u32[]{:S(2)}, u32[]{:S(2)}) collective-permute-start(bf16[96,384]{1,0:T(8,128)(2,1)S(1)} %get-tuple-element.86), channel_id=1, source_target_pairs={{0,1},{1,0},{2,3},{3,2},{4,5},{5,4},{6,7},{7,6},{8,9},{9,8},{10,11... | collective-permute-start | bytes 221192 | tf_op jit(solution)/shard_map/ppermute | solution.py:525
  42.0 5.6 %collective-permute-start.10 = (bf16[96,384]{1,0:T(8,128)(2,1)S(1)}, bf16[96,384]{1,0:T(8,128)(2,1)S(1)}, u32[]{:S(2)}, u32[]{:S(2)}) collective-permute-start(bf16[96,384]{1,0:T(8,128)(2,1)S(1)} %get-tuple-element.87), channel_id=1, source_target_pairs={{0,2},{1,3},{2,0},{3,1},{4,6},{5,7},{6,4},{7,5},{8,10},{9,11},{10,... | collective-permute-start | bytes 221192 | tf_op jit(solution)/shard_map/ppermute | solution.py:525
  43.5 5.6 %collective-permute-start.11 = (bf16[96,384]{1,0:T(8,128)(2,1)S(1)}, bf16[96,384]{1,0:T(8,128)(2,1)S(1)}, u32[]{:S(2)}, u32[]{:S(2)}) collective-permute-start(bf16[96,384]{1,0:T(8,128)(2,1)S(1)} %get-tuple-element.88), channel_id=1, source_target_pairs={{0,3},{1,2},{2,1},{3,0},{4,7},{5,6},{6,5},{7,4},{8,11},{9,10},{10,... | collective-permute-start | bytes 221192 | tf_op jit(solution)/shard_map/ppermute | solution.py:525

commit v14 on v13

--- a/solution.py
+++ b/solution.py
@@ -329,19 +329,25 @@
             taper[...] = near(apart[...], span[: apart.shape[0]])
             factor[...] = ensemble_share / (span * span)
 
-        def first_half(weights, turn, stacked, ring, taper, factor, *refs):
-            blocks, (total_out, weighted_out, image_out, fields) = refs[:-4], refs[-4:]
+        def arrange(turn, *refs):
+            blocks, (fields, kept_fields, weighted) = refs[:-3], refs[-3:]
             if few:
                 blocks = [block[...].astype(f32) for block in blocks]
             values = jnp.stack(chosen(turn[:, :1], blocks, -1)).astype(f32)
             field = []
             for index in range(arrays):
                 piece = values[:, index * own : (index + 1) * own].reshape(per_member, padded)
-                fields[index] = piece[:, :kept]
+                kept_fields[index] = piece[:, :kept]
                 field.append(piece)
-            precise, static = field[slots], field[slots + 1]
+            for index in range(slots, arrays):
+                fields[index - slots] = field[index]
+            for t in range(slots):
+                weighted[t] = field[slots] * field[t]
+
+        def first_half(weights, stacked, ring, taper, factor, fields, ready, total_out, weighted_out, image_out):
+            precise, static = fields[0], fields[1]
             ensemble, scale = load_members(weights, stacked)
-            weighted = [precise * field[t] for t in range(slots)]
+            weighted = [ready[t] for t in range(slots)]
             grad = spread(fold(ensemble, scale, weighted), ring[...], taper[...], factor[...])
             total = jnp.zeros((per_member, padded), f32)
             for t, image in enumerate(images_of(ensemble, grad, ring[...], taper[...], scale * factor[...])):
@@ -631,17 +637,27 @@
         ]
         ring = ring_kernel(width, padded)
 
-        total, weighted, image_first, fields = call(
+        fields, kept_fields, ready = call(
+            arrange,
+            [
+                ((arrays - slots, per_member, padded), f32),
+                ((arrays, per_member, kept), f32),
+                ((slots, per_member, padded), f32),
+            ],
+            [],
+            [turn, *blocks],
+        )
+        total, weighted, image_first = call(
             first_half,
             [
                 ((per_member, kept), bf16),
                 ((slots, per_member, padded), f32),
                 ((slots, per_member, kept), f32),
-                ((arrays, per_member, kept), f32),
             ],
             [],
-            [weights, turn, stacked, ring, taper, factor, *blocks],
-        )
+            [weights, stacked, ring, taper, factor, fields, ready],
+        )
+        fields = kept_fields
         grad, image_second = call(
             second_half,
             [((members * bands, own, kept), bf16), ((slots, per_member, kept), f32)],

time: 51.1 us -> 51.2 us (level)
  waiting for transfers between devices: 13.4 us -> 10.8 us
  starting transfers between devices: 24.7 us -> 27.2 us
    all_to_all x1, waiting for transfers between devices: 6.1 us -> 3.53 us  [shards(): stacked = lax.all_to_all(pieces, BOTH, 0, 0, tiled=True)]
    ppermute x2, starting transfers between devices: 2.75 us -> 5.21 us  [shards(): lax.ppermute(smoothed, 'band', pairs[start::2] + [(to, at) for at, to in...]
    pallas_call x9 -> x10, Pallas kernels: 7.04 us -> 7.17 us  [call(): pl.pallas_call(body, out_shape=tuple((jax.ShapeDtypeStruct(shape, kind) f...]
where the time goes in v14:
time: 51.2 us; the launch traced here: 50.8 us
  starting transfers between devices  27.2 us (53%)
  waiting for transfers between devices  10.8 us (21%)
  Pallas kernels  10.5 us (21%)
  between operations  1.58 us (3%)
  local copies, waits for them, and re-layouts  0.72 us (1%)
    all_to_all x1, starting transfers between devices, shards(): stacked = lax.all_to_all(pieces, BOTH, 0, 0, tiled=True)  7.3 us
    pallas_call x10, Pallas kernels, call(): pl.pallas_call(body, out_shape=tuple((jax.ShapeDtypeStruct(shape, kind) f...  7.17 us
    ppermute x6, starting transfers between devices, trade(): lax.ppermute(blocks[shift], 'band', [(at, partner(at, shift, bands, 1)) f...  7.11 us
    ppermute x2, starting transfers between devices, shards(): lax.ppermute(smoothed, 'band', pairs[start::2] + [(to, at) for at, to in...  5.21 us
    ppermute x6, waiting for transfers between devices, trade(): lax.ppermute(blocks[shift], 'band', [(at, partner(at, shift, bands, 1)) f...  4.98 us
    ppermute x3, starting transfers between devices, around(): lax.ppermute(block, 'member', [(at, 2 * partner(at // 2, shift, members /...  4.45 us
    all_to_all x1, waiting for transfers between devices, shards(): stacked = lax.all_to_all(pieces, BOTH, 0, 0, tiled=True)  3.53 us
    all_to_all x1, starting transfers between devices, shards(): back = lax.all_to_all(grad, BOTH, 0, 0, tiled=True)  3.03 us
  transfers between devices with their start and end apart: 14, of which 8 were waited for; matrix products, arithmetic and copies ran while one was open for 0% of the time, Pallas kernels for 12%

profile of v14, /device:TPU:0, one launch (start us, length us, event | category | flops | bytes accessed | tf_op | source)
XLA Modules:
  0.0 50.8 jit_solution(8538190824996406166)
XLA Ops:
  1.3 2.0 %pack.1 = bf16[32,16,512]{2,1,0:T(8,128)(2,1)} custom-call(s32[1]{0:T(128)S(6)} %copy.17.slot.marks, bf16[1,2,16,4,1440]{4,3,2,1,0:T(4,128)(2,1)} %ensemble.2), custom_call_target="tpu_custom_call" | custom-call | tf_op jit(solution)/shard_map/pack/pallas_call | solution.py:574
  3.3 0.0 copy-start.1
  3.3 0.0 copy-start.2
  3.3 0.0 copy-start.7
  3.3 0.0 copy-start.8
  3.4 7.3 %all-to-all-start = ((bf16[32,16,512]{2,1,0:T(8,128)(2,1)}), bf16[32,16,512]{2,1,0:T(8,128)(2,1)S(1)}, u32[]{:S(2)}, u32[]{:S(2)}) async-start(bf16[32,16,512]{2,1,0:T(8,128)(2,1)} %pack.1), calls=%async_computation | async-start | bytes 1048576 | tf_op jit(solution)/shard_map/all_to_all | solution.py:593
  10.7 0.0 copy-start.10
  10.7 0.0 copy-done.1
  10.7 0.0 copy-done.2
  10.7 0.0 copy-done.7
  10.7 0.0 copy-done.8
  10.7 0.6 %copy-done.10 = f32[16,16]{1,0:T(8,128)S(1)} copy-done((f32[16,16]{1,0:T(8,128)S(1)}, f32[16,16]{1,0:T(8,128)}, u32[]{:S(2)}) %copy-start.10) | copy-done | bytes 1048
  11.4 0.0 copy-start.4
  11.4 0.0 copy-start.6
  11.4 0.0 copy-start.5
  11.4 1.1 %observe.1 = (bf16[32,512]{1,0:T(8,128)(2,1)S(1)}, bf16[32,512]{1,0:T(8,128)(2,1)S(1)}, bf16[32,512]{1,0:T(8,128)(2,1)S(1)}, bf16[32,512]{1,0:T(8,128)(2,1)S(1)}...) custom-call(s32[1,128]{1,0:T(1,128)S(1)} %broadcast_in_dim.6.place, s32[1,128]{1,0:T(1,128)S(1)} %broadcast_in_dim.7.turn, ...), custom_call_target="tpu_custom_call" | custom-call | tf_op jit(solution)/shard_map/observe/pallas_call | solution.py:152
  12.5 0.0 copy-start
  12.5 1.8 %collective-permute-start.1 = (bf16[32,512]{1,0:T(8,128)(2,1)S(1)}, bf16[32,512]{1,0:T(8,128)(2,1)S(1)}, u32[]{:S(2)}, u32[]{:S(2)}) collective-permute-start(bf16[32,512]{1,0:T(8,128)(2,1)S(1)} %get-tuple-element.62), channel_id=1, source_target_pairs={{0,2},{1,3},{2,0},{3,1},{4,6},{5,7},{6,4},{7,5},{8,10},{9,11},{10,... | collective-permute-start | bytes 98312 | tf_op jit(solution)/shard_map/ppermute | solution.py:531
  14.4 1.5 %collective-permute-start = (bf16[32,512]{1,0:T(8,128)(2,1)S(1)}, bf16[32,512]{1,0:T(8,128)(2,1)S(1)}, u32[]{:S(2)}, u32[]{:S(2)}) collective-permute-start(bf16[32,512]{1,0:T(8,128)(2,1)S(1)} %get-tuple-element.61), channel_id=1, source_target_pairs={{0,1},{1,0},{2,3},{3,2},{4,5},{5,4},{6,7},{7,6},{8,9},{9,8},{10,11... | collective-permute-start | bytes 98312 | tf_op jit(solution)/shard_map/ppermute | solution.py:531
  15.8 0.3 collective-permute-start.2
  16.1 0.0 copy-done.4
  16.1 0.0 copy-done.6
  16.1 0.0 copy-done.11
  16.1 0.0 copy-done.12
  16.1 1.4 %prepare.1 = (f32[8,64]{1,0:T(8,128)S(1)}, f32[64,64]{1,0:T(8,128)S(1)}, bf16[256,256]{1,0:T(8,128)(2,1)S(1)}, f32[256,1]{1,0:T(8,128)S(1)}, f32[8,128]{1,0:T(8,...) custom-call(s32[1]{0:T(128)} %bitcast.here, s32[16]{0:T(128)S(1)} %copy-done.11, f32[8]{0:T(128)S(1)} %copy-done.12, ...), custom_call_target="tpu_custom_call" | custom-call | tf_op jit(solution)/shard_map/prepare/pallas_call | solution.py:152
  17.5 0.0 collective-permute-done.1.refs_2_
  17.5 0.0 copy-done.5
  17.5 0.0 copy-done
  17.5 0.0 copy-start.3
  17.5 0.5 fold_smooth.1.middle
  18.0 0.7 %collective-permute-start.7 = (bf16[64,1440]{1,0:T(8,128)(2,1)S(1)}, bf16[64,1440]{1,0:T(8,128)(2,1)S(1)}, u32[]{:S(2)}, u32[]{:S(2)}) collective-permute-start(bf16[64,1440]{1,0:T(8,128)(2,1)S(1)} %fold_smooth.1.middle), channel_id=1, source_target_pairs={{1,2},{2,1},{5,6},{6,5},{9,10},{10,9},{13,14},{14,13},{17,18},{18,... | collective-permute-start | bytes 552968 | tf_op jit(solution)/shard_map/ppermute | solution.py:635
  18.7 4.5 %collective-permute-start.6 = (bf16[64,1440]{1,0:T(8,128)(2,1)S(1)}, bf16[64,1440]{1,0:T(8,128)(2,1)S(1)}, u32[]{:S(2)}, u32[]{:S(2)}) collective-permute-start(bf16[64,1440]{1,0:T(8,128)(2,1)S(1)} %fold_smooth.1.middle), channel_id=1, source_target_pairs={{0,1},{2,3},{1,0},{3,2},{4,5},{6,7},{5,4},{7,6},{8,9},{10,11},{9,8... | collective-permute-start | bytes 552968 | tf_op jit(solution)/shard_map/ppermute | solution.py:635
  23.2 0.0 collective-permute-done.refs_1_
  23.3 0.0 collective-permute-done.2.refs_3_
  23.3 0.1 arrange.1
  23.4 3.5 %all-to-all-done.stacked = bf16[32,16,512]{2,1,0:T(8,128)(2,1)S(1)} async-done(((bf16[32,16,512]{2,1,0:T(8,128)(2,1)}), bf16[32,16,512]{2,1,0:T(8,128)(2,1)S(1)}, u32[]{:S(2)}, u32[]{:S(2)}) %all-to-all-start) | async-done | bytes 524320 | tf_op jit(solution)/shard_map/all_to_all | solution.py:593
  26.9 0.0 copy-done.3
  26.9 1.1 %first_half.1 = (bf16[32,384]{1,0:T(8,128)(2,1)S(1)}, f32[2,32,512]{2,1,0:T(8,128)S(1)}, f32[2,32,384]{2,1,0:T(8,128)S(1)}) custom-call(f32[8,128]{1,0:T(8,128)S(1)} %get-tuple-element.56.weights, bf16[32,16,512]{2,1,0:T(8,128)(2,1)S(1)} %all-to-all-done.stacked, bf16[512,512]{1,0:T(8,128)(2,1)S(1)} %copy-done.3, ...), custom_call_target="tpu_custom_call" | custom-call | tf_op jit(solution)/shard_map/first_half/pallas_call | solution.py:152
  28.0 1.5 %collective-permute-start.5 = (bf16[32,384]{1,0:T(8,128)(2,1)S(1)}, bf16[32,384]{1,0:T(8,128)(2,1)S(1)}, u32[]{:S(2)}, u32[]{:S(2)}) collective-permute-start(bf16[32,384]{1,0:T(8,128)(2,1)S(1)} %get-tuple-element.71), channel_id=1, source_target_pairs={{0,24},{4,28},{8,16},{12,20},{16,8},{20,12},{24,0},{28,4},{1,25},{... | collective-permute-start | bytes 73736 | tf_op jit(solution)/shard_map/ppermute | solution.py:541
  29.6 1.1 %collective-permute-start.4 = (bf16[32,384]{1,0:T(8,128)(2,1)S(1)}, bf16[32,384]{1,0:T(8,128)(2,1)S(1)}, u32[]{:S(2)}, u32[]{:S(2)}) collective-permute-start(bf16[32,384]{1,0:T(8,128)(2,1)S(1)} %get-tuple-element.71), channel_id=1, source_target_pairs={{0,16},{4,20},{8,24},{12,28},{16,0},{20,4},{24,8},{28,12},{1,17},{... | collective-permute-start | bytes 73736 | tf_op jit(solution)/shard_map/ppermute | solution.py:541
  30.6 1.9 %collective-permute-start.3 = (bf16[32,384]{1,0:T(8,128)(2,1)S(1)}, bf16[32,384]{1,0:T(8,128)(2,1)S(1)}, u32[]{:S(2)}, u32[]{:S(2)}) collective-permute-start(bf16[32,384]{1,0:T(8,128)(2,1)S(1)} %get-tuple-element.71), channel_id=1, source_target_pairs={{0,8},{4,12},{8,0},{12,4},{16,24},{20,28},{24,16},{28,20},{1,9},{5... | collective-permute-start | bytes 73736 | tf_op jit(solution)/shard_map/ppermute | solution.py:541
  32.5 1.1 %second_half.1 = (bf16[32,8,384]{2,1,0:T(8,128)(2,1)S(1)}, f32[2,32,384]{2,1,0:T(8,128)S(1)}) custom-call(f32[8,128]{1,0:T(8,128)S(1)} %get-tuple-element.56.weights, bf16[32,16,512]{2,1,0:T(8,128)(2,1)S(1)} %all-to-all-done.stacked, bf16[512,512]{1,0:T(8,128)(2,1)S(1)} %copy-done.3, bf16[256,256]{1,0:T(8,128)(2,1)S(1)} %get-tuple-element.58.taper, ...), custom_call_target="tpu_custom_call" | custom-call | flops 1000000000 | tf_op jit(solution)/shard_map/second_half/pallas_call | solution.py:152
  33.6 0.2 collective-permute-done.5
  33.7 0.6 %collective-permute-done.4 = bf16[32,384]{1,0:T(8,128)(2,1)S(1)} collective-permute-done((bf16[32,384]{1,0:T(8,128)(2,1)S(1)}, bf16[32,384]{1,0:T(8,128)(2,1)S(1)}, u32[]{:S(2)}, u32[]{:S(2)}) %collective-permute-start.4) | collective-permute-done | bytes 24608 | tf_op jit(solution)/shard_map/ppermute | solution.py:541
  34.3 0.3 collective-permute-done.3
  34.6 0.0 collective-permute-done.7.above
  34.6 0.0 collective-permute-done.6.below
  34.6 0.1 collective-permute-start.8
  34.7 1.3 %collective-permute-done.8.refs_1_ = bf16[4,32,384]{2,1,0:T(8,128)(2,1)S(1)} collective-permute-done((bf16[4,32,384]{2,1,0:T(8,128)(2,1)S(1)}, bf16[4,32,384]{2,1,0:T(8,128)(2,1)S(1)}, u32[]{:S(2)}, u32[]{:S(2)}) %collective-permute-start.8) | collective-permute-done | bytes 98336 | tf_op jit(solution)/shard_map/ppermute | solution.py:549
  36.0 0.9 %combine.1 = (bf16[32,8,384]{2,1,0:T(8,128)(2,1)}, f32[2,32,384]{2,1,0:T(8,128)S(1)}) custom-call(bf16[32,8,384]{2,1,0:T(8,128)(2,1)S(1)} %get-tuple-element.69.grad, f32[2,32,384]{2,1,0:T(8,128)S(1)} %get-tuple-element.70.first, f32[2,32,384]{2,1,0:T(8,128)S(1)} %get-tuple-element.77.second, f32[4,32,384]{2,1,0:T(8,128)S(1)} %get-tuple-element.78.fields, ...), custom_call_target="tpu_custom_call" | custom-call | tf_op jit(solution)/shard_map/combine/pallas_call | solution.py:152
  36.9 3.0 %all-to-all-start.1 = ((bf16[32,8,384]{2,1,0:T(8,128)(2,1)}), bf16[32,8,384]{2,1,0:T(8,128)(2,1)S(1)}, u32[]{:S(2)}, u32[]{:S(2)}) async-start(bf16[32,8,384]{2,1,0:T(8,128)(2,1)} %get-tuple-element.81), calls=%async_computation.1 | async-start | bytes 393216 | tf_op jit(solution)/shard_map/all_to_all | solution.py:676
  40.0 0.0 copy-start.9
  40.0 0.2 hand_out.1
  40.2 1.8 %collective-permute-start.9 = (bf16[96,384]{1,0:T(8,128)(2,1)S(1)}, bf16[96,384]{1,0:T(8,128)(2,1)S(1)}, u32[]{:S(2)}, u32[]{:S(2)}) collective-permute-start(bf16[96,384]{1,0:T(8,128)(2,1)S(1)} %get-tuple-element.90), channel_id=1, source_target_pairs={{0,1},{1,0},{2,3},{3,2},{4,5},{5,4},{6,7},{7,6},{8,9},{9,8},{10,11... | collective-permute-start | bytes 221192 | tf_op jit(solution)/shard_map/ppermute | solution.py:531
  42.0 1.5 %collective-permute-start.10 = (bf16[96,384]{1,0:T(8,128)(2,1)S(1)}, bf16[96,384]{1,0:T(8,128)(2,1)S(1)}, u32[]{:S(2)}, u32[]{:S(2)}) collective-permute-start(bf16[96,384]{1,0:T(8,128)(2,1)S(1)} %get-tuple-element.91), channel_id=1, source_target_pairs={{0,2},{1,3},{2,0},{3,1},{4,6},{5,7},{6,4},{7,5},{8,10},{9,11},{10,... | collective-permute-start | bytes 221192 | tf_op jit(solution)/shard_map/ppermute | solution.py:531
  43.5 0.3 collective-permute-start.11
  43.7 0.0 copy-done.9
  43.7 0.3 first_gradient.1.grad_first
  44.1 1.6 %collective-permute-done.9.refs_1_ = bf16[96,384]{1,0:T(8,128)(2,1)S(1)} collective-permute-done((bf16[96,384]{1,0:T(8,128)(2,1)S(1)}, bf16[96,384]{1,0:T(8,128)(2,1)S(1)}, u32[]{:S(2)}, u32[]{:S(2)}) %collective-permute-start.9) | collective-permute-done | bytes 73760 | tf_op jit(solution)/shard_map/ppermute | solution.py:531
  45.7 1.9 %collective-permute-done.10.refs_2_ = bf16[96,384]{1,0:T(8,128)(2,1)S(1)} collective-permute-done((bf16[96,384]{1,0:T(8,128)(2,1)S(1)}, bf16[96,384]{1,0:T(8,128)(2,1)S(1)}, u32[]{:S(2)}, u32[]{:S(2)}) %collective-permute-start.10) | collective-permute-done | bytes 73760 | tf_op jit(solution)/shard_map/ppermute | solution.py:531
  47.6 1.5 %collective-permute-done.11.refs_3_ = bf16[96,384]{1,0:T(8,128)(2,1)S(1)} collective-permute-done((bf16[96,384]{1,0:T(8,128)(2,1)S(1)}, bf16[96,384]{1,0:T(8,128)(2,1)S(1)}, u32[]{:S(2)}, u32[]{:S(2)}) %collective-permute-start.11) | collective-permute-done | bytes 73760 | tf_op jit(solution)/shard_map/ppermute | solution.py:531
  49.0 0.4 join.1
  49.5 0.0 all-to-all-done.1.back
  49.5 1.3 %finish.1 = (f32[1,16,4,1440]{3,2,1,0:T(4,128)}, f32[16,4,1440]{2,1,0:T(4,128)}, f32[2,2,4,1440]{3,2,1,0:T(4,128)}) custom-call(bf16[32,8,384]{2,1,0:T(8,128)(2,1)S(1)} %all-to-all-done.1.back, f32[64,1440]{1,0:T(8,128)S(1)} %first_gradient.1.grad_first, f32[64,1440]{1,0:T(8,128)S(1)} %get-tuple-element.85.pulled_first, ...), custom_call_target="tpu_custom_call" | custom-call | tf_op jit(solution)/shard_map/finish/pallas_call | solution.py:696
  (5 shorter events, 0.0 us)
Async XLA Ops:
  3.3 7.4 %copy-start.1 = (bf16[2,16,4,1440]{3,2,1,0:T(4,128)(2,1)S(1)}, bf16[2,16,4,1440]{3,2,1,0:T(4,128)(2,1)}, u32[]{:S(2)}) copy-start(bf16[2,16,4,1440]{3,2,1,0:T(4,128)(2,1)} %innovation.1) | copy-start | bytes 1105924
  3.3 7.4 %copy-start.2 = (bf16[16,4,1440]{2,1,0:T(4,128)(2,1)S(1)}, bf16[16,4,1440]{2,1,0:T(4,128)(2,1)}, u32[]{:S(2)}) copy-start(bf16[16,4,1440]{2,1,0:T(4,128)(2,1)} %precision.1) | copy-start | bytes 552964
  3.3 7.4 %copy-start.7 = (f32[64,64]{1,0:T(8,128)S(1)}, f32[64,64]{1,0:T(8,128)}, u32[]{:S(2)}) copy-start(f32[64,64]{1,0:T(8,128)} %constant.24.clone.same) | copy-start | bytes 49156
  3.3 7.4 %copy-start.8 = (f32[64,16]{1,0:T(8,128)S(1)}, f32[64,16]{1,0:T(8,128)}, u32[]{:S(2)}) copy-start(f32[64,16]{1,0:T(8,128)} %constant.23.clone.of_level) | copy-start | bytes 12292
  3.4 23.6 %all-to-all-start = ((bf16[32,16,512]{2,1,0:T(8,128)(2,1)}), bf16[32,16,512]{2,1,0:T(8,128)(2,1)S(1)}, u32[]{:S(2)}, u32[]{:S(2)}) async-start(bf16[32,16,512]{2,1,0:T(8,128)(2,1)} %pack.1), calls=%async_computation | async-start | bytes 1048576 | tf_op jit(solution)/shard_map/all_to_all | solution.py:593
  10.7 0.7 %copy-start.10 = (f32[16,16]{1,0:T(8,128)S(1)}, f32[16,16]{1,0:T(8,128)}, u32[]{:S(2)}) copy-start(f32[16,16]{1,0:T(8,128)} %root.1) | copy-start | bytes 3076
  11.4 4.7 %copy-start.4 = (f32[256,256]{1,0:T(8,128)S(1)}, f32[256,256]{1,0:T(8,128)}, u32[]{:S(2)}) copy-start(f32[256,256]{1,0:T(8,128)} %constant.25.clone.apart) | copy-start | bytes 786436
  11.4 4.7 %copy-start.6 = (f32[256,1]{1,0:T(8,128)S(1)}, f32[256,1]{1,0:T(8,128)}, u32[]{:S(2)}) copy-start(f32[256,1]{1,0:T(8,128)} %constant.26.clone.level) | copy-start | bytes 3076
  11.4 4.7 %copy-start.11 = (s32[16]{0:T(128)S(1)}, s32[16]{0:T(128)}, u32[]{:S(2)}) copy-start(s32[16]{0:T(128)} %widths.1) | copy-start | bytes 196
  11.4 4.7 %copy-start.12 = (f32[8]{0:T(128)S(1)}, f32[8]{0:T(128)}, u32[]{:S(2)}) copy-start(f32[8]{0:T(128)} %weight.1) | copy-start | bytes 100
  11.4 6.1 %copy-start.5 = (bf16[512,256]{1,0:T(8,128)(2,1)S(1)}, bf16[512,256]{1,0:T(8,128)(2,1)}, u32[]{:S(2)}) copy-start(bf16[512,256]{1,0:T(8,128)(2,1)} %constant.27.clone.kernel) | copy-start | bytes 786436
  12.5 5.0 %copy-start = (bf16[1,2,16,4,1440]{4,3,2,1,0:T(4,128)(2,1)S(1)}, bf16[1,2,16,4,1440]{4,3,2,1,0:T(4,128)(2,1)}, u32[]{:S(2)}) copy-start(bf16[1,2,16,4,1440]{4,3,2,1,0:T(4,128)(2,1)} %ensemble.2) | copy-start | bytes 1105924
  12.5 4.9 %collective-permute-start.1 = (bf16[32,512]{1,0:T(8,128)(2,1)S(1)}, bf16[32,512]{1,0:T(8,128)(2,1)S(1)}, u32[]{:S(2)}, u32[]{:S(2)}) collective-permute-start(bf16[32,512]{1,0:T(8,128)(2,1)S(1)} %get-tuple-element.62), channel_id=1, source_target_pairs={{0,2},{1,3},{2,0},{3,1},{4,6},{5,7},{6,4},{7,5},{8,10},{9,11},{10,... | collective-permute-start | bytes 98312 | tf_op jit(solution)/shard_map/ppermute | solution.py:531
  14.4 8.9 %collective-permute-start = (bf16[32,512]{1,0:T(8,128)(2,1)S(1)}, bf16[32,512]{1,0:T(8,128)(2,1)S(1)}, u32[]{:S(2)}, u32[]{:S(2)}) collective-permute-start(bf16[32,512]{1,0:T(8,128)(2,1)S(1)} %get-tuple-element.61), channel_id=1, source_target_pairs={{0,1},{1,0},{2,3},{3,2},{4,5},{5,4},{6,7},{7,6},{8,9},{9,8},{10,11... | collective-permute-start | bytes 98312 | tf_op jit(solution)/shard_map/ppermute | solution.py:531
  15.8 7.4 %collective-permute-start.2 = (bf16[32,512]{1,0:T(8,128)(2,1)S(1)}, bf16[32,512]{1,0:T(8,128)(2,1)S(1)}, u32[]{:S(2)}, u32[]{:S(2)}) collective-permute-start(bf16[32,512]{1,0:T(8,128)(2,1)S(1)} %get-tuple-element.65), channel_id=1, source_target_pairs={{0,3},{1,2},{2,1},{3,0},{4,7},{5,6},{6,5},{7,4},{8,11},{9,10},{10,... | collective-permute-start | bytes 98312 | tf_op jit(solution)/shard_map/ppermute | solution.py:531
  17.5 9.4 %copy-start.3 = (bf16[512,512]{1,0:T(8,128)(2,1)S(1)}, bf16[512,512]{1,0:T(8,128)(2,1)}, u32[]{:S(2)}) copy-start(bf16[512,512]{1,0:T(8,128)(2,1)} %constant.28.clone.ring) | copy-start | bytes 1572868
  18.0 16.6 %collective-permute-start.7 = (bf16[64,1440]{1,0:T(8,128)(2,1)S(1)}, bf16[64,1440]{1,0:T(8,128)(2,1)S(1)}, u32[]{:S(2)}, u32[]{:S(2)}) collective-permute-start(bf16[64,1440]{1,0:T(8,128)(2,1)S(1)} %fold_smooth.1.middle), channel_id=1, source_target_pairs={{1,2},{2,1},{5,6},{6,5},{9,10},{10,9},{13,14},{14,13},{17,18},{18,... | collective-permute-start | bytes 552968 | tf_op jit(solution)/shard_map/ppermute | solution.py:635
  18.7 15.9 %collective-permute-start.6 = (bf16[64,1440]{1,0:T(8,128)(2,1)S(1)}, bf16[64,1440]{1,0:T(8,128)(2,1)S(1)}, u32[]{:S(2)}, u32[]{:S(2)}) collective-permute-start(bf16[64,1440]{1,0:T(8,128)(2,1)S(1)} %fold_smooth.1.middle), channel_id=1, source_target_pairs={{0,1},{2,3},{1,0},{3,2},{4,5},{6,7},{5,4},{7,6},{8,9},{10,11},{9,8... | collective-permute-start | bytes 552968 | tf_op jit(solution)/shard_map/ppermute | solution.py:635
  28.0 5.7 %collective-permute-start.5 = (bf16[32,384]{1,0:T(8,128)(2,1)S(1)}, bf16[32,384]{1,0:T(8,128)(2,1)S(1)}, u32[]{:S(2)}, u32[]{:S(2)}) collective-permute-start(bf16[32,384]{1,0:T(8,128)(2,1)S(1)} %get-tuple-element.71), channel_id=1, source_target_pairs={{0,24},{4,28},{8,16},{12,20},{16,8},{20,12},{24,0},{28,4},{1,25},{... | collective-permute-start | bytes 73736 | tf_op jit(solution)/shard_map/ppermute | solution.py:541
  29.6 4.7 %collective-permute-start.4 = (bf16[32,384]{1,0:T(8,128)(2,1)S(1)}, bf16[32,384]{1,0:T(8,128)(2,1)S(1)}, u32[]{:S(2)}, u32[]{:S(2)}) collective-permute-start(bf16[32,384]{1,0:T(8,128)(2,1)S(1)} %get-tuple-element.71), channel_id=1, source_target_pairs={{0,16},{4,20},{8,24},{12,28},{16,0},{20,4},{24,8},{28,12},{1,17},{... | collective-permute-start | bytes 73736 | tf_op jit(solution)/shard_map/ppermute | solution.py:541
  30.6 3.9 %collective-permute-start.3 = (bf16[32,384]{1,0:T(8,128)(2,1)S(1)}, bf16[32,384]{1,0:T(8,128)(2,1)S(1)}, u32[]{:S(2)}, u32[]{:S(2)}) collective-permute-start(bf16[32,384]{1,0:T(8,128)(2,1)S(1)} %get-tuple-element.71), channel_id=1, source_target_pairs={{0,8},{4,12},{8,0},{12,4},{16,24},{20,28},{24,16},{28,20},{1,9},{5... | collective-permute-start | bytes 73736 | tf_op jit(solution)/shard_map/ppermute | solution.py:541
  34.6 1.4 %collective-permute-start.8 = (bf16[4,32,384]{2,1,0:T(8,128)(2,1)S(1)}, bf16[4,32,384]{2,1,0:T(8,128)(2,1)S(1)}, u32[]{:S(2)}, u32[]{:S(2)}) collective-permute-start(bf16[4,32,384]{2,1,0:T(8,128)(2,1)S(1)} %pad_maximum_fusion.refs_0_), channel_id=1, source_target_pairs={{0,4},{4,0},{8,12},{12,8},{16,20},{20,16},{24,28},{28,24},{1,5},{5... | collective-permute-start | bytes 294920 | tf_op jit(solution)/shard_map/ppermute | solution.py:549
  36.9 12.6 %all-to-all-start.1 = ((bf16[32,8,384]{2,1,0:T(8,128)(2,1)}), bf16[32,8,384]{2,1,0:T(8,128)(2,1)S(1)}, u32[]{:S(2)}, u32[]{:S(2)}) async-start(bf16[32,8,384]{2,1,0:T(8,128)(2,1)} %get-tuple-element.81), calls=%async_computation.1 | async-start | bytes 393216 | tf_op jit(solution)/shard_map/all_to_all | solution.py:676
  40.0 3.8 %copy-start.9 = (f32[64,192]{1,0:T(8,128)S(1)}, f32[64,192]{1,0:T(8,128)}, u32[]{:S(2)}) copy-start(f32[64,192]{1,0:T(8,128)} %constant.29.clone.apart) | copy-start | bytes 147460
  40.2 5.5 %collective-permute-start.9 = (bf16[96,384]{1,0:T(8,128)(2,1)S(1)}, bf16[96,384]{1,0:T(8,128)(2,1)S(1)}, u32[]{:S(2)}, u32[]{:S(2)}) collective-permute-start(bf16[96,384]{1,0:T(8,128)(2,1)S(1)} %get-tuple-element.90), channel_id=1, source_target_pairs={{0,1},{1,0},{2,3},{3,2},{4,5},{5,4},{6,7},{7,6},{8,9},{9,8},{10,11... | collective-permute-start | bytes 221192 | tf_op jit(solution)/shard_map/ppermute | solution.py:531
  42.0 5.6 %collective-permute-start.10 = (bf16[96,384]{1,0:T(8,128)(2,1)S(1)}, bf16[96,384]{1,0:T(8,128)(2,1)S(1)}, u32[]{:S(2)}, u32[]{:S(2)}) collective-permute-start(bf16[96,384]{1,0:T(8,128)(2,1)S(1)} %get-tuple-element.91), channel_id=1, source_target_pairs={{0,2},{1,3},{2,0},{3,1},{4,6},{5,7},{6,4},{7,5},{8,10},{9,11},{10,... | collective-permute-start | bytes 221192 | tf_op jit(solution)/shard_map/ppermute | solution.py:531
  43.5 5.6 %collective-permute-start.11 = (bf16[96,384]{1,0:T(8,128)(2,1)S(1)}, bf16[96,384]{1,0:T(8,128)(2,1)S(1)}, u32[]{:S(2)}, u32[]{:S(2)}) collective-permute-start(bf16[96,384]{1,0:T(8,128)(2,1)S(1)} %get-tuple-element.92), channel_id=1, source_target_pairs={{0,3},{1,2},{2,1},{3,0},{4,7},{5,6},{6,5},{7,4},{8,11},{9,10},{10,... | collective-permute-start | bytes 221192 | tf_op jit(solution)/shard_map/ppermute | solution.py:531

commit v15 on v13

--- a/solution.py
+++ b/solution.py
@@ -416,10 +416,14 @@
                     high = part.astype(bf16).astype(f32)
                     row = row + jnp.where(lane == PARTS * index + piece, high, 0.0)
                     part = part - high
-            row = jnp.broadcast_to(row, (own, kept))
-            lane = lax.broadcasted_iota(jnp.int32, (own, kept), 1)
+            tile = lon_share // LANES * LANES
+            row = jnp.broadcast_to(row, (own, kept))[:, tile:]
+            lane = lax.broadcasted_iota(jnp.int32, (own, kept - tile), 1) + tile
             for block in range(members * bands):
-                out[block] = jnp.where(lane < lon_share, grad[block].astype(f32), row).astype(bf16)
+                last = jnp.where(lane < lon_share, grad[block, :, tile:].astype(f32), row)
+                if tile:
+                    out[block, :, :tile] = grad[block, :, :tile]
+                out[block, :, tile:] = last.astype(bf16)
 
         def hand_out(turn, first, second, *refs):
             blocks, outs = refs[: len(totals)], refs[len(totals) :]

time: 51.1 us -> 51.1 us (level)
  no operation moved by 1% of the time
where the time goes in v15:
time: 51.1 us; the launch traced here: 50.7 us
  starting transfers between devices  24.7 us (48%)
  waiting for transfers between devices  13.4 us (26%)
  Pallas kernels  10.3 us (20%)
  between operations  1.59 us (3%)
  local copies, waits for them, and re-layouts  0.72 us (1%)
    all_to_all x1, starting transfers between devices, shards(): stacked = lax.all_to_all(pieces, BOTH, 0, 0, tiled=True)  7.3 us
    ppermute x6, starting transfers between devices, trade(): lax.ppermute(blocks[shift], 'band', [(at, partner(at, shift, bands, 1)) f...  7.11 us
    pallas_call x9, Pallas kernels, call(): pl.pallas_call(body, out_shape=tuple((jax.ShapeDtypeStruct(shape, kind) f...  7.04 us
    all_to_all x1, waiting for transfers between devices, shards(): stacked = lax.all_to_all(pieces, BOTH, 0, 0, tiled=True)  6.1 us
    ppermute x6, waiting for transfers between devices, trade(): lax.ppermute(blocks[shift], 'band', [(at, partner(at, shift, bands, 1)) f...  4.98 us
    ppermute x3, starting transfers between devices, around(): lax.ppermute(block, 'member', [(at, 2 * partner(at // 2, shift, members /...  4.45 us
    all_to_all x1, starting transfers between devices, shards(): back = lax.all_to_all(grad, BOTH, 0, 0, tiled=True)  3.03 us
    ppermute x2, starting transfers between devices, shards(): lax.ppermute(smoothed, 'band', pairs[start::2] + [(to, at) for at, to in...  2.75 us
  transfers between devices with their start and end apart: 14, of which 8 were waited for; matrix products, arithmetic and copies ran while one was open for 0% of the time, Pallas kernels for 12%

profile of v15, /device:TPU:0, one launch (start us, length us, event | category | flops | bytes accessed | tf_op | source)
XLA Modules:
  0.0 50.7 jit_solution(232298461285455167)
XLA Ops:
  1.3 2.0 %pack.1 = bf16[32,16,512]{2,1,0:T(8,128)(2,1)} custom-call(s32[1]{0:T(128)S(6)} %copy.17.slot.marks, bf16[1,2,16,4,1440]{4,3,2,1,0:T(4,128)(2,1)} %ensemble.2), custom_call_target="tpu_custom_call" | custom-call | tf_op jit(solution)/shard_map/pack/pallas_call | solution.py:572
  3.3 0.0 copy-start.1
  3.3 0.0 copy-start.2
  3.3 0.0 copy-start.7
  3.3 0.0 copy-start.8
  3.3 7.3 %all-to-all-start = ((bf16[32,16,512]{2,1,0:T(8,128)(2,1)}), bf16[32,16,512]{2,1,0:T(8,128)(2,1)S(1)}, u32[]{:S(2)}, u32[]{:S(2)}) async-start(bf16[32,16,512]{2,1,0:T(8,128)(2,1)} %pack.1), calls=%async_computation | async-start | bytes 1048576 | tf_op jit(solution)/shard_map/all_to_all | solution.py:591
  10.6 0.0 copy-start.10
  10.7 0.0 copy-done.1
  10.7 0.0 copy-done.2
  10.7 0.0 copy-done.7
  10.7 0.0 copy-done.8
  10.7 0.6 %copy-done.10 = f32[16,16]{1,0:T(8,128)S(1)} copy-done((f32[16,16]{1,0:T(8,128)S(1)}, f32[16,16]{1,0:T(8,128)}, u32[]{:S(2)}) %copy-start.10) | copy-done | bytes 1048
  11.3 0.0 copy-start.4
  11.3 0.0 copy-start.6
  11.3 0.0 copy-start.11
  11.4 0.0 copy-start.5
  11.4 1.1 %observe.1 = (bf16[32,512]{1,0:T(8,128)(2,1)S(1)}, bf16[32,512]{1,0:T(8,128)(2,1)S(1)}, bf16[32,512]{1,0:T(8,128)(2,1)S(1)}, bf16[32,512]{1,0:T(8,128)(2,1)S(1)}...) custom-call(s32[1,128]{1,0:T(1,128)S(1)} %broadcast_in_dim.6.place, s32[1,128]{1,0:T(1,128)S(1)} %broadcast_in_dim.7.turn, ...), custom_call_target="tpu_custom_call" | custom-call | tf_op jit(solution)/shard_map/observe/pallas_call | solution.py:152
  12.5 0.0 copy-start
  12.5 1.8 %collective-permute-start.1 = (bf16[32,512]{1,0:T(8,128)(2,1)S(1)}, bf16[32,512]{1,0:T(8,128)(2,1)S(1)}, u32[]{:S(2)}, u32[]{:S(2)}) collective-permute-start(bf16[32,512]{1,0:T(8,128)(2,1)S(1)} %get-tuple-element.60), channel_id=1, source_target_pairs={{0,2},{1,3},{2,0},{3,1},{4,6},{5,7},{6,4},{7,5},{8,10},{9,11},{10,... | collective-permute-start | bytes 98312 | tf_op jit(solution)/shard_map/ppermute | solution.py:529
  14.3 1.5 %collective-permute-start = (bf16[32,512]{1,0:T(8,128)(2,1)S(1)}, bf16[32,512]{1,0:T(8,128)(2,1)S(1)}, u32[]{:S(2)}, u32[]{:S(2)}) collective-permute-start(bf16[32,512]{1,0:T(8,128)(2,1)S(1)} %get-tuple-element.59), channel_id=1, source_target_pairs={{0,1},{1,0},{2,3},{3,2},{4,5},{5,4},{6,7},{7,6},{8,9},{9,8},{10,11... | collective-permute-start | bytes 98312 | tf_op jit(solution)/shard_map/ppermute | solution.py:529
  15.8 0.3 collective-permute-start.2
  16.1 0.0 copy-done.4
  16.1 0.0 copy-done.6
  16.1 0.0 copy-done.11
  16.1 0.0 copy-done.12
  16.1 1.4 %prepare.1 = (f32[8,64]{1,0:T(8,128)S(1)}, f32[64,64]{1,0:T(8,128)S(1)}, bf16[256,256]{1,0:T(8,128)(2,1)S(1)}, f32[256,1]{1,0:T(8,128)S(1)}, f32[8,128]{1,0:T(8,...) custom-call(s32[1]{0:T(128)} %bitcast.here, s32[16]{0:T(128)S(1)} %copy-done.11, f32[8]{0:T(128)S(1)} %copy-done.12, ...), custom_call_target="tpu_custom_call" | custom-call | tf_op jit(solution)/shard_map/prepare/pallas_call | solution.py:152
  17.4 0.0 collective-permute-done.1.refs_2_
  17.4 0.0 copy-done.5
  17.5 0.0 copy-done
  17.5 0.0 copy-start.3
  17.5 0.5 fold_smooth.1.middle
  18.0 2.1 %collective-permute-start.6 = (bf16[64,1440]{1,0:T(8,128)(2,1)S(1)}, bf16[64,1440]{1,0:T(8,128)(2,1)S(1)}, u32[]{:S(2)}, u32[]{:S(2)}) collective-permute-start(bf16[64,1440]{1,0:T(8,128)(2,1)S(1)} %fold_smooth.1.middle), channel_id=1, source_target_pairs={{0,1},{2,3},{1,0},{3,2},{4,5},{6,7},{5,4},{7,6},{8,9},{10,11},{9,8... | collective-permute-start | bytes 552968 | tf_op jit(solution)/shard_map/ppermute | solution.py:633
  20.1 0.7 %collective-permute-start.7 = (bf16[64,1440]{1,0:T(8,128)(2,1)S(1)}, bf16[64,1440]{1,0:T(8,128)(2,1)S(1)}, u32[]{:S(2)}, u32[]{:S(2)}) collective-permute-start(bf16[64,1440]{1,0:T(8,128)(2,1)S(1)} %fold_smooth.1.middle), channel_id=1, source_target_pairs={{1,2},{2,1},{5,6},{6,5},{9,10},{10,9},{13,14},{14,13},{17,18},{18,... | collective-permute-start | bytes 552968 | tf_op jit(solution)/shard_map/ppermute | solution.py:633
  20.8 0.0 collective-permute-done.refs_1_
  20.8 0.0 collective-permute-done.2.refs_3_
  20.8 6.1 %all-to-all-done.stacked = bf16[32,16,512]{2,1,0:T(8,128)(2,1)S(1)} async-done(((bf16[32,16,512]{2,1,0:T(8,128)(2,1)}), bf16[32,16,512]{2,1,0:T(8,128)(2,1)S(1)}, u32[]{:S(2)}, u32[]{:S(2)}) %all-to-all-start) | async-done | bytes 524320 | tf_op jit(solution)/shard_map/all_to_all | solution.py:591
  26.9 0.0 copy-done.3
  26.9 1.1 %first_half.1 = (bf16[32,384]{1,0:T(8,128)(2,1)S(1)}, f32[2,32,512]{2,1,0:T(8,128)S(1)}, f32[2,32,384]{2,1,0:T(8,128)S(1)}, f32[4,32,384]{2,1,0:T(8,128)S(1)}) custom-call(f32[8,128]{1,0:T(8,128)S(1)} %get-tuple-element.54.weights, s32[1,128]{1,0:T(1,128)S(1)} %broadcast_in_dim.7.turn, bf16[32,16,512]{2,1,0:T(8,128)(2,1)S(1)} %all-to-all-done.stacked, ...), custom_call_target="tpu_custom_call" | custom-call | tf_op jit(solution)/shard_map/first_half/pallas_call | solution.py:152
  28.0 1.5 %collective-permute-start.5 = (bf16[32,384]{1,0:T(8,128)(2,1)S(1)}, bf16[32,384]{1,0:T(8,128)(2,1)S(1)}, u32[]{:S(2)}, u32[]{:S(2)}) collective-permute-start(bf16[32,384]{1,0:T(8,128)(2,1)S(1)} %get-tuple-element.67), channel_id=1, source_target_pairs={{0,24},{4,28},{8,16},{12,20},{16,8},{20,12},{24,0},{28,4},{1,25},{... | collective-permute-start | bytes 73736 | tf_op jit(solution)/shard_map/ppermute | solution.py:539
  29.6 1.1 %collective-permute-start.4 = (bf16[32,384]{1,0:T(8,128)(2,1)S(1)}, bf16[32,384]{1,0:T(8,128)(2,1)S(1)}, u32[]{:S(2)}, u32[]{:S(2)}) collective-permute-start(bf16[32,384]{1,0:T(8,128)(2,1)S(1)} %get-tuple-element.67), channel_id=1, source_target_pairs={{0,16},{4,20},{8,24},{12,28},{16,0},{20,4},{24,8},{28,12},{1,17},{... | collective-permute-start | bytes 73736 | tf_op jit(solution)/shard_map/ppermute | solution.py:539
  30.6 1.8 %collective-permute-start.3 = (bf16[32,384]{1,0:T(8,128)(2,1)S(1)}, bf16[32,384]{1,0:T(8,128)(2,1)S(1)}, u32[]{:S(2)}, u32[]{:S(2)}) collective-permute-start(bf16[32,384]{1,0:T(8,128)(2,1)S(1)} %get-tuple-element.67), channel_id=1, source_target_pairs={{0,8},{4,12},{8,0},{12,4},{16,24},{20,28},{24,16},{28,20},{1,9},{5... | collective-permute-start | bytes 73736 | tf_op jit(solution)/shard_map/ppermute | solution.py:539
  32.5 1.1 %second_half.1 = (bf16[32,8,384]{2,1,0:T(8,128)(2,1)S(1)}, f32[2,32,384]{2,1,0:T(8,128)S(1)}) custom-call(f32[8,128]{1,0:T(8,128)S(1)} %get-tuple-element.54.weights, bf16[32,16,512]{2,1,0:T(8,128)(2,1)S(1)} %all-to-all-done.stacked, bf16[512,512]{1,0:T(8,128)(2,1)S(1)} %copy-done.3, bf16[256,256]{1,0:T(8,128)(2,1)S(1)} %get-tuple-element.56.taper, ...), custom_call_target="tpu_custom_call" | custom-call | flops 1000000000 | tf_op jit(solution)/shard_map/second_half/pallas_call | solution.py:152
  33.5 0.2 collective-permute-done.5
  33.7 0.6 %collective-permute-done.4 = bf16[32,384]{1,0:T(8,128)(2,1)S(1)} collective-permute-done((bf16[32,384]{1,0:T(8,128)(2,1)S(1)}, bf16[32,384]{1,0:T(8,128)(2,1)S(1)}, u32[]{:S(2)}, u32[]{:S(2)}) %collective-permute-start.4) | collective-permute-done | bytes 24608 | tf_op jit(solution)/shard_map/ppermute | solution.py:539
  34.3 0.3 collective-permute-done.3
  34.6 0.0 collective-permute-done.6.below
  34.6 0.0 collective-permute-done.7.above
  34.6 0.1 collective-permute-start.8
  34.7 1.3 %collective-permute-done.8.refs_1_ = bf16[4,32,384]{2,1,0:T(8,128)(2,1)S(1)} collective-permute-done((bf16[4,32,384]{2,1,0:T(8,128)(2,1)S(1)}, bf16[4,32,384]{2,1,0:T(8,128)(2,1)S(1)}, u32[]{:S(2)}, u32[]{:S(2)}) %collective-permute-start.8) | collective-permute-done | bytes 98336 | tf_op jit(solution)/shard_map/ppermute | solution.py:547
  36.0 0.9 %combine.1 = (bf16[32,8,384]{2,1,0:T(8,128)(2,1)}, f32[2,32,384]{2,1,0:T(8,128)S(1)}) custom-call(bf16[32,8,384]{2,1,0:T(8,128)(2,1)S(1)} %get-tuple-element.65.grad, f32[2,32,384]{2,1,0:T(8,128)S(1)} %get-tuple-element.66.first, f32[2,32,384]{2,1,0:T(8,128)S(1)} %get-tuple-element.73.second, f32[4,32,384]{2,1,0:T(8,128)S(1)} %get-tuple-element.74.fields, ...), custom_call_target="tpu_custom_call" | custom-call | tf_op jit(solution)/shard_map/combine/pallas_call | solution.py:152
  36.9 3.0 %all-to-all-start.1 = ((bf16[32,8,384]{2,1,0:T(8,128)(2,1)}), bf16[32,8,384]{2,1,0:T(8,128)(2,1)S(1)}, u32[]{:S(2)}, u32[]{:S(2)}) async-start(bf16[32,8,384]{2,1,0:T(8,128)(2,1)} %get-tuple-element.77), calls=%async_computation.1 | async-start | bytes 393216 | tf_op jit(solution)/shard_map/all_to_all | solution.py:664
  39.9 0.0 copy-start.9
  39.9 0.2 hand_out.1
  40.2 1.8 %collective-permute-start.9 = (bf16[96,384]{1,0:T(8,128)(2,1)S(1)}, bf16[96,384]{1,0:T(8,128)(2,1)S(1)}, u32[]{:S(2)}, u32[]{:S(2)}) collective-permute-start(bf16[96,384]{1,0:T(8,128)(2,1)S(1)} %get-tuple-element.86), channel_id=1, source_target_pairs={{0,1},{1,0},{2,3},{3,2},{4,5},{5,4},{6,7},{7,6},{8,9},{9,8},{10,11... | collective-permute-start | bytes 221192 | tf_op jit(solution)/shard_map/ppermute | solution.py:529
  42.0 1.5 %collective-permute-start.10 = (bf16[96,384]{1,0:T(8,128)(2,1)S(1)}, bf16[96,384]{1,0:T(8,128)(2,1)S(1)}, u32[]{:S(2)}, u32[]{:S(2)}) collective-permute-start(bf16[96,384]{1,0:T(8,128)(2,1)S(1)} %get-tuple-element.87), channel_id=1, source_target_pairs={{0,2},{1,3},{2,0},{3,1},{4,6},{5,7},{6,4},{7,5},{8,10},{9,11},{10,... | collective-permute-start | bytes 221192 | tf_op jit(solution)/shard_map/ppermute | solution.py:529
  43.5 0.3 collective-permute-start.11
  43.7 0.0 copy-done.9
  43.7 0.3 first_gradient.1.grad_first
  44.1 1.6 %collective-permute-done.9.refs_1_ = bf16[96,384]{1,0:T(8,128)(2,1)S(1)} collective-permute-done((bf16[96,384]{1,0:T(8,128)(2,1)S(1)}, bf16[96,384]{1,0:T(8,128)(2,1)S(1)}, u32[]{:S(2)}, u32[]{:S(2)}) %collective-permute-start.9) | collective-permute-done | bytes 73760 | tf_op jit(solution)/shard_map/ppermute | solution.py:529
  45.7 1.9 %collective-permute-done.10.refs_2_ = bf16[96,384]{1,0:T(8,128)(2,1)S(1)} collective-permute-done((bf16[96,384]{1,0:T(8,128)(2,1)S(1)}, bf16[96,384]{1,0:T(8,128)(2,1)S(1)}, u32[]{:S(2)}, u32[]{:S(2)}) %collective-permute-start.10) | collective-permute-done | bytes 73760 | tf_op jit(solution)/shard_map/ppermute | solution.py:529
  47.6 1.5 %collective-permute-done.11.refs_3_ = bf16[96,384]{1,0:T(8,128)(2,1)S(1)} collective-permute-done((bf16[96,384]{1,0:T(8,128)(2,1)S(1)}, bf16[96,384]{1,0:T(8,128)(2,1)S(1)}, u32[]{:S(2)}, u32[]{:S(2)}) %collective-permute-start.11) | collective-permute-done | bytes 73760 | tf_op jit(solution)/shard_map/ppermute | solution.py:529
  49.0 0.4 join.1
  49.5 0.0 all-to-all-done.1.back
  49.5 1.3 %finish.1 = (f32[1,16,4,1440]{3,2,1,0:T(4,128)}, f32[16,4,1440]{2,1,0:T(4,128)}, f32[2,2,4,1440]{3,2,1,0:T(4,128)}) custom-call(bf16[32,8,384]{2,1,0:T(8,128)(2,1)S(1)} %all-to-all-done.1.back, f32[64,1440]{1,0:T(8,128)S(1)} %first_gradient.1.grad_first, f32[64,1440]{1,0:T(8,128)S(1)} %get-tuple-element.81.pulled_first, ...), custom_call_target="tpu_custom_call" | custom-call | tf_op jit(solution)/shard_map/finish/pallas_call | solution.py:684
  (4 shorter events, 0.0 us)
Async XLA Ops:
  3.3 7.4 %copy-start.1 = (bf16[2,16,4,1440]{3,2,1,0:T(4,128)(2,1)S(1)}, bf16[2,16,4,1440]{3,2,1,0:T(4,128)(2,1)}, u32[]{:S(2)}) copy-start(bf16[2,16,4,1440]{3,2,1,0:T(4,128)(2,1)} %innovation.1) | copy-start | bytes 1105924
  3.3 7.4 %copy-start.2 = (bf16[16,4,1440]{2,1,0:T(4,128)(2,1)S(1)}, bf16[16,4,1440]{2,1,0:T(4,128)(2,1)}, u32[]{:S(2)}) copy-start(bf16[16,4,1440]{2,1,0:T(4,128)(2,1)} %precision.1) | copy-start | bytes 552964
  3.3 7.4 %copy-start.7 = (f32[64,16]{1,0:T(8,128)S(1)}, f32[64,16]{1,0:T(8,128)}, u32[]{:S(2)}) copy-start(f32[64,16]{1,0:T(8,128)} %constant.23.clone.of_level) | copy-start | bytes 12292
  3.3 7.4 %copy-start.8 = (f32[64,64]{1,0:T(8,128)S(1)}, f32[64,64]{1,0:T(8,128)}, u32[]{:S(2)}) copy-start(f32[64,64]{1,0:T(8,128)} %constant.24.clone.same) | copy-start | bytes 49156
  3.3 23.6 %all-to-all-start = ((bf16[32,16,512]{2,1,0:T(8,128)(2,1)}), bf16[32,16,512]{2,1,0:T(8,128)(2,1)S(1)}, u32[]{:S(2)}, u32[]{:S(2)}) async-start(bf16[32,16,512]{2,1,0:T(8,128)(2,1)} %pack.1), calls=%async_computation | async-start | bytes 1048576 | tf_op jit(solution)/shard_map/all_to_all | solution.py:591
  10.6 0.7 %copy-start.10 = (f32[16,16]{1,0:T(8,128)S(1)}, f32[16,16]{1,0:T(8,128)}, u32[]{:S(2)}) copy-start(f32[16,16]{1,0:T(8,128)} %root.1) | copy-start | bytes 3076
  11.3 4.7 %copy-start.4 = (f32[256,256]{1,0:T(8,128)S(1)}, f32[256,256]{1,0:T(8,128)}, u32[]{:S(2)}) copy-start(f32[256,256]{1,0:T(8,128)} %constant.25.clone.apart) | copy-start | bytes 786436
  11.3 4.7 %copy-start.6 = (f32[256,1]{1,0:T(8,128)S(1)}, f32[256,1]{1,0:T(8,128)}, u32[]{:S(2)}) copy-start(f32[256,1]{1,0:T(8,128)} %constant.26.clone.level) | copy-start | bytes 3076
  11.3 4.7 %copy-start.11 = (s32[16]{0:T(128)S(1)}, s32[16]{0:T(128)}, u32[]{:S(2)}) copy-start(s32[16]{0:T(128)} %widths.1) | copy-start | bytes 196
  11.4 4.7 %copy-start.12 = (f32[8]{0:T(128)S(1)}, f32[8]{0:T(128)}, u32[]{:S(2)}) copy-start(f32[8]{0:T(128)} %weight.1) | copy-start | bytes 100
  11.4 6.1 %copy-start.5 = (bf16[512,256]{1,0:T(8,128)(2,1)S(1)}, bf16[512,256]{1,0:T(8,128)(2,1)}, u32[]{:S(2)}) copy-start(bf16[512,256]{1,0:T(8,128)(2,1)} %constant.27.clone.kernel) | copy-start | bytes 786436
  12.5 5.0 %copy-start = (bf16[1,2,16,4,1440]{4,3,2,1,0:T(4,128)(2,1)S(1)}, bf16[1,2,16,4,1440]{4,3,2,1,0:T(4,128)(2,1)}, u32[]{:S(2)}) copy-start(bf16[1,2,16,4,1440]{4,3,2,1,0:T(4,128)(2,1)} %ensemble.2) | copy-start | bytes 1105924
  12.5 4.9 %collective-permute-start.1 = (bf16[32,512]{1,0:T(8,128)(2,1)S(1)}, bf16[32,512]{1,0:T(8,128)(2,1)S(1)}, u32[]{:S(2)}, u32[]{:S(2)}) collective-permute-start(bf16[32,512]{1,0:T(8,128)(2,1)S(1)} %get-tuple-element.60), channel_id=1, source_target_pairs={{0,2},{1,3},{2,0},{3,1},{4,6},{5,7},{6,4},{7,5},{8,10},{9,11},{10,... | collective-permute-start | bytes 98312 | tf_op jit(solution)/shard_map/ppermute | solution.py:529
  14.3 6.4 %collective-permute-start = (bf16[32,512]{1,0:T(8,128)(2,1)S(1)}, bf16[32,512]{1,0:T(8,128)(2,1)S(1)}, u32[]{:S(2)}, u32[]{:S(2)}) collective-permute-start(bf16[32,512]{1,0:T(8,128)(2,1)S(1)} %get-tuple-element.59), channel_id=1, source_target_pairs={{0,1},{1,0},{2,3},{3,2},{4,5},{5,4},{6,7},{7,6},{8,9},{9,8},{10,11... | collective-permute-start | bytes 98312 | tf_op jit(solution)/shard_map/ppermute | solution.py:529
  15.8 5.0 %collective-permute-start.2 = (bf16[32,512]{1,0:T(8,128)(2,1)S(1)}, bf16[32,512]{1,0:T(8,128)(2,1)S(1)}, u32[]{:S(2)}, u32[]{:S(2)}) collective-permute-start(bf16[32,512]{1,0:T(8,128)(2,1)S(1)} %get-tuple-element.63), channel_id=1, source_target_pairs={{0,3},{1,2},{2,1},{3,0},{4,7},{5,6},{6,5},{7,4},{8,11},{9,10},{10,... | collective-permute-start | bytes 98312 | tf_op jit(solution)/shard_map/ppermute | solution.py:529
  17.5 9.4 %copy-start.3 = (bf16[512,512]{1,0:T(8,128)(2,1)S(1)}, bf16[512,512]{1,0:T(8,128)(2,1)}, u32[]{:S(2)}) copy-start(bf16[512,512]{1,0:T(8,128)(2,1)} %constant.28.clone.ring) | copy-start | bytes 1572868
  18.0 16.5 %collective-permute-start.6 = (bf16[64,1440]{1,0:T(8,128)(2,1)S(1)}, bf16[64,1440]{1,0:T(8,128)(2,1)S(1)}, u32[]{:S(2)}, u32[]{:S(2)}) collective-permute-start(bf16[64,1440]{1,0:T(8,128)(2,1)S(1)} %fold_smooth.1.middle), channel_id=1, source_target_pairs={{0,1},{2,3},{1,0},{3,2},{4,5},{6,7},{5,4},{7,6},{8,9},{10,11},{9,8... | collective-permute-start | bytes 552968 | tf_op jit(solution)/shard_map/ppermute | solution.py:633
  20.1 14.5 %collective-permute-start.7 = (bf16[64,1440]{1,0:T(8,128)(2,1)S(1)}, bf16[64,1440]{1,0:T(8,128)(2,1)S(1)}, u32[]{:S(2)}, u32[]{:S(2)}) collective-permute-start(bf16[64,1440]{1,0:T(8,128)(2,1)S(1)} %fold_smooth.1.middle), channel_id=1, source_target_pairs={{1,2},{2,1},{5,6},{6,5},{9,10},{10,9},{13,14},{14,13},{17,18},{18,... | collective-permute-start | bytes 552968 | tf_op jit(solution)/shard_map/ppermute | solution.py:633
  28.0 5.7 %collective-permute-start.5 = (bf16[32,384]{1,0:T(8,128)(2,1)S(1)}, bf16[32,384]{1,0:T(8,128)(2,1)S(1)}, u32[]{:S(2)}, u32[]{:S(2)}) collective-permute-start(bf16[32,384]{1,0:T(8,128)(2,1)S(1)} %get-tuple-element.67), channel_id=1, source_target_pairs={{0,24},{4,28},{8,16},{12,20},{16,8},{20,12},{24,0},{28,4},{1,25},{... | collective-permute-start | bytes 73736 | tf_op jit(solution)/shard_map/ppermute | solution.py:539
  29.6 4.7 %collective-permute-start.4 = (bf16[32,384]{1,0:T(8,128)(2,1)S(1)}, bf16[32,384]{1,0:T(8,128)(2,1)S(1)}, u32[]{:S(2)}, u32[]{:S(2)}) collective-permute-start(bf16[32,384]{1,0:T(8,128)(2,1)S(1)} %get-tuple-element.67), channel_id=1, source_target_pairs={{0,16},{4,20},{8,24},{12,28},{16,0},{20,4},{24,8},{28,12},{1,17},{... | collective-permute-start | bytes 73736 | tf_op jit(solution)/shard_map/ppermute | solution.py:539
  30.6 3.9 %collective-permute-start.3 = (bf16[32,384]{1,0:T(8,128)(2,1)S(1)}, bf16[32,384]{1,0:T(8,128)(2,1)S(1)}, u32[]{:S(2)}, u32[]{:S(2)}) collective-permute-start(bf16[32,384]{1,0:T(8,128)(2,1)S(1)} %get-tuple-element.67), channel_id=1, source_target_pairs={{0,8},{4,12},{8,0},{12,4},{16,24},{20,28},{24,16},{28,20},{1,9},{5... | collective-permute-start | bytes 73736 | tf_op jit(solution)/shard_map/ppermute | solution.py:539
  34.6 1.4 %collective-permute-start.8 = (bf16[4,32,384]{2,1,0:T(8,128)(2,1)S(1)}, bf16[4,32,384]{2,1,0:T(8,128)(2,1)S(1)}, u32[]{:S(2)}, u32[]{:S(2)}) collective-permute-start(bf16[4,32,384]{2,1,0:T(8,128)(2,1)S(1)} %pad_maximum_fusion.refs_0_), channel_id=1, source_target_pairs={{0,4},{4,0},{8,12},{12,8},{16,20},{20,16},{24,28},{28,24},{1,5},{5... | collective-permute-start | bytes 294920 | tf_op jit(solution)/shard_map/ppermute | solution.py:547
  36.9 12.6 %all-to-all-start.1 = ((bf16[32,8,384]{2,1,0:T(8,128)(2,1)}), bf16[32,8,384]{2,1,0:T(8,128)(2,1)S(1)}, u32[]{:S(2)}, u32[]{:S(2)}) async-start(bf16[32,8,384]{2,1,0:T(8,128)(2,1)} %get-tuple-element.77), calls=%async_computation.1 | async-start | bytes 393216 | tf_op jit(solution)/shard_map/all_to_all | solution.py:664
  39.9 3.8 %copy-start.9 = (f32[64,192]{1,0:T(8,128)S(1)}, f32[64,192]{1,0:T(8,128)}, u32[]{:S(2)}) copy-start(f32[64,192]{1,0:T(8,128)} %constant.29.clone.apart) | copy-start | bytes 147460
  40.2 5.5 %collective-permute-start.9 = (bf16[96,384]{1,0:T(8,128)(2,1)S(1)}, bf16[96,384]{1,0:T(8,128)(2,1)S(1)}, u32[]{:S(2)}, u32[]{:S(2)}) collective-permute-start(bf16[96,384]{1,0:T(8,128)(2,1)S(1)} %get-tuple-element.86), channel_id=1, source_target_pairs={{0,1},{1,0},{2,3},{3,2},{4,5},{5,4},{6,7},{7,6},{8,9},{9,8},{10,11... | collective-permute-start | bytes 221192 | tf_op jit(solution)/shard_map/ppermute | solution.py:529
  42.0 5.6 %collective-permute-start.10 = (bf16[96,384]{1,0:T(8,128)(2,1)S(1)}, bf16[96,384]{1,0:T(8,128)(2,1)S(1)}, u32[]{:S(2)}, u32[]{:S(2)}) collective-permute-start(bf16[96,384]{1,0:T(8,128)(2,1)S(1)} %get-tuple-element.87), channel_id=1, source_target_pairs={{0,2},{1,3},{2,0},{3,1},{4,6},{5,7},{6,4},{7,5},{8,10},{9,11},{10,... | collective-permute-start | bytes 221192 | tf_op jit(solution)/shard_map/ppermute | solution.py:529
  43.5 5.6 %collective-permute-start.11 = (bf16[96,384]{1,0:T(8,128)(2,1)S(1)}, bf16[96,384]{1,0:T(8,128)(2,1)S(1)}, u32[]{:S(2)}, u32[]{:S(2)}) collective-permute-start(bf16[96,384]{1,0:T(8,128)(2,1)S(1)} %get-tuple-element.88), channel_id=1, source_target_pairs={{0,3},{1,2},{2,1},{3,0},{4,7},{5,6},{6,5},{7,4},{8,11},{9,10},{10,... | collective-permute-start | bytes 221192 | tf_op jit(solution)/shard_map/ppermute | solution.py:529

commit v16 on v13

--- a/solution.py
+++ b/solution.py
@@ -162,7 +162,7 @@
 
         f32, bf16 = jnp.float32, jnp.bfloat16
 
-        def fold_smooth(own_weight, ensemble, innovation, precision, kernel, out):
+        def fold_smooth(slot, weight, ensemble, innovation, precision, kernel, out):
             total = []
             for at in range(levels):
                 precise = precision[at].astype(f32)
@@ -171,7 +171,10 @@
                     weighted = precise * innovation[t, at].astype(f32)
                     part = part + ensemble[0, t, at].astype(f32) * weighted
                 total.append(part)
-            total = own_weight[:, :1] * jnp.concatenate(total, axis=0)
+            chosen_weight = jnp.where(
+                lax.broadcasted_iota(jnp.int32, weight.shape, 1) == slot[...], weight[...], 0.0
+            )
+            total = jnp.sum(chosen_weight, axis=1, keepdims=True) * jnp.concatenate(total, axis=0)
             step = kernel.shape[1]
             margin = (kernel.shape[0] - step) // 2
             steps = -(-lon // step)
@@ -297,11 +300,10 @@
                 own_static[band] = piece[(slots + 1) * own :, :kept]
             deal(turn[:, :1], pieces, outs)
 
-        def prepare(here, widths, weight, marks, root, of_level, same, apart, level, *refs):
-            mixing, pulling, taper, factor, weights, own_weight, row_span, mixed, pulls = refs
+        def prepare(here, widths, weight, root, of_level, same, apart, level, *refs):
+            mixing, pulling, taper, factor, weights, row_span, mixed, pulls = refs
             for member in range(members):
                 weights[member : member + 1] = jnp.full((1, LANES), weight[member], f32)
-            own_weight[...] = jnp.full((1, LANES), weight[marks[0]], f32)
             for at in range(levels):
                 row_span[at * rows : (at + 1) * rows] = jnp.full(
                     (rows, LANES), widths[at].astype(f32) + 1.0, f32
@@ -599,7 +601,7 @@
         )
         blocks, (own_static, pulled) = trade(results[:-2]), results[-2:]
         own_static, between = lax.optimization_barrier((own_static, between))
-        mixing, pulling, taper, factor, weights, own_weight, row_span = call(
+        mixing, pulling, taper, factor, weights, row_span = call(
             prepare,
             [
                 ((own, everything), f32),
@@ -607,10 +609,9 @@
                 (apart.shape, bf16),
                 (every_level.shape, f32),
                 ((members, LANES), f32),
-                ((1, LANES), f32),
                 ((everything, LANES), f32),
             ],
-            [here, halfwidth, member_weight, member_of_slot],
+            [here, halfwidth, member_weight],
             [*between, jnp.asarray(apart), jnp.asarray(every_level)],
             scratch=[((levels, rows, everything), f32)] * 2,
         )
@@ -622,7 +623,7 @@
             fold_smooth,
             [((everything, lon), bf16)],
             [],
-            [own_weight, ensemble, innovation, precision, lon_kernel(LANES, 2 * LANES)],
+            [member_of_slot[None], member_weight[None], ensemble, innovation, precision, lon_kernel(LANES, 2 * LANES)],
         )
         pairs = [(at, at + 1) for at in range(bands - 1)]
         below, above = [

time: 51.1 us -> 51.2 us (level)
  no operation moved by 1% of the time
where the time goes in v16:
time: 51.2 us; the launch traced here: 50.7 us
  starting transfers between devices  24.7 us (48%)
  waiting for transfers between devices  13.3 us (26%)
  Pallas kernels  10.4 us (20%)
  between operations  1.59 us (3%)
  local copies, waits for them, and re-layouts  0.72 us (1%)
    all_to_all x1, starting transfers between devices, shards(): stacked = lax.all_to_all(pieces, BOTH, 0, 0, tiled=True)  7.3 us
    pallas_call x9, Pallas kernels, call(): pl.pallas_call(body, out_shape=tuple((jax.ShapeDtypeStruct(shape, kind) f...  7.14 us
    ppermute x6, starting transfers between devices, trade(): lax.ppermute(blocks[shift], 'band', [(at, partner(at, shift, bands, 1)) f...  7.11 us
    all_to_all x1, waiting for transfers between devices, shards(): stacked = lax.all_to_all(pieces, BOTH, 0, 0, tiled=True)  6 us
    ppermute x6, waiting for transfers between devices, trade(): lax.ppermute(blocks[shift], 'band', [(at, partner(at, shift, bands, 1)) f...  4.98 us
    ppermute x3, starting transfers between devices, around(): lax.ppermute(block, 'member', [(at, 2 * partner(at // 2, shift, members /...  4.45 us
    all_to_all x1, starting transfers between devices, shards(): back = lax.all_to_all(grad, BOTH, 0, 0, tiled=True)  3.03 us
    ppermute x2, starting transfers between devices, shards(): lax.ppermute(smoothed, 'band', pairs[start::2] + [(to, at) for at, to in...  2.75 us
  transfers between devices with their start and end apart: 14, of which 8 were waited for; matrix products, arithmetic and copies ran while one was open for 0% of the time, Pallas kernels for 12%

profile of v16, /device:TPU:0, one launch (start us, length us, event | category | flops | bytes accessed | tf_op | source)
XLA Modules:
  0.0 50.7 jit_solution(6489519280325194629)
XLA Ops:
  1.3 2.0 %pack.1 = bf16[32,16,512]{2,1,0:T(8,128)(2,1)} custom-call(s32[1]{0:T(128)} %copy.17.slot, bf16[1,2,16,4,1440]{4,3,2,1,0:T(4,128)(2,1)} %ensemble.2), custom_call_target="tpu_custom_call" | custom-call | tf_op jit(solution)/shard_map/pack/pallas_call | solution.py:570
  3.3 0.0 copy-start.1
  3.3 0.0 copy-start.2
  3.3 0.0 copy-start.7
  3.3 0.0 copy-start.8
  3.3 7.3 %all-to-all-start = ((bf16[32,16,512]{2,1,0:T(8,128)(2,1)}), bf16[32,16,512]{2,1,0:T(8,128)(2,1)S(1)}, u32[]{:S(2)}, u32[]{:S(2)}) async-start(bf16[32,16,512]{2,1,0:T(8,128)(2,1)} %pack.1), calls=%async_computation | async-start | bytes 1048576 | tf_op jit(solution)/shard_map/all_to_all | solution.py:589
  10.6 0.0 copy-start.10
  10.7 0.0 copy-done.1
  10.7 0.0 copy-done.2
  10.7 0.0 copy-done.7
  10.7 0.0 copy-done.8
  10.7 0.6 %copy-done.10 = f32[16,16]{1,0:T(8,128)S(1)} copy-done((f32[16,16]{1,0:T(8,128)S(1)}, f32[16,16]{1,0:T(8,128)}, u32[]{:S(2)}) %copy-start.10) | copy-done | bytes 1048
  11.3 0.0 copy-start.5
  11.3 0.0 copy-start.6
  11.3 0.0 copy-start.11
  11.4 0.0 copy-start.4
  11.4 1.1 %observe.1 = (bf16[32,512]{1,0:T(8,128)(2,1)S(1)}, bf16[32,512]{1,0:T(8,128)(2,1)S(1)}, bf16[32,512]{1,0:T(8,128)(2,1)S(1)}, bf16[32,512]{1,0:T(8,128)(2,1)S(1)}...) custom-call(s32[1,128]{1,0:T(1,128)S(1)} %broadcast_in_dim.12.place, s32[1,128]{1,0:T(1,128)S(1)} %broadcast_in_dim.13.turn, ...), custom_call_target="tpu_custom_call" | custom-call | tf_op jit(solution)/shard_map/observe/pallas_call | solution.py:152
  12.5 0.0 copy-start
  12.5 1.8 %collective-permute-start.1 = (bf16[32,512]{1,0:T(8,128)(2,1)S(1)}, bf16[32,512]{1,0:T(8,128)(2,1)S(1)}, u32[]{:S(2)}, u32[]{:S(2)}) collective-permute-start(bf16[32,512]{1,0:T(8,128)(2,1)S(1)} %get-tuple-element.59), channel_id=1, source_target_pairs={{0,2},{1,3},{2,0},{3,1},{4,6},{5,7},{6,4},{7,5},{8,10},{9,11},{10,... | collective-permute-start | bytes 98312 | tf_op jit(solution)/shard_map/ppermute | solution.py:527
  14.3 1.5 %collective-permute-start = (bf16[32,512]{1,0:T(8,128)(2,1)S(1)}, bf16[32,512]{1,0:T(8,128)(2,1)S(1)}, u32[]{:S(2)}, u32[]{:S(2)}) collective-permute-start(bf16[32,512]{1,0:T(8,128)(2,1)S(1)} %get-tuple-element.58), channel_id=1, source_target_pairs={{0,1},{1,0},{2,3},{3,2},{4,5},{5,4},{6,7},{7,6},{8,9},{9,8},{10,11... | collective-permute-start | bytes 98312 | tf_op jit(solution)/shard_map/ppermute | solution.py:527
  15.8 0.3 collective-permute-start.2
  16.1 0.0 copy-done.5
  16.1 0.0 copy-done.6
  16.1 0.0 copy-done.11
  16.1 0.0 copy-done.12
  16.1 1.4 %prepare.1 = (f32[8,64]{1,0:T(8,128)S(1)}, f32[64,64]{1,0:T(8,128)S(1)}, bf16[256,256]{1,0:T(8,128)(2,1)S(1)}, f32[256,1]{1,0:T(8,128)S(1)}, f32[8,128]{1,0:T(8,128)S(1)}, /*index=5*/f32[64,128]{1,0:T(8,128)S(1)}) custom-call(s32[1]{0:T(128)} %bitcast.here, s32[16]{0:T(128)S(1)} %copy-done.12, f32[8]{0:T(128)S(1)} %copy-done.11, f32[16,16]{1,0:T(8,128)S(1)} %copy-done.10, ...), custom_call_target="tpu_custom_call" | custom-call | tf_op jit(solution)/shard_map/prepare/pallas_call | solution.py:152
  17.4 0.0 collective-permute-done.1.refs_2_
  17.4 0.0 copy-done.4
  17.5 0.0 copy-done
  17.5 0.0 copy-start.3
  17.5 0.6 %fold_smooth.1.middle = bf16[64,1440]{1,0:T(8,128)(2,1)S(1)} custom-call(s32[1,1]{1,0:T(1,128)} %bitcast.7.slot, f32[1,8]{1,0:T(1,128)S(1)} %bitcast.9, bf16[1,2,16,4,1440]{4,3,2,1,0:T(4,128)(2,1)S(1)} %copy-done, bf16[2,16,4,1440]{3,2,1,0:T(4,128)(2,1)S(1)} %copy-done.1, bf16[16,4,1440]{2,1,0:T(4,128)(2,1)S(1)} %copy-done.2, bf16[512,256]{1,0:T(8,128)(2,1)S(1)} %copy-done.4), custom_call_target="tpu_custom_call" | custom-call | tf_op jit(solution)/shard_map/fold_smooth/pallas_call | solution.py:152
  18.1 2.1 %collective-permute-start.6 = (bf16[64,1440]{1,0:T(8,128)(2,1)S(1)}, bf16[64,1440]{1,0:T(8,128)(2,1)S(1)}, u32[]{:S(2)}, u32[]{:S(2)}) collective-permute-start(bf16[64,1440]{1,0:T(8,128)(2,1)S(1)} %fold_smooth.1.middle), channel_id=1, source_target_pairs={{0,1},{2,3},{1,0},{3,2},{4,5},{6,7},{5,4},{7,6},{8,9},{10,11},{9,8... | collective-permute-start | bytes 552968 | tf_op jit(solution)/shard_map/ppermute | solution.py:630
  20.2 0.7 %collective-permute-start.7 = (bf16[64,1440]{1,0:T(8,128)(2,1)S(1)}, bf16[64,1440]{1,0:T(8,128)(2,1)S(1)}, u32[]{:S(2)}, u32[]{:S(2)}) collective-permute-start(bf16[64,1440]{1,0:T(8,128)(2,1)S(1)} %fold_smooth.1.middle), channel_id=1, source_target_pairs={{1,2},{2,1},{5,6},{6,5},{9,10},{10,9},{13,14},{14,13},{17,18},{18,... | collective-permute-start | bytes 552968 | tf_op jit(solution)/shard_map/ppermute | solution.py:630
  20.9 0.0 collective-permute-done.refs_1_
  20.9 0.0 collective-permute-done.2.refs_3_
  20.9 6.0 %all-to-all-done.stacked = bf16[32,16,512]{2,1,0:T(8,128)(2,1)S(1)} async-done(((bf16[32,16,512]{2,1,0:T(8,128)(2,1)}), bf16[32,16,512]{2,1,0:T(8,128)(2,1)S(1)}, u32[]{:S(2)}, u32[]{:S(2)}) %all-to-all-start) | async-done | bytes 524320 | tf_op jit(solution)/shard_map/all_to_all | solution.py:589
  26.9 0.0 copy-done.3
  26.9 1.1 %first_half.1 = (bf16[32,384]{1,0:T(8,128)(2,1)S(1)}, f32[2,32,512]{2,1,0:T(8,128)S(1)}, f32[2,32,384]{2,1,0:T(8,128)S(1)}, f32[4,32,384]{2,1,0:T(8,128)S(1)}) custom-call(f32[8,128]{1,0:T(8,128)S(1)} %get-tuple-element.53.weights, s32[1,128]{1,0:T(1,128)S(1)} %broadcast_in_dim.13.turn, bf16[32,16,512]{2,1,0:T(8,128)(2,1)S(1)} %all-to-all-done.stacked, ...), custom_call_target="tpu_custom_call" | custom-call | tf_op jit(solution)/shard_map/first_half/pallas_call | solution.py:152
  28.0 1.5 %collective-permute-start.5 = (bf16[32,384]{1,0:T(8,128)(2,1)S(1)}, bf16[32,384]{1,0:T(8,128)(2,1)S(1)}, u32[]{:S(2)}, u32[]{:S(2)}) collective-permute-start(bf16[32,384]{1,0:T(8,128)(2,1)S(1)} %get-tuple-element.66), channel_id=1, source_target_pairs={{0,24},{4,28},{8,16},{12,20},{16,8},{20,12},{24,0},{28,4},{1,25},{... | collective-permute-start | bytes 73736 | tf_op jit(solution)/shard_map/ppermute | solution.py:537
  29.6 1.1 %collective-permute-start.4 = (bf16[32,384]{1,0:T(8,128)(2,1)S(1)}, bf16[32,384]{1,0:T(8,128)(2,1)S(1)}, u32[]{:S(2)}, u32[]{:S(2)}) collective-permute-start(bf16[32,384]{1,0:T(8,128)(2,1)S(1)} %get-tuple-element.66), channel_id=1, source_target_pairs={{0,16},{4,20},{8,24},{12,28},{16,0},{20,4},{24,8},{28,12},{1,17},{... | collective-permute-start | bytes 73736 | tf_op jit(solution)/shard_map/ppermute | solution.py:537
  30.6 1.8 %collective-permute-start.3 = (bf16[32,384]{1,0:T(8,128)(2,1)S(1)}, bf16[32,384]{1,0:T(8,128)(2,1)S(1)}, u32[]{:S(2)}, u32[]{:S(2)}) collective-permute-start(bf16[32,384]{1,0:T(8,128)(2,1)S(1)} %get-tuple-element.66), channel_id=1, source_target_pairs={{0,8},{4,12},{8,0},{12,4},{16,24},{20,28},{24,16},{28,20},{1,9},{5... | collective-permute-start | bytes 73736 | tf_op jit(solution)/shard_map/ppermute | solution.py:537
  32.5 1.1 %second_half.1 = (bf16[32,8,384]{2,1,0:T(8,128)(2,1)S(1)}, f32[2,32,384]{2,1,0:T(8,128)S(1)}) custom-call(f32[8,128]{1,0:T(8,128)S(1)} %get-tuple-element.53.weights, bf16[32,16,512]{2,1,0:T(8,128)(2,1)S(1)} %all-to-all-done.stacked, bf16[512,512]{1,0:T(8,128)(2,1)S(1)} %copy-done.3, bf16[256,256]{1,0:T(8,128)(2,1)S(1)} %get-tuple-element.55.taper, ...), custom_call_target="tpu_custom_call" | custom-call | flops 1000000000 | tf_op jit(solution)/shard_map/second_half/pallas_call | solution.py:152
  33.5 0.2 collective-permute-done.5
  33.7 0.6 %collective-permute-done.4 = bf16[32,384]{1,0:T(8,128)(2,1)S(1)} collective-permute-done((bf16[32,384]{1,0:T(8,128)(2,1)S(1)}, bf16[32,384]{1,0:T(8,128)(2,1)S(1)}, u32[]{:S(2)}, u32[]{:S(2)}) %collective-permute-start.4) | collective-permute-done | bytes 24608 | tf_op jit(solution)/shard_map/ppermute | solution.py:537
  34.3 0.3 collective-permute-done.3
  34.6 0.0 collective-permute-done.6.below
  34.6 0.0 collective-permute-done.7.above
  34.6 0.1 collective-permute-start.8
  34.7 1.3 %collective-permute-done.8.refs_1_ = bf16[4,32,384]{2,1,0:T(8,128)(2,1)S(1)} collective-permute-done((bf16[4,32,384]{2,1,0:T(8,128)(2,1)S(1)}, bf16[4,32,384]{2,1,0:T(8,128)(2,1)S(1)}, u32[]{:S(2)}, u32[]{:S(2)}) %collective-permute-start.8) | collective-permute-done | bytes 98336 | tf_op jit(solution)/shard_map/ppermute | solution.py:545
  36.0 0.9 %combine.1 = (bf16[32,8,384]{2,1,0:T(8,128)(2,1)}, f32[2,32,384]{2,1,0:T(8,128)S(1)}) custom-call(bf16[32,8,384]{2,1,0:T(8,128)(2,1)S(1)} %get-tuple-element.64.grad, f32[2,32,384]{2,1,0:T(8,128)S(1)} %get-tuple-element.65.first, f32[2,32,384]{2,1,0:T(8,128)S(1)} %get-tuple-element.71.second, f32[4,32,384]{2,1,0:T(8,128)S(1)} %get-tuple-element.72.fields, ...), custom_call_target="tpu_custom_call" | custom-call | tf_op jit(solution)/shard_map/combine/pallas_call | solution.py:152
  36.9 3.0 %all-to-all-start.1 = ((bf16[32,8,384]{2,1,0:T(8,128)(2,1)}), bf16[32,8,384]{2,1,0:T(8,128)(2,1)S(1)}, u32[]{:S(2)}, u32[]{:S(2)}) async-start(bf16[32,8,384]{2,1,0:T(8,128)(2,1)} %get-tuple-element.75), calls=%async_computation.1 | async-start | bytes 393216 | tf_op jit(solution)/shard_map/all_to_all | solution.py:661
  39.9 0.0 copy-start.9
  39.9 0.2 hand_out.1
  40.2 1.8 %collective-permute-start.9 = (bf16[96,384]{1,0:T(8,128)(2,1)S(1)}, bf16[96,384]{1,0:T(8,128)(2,1)S(1)}, u32[]{:S(2)}, u32[]{:S(2)}) collective-permute-start(bf16[96,384]{1,0:T(8,128)(2,1)S(1)} %get-tuple-element.84), channel_id=1, source_target_pairs={{0,1},{1,0},{2,3},{3,2},{4,5},{5,4},{6,7},{7,6},{8,9},{9,8},{10,11... | collective-permute-start | bytes 221192 | tf_op jit(solution)/shard_map/ppermute | solution.py:527
  42.0 1.5 %collective-permute-start.10 = (bf16[96,384]{1,0:T(8,128)(2,1)S(1)}, bf16[96,384]{1,0:T(8,128)(2,1)S(1)}, u32[]{:S(2)}, u32[]{:S(2)}) collective-permute-start(bf16[96,384]{1,0:T(8,128)(2,1)S(1)} %get-tuple-element.85), channel_id=1, source_target_pairs={{0,2},{1,3},{2,0},{3,1},{4,6},{5,7},{6,4},{7,5},{8,10},{9,11},{10,... | collective-permute-start | bytes 221192 | tf_op jit(solution)/shard_map/ppermute | solution.py:527
  43.5 0.3 collective-permute-start.11
  43.7 0.0 copy-done.9
  43.7 0.3 first_gradient.1.grad_first
  44.1 1.6 %collective-permute-done.9.refs_1_ = bf16[96,384]{1,0:T(8,128)(2,1)S(1)} collective-permute-done((bf16[96,384]{1,0:T(8,128)(2,1)S(1)}, bf16[96,384]{1,0:T(8,128)(2,1)S(1)}, u32[]{:S(2)}, u32[]{:S(2)}) %collective-permute-start.9) | collective-permute-done | bytes 73760 | tf_op jit(solution)/shard_map/ppermute | solution.py:527
  45.7 1.9 %collective-permute-done.10.refs_2_ = bf16[96,384]{1,0:T(8,128)(2,1)S(1)} collective-permute-done((bf16[96,384]{1,0:T(8,128)(2,1)S(1)}, bf16[96,384]{1,0:T(8,128)(2,1)S(1)}, u32[]{:S(2)}, u32[]{:S(2)}) %collective-permute-start.10) | collective-permute-done | bytes 73760 | tf_op jit(solution)/shard_map/ppermute | solution.py:527
  47.6 1.5 %collective-permute-done.11.refs_3_ = bf16[96,384]{1,0:T(8,128)(2,1)S(1)} collective-permute-done((bf16[96,384]{1,0:T(8,128)(2,1)S(1)}, bf16[96,384]{1,0:T(8,128)(2,1)S(1)}, u32[]{:S(2)}, u32[]{:S(2)}) %collective-permute-start.11) | collective-permute-done | bytes 73760 | tf_op jit(solution)/shard_map/ppermute | solution.py:527
  49.0 0.4 join.1
  49.5 0.0 all-to-all-done.1.back
  49.5 1.3 %finish.1 = (f32[1,16,4,1440]{3,2,1,0:T(4,128)}, f32[16,4,1440]{2,1,0:T(4,128)}, f32[2,2,4,1440]{3,2,1,0:T(4,128)}) custom-call(bf16[32,8,384]{2,1,0:T(8,128)(2,1)S(1)} %all-to-all-done.1.back, f32[64,1440]{1,0:T(8,128)S(1)} %first_gradient.1.grad_first, f32[64,1440]{1,0:T(8,128)S(1)} %get-tuple-element.79.pulled_first, ...), custom_call_target="tpu_custom_call" | custom-call | tf_op jit(solution)/shard_map/finish/pallas_call | solution.py:681
  (4 shorter events, 0.0 us)
Async XLA Ops:
  3.3 7.4 %copy-start.1 = (bf16[2,16,4,1440]{3,2,1,0:T(4,128)(2,1)S(1)}, bf16[2,16,4,1440]{3,2,1,0:T(4,128)(2,1)}, u32[]{:S(2)}) copy-start(bf16[2,16,4,1440]{3,2,1,0:T(4,128)(2,1)} %innovation.1) | copy-start | bytes 1105924
  3.3 7.4 %copy-start.2 = (bf16[16,4,1440]{2,1,0:T(4,128)(2,1)S(1)}, bf16[16,4,1440]{2,1,0:T(4,128)(2,1)}, u32[]{:S(2)}) copy-start(bf16[16,4,1440]{2,1,0:T(4,128)(2,1)} %precision.1) | copy-start | bytes 552964
  3.3 7.4 %copy-start.7 = (f32[64,16]{1,0:T(8,128)S(1)}, f32[64,16]{1,0:T(8,128)}, u32[]{:S(2)}) copy-start(f32[64,16]{1,0:T(8,128)} %constant.23.clone.of_level) | copy-start | bytes 12292
  3.3 7.4 %copy-start.8 = (f32[64,64]{1,0:T(8,128)S(1)}, f32[64,64]{1,0:T(8,128)}, u32[]{:S(2)}) copy-start(f32[64,64]{1,0:T(8,128)} %constant.24.clone.same) | copy-start | bytes 49156
  3.3 23.6 %all-to-all-start = ((bf16[32,16,512]{2,1,0:T(8,128)(2,1)}), bf16[32,16,512]{2,1,0:T(8,128)(2,1)S(1)}, u32[]{:S(2)}, u32[]{:S(2)}) async-start(bf16[32,16,512]{2,1,0:T(8,128)(2,1)} %pack.1), calls=%async_computation | async-start | bytes 1048576 | tf_op jit(solution)/shard_map/all_to_all | solution.py:589
  10.6 0.7 %copy-start.10 = (f32[16,16]{1,0:T(8,128)S(1)}, f32[16,16]{1,0:T(8,128)}, u32[]{:S(2)}) copy-start(f32[16,16]{1,0:T(8,128)} %root.1) | copy-start | bytes 3076
  11.3 4.7 %copy-start.5 = (f32[256,256]{1,0:T(8,128)S(1)}, f32[256,256]{1,0:T(8,128)}, u32[]{:S(2)}) copy-start(f32[256,256]{1,0:T(8,128)} %constant.25.clone.apart) | copy-start | bytes 786436
  11.3 4.7 %copy-start.6 = (f32[256,1]{1,0:T(8,128)S(1)}, f32[256,1]{1,0:T(8,128)}, u32[]{:S(2)}) copy-start(f32[256,1]{1,0:T(8,128)} %constant.26.clone.level) | copy-start | bytes 3076
  11.3 4.7 %copy-start.11 = (f32[8]{0:T(128)S(1)}, f32[8]{0:T(128)}, u32[]{:S(2)}) copy-start(f32[8]{0:T(128)} %weight.1) | copy-start | bytes 100
  11.4 4.7 %copy-start.12 = (s32[16]{0:T(128)S(1)}, s32[16]{0:T(128)}, u32[]{:S(2)}) copy-start(s32[16]{0:T(128)} %widths.1) | copy-start | bytes 196
  11.4 6.1 %copy-start.4 = (bf16[512,256]{1,0:T(8,128)(2,1)S(1)}, bf16[512,256]{1,0:T(8,128)(2,1)}, u32[]{:S(2)}) copy-start(bf16[512,256]{1,0:T(8,128)(2,1)} %constant.27.clone.kernel) | copy-start | bytes 786436
  12.5 5.0 %copy-start = (bf16[1,2,16,4,1440]{4,3,2,1,0:T(4,128)(2,1)S(1)}, bf16[1,2,16,4,1440]{4,3,2,1,0:T(4,128)(2,1)}, u32[]{:S(2)}) copy-start(bf16[1,2,16,4,1440]{4,3,2,1,0:T(4,128)(2,1)} %ensemble.2) | copy-start | bytes 1105924
  12.5 4.9 %collective-permute-start.1 = (bf16[32,512]{1,0:T(8,128)(2,1)S(1)}, bf16[32,512]{1,0:T(8,128)(2,1)S(1)}, u32[]{:S(2)}, u32[]{:S(2)}) collective-permute-start(bf16[32,512]{1,0:T(8,128)(2,1)S(1)} %get-tuple-element.59), channel_id=1, source_target_pairs={{0,2},{1,3},{2,0},{3,1},{4,6},{5,7},{6,4},{7,5},{8,10},{9,11},{10,... | collective-permute-start | bytes 98312 | tf_op jit(solution)/shard_map/ppermute | solution.py:527
  14.3 6.5 %collective-permute-start = (bf16[32,512]{1,0:T(8,128)(2,1)S(1)}, bf16[32,512]{1,0:T(8,128)(2,1)S(1)}, u32[]{:S(2)}, u32[]{:S(2)}) collective-permute-start(bf16[32,512]{1,0:T(8,128)(2,1)S(1)} %get-tuple-element.58), channel_id=1, source_target_pairs={{0,1},{1,0},{2,3},{3,2},{4,5},{5,4},{6,7},{7,6},{8,9},{9,8},{10,11... | collective-permute-start | bytes 98312 | tf_op jit(solution)/shard_map/ppermute | solution.py:527
  15.8 5.1 %collective-permute-start.2 = (bf16[32,512]{1,0:T(8,128)(2,1)S(1)}, bf16[32,512]{1,0:T(8,128)(2,1)S(1)}, u32[]{:S(2)}, u32[]{:S(2)}) collective-permute-start(bf16[32,512]{1,0:T(8,128)(2,1)S(1)} %get-tuple-element.62), channel_id=1, source_target_pairs={{0,3},{1,2},{2,1},{3,0},{4,7},{5,6},{6,5},{7,4},{8,11},{9,10},{10,... | collective-permute-start | bytes 98312 | tf_op jit(solution)/shard_map/ppermute | solution.py:527
  17.5 9.4 %copy-start.3 = (bf16[512,512]{1,0:T(8,128)(2,1)S(1)}, bf16[512,512]{1,0:T(8,128)(2,1)}, u32[]{:S(2)}) copy-start(bf16[512,512]{1,0:T(8,128)(2,1)} %constant.28.clone.ring) | copy-start | bytes 1572868
  18.1 16.4 %collective-permute-start.6 = (bf16[64,1440]{1,0:T(8,128)(2,1)S(1)}, bf16[64,1440]{1,0:T(8,128)(2,1)S(1)}, u32[]{:S(2)}, u32[]{:S(2)}) collective-permute-start(bf16[64,1440]{1,0:T(8,128)(2,1)S(1)} %fold_smooth.1.middle), channel_id=1, source_target_pairs={{0,1},{2,3},{1,0},{3,2},{4,5},{6,7},{5,4},{7,6},{8,9},{10,11},{9,8... | collective-permute-start | bytes 552968 | tf_op jit(solution)/shard_map/ppermute | solution.py:630
  20.2 14.4 %collective-permute-start.7 = (bf16[64,1440]{1,0:T(8,128)(2,1)S(1)}, bf16[64,1440]{1,0:T(8,128)(2,1)S(1)}, u32[]{:S(2)}, u32[]{:S(2)}) collective-permute-start(bf16[64,1440]{1,0:T(8,128)(2,1)S(1)} %fold_smooth.1.middle), channel_id=1, source_target_pairs={{1,2},{2,1},{5,6},{6,5},{9,10},{10,9},{13,14},{14,13},{17,18},{18,... | collective-permute-start | bytes 552968 | tf_op jit(solution)/shard_map/ppermute | solution.py:630
  28.0 5.7 %collective-permute-start.5 = (bf16[32,384]{1,0:T(8,128)(2,1)S(1)}, bf16[32,384]{1,0:T(8,128)(2,1)S(1)}, u32[]{:S(2)}, u32[]{:S(2)}) collective-permute-start(bf16[32,384]{1,0:T(8,128)(2,1)S(1)} %get-tuple-element.66), channel_id=1, source_target_pairs={{0,24},{4,28},{8,16},{12,20},{16,8},{20,12},{24,0},{28,4},{1,25},{... | collective-permute-start | bytes 73736 | tf_op jit(solution)/shard_map/ppermute | solution.py:537
  29.6 4.7 %collective-permute-start.4 = (bf16[32,384]{1,0:T(8,128)(2,1)S(1)}, bf16[32,384]{1,0:T(8,128)(2,1)S(1)}, u32[]{:S(2)}, u32[]{:S(2)}) collective-permute-start(bf16[32,384]{1,0:T(8,128)(2,1)S(1)} %get-tuple-element.66), channel_id=1, source_target_pairs={{0,16},{4,20},{8,24},{12,28},{16,0},{20,4},{24,8},{28,12},{1,17},{... | collective-permute-start | bytes 73736 | tf_op jit(solution)/shard_map/ppermute | solution.py:537
  30.6 3.9 %collective-permute-start.3 = (bf16[32,384]{1,0:T(8,128)(2,1)S(1)}, bf16[32,384]{1,0:T(8,128)(2,1)S(1)}, u32[]{:S(2)}, u32[]{:S(2)}) collective-permute-start(bf16[32,384]{1,0:T(8,128)(2,1)S(1)} %get-tuple-element.66), channel_id=1, source_target_pairs={{0,8},{4,12},{8,0},{12,4},{16,24},{20,28},{24,16},{28,20},{1,9},{5... | collective-permute-start | bytes 73736 | tf_op jit(solution)/shard_map/ppermute | solution.py:537
  34.6 1.4 %collective-permute-start.8 = (bf16[4,32,384]{2,1,0:T(8,128)(2,1)S(1)}, bf16[4,32,384]{2,1,0:T(8,128)(2,1)S(1)}, u32[]{:S(2)}, u32[]{:S(2)}) collective-permute-start(bf16[4,32,384]{2,1,0:T(8,128)(2,1)S(1)} %pad_maximum_fusion.refs_0_), channel_id=1, source_target_pairs={{0,4},{4,0},{8,12},{12,8},{16,20},{20,16},{24,28},{28,24},{1,5},{5... | collective-permute-start | bytes 294920 | tf_op jit(solution)/shard_map/ppermute | solution.py:545
  36.9 12.6 %all-to-all-start.1 = ((bf16[32,8,384]{2,1,0:T(8,128)(2,1)}), bf16[32,8,384]{2,1,0:T(8,128)(2,1)S(1)}, u32[]{:S(2)}, u32[]{:S(2)}) async-start(bf16[32,8,384]{2,1,0:T(8,128)(2,1)} %get-tuple-element.75), calls=%async_computation.1 | async-start | bytes 393216 | tf_op jit(solution)/shard_map/all_to_all | solution.py:661
  39.9 3.8 %copy-start.9 = (f32[64,192]{1,0:T(8,128)S(1)}, f32[64,192]{1,0:T(8,128)}, u32[]{:S(2)}) copy-start(f32[64,192]{1,0:T(8,128)} %constant.29.clone.apart) | copy-start | bytes 147460
  40.2 5.5 %collective-permute-start.9 = (bf16[96,384]{1,0:T(8,128)(2,1)S(1)}, bf16[96,384]{1,0:T(8,128)(2,1)S(1)}, u32[]{:S(2)}, u32[]{:S(2)}) collective-permute-start(bf16[96,384]{1,0:T(8,128)(2,1)S(1)} %get-tuple-element.84), channel_id=1, source_target_pairs={{0,1},{1,0},{2,3},{3,2},{4,5},{5,4},{6,7},{7,6},{8,9},{9,8},{10,11... | collective-permute-start | bytes 221192 | tf_op jit(solution)/shard_map/ppermute | solution.py:527
  42.0 5.6 %collective-permute-start.10 = (bf16[96,384]{1,0:T(8,128)(2,1)S(1)}, bf16[96,384]{1,0:T(8,128)(2,1)S(1)}, u32[]{:S(2)}, u32[]{:S(2)}) collective-permute-start(bf16[96,384]{1,0:T(8,128)(2,1)S(1)} %get-tuple-element.85), channel_id=1, source_target_pairs={{0,2},{1,3},{2,0},{3,1},{4,6},{5,7},{6,4},{7,5},{8,10},{9,11},{10,... | collective-permute-start | bytes 221192 | tf_op jit(solution)/shard_map/ppermute | solution.py:527
  43.5 5.6 %collective-permute-start.11 = (bf16[96,384]{1,0:T(8,128)(2,1)S(1)}, bf16[96,384]{1,0:T(8,128)(2,1)S(1)}, u32[]{:S(2)}, u32[]{:S(2)}) collective-permute-start(bf16[96,384]{1,0:T(8,128)(2,1)S(1)} %get-tuple-element.86), channel_id=1, source_target_pairs={{0,3},{1,2},{2,1},{3,0},{4,7},{5,6},{6,5},{7,4},{8,11},{9,10},{10,... | collective-permute-start | bytes 221192 | tf_op jit(solution)/shard_map/ppermute | solution.py:527
